TPU v7x, 32 devices: a whole 2x2x4 slice. The times are simulated.
32 devices in a mesh: member: 4 (over y, core), band: 8 (over z, x).
Axes of the slice: x: 2, y: 2, z: 4, core: 2. Of those that a mesh axis runs over, the one named last changes fastest.
Arguments:
- starting_condition: bfloat16 [16, 64, 64, 1440], P('member', 'band'), may hold values from -6 to 6
- filter_kernel_tensor: bfloat16 [3, 3, 64, 64], replicated, may hold values from -0.25 to 0.25
- filter_offset_vector: float32 [64], replicated, may hold values from -3 to 3
- measured_cell_position: int32 [16384], P('band'), may hold values from 0 to 737279
- measured_slot_number: int32 [8], P('band'), may hold values from 512 to 2048, as said below
- measured_reading: float32 [16384], P('band'), may hold values from -6 to 6
- measured_precision_factor: float32 [16384], P('band'), may hold values from 0.002 to 0.02
Outputs:
- analysis: bfloat16 [16, 64, 64, 1440], P('member', 'band')
Inputs may be any that keep to these rules, and one draw needn't show every extreme that they name: `measured_slot_number`: some band has all 2048 slots live.
All inputs are finite; a program needn't handle non-finite values.
Results may differ from a plain program's by a relative error of at most 0.0071.
Values may be sent and summed in bfloat16 or wider, within the bound.
No kernel may reach another device: no remote copies, remote signals or barrier semaphores. Data moves between devices by JAX's collectives and lax.ppermute only.
A program may use at most 192 MiB of HBM per device.

v0:
```python
import functools
import jax
import jax.numpy as jnp
from jax import lax
from jax.experimental import pallas as pl
from jax.experimental.pallas import tpu as pltpu
from jax.sharding import PartitionSpec as P

STEPS = 2
NS_STEPS = 16
LANES = 128
SUB = 16
bf16 = jnp.bfloat16
f32 = jnp.float32
MB = 1024 * 1024


def round_up(value, unit):
    return -(-value // unit) * unit


def pair_matrix(kernel):
    width = kernel.shape[2]
    mats = [jnp.transpose(kernel[a], (1, 0, 2)).reshape(width, 3 * width) for a in range(3)]
    zero = jnp.zeros_like(mats[0])
    return jnp.concatenate(
        [jnp.concatenate(mats + [zero], axis=1), jnp.concatenate([zero] + mats, axis=1)], axis=0
    )


def close_circle(stack, base, width, length):
    padded = stack.shape[-1]
    last = padded - LANES
    tail = length - last
    first = stack[pl.ds(base + width, width), 0:LANES]
    end = stack[pl.ds(base + width, width), last:padded]
    lane = lax.broadcasted_iota(jnp.int32, end.shape, 1)
    end = jnp.where(lane == tail, pltpu.roll(first, tail, 1), end)
    end = jnp.where(lane == LANES - 1, pltpu.roll(end, LANES - tail, 1), end)
    stack[pl.ds(base + width, width), last:padded] = end


def shift_both(stack, base, width):
    padded = stack.shape[-1]
    center = stack[pl.ds(base + width, width), :]
    stack[pl.ds(base, width), :] = pltpu.roll(center, 1, 1)
    stack[pl.ds(base + 2 * width, width), :] = pltpu.roll(center, padded - 1, 1)


def load_row(stack, base, width, length, row):
    stack[pl.ds(base + width, width), 0:length] = row
    close_circle(stack, base, width, length)
    shift_both(stack, base, width)


def pair(stack, base, weights, bias, width, lanes):
    total = jnp.dot(
        weights[...], stack[pl.ds(base, 12 * width), lanes], preferred_element_type=f32
    )
    center = jnp.concatenate(
        [
            stack[pl.ds(base + 4 * width, width), lanes],
            stack[pl.ds(base + 7 * width, width), lanes],
        ],
        axis=0,
    ).astype(f32)
    offset = jnp.concatenate([bias[...]] * (total.shape[1] // LANES), axis=1)
    return (center + jnp.tanh(total + offset)).astype(bf16)


def spans(padded, size=256):
    return [slice(at, min(at + size, padded)) for at in range(0, padded, size)]


def write_tiles(out, row, value, at, width, length):
    full = length // LANES
    for lane in range(at, at + value.shape[1], LANES):
        tile = lane // LANES
        block = value[:, lane - at : lane - at + LANES]
        if tile < full:
            for chunk in range(width // SUB):
                out[0, row, chunk * full + tile] = block[chunk * SUB : (chunk + 1) * SUB]
        else:
            tail = length - full * LANES
            packed = block[0:SUB]
            where = lax.broadcasted_iota(jnp.int32, packed.shape, 1) // tail
            for chunk in range(1, width // SUB):
                moved = pltpu.roll(block[chunk * SUB : (chunk + 1) * SUB], chunk * tail, 1)
                packed = jnp.where(where == chunk, moved, packed)
            out[0, row, full * (width // SUB)] = packed


def two_steps(first, second, rows, weights, bias, emit, mask, width, length):
    padded = first.shape[-1]
    unit = 3 * width
    for top in range(0, rows - 2, 2):
        for lanes in spans(padded):
            value = pair(first, top * unit, weights, bias, width, lanes)
            for half in range(2):
                part = value[half * width : (half + 1) * width]
                if mask is not None:
                    part = mask(top + half, part)
                second[pl.ds((top + half) * unit + width, width), lanes] = part
        for half in range(2):
            base = (top + half) * unit
            close_circle(second, base, width, length)
            shift_both(second, base, width)
    for top in range(0, rows - 4, 2):
        for lanes in spans(padded):
            value = pair(second, top * unit, weights, bias, width, lanes)
            for half in range(2):
                emit(top + half, value[half * width : (half + 1) * width], lanes.start)


def inner_body(x, weights, bias, out, first, second, *, width, length):
    rows = x.shape[1]
    for row in range(rows):
        load_row(first, row * 3 * width, width, length, x[0, row])

    def emit(row, value, at):
        write_tiles(out, row, value, at, width, length)

    two_steps(first, second, rows, weights, bias, emit, None, width, length)


def inner(x, weights, bias, start, count):
    _, height, width, length = x.shape
    padded = round_up(length, LANES)
    tiles = width * length // (SUB * LANES)
    unit = 3 * width
    return pl.pallas_call(
        functools.partial(inner_body, width=width, length=length),
        grid=(count,),
        in_specs=[
            pl.BlockSpec((1, height, width, length), lambda m: (m + start, 0, 0, 0)),
            pl.BlockSpec(weights.shape, lambda m: (0, 0)),
            pl.BlockSpec(bias.shape, lambda m: (0, 0)),
        ],
        out_specs=pl.BlockSpec((1, height - 4, tiles, SUB, LANES), lambda m: (m, 0, 0, 0, 0)),
        out_shape=jax.ShapeDtypeStruct((count, height - 4, tiles, SUB, LANES), bf16),
        scratch_shapes=[
            pltpu.VMEM((height * unit, padded), bf16),
            pltpu.VMEM(((height - 2) * unit, padded), bf16),
        ],
        compiler_params=pltpu.CompilerParams(vmem_limit_bytes=48 * MB),
        cost_estimate=pl.CostEstimate(
            flops=2 * count * (2 * height - 6) * 12 * width * width * length,
            bytes_accessed=count * height * width * length * 3,
            transcendentals=count * (2 * height - 6) * width * length,
        ),
        name="inner_rows",
    )(x, weights, bias)


def outer_body(ends, x, low, high, weights, bias, top, bottom, first, second, *, width, length):
    unit = 3 * width
    height = x.shape[1]
    for side in range(2):
        for row in range(6):
            if side == 0:
                source = low[0, row] if row < 2 else x[0, row - 2]
            else:
                source = x[0, height - 4 + row] if row < 4 else high[0, row - 4]
            load_row(first, row * unit, width, length, source)

        def emit(row, value, at, side=side):
            write_tiles(bottom if side else top, row, value, at, width, length)

        def mask(row, value, side=side):
            if row == (0 if side == 0 else 3):
                return jnp.where(ends[side] > 0, value, jnp.zeros_like(value))
            return value

        two_steps(first, second, 6, weights, bias, emit, mask, width, length)


def outer(ends, x, low, high, weights, bias, start):
    _, height, width, length = x.shape
    count = low.shape[0]
    padded = round_up(length, LANES)
    tiles = width * length // (SUB * LANES)
    unit = 3 * width
    return pl.pallas_call(
        functools.partial(outer_body, width=width, length=length),
        grid=(count,),
        in_specs=[
            pl.BlockSpec(memory_space=pltpu.SMEM),
            pl.BlockSpec((1, height, width, length), lambda m: (m + start, 0, 0, 0)),
            pl.BlockSpec((1, 2, width, length), lambda m: (m, 0, 0, 0)),
            pl.BlockSpec((1, 2, width, length), lambda m: (m, 0, 0, 0)),
            pl.BlockSpec(weights.shape, lambda m: (0, 0)),
            pl.BlockSpec(bias.shape, lambda m: (0, 0)),
        ],
        out_specs=[pl.BlockSpec((1, 2, tiles, SUB, LANES), lambda m: (m, 0, 0, 0, 0))] * 2,
        out_shape=[jax.ShapeDtypeStruct((count, 2, tiles, SUB, LANES), bf16)] * 2,
        scratch_shapes=[
            pltpu.VMEM((6 * unit, padded), bf16),
            pltpu.VMEM((4 * unit, padded), bf16),
        ],
        compiler_params=pltpu.CompilerParams(vmem_limit_bytes=48 * MB),
        cost_estimate=pl.CostEstimate(
            flops=2 * count * 12 * 12 * width * width * length,
            bytes_accessed=count * height * width * length * 3,
            transcendentals=count * 12 * width * length,
        ),
        name="outer_rows",
    )(ends, x, low, high, weights, bias)


def gather_body(rows, chosen, *refs, members):
    blocks, (out, cells, picked) = refs[: 3 * members], refs[3 * members :]
    for member in range(members):
        at = 0
        for block in blocks[3 * member : 3 * member + 3]:
            for row in range(block.shape[1]):
                size = block.shape[2] * SUB
                cells[member, at : at + size] = (
                    block[0, row].reshape(size, LANES).astype(f32)
                )
                at += size

    slots = chosen.shape[0]
    group = 16

    @pl.loop(0, slots // group)
    def _(step):
        for inside in range(group):
            slot = step * group + inside
            row = rows[slot]
            for member in range(members):
                picked[member, pl.ds(slot, 1)] = cells[member, pl.ds(row, 1)]

    ones = jnp.ones((8, LANES), bf16)
    for member in range(members):
        single = jnp.where(chosen[...] > 0, picked[member], 0.0).astype(bf16)
        line = lax.dot_general(
            ones, single, (((1,), (1,)), ((), ())), preferred_element_type=f32
        )
        out[member] = line[0:1].astype(bf16)


def gather(rows, chosen, pieces):
    slots = chosen.shape[0]
    specs, arrays, total = [], [], 0
    for parts in pieces:
        total = 0
        for array, index in parts:
            specs.append(
                pl.BlockSpec((1,) + array.shape[1:], lambda i, index=index: (index, 0, 0, 0, 0))
            )
            arrays.append(array)
            total += array.shape[1] * array.shape[2] * SUB
    members = len(pieces)
    return pl.pallas_call(
        functools.partial(gather_body, members=members),
        grid=(1,),
        in_specs=[
            pl.BlockSpec(memory_space=pltpu.SMEM),
            pl.BlockSpec(chosen.shape, lambda i: (0, 0)),
        ]
        + specs,
        out_specs=pl.BlockSpec((members, 1, slots), lambda i: (0, 0, 0)),
        out_shape=jax.ShapeDtypeStruct((members, 1, slots), bf16),
        scratch_shapes=[
            pltpu.VMEM((members, total, LANES), f32),
            pltpu.VMEM((members, slots, LANES), f32),
        ],
        compiler_params=pltpu.CompilerParams(vmem_limit_bytes=48 * MB),
        cost_estimate=pl.CostEstimate(
            flops=members * slots * LANES * 64, bytes_accessed=members * total * LANES * 2, transcendentals=0
        ),
        name="gather_cells",
    )(rows, chosen, *arrays)


def slot_places(position, height, width, length):
    full = length // LANES
    tail = length - full * LANES
    tiles = width * length // (SUB * LANES)
    row, rest = position // (width * length), position % (width * length)
    channel, cell = rest // length, rest % length
    order = jnp.where(row < 2, row + height - 4, jnp.where(row < height - 2, row - 2, row))
    chunk, sub = channel // SUB, channel % SUB
    in_full = cell < full * LANES
    tile = jnp.where(in_full, chunk * full + cell // LANES, tiles - 1)
    lane = jnp.where(in_full, cell % LANES, chunk * tail + cell - full * LANES)
    return ((order * tiles + tile) * SUB + sub).astype(jnp.int32), lane.astype(jnp.int32)


def mix_body(weights, *refs, width, length, sources):
    blocks, out = refs[:sources], refs[-1]
    full = length // LANES
    tail = length - full * LANES
    chunks = width // SUB
    members = out.shape[0]

    def stacked(tile):
        parts = []
        for block in blocks:
            for member in range(block.shape[0]):
                parts.append(block[member, 0, tile])
        return jnp.concatenate(parts, axis=0)

    for chunk in range(chunks):
        for lane in range(0, full, 2):
            several = [stacked(chunk * full + at) for at in range(lane, min(lane + 2, full))]
            value = jnp.concatenate(several, axis=1)
            result = jnp.dot(weights[...], value, preferred_element_type=f32).astype(bf16)
            for member in range(members):
                out[
                    member,
                    0,
                    chunk * SUB : (chunk + 1) * SUB,
                    lane * LANES : lane * LANES + value.shape[1],
                ] = result[member * SUB : (member + 1) * SUB]
    result = jnp.dot(
        weights[...], stacked(full * chunks), preferred_element_type=f32
    ).astype(bf16)
    for member in range(members):
        for chunk in range(chunks):
            part = result[member * SUB : (member + 1) * SUB]
            if chunk:
                part = pltpu.roll(part, LANES - chunk * tail, 1)
            out[member, 0, chunk * SUB : (chunk + 1) * SUB, full * LANES : length] = part[:, :tail]


def mix(weights, pieces, shape, start, before):
    members, height, width, length = shape
    count = pieces[0].shape[1]
    tiles = pieces[0].shape[2]
    specs = [
        pl.BlockSpec((p.shape[0], 1, tiles, SUB, LANES), lambda r: (0, r, 0, 0, 0)) for p in pieces
    ]
    arrays = list(pieces)
    alias = {}
    if before is not None:
        specs.append(pl.BlockSpec(memory_space=pl.ANY))
        arrays.append(before)
        alias = {len(arrays): 0}
    return pl.pallas_call(
        functools.partial(mix_body, width=width, length=length, sources=len(pieces)),
        grid=(count,),
        in_specs=[pl.BlockSpec(weights.shape, lambda r: (0, 0))] + specs,
        out_specs=pl.BlockSpec((members, 1, width, length), lambda r: (0, r + start, 0, 0)),
        out_shape=jax.ShapeDtypeStruct(shape, bf16),
        input_output_aliases=alias,
        compiler_params=pltpu.CompilerParams(vmem_limit_bytes=48 * MB),
        cost_estimate=pl.CostEstimate(
            flops=2 * weights.size * count * tiles * LANES,
            bytes_accessed=count * width * length * 2 * 5 * members,
            transcendentals=0,
        ),
        name="mix_rows",
    )(weights, *arrays)


def transform(gram, drive, ensemble_vectors):
    highest = lax.Precision.HIGHEST
    eye = jnp.eye(ensemble_vectors, dtype=jnp.float32)
    system = eye + gram / (ensemble_vectors - 1.0)
    scale = jnp.trace(system)
    iterate = system / scale
    root = eye
    for number in range(NS_STEPS):
        factor = 0.5 * (3.0 * eye - jnp.dot(root, iterate, precision=highest))
        iterate = jnp.dot(iterate, factor, precision=highest)
        root = jnp.dot(factor, root, precision=highest)
    spread = root / jnp.sqrt(scale)
    inverse = jnp.dot(root, root, precision=highest)
    mean_weights = jnp.dot(inverse, drive, precision=highest) / (scale * (ensemble_vectors - 1.0))
    centering = eye - 1.0 / ensemble_vectors
    mixing = 1.0 / ensemble_vectors + jnp.dot(
        centering, mean_weights[:, None] + spread, precision=highest
    )
    return mixing.astype(jnp.bfloat16)


def halo(x, start, count):
    size = lax.axis_size("band")
    forward = [(i, i + 1) for i in range(size - 1)]
    backward = [(target, source) for source, target in forward]
    part = x[start : start + count]
    low = lax.ppermute(part[:, x.shape[1] - 2 :], "band", forward)
    high = lax.ppermute(part[:, :2], "band", backward)
    return low, high


def swap(block, bit):
    size = lax.axis_size("member")
    return lax.ppermute(block, "member", [(i, i ^ bit) for i in range(size)])


def local(
    starting_condition,
    filter_kernel_tensor,
    filter_offset_vector,
    measured_cell_position,
    measured_slot_number,
    measured_reading,
    measured_precision_factor,
):
    x = starting_condition
    members, height, width, length = x.shape
    weights = pair_matrix(filter_kernel_tensor)
    bias = jnp.broadcast_to(
        jnp.concatenate([filter_offset_vector] * 2)[:, None], (2 * width, LANES)
    )
    band = lax.axis_index("band")
    bands = lax.axis_size("band")
    ends = jnp.stack([band > 0, band < bands - 1]).astype(jnp.int32)
    rows, lanes = slot_places(measured_cell_position, height, width, length)
    chosen = (lanes[:, None] == jnp.arange(LANES, dtype=jnp.int32)[None, :]).astype(f32)

    inner_parts = [inner(x, weights, bias, 0, 1), inner(x, weights, bias, 1, members - 1)]
    half = members // 2
    halos = [halo(x, 0, half), halo(x, half, members - half)]
    tops, bottoms = [], []
    for number, (low, high) in enumerate(halos):
        top, bottom = outer(ends, x, low, high, weights, bias, number * half)
        tops.append(top)
        bottoms.append(bottom)

    def place(parts, member):
        for part in parts:
            if member < part.shape[0]:
                return part, member
            member -= part.shape[0]

    predicted = jnp.concatenate(
        [
            gather(
                rows,
                chosen,
                [
                    [place(inner_parts, m), place(tops, m), place(bottoms, m)]
                    for m in range(first, first + half)
                ],
            )
            for first in range(0, members, half)
        ],
        axis=0,
    )[:, 0]
    predicted = lax.all_gather(predicted, "member", axis=0, tiled=True).astype(f32)
    ensemble_vectors = predicted.shape[0]
    slots = jnp.arange(measured_cell_position.shape[0], dtype=jnp.int32)
    live = (slots < measured_slot_number[0]).astype(f32)
    mean = jnp.mean(predicted, axis=0)
    anomaly = predicted - mean[None, :]
    weighted = anomaly * (measured_precision_factor * live)[None, :]
    gram_part = jnp.dot(weighted, anomaly.T, precision=lax.Precision.HIGHEST)
    drive_part = jnp.dot(weighted, measured_reading - mean, precision=lax.Precision.HIGHEST)
    gram, drive = lax.psum((gram_part, drive_part), "band")
    mixing = transform(gram, drive, ensemble_vectors)

    me = lax.axis_index("member")
    owned = lax.dynamic_slice_in_dim(mixing, me * members, members, 1)
    order = jnp.concatenate(
        [jnp.arange(members, dtype=jnp.int32) + (me ^ bit) * members for bit in (0, 1, 2, 3)]
    )
    share = jnp.take(owned, order, axis=0)
    blend = (
        share.T[:, None, :, None] * jnp.eye(SUB, dtype=bf16)[None, :, None, :]
    ).reshape(members * SUB, ensemble_vectors * SUB)

    def everyone(parts):
        across = [swap(part, 2) for part in parts]
        return parts + [swap(p, 1) for p in parts] + across + [swap(p, 1) for p in across]

    inner_all, top_all, bottom_all = everyone(inner_parts), everyone(tops), everyone(bottoms)
    result = mix(blend, inner_all, x.shape, 2, None)
    result = mix(blend, top_all, x.shape, 0, result)
    return mix(blend, bottom_all, x.shape, height - 2, result)


def solution(mesh):
    return jax.shard_map(
        local,
        mesh=mesh,
        in_specs=(
            P("member", "band", None, None),
            P(),
            P(),
            P("band"),
            P("band"),
            P("band"),
            P("band"),
        ),
        out_specs=P("member", "band", None, None),
        check_vma=False,
    )
```

profile of v0, /device:TPU:0, one launch (start us, length us, event | category | flops | bytes accessed | tf_op | source)
XLA Modules:
  0.0 203.8 jit_solution(18035260969383231846)
XLA Ops:
  0.0 3.7 %fusion.63 = (bf16[2,2,64,1440]{3,2,1,0:T(8,128)(2,1)}, bf16[2,2,64,1440]{3,2,1,0:T(8,128)(2,1)}, bf16[2,2,64,1440]{3,2,1,0:T(8,128)(2,1)}, bf16[2,2,64,1440]{3,2,1,0:T(8,128)(2,1)}) fusion(bf16[4,8,64,1440]{3,2,1,0:T(8,128)(2,1)} %x.7), kind=kLoop, calls=%fused_computation.129 | loop fusion | bytes 5898240 | tf_op jit(solution)/shard_map/slice | solution.py:384
  3.7 5.7 %collective-permute-start = (bf16[2,2,64,1440]{3,2,1,0:T(8,128)(2,1)}, bf16[2,2,64,1440]{3,2,1,0:T(8,128)(2,1)}, u32[]{:S(2)}, u32[]{:S(2)}) collective-permute-start(bf16[2,2,64,1440]{3,2,1,0:T(8,128)(2,1)} %get-tuple-element.17), channel_id=1, source_target_pairs={{0,1},{1,2},{2,3},{3,4},{4,5},{5,6},{6,7},{8,9},{9,10},{10,11},{11... | collective-permute-start | bytes 2211848 | tf_op jit(solution)/shard_map/ppermute | solution.py:383
  9.4 1.3 collective-permute-start.1
  10.7 5.5 %collective-permute-start.2 = (bf16[2,2,64,1440]{3,2,1,0:T(8,128)(2,1)}, bf16[2,2,64,1440]{3,2,1,0:T(8,128)(2,1)}, u32[]{:S(2)}, u32[]{:S(2)}) collective-permute-start(bf16[2,2,64,1440]{3,2,1,0:T(8,128)(2,1)} %get-tuple-element.16), channel_id=1, source_target_pairs={{0,1},{1,2},{2,3},{3,4},{4,5},{5,6},{6,7},{8,9},{9,10},{10,11},{11... | collective-permute-start | bytes 2211848 | tf_op jit(solution)/shard_map/ppermute | solution.py:383
  16.2 1.3 collective-permute-start.3
  18.4 8.7 %inner_rows.3.refs_3_.refs_0_.refs_1_ = bf16[3,4,45,16,128]{4,3,2,1,0:T(8,128)(2,1)S(1)} custom-call(bf16[4,8,64,1440]{3,2,1,0:T(8,128)(2,1)} %x.7, bf16[128,768]{1,0:T(8,128)(2,1)S(1)} %maximum_maximum_fusion.weights, f32[128,128]{1,0:T(8,128)S(1)} %broadcast_in_dim.35.bias), custom_call_target="tpu_custom_call" | custom-call | flops 4246732800 | bytes 6635520 | tf_op jit(solution)/shard_map/inner_rows/pallas_call | solution.py:131
  27.2 1.6 collective-permute-start.19
  28.8 3.8 %inner_rows.2.refs_0_ = bf16[1,4,45,16,128]{4,3,2,1,0:T(8,128)(2,1)S(1)} custom-call(bf16[4,8,64,1440]{3,2,1,0:T(8,128)(2,1)} %x.7, bf16[128,768]{1,0:T(8,128)(2,1)S(1)} %maximum_maximum_fusion.weights, f32[128,128]{1,0:T(8,128)S(1)} %broadcast_in_dim.35.bias), custom_call_target="tpu_custom_call" | custom-call | flops 1415577600 | bytes 2211840 | tf_op jit(solution)/shard_map/inner_rows/pallas_call | solution.py:131
  33.6 0.3 fusion.17.chosen
  34.0 26.5 %collective-permute-done.low = bf16[2,2,64,1440]{3,2,1,0:T(8,128)(2,1)} collective-permute-done((bf16[2,2,64,1440]{3,2,1,0:T(8,128)(2,1)}, bf16[2,2,64,1440]{3,2,1,0:T(8,128)(2,1)}, u32[]{:S(2)}, u32[]{:S(2)}) %collective-permute-start) | collective-permute-done | bytes 737312 | tf_op jit(solution)/shard_map/ppermute | solution.py:383
  60.5 1.5 collective-permute-start.18
  62.0 8.1 %outer_rows.2 = (bf16[2,2,45,16,128]{4,3,2,1,0:T(8,128)(2,1)S(1)}, bf16[2,2,45,16,128]{4,3,2,1,0:T(8,128)(2,1)S(1)}) custom-call(s32[2]{0:T(128)S(1)} %add_convert_fusion.ends, bf16[4,8,64,1440]{3,2,1,0:T(8,128)(2,1)} %x.7, bf16[2,2,64,1440]{3,2,1,0:T(8,128)(2,1)} %collective-permute-done.low, bf16[2,2,64,1440]{3,2,1,0:T(8,128)(2,1)} %collective-permute-done.1.high, ...), custom_call_target="tpu_custom_call" | custom-call | flops 3397386240 | bytes 4423680 | tf_op jit(solution)/shard_map/outer_rows/pallas_call | solution.py:183
  70.1 4.2 %gather_cells.2 = bf16[2,1,2048]{2,1,0:T(2,128)(2,1)S(1)} custom-call(s32[2048]{0:T(1024)S(1)} %get-tuple-element.25.rows, f32[2048,128]{1,0:T(8,128)S(1)} %fusion.17.chosen, bf16[1,4,45,16,128]{4,3,2,1,0:T(8,128)(2,1)S(1)} %inner_rows.2.refs_0_, bf16[2,2,45,16,128]{4,3,2,1,0:T(8,128)(2,1)S(1)} %get-tuple-element.9.refs_1_.refs_4_.refs_0_, ...), custom_call_target="tpu_custom_call" | custom-call | flops 33554432 | bytes 2949120 | tf_op jit(solution)/shard_map/gather_cells/pallas_call | solution.py:254
  74.3 1.9 collective-permute-done.2.low
  76.2 8.3 %outer_rows.3 = (bf16[2,2,45,16,128]{4,3,2,1,0:T(8,128)(2,1)S(1)}, bf16[2,2,45,16,128]{4,3,2,1,0:T(8,128)(2,1)S(1)}) custom-call(s32[2]{0:T(128)S(1)} %add_convert_fusion.ends, bf16[4,8,64,1440]{3,2,1,0:T(8,128)(2,1)} %x.7, bf16[2,2,64,1440]{3,2,1,0:T(8,128)(2,1)} %collective-permute-done.2.low, bf16[2,2,64,1440]{3,2,1,0:T(8,128)(2,1)} %collective-permute-done.3.high, ...), custom_call_target="tpu_custom_call" | custom-call | flops 3397386240 | bytes 4423680 | tf_op jit(solution)/shard_map/outer_rows/pallas_call | solution.py:183
  84.5 4.2 %gather_cells.3 = bf16[2,1,2048]{2,1,0:T(2,128)(2,1)S(1)} custom-call(s32[2048]{0:T(1024)S(1)} %get-tuple-element.25.rows, f32[2048,128]{1,0:T(8,128)S(1)} %fusion.17.chosen, bf16[3,4,45,16,128]{4,3,2,1,0:T(8,128)(2,1)S(1)} %inner_rows.3.refs_3_.refs_0_.refs_1_, bf16[2,2,45,16,128]{4,3,2,1,0:T(8,128)(2,1)S(1)} %get-tuple-element.11.refs_1_.refs_4_, ...), custom_call_target="tpu_custom_call" | custom-call | flops 33554432 | bytes 2949120 | tf_op jit(solution)/shard_map/gather_cells/pallas_call | solution.py:254
  88.8 5.4 %all-gather = bf16[16,1,2048]{2,1,0:T(2,128)(2,1)S(1)} all-gather(bf16[4,1,2048]{2,1,0:T(2,128)(2,1)S(1)} %pad_maximum_fusion), channel_id=2, replica_groups=mesh['member'=4,'band'=8] {'member'}, dimensions={0}, use_global_device_ids=true | all-gather | bytes 81920 | tf_op jit(solution)/shard_map/all_gather | solution.py:443
  94.5 0.3 fusion.19
  94.8 0.3 convolution_bitcast_fusion.1
  95.1 22.4 %all-reduce = (f32[16,16]{1,0:T(8,128)S(1)}, f32[16]{0:T(128)S(1)}) all-reduce(f32[16,16]{1,0:T(8,128)S(1)} %fusion.19, f32[16]{0:T(128)S(1)} %convolution_bitcast_fusion.1), channel_id=1, replica_groups=mesh['member'=4,'band'=8] {'band'}, use_global_device_ids=true, to_apply=%region_1.2 | all-reduce | flops 272 | bytes 2176 | tf_op jit(solution)/shard_map/psum | solution.py:452
  117.5 0.7 select_reduce_fusion
  118.2 0.8 fusion.15
  119.0 0.8 fusion.50
  119.9 0.1 fusion.14
  120.0 0.1 fusion.65
  120.3 0.1 fusion.13
  120.5 0.1 fusion.67
  120.7 0.1 fusion.12
  120.9 0.1 fusion.69
  121.2 0.1 fusion.11
  121.3 0.1 fusion.71
  121.6 0.1 fusion.10
  121.7 0.1 fusion.73
  122.0 0.1 fusion.9
  122.1 0.1 fusion.75
  122.4 0.1 fusion.8
  122.5 0.1 fusion.77
  122.8 1.5 collective-permute-start.12
  124.8 0.1 fusion.6
  125.4 0.1 fusion.83
  125.6 0.1 fusion.4
  126.1 0.1 fusion.3
  126.5 0.5 collective-permute-start.21
  127.3 0.6 collective-permute-start.13
  127.8 0.9 copy-done.8
  128.7 13.9 %collective-permute-done.12.refs_4_ = bf16[2,2,45,16,128]{4,3,2,1,0:T(8,128)(2,1)} collective-permute-done((bf16[2,2,45,16,128]{4,3,2,1,0:T(8,128)(2,1)}, bf16[2,2,45,16,128]{4,3,2,1,0:T(8,128)(2,1)}, u32[]{:S(2)}, u32[]{:S(2)}) %collective-permute-start.12) | collective-permute-done | bytes 737312 | tf_op jit(solution)/shard_map/ppermute | solution.py:390
  142.8 0.1 fusion.91
  143.1 12.2 %collective-permute-done.13.refs_5_ = bf16[2,2,45,16,128]{4,3,2,1,0:T(8,128)(2,1)} collective-permute-done((bf16[2,2,45,16,128]{4,3,2,1,0:T(8,128)(2,1)}, bf16[2,2,45,16,128]{4,3,2,1,0:T(8,128)(2,1)}, u32[]{:S(2)}, u32[]{:S(2)}) %collective-permute-start.13) | collective-permute-done | bytes 737312 | tf_op jit(solution)/shard_map/ppermute | solution.py:390
  155.3 1.5 collective-permute-start.6
  156.8 0.9 copy-done.10
  157.7 0.5 collective-permute-start.7
  158.2 0.9 copy-done.12
  160.9 0.1 fusion.16
  161.0 14.0 %collective-permute-done.6.refs_4_ = bf16[2,2,45,16,128]{4,3,2,1,0:T(8,128)(2,1)} collective-permute-done((bf16[2,2,45,16,128]{4,3,2,1,0:T(8,128)(2,1)}, bf16[2,2,45,16,128]{4,3,2,1,0:T(8,128)(2,1)}, u32[]{:S(2)}, u32[]{:S(2)}) %collective-permute-start.6) | collective-permute-done | bytes 737312 | tf_op jit(solution)/shard_map/ppermute | solution.py:390
  175.0 10.5 %collective-permute-done.7.refs_5_ = bf16[2,2,45,16,128]{4,3,2,1,0:T(8,128)(2,1)} collective-permute-done((bf16[2,2,45,16,128]{4,3,2,1,0:T(8,128)(2,1)}, bf16[2,2,45,16,128]{4,3,2,1,0:T(8,128)(2,1)}, u32[]{:S(2)}, u32[]{:S(2)}) %collective-permute-start.7) | collective-permute-done | bytes 737312 | tf_op jit(solution)/shard_map/ppermute | solution.py:390
  185.5 0.5 collective-permute-start.15
  186.1 0.4 collective-permute-start.9
  186.6 0.3 fusion.25
  186.9 0.6 gather_fusion
  187.8 0.2 mul.197.weights
  188.0 1.1 copy-done.9
  189.2 6.8 %mix_rows.3.refs_8_ = bf16[4,8,64,1440]{3,2,1,0:T(8,128)(2,1)} custom-call(bf16[64,256]{1,0:T(8,128)(2,1)S(1)} %mul.197.weights, bf16[1,4,45,16,128]{4,3,2,1,0:T(8,128)(2,1)S(1)} %inner_rows.2.refs_0_, bf16[3,4,45,16,128]{4,3,2,1,0:T(8,128)(2,1)S(1)} %inner_rows.3.refs_3_.refs_0_.refs_1_, bf16[1,4,45,16,128]{4,3,2,1,0:T(8,128)(2,1)} %collective-permute-done.16.refs_2_, ...), custom_call_target="tpu_custom_call" | custom-call | flops 754974720 | bytes 14745600 | tf_op jit(solution)/shard_map/mix_rows/pallas_call | solution.py:340
  196.0 3.9 %mix_rows.4.refs_8_ = bf16[4,8,64,1440]{3,2,1,0:T(8,128)(2,1)} custom-call(bf16[64,256]{1,0:T(8,128)(2,1)S(1)} %mul.197.weights, bf16[2,2,45,16,128]{4,3,2,1,0:T(8,128)(2,1)S(1)} %copy-done.5, bf16[2,2,45,16,128]{4,3,2,1,0:T(8,128)(2,1)S(1)} %copy-done.7, bf16[2,2,45,16,128]{4,3,2,1,0:T(8,128)(2,1)S(1)} %copy-done.11, ...), custom_call_target="tpu_custom_call", output_to_operand_aliasing={{}: (9, {})} | custom-call | flops 377487360 | bytes 7372800 | tf_op jit(solution)/shard_map/mix_rows/pallas_call | solution.py:340
  199.9 3.9 %mix_rows.5 = bf16[4,8,64,1440]{3,2,1,0:T(8,128)(2,1)} custom-call(bf16[64,256]{1,0:T(8,128)(2,1)S(1)} %mul.197.weights, bf16[2,2,45,16,128]{4,3,2,1,0:T(8,128)(2,1)S(1)} %copy-done.1, bf16[2,2,45,16,128]{4,3,2,1,0:T(8,128)(2,1)S(1)} %copy-done.3, bf16[2,2,45,16,128]{4,3,2,1,0:T(8,128)(2,1)} %collective-permute-done.4.refs_2_, ...), custom_call_target="tpu_custom_call", output_to_operand_aliasing={{}: (9, {})} | custom-call | flops 377487360 | bytes 7372800 | tf_op jit(solution)/shard_map/mix_rows/pallas_call | solution.py:340
  (117 shorter events, 5.7 us)
Async XLA Ops:
  0.0 17.5 %copy-start.14 = (bf16[3,3,64,64]{3,2,1,0:T(8,128)(2,1)S(1)}, bf16[3,3,64,64]{3,2,1,0:T(8,128)(2,1)}, u32[]{:S(2)}) copy-start(bf16[3,3,64,64]{3,2,1,0:T(8,128)(2,1)} %param.8) | copy-start | bytes 221188
  0.0 18.1 %copy-start.18 = (f32[64]{0:T(128)S(1)}, f32[64]{0:T(128)}, u32[]{:S(2)}) copy-start(f32[64]{0:T(128)} %param.9) | copy-start | bytes 772
  3.7 56.8 %collective-permute-start = (bf16[2,2,64,1440]{3,2,1,0:T(8,128)(2,1)}, bf16[2,2,64,1440]{3,2,1,0:T(8,128)(2,1)}, u32[]{:S(2)}, u32[]{:S(2)}) collective-permute-start(bf16[2,2,64,1440]{3,2,1,0:T(8,128)(2,1)} %get-tuple-element.17), channel_id=1, source_target_pairs={{0,1},{1,2},{2,3},{3,4},{4,5},{5,6},{6,7},{8,9},{9,10},{10,11},{11... | collective-permute-start | bytes 2211848 | tf_op jit(solution)/shard_map/ppermute | solution.py:383
  9.4 51.1 %collective-permute-start.1 = (bf16[2,2,64,1440]{3,2,1,0:T(8,128)(2,1)}, bf16[2,2,64,1440]{3,2,1,0:T(8,128)(2,1)}, u32[]{:S(2)}, u32[]{:S(2)}) collective-permute-start(bf16[2,2,64,1440]{3,2,1,0:T(8,128)(2,1)} %get-tuple-element.15), channel_id=1, source_target_pairs={{1,0},{2,1},{3,2},{4,3},{5,4},{6,5},{7,6},{9,8},{10,9},{11,10},{12... | collective-permute-start | bytes 2211848 | tf_op jit(solution)/shard_map/ppermute | solution.py:384
  10.7 65.5 %collective-permute-start.2 = (bf16[2,2,64,1440]{3,2,1,0:T(8,128)(2,1)}, bf16[2,2,64,1440]{3,2,1,0:T(8,128)(2,1)}, u32[]{:S(2)}, u32[]{:S(2)}) collective-permute-start(bf16[2,2,64,1440]{3,2,1,0:T(8,128)(2,1)} %get-tuple-element.16), channel_id=1, source_target_pairs={{0,1},{1,2},{2,3},{3,4},{4,5},{5,6},{6,7},{8,9},{9,10},{10,11},{11... | collective-permute-start | bytes 2211848 | tf_op jit(solution)/shard_map/ppermute | solution.py:383
  16.2 60.0 %collective-permute-start.3 = (bf16[2,2,64,1440]{3,2,1,0:T(8,128)(2,1)}, bf16[2,2,64,1440]{3,2,1,0:T(8,128)(2,1)}, u32[]{:S(2)}, u32[]{:S(2)}) collective-permute-start(bf16[2,2,64,1440]{3,2,1,0:T(8,128)(2,1)} %get-tuple-element.18), channel_id=1, source_target_pairs={{1,0},{2,1},{3,2},{4,3},{5,4},{6,5},{7,6},{9,8},{10,9},{11,10},{12... | collective-permute-start | bytes 2211848 | tf_op jit(solution)/shard_map/ppermute | solution.py:384
  27.1 6.3 %copy-start.16 = (f32[2048]{0:T(1024)S(1)}, f32[2048]{0:T(1024)}, u32[]{:S(2)}) copy-start(f32[2048]{0:T(1024)} %param.13) | copy-start | bytes 24580
  27.2 6.4 %copy-start.15 = (s32[2048]{0:T(1024)S(1)}, s32[2048]{0:T(1024)}, u32[]{:S(2)}) copy-start(s32[2048]{0:T(1024)} %param.10) | copy-start | bytes 24580
  27.2 99.3 %collective-permute-start.19 = (bf16[3,4,45,16,128]{4,3,2,1,0:T(8,128)(2,1)S(1)}, bf16[3,4,45,16,128]{4,3,2,1,0:T(8,128)(2,1)}, u32[]{:S(2)}, u32[]{:S(2)}) collective-permute-start(bf16[3,4,45,16,128]{4,3,2,1,0:T(8,128)(2,1)S(1)} %inner_rows.3.refs_3_.refs_0_.refs_1_), channel_id=1, source_target_pairs={{0,16},{8,24},{16,0},{24,8},{1,17},{9,25},{17,1},{25,9},{2,18},{10... | collective-permute-start | bytes 6635528 | tf_op jit(solution)/shard_map/ppermute | solution.py:390
  60.5 125.0 %collective-permute-start.17 = (bf16[3,4,45,16,128]{4,3,2,1,0:T(8,128)(2,1)S(1)}, bf16[3,4,45,16,128]{4,3,2,1,0:T(8,128)(2,1)}, u32[]{:S(2)}, u32[]{:S(2)}) collective-permute-start(bf16[3,4,45,16,128]{4,3,2,1,0:T(8,128)(2,1)S(1)} %inner_rows.3.refs_3_.refs_0_.refs_1_), channel_id=1, source_target_pairs={{0,8},{8,0},{16,24},{24,16},{1,9},{9,1},{17,25},{25,17},{2,10},{10... | collective-permute-start | bytes 6635528 | tf_op jit(solution)/shard_map/ppermute | solution.py:390
  60.5 64.5 %collective-permute-start.18 = (bf16[1,4,45,16,128]{4,3,2,1,0:T(8,128)(2,1)S(1)}, bf16[1,4,45,16,128]{4,3,2,1,0:T(8,128)(2,1)}, u32[]{:S(2)}, u32[]{:S(2)}) collective-permute-start(bf16[1,4,45,16,128]{4,3,2,1,0:T(8,128)(2,1)S(1)} %inner_rows.2.refs_0_), channel_id=1, source_target_pairs={{0,16},{8,24},{16,0},{24,8},{1,17},{9,25},{17,1},{25,9},{2,18},{10... | collective-permute-start | bytes 2211848 | tf_op jit(solution)/shard_map/ppermute | solution.py:390
  70.1 4.2 %copy-start = (bf16[2,2,45,16,128]{4,3,2,1,0:T(8,128)(2,1)}, bf16[2,2,45,16,128]{4,3,2,1,0:T(8,128)(2,1)S(1)}, u32[]{:S(2)}) copy-start(bf16[2,2,45,16,128]{4,3,2,1,0:T(8,128)(2,1)S(1)} %get-tuple-element.10.refs_2_.refs_5_.refs_0_) | copy-start | bytes 2211844
  70.1 6.1 %copy-start.4 = (bf16[2,2,45,16,128]{4,3,2,1,0:T(8,128)(2,1)}, bf16[2,2,45,16,128]{4,3,2,1,0:T(8,128)(2,1)S(1)}, u32[]{:S(2)}) copy-start(bf16[2,2,45,16,128]{4,3,2,1,0:T(8,128)(2,1)S(1)} %get-tuple-element.9.refs_1_.refs_4_.refs_0_) | copy-start | bytes 2211844
  76.2 51.1 %collective-permute-start.16 = (bf16[1,4,45,16,128]{4,3,2,1,0:T(8,128)(2,1)S(1)}, bf16[1,4,45,16,128]{4,3,2,1,0:T(8,128)(2,1)}, u32[]{:S(2)}, u32[]{:S(2)}) collective-permute-start(bf16[1,4,45,16,128]{4,3,2,1,0:T(8,128)(2,1)S(1)} %inner_rows.2.refs_0_), channel_id=1, source_target_pairs={{0,8},{8,0},{16,24},{24,16},{1,9},{9,1},{17,25},{25,17},{2,10},{10... | collective-permute-start | bytes 2211848 | tf_op jit(solution)/shard_map/ppermute | solution.py:390
  84.5 4.2 %copy-start.2 = (bf16[2,2,45,16,128]{4,3,2,1,0:T(8,128)(2,1)}, bf16[2,2,45,16,128]{4,3,2,1,0:T(8,128)(2,1)S(1)}, u32[]{:S(2)}) copy-start(bf16[2,2,45,16,128]{4,3,2,1,0:T(8,128)(2,1)S(1)} %get-tuple-element.12.refs_2_.refs_5_.refs_1_) | copy-start | bytes 2211844
  84.5 4.3 %copy-start.6 = (bf16[2,2,45,16,128]{4,3,2,1,0:T(8,128)(2,1)}, bf16[2,2,45,16,128]{4,3,2,1,0:T(8,128)(2,1)S(1)}, u32[]{:S(2)}) copy-start(bf16[2,2,45,16,128]{4,3,2,1,0:T(8,128)(2,1)S(1)} %get-tuple-element.11.refs_1_.refs_4_) | copy-start | bytes 2211844
  84.5 10.0 %copy-start.17 = (f32[2048]{0:T(1024)S(1)}, f32[2048]{0:T(1024)}, u32[]{:S(2)}) copy-start(f32[2048]{0:T(1024)} %param.12) | copy-start | bytes 24580
  122.8 19.8 %collective-permute-start.12 = (bf16[2,2,45,16,128]{4,3,2,1,0:T(8,128)(2,1)}, bf16[2,2,45,16,128]{4,3,2,1,0:T(8,128)(2,1)}, u32[]{:S(2)}, u32[]{:S(2)}) collective-permute-start(bf16[2,2,45,16,128]{4,3,2,1,0:T(8,128)(2,1)} %copy-done.4), channel_id=1, source_target_pairs={{0,16},{8,24},{16,0},{24,8},{1,17},{9,25},{17,1},{25,9},{2,18},{10... | collective-permute-start | bytes 2211848 | tf_op jit(solution)/shard_map/ppermute | solution.py:390
  125.0 2.8 %collective-permute-start.20 = (bf16[1,4,45,16,128]{4,3,2,1,0:T(8,128)(2,1)}, bf16[1,4,45,16,128]{4,3,2,1,0:T(8,128)(2,1)S(1)}, u32[]{:S(2)}, u32[]{:S(2)}) collective-permute-start(bf16[1,4,45,16,128]{4,3,2,1,0:T(8,128)(2,1)} %collective-permute-done.18.refs_4_), channel_id=1, source_target_pairs={{0,8},{8,0},{16,24},{24,16},{1,9},{9,1},{17,25},{25,17},{2,10},{10... | collective-permute-start | bytes 2211848 | tf_op jit(solution)/shard_map/ppermute | solution.py:390
  126.5 59.7 %collective-permute-start.21 = (bf16[3,4,45,16,128]{4,3,2,1,0:T(8,128)(2,1)}, bf16[3,4,45,16,128]{4,3,2,1,0:T(8,128)(2,1)}, u32[]{:S(2)}, u32[]{:S(2)}) collective-permute-start(bf16[3,4,45,16,128]{4,3,2,1,0:T(8,128)(2,1)} %collective-permute-done.19.refs_5_), channel_id=1, source_target_pairs={{0,8},{8,0},{16,24},{24,16},{1,9},{9,1},{17,25},{25,17},{2,10},{10... | collective-permute-start | bytes 6635528 | tf_op jit(solution)/shard_map/ppermute | solution.py:390
  127.3 28.0 %collective-permute-start.13 = (bf16[2,2,45,16,128]{4,3,2,1,0:T(8,128)(2,1)}, bf16[2,2,45,16,128]{4,3,2,1,0:T(8,128)(2,1)}, u32[]{:S(2)}, u32[]{:S(2)}) collective-permute-start(bf16[2,2,45,16,128]{4,3,2,1,0:T(8,128)(2,1)} %copy-done.6), channel_id=1, source_target_pairs={{0,16},{8,24},{16,0},{24,8},{1,17},{9,25},{17,1},{25,9},{2,18},{10... | collective-permute-start | bytes 2211848 | tf_op jit(solution)/shard_map/ppermute | solution.py:390
  127.8 0.9 copy-start.8
  128.7 28.1 %collective-permute-start.10 = (bf16[2,2,45,16,128]{4,3,2,1,0:T(8,128)(2,1)}, bf16[2,2,45,16,128]{4,3,2,1,0:T(8,128)(2,1)S(1)}, u32[]{:S(2)}, u32[]{:S(2)}) collective-permute-start(bf16[2,2,45,16,128]{4,3,2,1,0:T(8,128)(2,1)} %copy-done.4), channel_id=1, source_target_pairs={{0,8},{8,0},{16,24},{24,16},{1,9},{9,1},{17,25},{25,17},{2,10},{10... | collective-permute-start | bytes 2211848 | tf_op jit(solution)/shard_map/ppermute | solution.py:390
  142.6 15.6 %collective-permute-start.11 = (bf16[2,2,45,16,128]{4,3,2,1,0:T(8,128)(2,1)}, bf16[2,2,45,16,128]{4,3,2,1,0:T(8,128)(2,1)S(1)}, u32[]{:S(2)}, u32[]{:S(2)}) collective-permute-start(bf16[2,2,45,16,128]{4,3,2,1,0:T(8,128)(2,1)} %copy-done.6), channel_id=1, source_target_pairs={{0,8},{8,0},{16,24},{24,16},{1,9},{9,1},{17,25},{25,17},{2,10},{10... | collective-permute-start | bytes 2211848 | tf_op jit(solution)/shard_map/ppermute | solution.py:390
  155.3 19.7 %collective-permute-start.6 = (bf16[2,2,45,16,128]{4,3,2,1,0:T(8,128)(2,1)}, bf16[2,2,45,16,128]{4,3,2,1,0:T(8,128)(2,1)}, u32[]{:S(2)}, u32[]{:S(2)}) collective-permute-start(bf16[2,2,45,16,128]{4,3,2,1,0:T(8,128)(2,1)} %copy-done), channel_id=1, source_target_pairs={{0,16},{8,24},{16,0},{24,8},{1,17},{9,25},{17,1},{25,9},{2,18},{10... | collective-permute-start | bytes 2211848 | tf_op jit(solution)/shard_map/ppermute | solution.py:390
  156.8 0.9 copy-start.10
  157.7 27.8 %collective-permute-start.7 = (bf16[2,2,45,16,128]{4,3,2,1,0:T(8,128)(2,1)}, bf16[2,2,45,16,128]{4,3,2,1,0:T(8,128)(2,1)}, u32[]{:S(2)}, u32[]{:S(2)}) collective-permute-start(bf16[2,2,45,16,128]{4,3,2,1,0:T(8,128)(2,1)} %copy-done.2), channel_id=1, source_target_pairs={{0,16},{8,24},{16,0},{24,8},{1,17},{9,25},{17,1},{25,9},{2,18},{10... | collective-permute-start | bytes 2211848 | tf_op jit(solution)/shard_map/ppermute | solution.py:390
  158.2 0.9 copy-start.12
  159.1 27.0 %collective-permute-start.14 = (bf16[2,2,45,16,128]{4,3,2,1,0:T(8,128)(2,1)}, bf16[2,2,45,16,128]{4,3,2,1,0:T(8,128)(2,1)}, u32[]{:S(2)}, u32[]{:S(2)}) collective-permute-start(bf16[2,2,45,16,128]{4,3,2,1,0:T(8,128)(2,1)} %collective-permute-done.12.refs_4_), channel_id=1, source_target_pairs={{0,8},{8,0},{16,24},{24,16},{1,9},{9,1},{17,25},{25,17},{2,10},{10... | collective-permute-start | bytes 2211848 | tf_op jit(solution)/shard_map/ppermute | solution.py:390
  175.0 24.8 %collective-permute-start.4 = (bf16[2,2,45,16,128]{4,3,2,1,0:T(8,128)(2,1)}, bf16[2,2,45,16,128]{4,3,2,1,0:T(8,128)(2,1)}, u32[]{:S(2)}, u32[]{:S(2)}) collective-permute-start(bf16[2,2,45,16,128]{4,3,2,1,0:T(8,128)(2,1)} %copy-done), channel_id=1, source_target_pairs={{0,8},{8,0},{16,24},{24,16},{1,9},{9,1},{17,25},{25,17},{2,10},{10... | collective-permute-start | bytes 2211848 | tf_op jit(solution)/shard_map/ppermute | solution.py:390
  185.5 14.3 %collective-permute-start.5 = (bf16[2,2,45,16,128]{4,3,2,1,0:T(8,128)(2,1)}, bf16[2,2,45,16,128]{4,3,2,1,0:T(8,128)(2,1)}, u32[]{:S(2)}, u32[]{:S(2)}) collective-permute-start(bf16[2,2,45,16,128]{4,3,2,1,0:T(8,128)(2,1)} %copy-done.2), channel_id=1, source_target_pairs={{0,8},{8,0},{16,24},{24,16},{1,9},{9,1},{17,25},{25,17},{2,10},{10... | collective-permute-start | bytes 2211848 | tf_op jit(solution)/shard_map/ppermute | solution.py:390
  185.5 10.4 %collective-permute-start.15 = (bf16[2,2,45,16,128]{4,3,2,1,0:T(8,128)(2,1)}, bf16[2,2,45,16,128]{4,3,2,1,0:T(8,128)(2,1)}, u32[]{:S(2)}, u32[]{:S(2)}) collective-permute-start(bf16[2,2,45,16,128]{4,3,2,1,0:T(8,128)(2,1)} %collective-permute-done.13.refs_5_), channel_id=1, source_target_pairs={{0,8},{8,0},{16,24},{24,16},{1,9},{9,1},{17,25},{25,17},{2,10},{10... | collective-permute-start | bytes 2211848 | tf_op jit(solution)/shard_map/ppermute | solution.py:390
  186.0 13.8 %collective-permute-start.8 = (bf16[2,2,45,16,128]{4,3,2,1,0:T(8,128)(2,1)}, bf16[2,2,45,16,128]{4,3,2,1,0:T(8,128)(2,1)}, u32[]{:S(2)}, u32[]{:S(2)}) collective-permute-start(bf16[2,2,45,16,128]{4,3,2,1,0:T(8,128)(2,1)} %collective-permute-done.6.refs_4_), channel_id=1, source_target_pairs={{0,8},{8,0},{16,24},{24,16},{1,9},{9,1},{17,25},{25,17},{2,10},{10... | collective-permute-start | bytes 2211848 | tf_op jit(solution)/shard_map/ppermute | solution.py:390
  186.1 13.8 %collective-permute-start.9 = (bf16[2,2,45,16,128]{4,3,2,1,0:T(8,128)(2,1)}, bf16[2,2,45,16,128]{4,3,2,1,0:T(8,128)(2,1)}, u32[]{:S(2)}, u32[]{:S(2)}) collective-permute-start(bf16[2,2,45,16,128]{4,3,2,1,0:T(8,128)(2,1)} %collective-permute-done.7.refs_5_), channel_id=1, source_target_pairs={{0,8},{8,0},{16,24},{24,16},{1,9},{9,1},{17,25},{25,17},{2,10},{10... | collective-permute-start | bytes 2211848 | tf_op jit(solution)/shard_map/ppermute | solution.py:390
  188.0 1.1 copy-start.9
  189.2 6.8 %copy-start.5 = (bf16[2,2,45,16,128]{4,3,2,1,0:T(8,128)(2,1)S(1)}, bf16[2,2,45,16,128]{4,3,2,1,0:T(8,128)(2,1)}, u32[]{:S(2)}) copy-start(bf16[2,2,45,16,128]{4,3,2,1,0:T(8,128)(2,1)} %copy-done.4) | copy-start | bytes 2211844
  189.2 6.8 %copy-start.7 = (bf16[2,2,45,16,128]{4,3,2,1,0:T(8,128)(2,1)S(1)}, bf16[2,2,45,16,128]{4,3,2,1,0:T(8,128)(2,1)}, u32[]{:S(2)}) copy-start(bf16[2,2,45,16,128]{4,3,2,1,0:T(8,128)(2,1)} %copy-done.6) | copy-start | bytes 2211844
  189.2 6.8 %copy-start.11 = (bf16[2,2,45,16,128]{4,3,2,1,0:T(8,128)(2,1)S(1)}, bf16[2,2,45,16,128]{4,3,2,1,0:T(8,128)(2,1)}, u32[]{:S(2)}) copy-start(bf16[2,2,45,16,128]{4,3,2,1,0:T(8,128)(2,1)} %copy-done.10) | copy-start | bytes 2211844
  189.2 6.8 %copy-start.13 = (bf16[2,2,45,16,128]{4,3,2,1,0:T(8,128)(2,1)S(1)}, bf16[2,2,45,16,128]{4,3,2,1,0:T(8,128)(2,1)}, u32[]{:S(2)}) copy-start(bf16[2,2,45,16,128]{4,3,2,1,0:T(8,128)(2,1)} %copy-done.12) | copy-start | bytes 2211844
  195.9 4.0 %copy-start.1 = (bf16[2,2,45,16,128]{4,3,2,1,0:T(8,128)(2,1)S(1)}, bf16[2,2,45,16,128]{4,3,2,1,0:T(8,128)(2,1)}, u32[]{:S(2)}) copy-start(bf16[2,2,45,16,128]{4,3,2,1,0:T(8,128)(2,1)} %copy-done) | copy-start | bytes 2211844
  195.9 4.0 %copy-start.3 = (bf16[2,2,45,16,128]{4,3,2,1,0:T(8,128)(2,1)S(1)}, bf16[2,2,45,16,128]{4,3,2,1,0:T(8,128)(2,1)}, u32[]{:S(2)}) copy-start(bf16[2,2,45,16,128]{4,3,2,1,0:T(8,128)(2,1)} %copy-done.2) | copy-start | bytes 2211844
where the time goes:
time: 204 us
  waiting for transfers between devices  79 us (39%)
  Pallas kernels  51.9 us (25%)
  blocking collectives  27.8 us (14%)
  starting transfers between devices  22.6 us (11%)
  local copies, waits for them, and re-layouts  9.16 us (4%)
  matrix products  8.84 us (4%)
  between operations  2.52 us (1%)
    ppermute x18, waiting for transfers between devices, swap(): return lax.ppermute(block, 'member', [(i, i ^ bit) for i in range(size)])  50.6 us
    ppermute x2, waiting for transfers between devices, halo(): low = lax.ppermute(part[:, x.shape[1] - 2:], 'band', forward)  28.4 us
    psum x1, blocking collectives, local(): gram, drive = lax.psum((gram_part, drive_part), 'band')  22.4 us
    pallas_call x2, Pallas kernels, outer(): pl.pallas_call(functools.partial(outer_body, width=width, length=length),...  16.4 us
    pallas_call x3, Pallas kernels, mix(): pl.pallas_call(functools.partial(mix_body, width=width, length=length, so...  14.5 us
    pallas_call x2, Pallas kernels, inner(): pl.pallas_call(functools.partial(inner_body, width=width, length=length),...  12.6 us
    ppermute x2, starting transfers between devices, halo(): low = lax.ppermute(part[:, x.shape[1] - 2:], 'band', forward)  11.2 us
    ppermute x18, starting transfers between devices, swap(): return lax.ppermute(block, 'member', [(i, i ^ bit) for i in range(size)])  8.85 us
  transfers between devices with their start and end apart: 22, of which 6 were waited for; matrix products, arithmetic and copies ran while one was open for 6% of the time, Pallas kernels for 24%

commit v1 on v0

--- a/solution.py
+++ b/solution.py
@@ -13,19 +13,20 @@
 bf16 = jnp.bfloat16
 f32 = jnp.float32
 MB = 1024 * 1024
+SMALL = pl.CostEstimate(flops=200_000_000, bytes_accessed=500_000, transcendentals=0)
 
 
 def round_up(value, unit):
     return -(-value // unit) * unit
 
 
-def pair_matrix(kernel):
-    width = kernel.shape[2]
-    mats = [jnp.transpose(kernel[a], (1, 0, 2)).reshape(width, 3 * width) for a in range(3)]
-    zero = jnp.zeros_like(mats[0])
-    return jnp.concatenate(
-        [jnp.concatenate(mats + [zero], axis=1), jnp.concatenate([zero] + mats, axis=1)], axis=0
-    )
+def pair_matrix(kernel, weights, width):
+    weights[...] = jnp.zeros_like(weights)
+    for row in range(2):
+        for a in range(3):
+            for b in range(3):
+                at = ((row + a) * 3 + b) * width
+                weights[row * width : (row + 1) * width, at : at + width] = kernel[a, b]
 
 
 def close_circle(stack, base, width, length):
@@ -112,7 +113,7 @@
                 emit(top + half, value[half * width : (half + 1) * width], lanes.start)
 
 
-def inner_body(x, weights, bias, out, first, second, *, width, length):
+def inner_rows(x, weights, bias, out, first, second, width, length):
     rows = x.shape[1]
     for row in range(rows):
         load_row(first, row * 3 * width, width, length, x[0, row])
@@ -121,6 +122,15 @@
         write_tiles(out, row, value, at, width, length)
 
     two_steps(first, second, rows, weights, bias, emit, None, width, length)
+
+
+def inner_body(x, weights, bias, out, first, second, *, width, length):
+    inner_rows(x, weights, bias, out, first, second, width, length)
+
+
+def opening_body(x, kernel, bias, out, weights, first, second, *, width, length):
+    pair_matrix(kernel, weights, width)
+    inner_rows(x, weights, bias, out, first, second, width, length)
 
 
 def inner(x, weights, bias, start, count):
@@ -128,31 +138,56 @@
     padded = round_up(length, LANES)
     tiles = width * length // (SUB * LANES)
     unit = 3 * width
-    return pl.pallas_call(
-        functools.partial(inner_body, width=width, length=length),
+    opening = weights.ndim == 4
+    out_specs = [pl.BlockSpec((1, height - 4, tiles, SUB, LANES), lambda m: (m, 0, 0, 0, 0))]
+    out_shape = [jax.ShapeDtypeStruct((count, height - 4, tiles, SUB, LANES), bf16)]
+    if opening:
+        out_specs.append(pl.BlockSpec((2 * width, 4 * unit), lambda m: (0, 0)))
+        out_shape.append(jax.ShapeDtypeStruct((2 * width, 4 * unit), bf16))
+    result = pl.pallas_call(
+        functools.partial(
+            opening_body if opening else inner_body, width=width, length=length
+        ),
         grid=(count,),
         in_specs=[
             pl.BlockSpec((1, height, width, length), lambda m: (m + start, 0, 0, 0)),
-            pl.BlockSpec(weights.shape, lambda m: (0, 0)),
+            pl.BlockSpec(weights.shape, lambda m: (0,) * weights.ndim),
             pl.BlockSpec(bias.shape, lambda m: (0, 0)),
         ],
-        out_specs=pl.BlockSpec((1, height - 4, tiles, SUB, LANES), lambda m: (m, 0, 0, 0, 0)),
-        out_shape=jax.ShapeDtypeStruct((count, height - 4, tiles, SUB, LANES), bf16),
+        out_specs=out_specs,
+        out_shape=out_shape,
         scratch_shapes=[
             pltpu.VMEM((height * unit, padded), bf16),
             pltpu.VMEM(((height - 2) * unit, padded), bf16),
         ],
-        compiler_params=pltpu.CompilerParams(vmem_limit_bytes=48 * MB),
-        cost_estimate=pl.CostEstimate(
-            flops=2 * count * (2 * height - 6) * 12 * width * width * length,
-            bytes_accessed=count * height * width * length * 3,
-            transcendentals=count * (2 * height - 6) * width * length,
-        ),
+        compiler_params=pltpu.CompilerParams(vmem_limit_bytes=60 * MB),
+        cost_estimate=SMALL,
         name="inner_rows",
     )(x, weights, bias)
-
-
-def outer_body(ends, x, low, high, weights, bias, top, bottom, first, second, *, width, length):
+    return result if opening else result[0]
+
+
+def edges_body(x, last, first, *, height):
+    last[...] = x[:, height - 2 :]
+    first[...] = x[:, :2]
+
+
+def edges(x, start, count):
+    _, height, width, length = x.shape
+    block = pl.BlockSpec((1, 2, width, length), lambda m: (m, 0, 0, 0))
+    return pl.pallas_call(
+        functools.partial(edges_body, height=height),
+        grid=(count,),
+        in_specs=[pl.BlockSpec((1, height, width, length), lambda m: (m + start, 0, 0, 0))],
+        out_specs=[block] * 2,
+        out_shape=[jax.ShapeDtypeStruct((count, 2, width, length), bf16)] * 2,
+        cost_estimate=SMALL,
+        name="edge_rows",
+    )(x)
+
+
+def outer_body(ends, x, low, high, weights, bias, *refs, width, length):
+    outs, (first, second) = refs[:-2], refs[-2:]
     unit = 3 * width
     height = x.shape[1]
     for side in range(2):
@@ -164,7 +199,7 @@
             load_row(first, row * unit, width, length, source)
 
         def emit(row, value, at, side=side):
-            write_tiles(bottom if side else top, row, value, at, width, length)
+            write_tiles(outs[-1 if side else 0], 2 * side * (2 - len(outs)) + row, value, at, width, length)
 
         def mask(row, value, side=side):
             if row == (0 if side == 0 else 3):
@@ -174,9 +209,10 @@
         two_steps(first, second, 6, weights, bias, emit, mask, width, length)
 
 
-def outer(ends, x, low, high, weights, bias, start):
+def outer(ends, x, low, high, weights, bias, start, split):
     _, height, width, length = x.shape
     count = low.shape[0]
+    arrays, each = (2, 2) if split else (1, 4)
     padded = round_up(length, LANES)
     tiles = width * length // (SUB * LANES)
     unit = 3 * width
@@ -191,27 +227,23 @@
             pl.BlockSpec(weights.shape, lambda m: (0, 0)),
             pl.BlockSpec(bias.shape, lambda m: (0, 0)),
         ],
-        out_specs=[pl.BlockSpec((1, 2, tiles, SUB, LANES), lambda m: (m, 0, 0, 0, 0))] * 2,
-        out_shape=[jax.ShapeDtypeStruct((count, 2, tiles, SUB, LANES), bf16)] * 2,
+        out_specs=[pl.BlockSpec((1, each, tiles, SUB, LANES), lambda m: (m, 0, 0, 0, 0))] * arrays,
+        out_shape=[jax.ShapeDtypeStruct((count, each, tiles, SUB, LANES), bf16)] * arrays,
         scratch_shapes=[
             pltpu.VMEM((6 * unit, padded), bf16),
             pltpu.VMEM((4 * unit, padded), bf16),
         ],
-        compiler_params=pltpu.CompilerParams(vmem_limit_bytes=48 * MB),
-        cost_estimate=pl.CostEstimate(
-            flops=2 * count * 12 * 12 * width * width * length,
-            bytes_accessed=count * height * width * length * 3,
-            transcendentals=count * 12 * width * length,
-        ),
+        compiler_params=pltpu.CompilerParams(vmem_limit_bytes=60 * MB),
+        cost_estimate=SMALL,
         name="outer_rows",
     )(ends, x, low, high, weights, bias)
 
 
-def gather_body(rows, chosen, *refs, members):
-    blocks, (out, cells, picked) = refs[: 3 * members], refs[3 * members :]
+def gather_body(rows, chosen, *refs, members, parts):
+    blocks, (out, cells, picked) = refs[:-3], refs[-3:]
     for member in range(members):
         at = 0
-        for block in blocks[3 * member : 3 * member + 3]:
+        for block in blocks[parts * member : parts * member + parts]:
             for row in range(block.shape[1]):
                 size = block.shape[2] * SUB
                 cells[member, at : at + size] = (
@@ -252,7 +284,7 @@
             total += array.shape[1] * array.shape[2] * SUB
     members = len(pieces)
     return pl.pallas_call(
-        functools.partial(gather_body, members=members),
+        functools.partial(gather_body, members=members, parts=len(pieces[0])),
         grid=(1,),
         in_specs=[
             pl.BlockSpec(memory_space=pltpu.SMEM),
@@ -265,10 +297,8 @@
             pltpu.VMEM((members, total, LANES), f32),
             pltpu.VMEM((members, slots, LANES), f32),
         ],
-        compiler_params=pltpu.CompilerParams(vmem_limit_bytes=48 * MB),
-        cost_estimate=pl.CostEstimate(
-            flops=members * slots * LANES * 64, bytes_accessed=members * total * LANES * 2, transcendentals=0
-        ),
+        compiler_params=pltpu.CompilerParams(vmem_limit_bytes=60 * MB),
+        cost_estimate=SMALL,
         name="gather_cells",
     )(rows, chosen, *arrays)
 
@@ -324,14 +354,16 @@
             out[member, 0, chunk * SUB : (chunk + 1) * SUB, full * LANES : length] = part[:, :tail]
 
 
-def mix(weights, pieces, shape, start, before):
+def mix(weights, pieces, shape, place, count, before):
     members, height, width, length = shape
-    count = pieces[0].shape[1]
-    tiles = pieces[0].shape[2]
+    tiles = pieces[0][0].shape[2]
     specs = [
-        pl.BlockSpec((p.shape[0], 1, tiles, SUB, LANES), lambda r: (0, r, 0, 0, 0)) for p in pieces
+        pl.BlockSpec(
+            (array.shape[0], 1, tiles, SUB, LANES), lambda r, first=first: (0, r + first, 0, 0, 0)
+        )
+        for array, first in pieces
     ]
-    arrays = list(pieces)
+    arrays = [array for array, _ in pieces]
     alias = {}
     if before is not None:
         specs.append(pl.BlockSpec(memory_space=pl.ANY))
@@ -341,48 +373,74 @@
         functools.partial(mix_body, width=width, length=length, sources=len(pieces)),
         grid=(count,),
         in_specs=[pl.BlockSpec(weights.shape, lambda r: (0, 0))] + specs,
-        out_specs=pl.BlockSpec((members, 1, width, length), lambda r: (0, r + start, 0, 0)),
+        out_specs=pl.BlockSpec((members, 1, width, length), lambda r: (0, r + place, 0, 0)),
         out_shape=jax.ShapeDtypeStruct(shape, bf16),
         input_output_aliases=alias,
-        compiler_params=pltpu.CompilerParams(vmem_limit_bytes=48 * MB),
-        cost_estimate=pl.CostEstimate(
-            flops=2 * weights.size * count * tiles * LANES,
-            bytes_accessed=count * width * length * 2 * 5 * members,
-            transcendentals=0,
-        ),
+        compiler_params=pltpu.CompilerParams(vmem_limit_bytes=60 * MB),
+        cost_estimate=SMALL,
         name="mix_rows",
     )(weights, *arrays)
 
 
-def transform(gram, drive, ensemble_vectors):
+def transform_body(gram, drive, blend, *, members):
     highest = lax.Precision.HIGHEST
-    eye = jnp.eye(ensemble_vectors, dtype=jnp.float32)
-    system = eye + gram / (ensemble_vectors - 1.0)
-    scale = jnp.trace(system)
+    count = gram.shape[0]
+    row = lax.broadcasted_iota(jnp.int32, (count, count), 0)
+    column = lax.broadcasted_iota(jnp.int32, (count, count), 1)
+    eye = (row == column).astype(f32)
+    system = eye + gram[...] / (count - 1.0)
+    scale = jnp.sum(jnp.sum(system * eye, axis=1, keepdims=True), axis=0, keepdims=True)
     iterate = system / scale
     root = eye
     for number in range(NS_STEPS):
-        factor = 0.5 * (3.0 * eye - jnp.dot(root, iterate, precision=highest))
-        iterate = jnp.dot(iterate, factor, precision=highest)
-        root = jnp.dot(factor, root, precision=highest)
+        factor = 0.5 * (
+            3.0 * eye - jnp.dot(root, iterate, precision=highest, preferred_element_type=f32)
+        )
+        iterate = jnp.dot(iterate, factor, precision=highest, preferred_element_type=f32)
+        root = jnp.dot(factor, root, precision=highest, preferred_element_type=f32)
     spread = root / jnp.sqrt(scale)
-    inverse = jnp.dot(root, root, precision=highest)
-    mean_weights = jnp.dot(inverse, drive, precision=highest) / (scale * (ensemble_vectors - 1.0))
-    centering = eye - 1.0 / ensemble_vectors
-    mixing = 1.0 / ensemble_vectors + jnp.dot(
-        centering, mean_weights[:, None] + spread, precision=highest
-    )
-    return mixing.astype(jnp.bfloat16)
-
-
-def halo(x, start, count):
+    inverse = jnp.dot(root, root, precision=highest, preferred_element_type=f32)
+    mean_weights = jnp.sum(inverse * drive[...], axis=1, keepdims=True) / (scale * (count - 1.0))
+    combined = mean_weights + spread
+    mixing = (
+        1.0 / count + combined - jnp.sum(combined, axis=0, keepdims=True) * (1.0 / count)
+    ).astype(bf16)
+    wide = (members * SUB, count)
+    own = lax.broadcasted_iota(jnp.int32, wide, 0) // SUB
+    pick = (own == lax.broadcasted_iota(jnp.int32, wide, 1)).astype(f32).astype(bf16)
+    picked = lax.dot_general(
+        pick, mixing, (((1,), (1,)), ((), ())), preferred_element_type=f32
+    ).astype(bf16)
+    shape = (count, count * SUB)
+    source = lax.broadcasted_iota(jnp.int32, shape, 1) // SUB
+    spread_out = (source == lax.broadcasted_iota(jnp.int32, shape, 0)).astype(f32).astype(bf16)
+    full = jnp.dot(picked, spread_out, preferred_element_type=f32)
+    first = lax.broadcasted_iota(jnp.int32, full.shape, 0) % SUB
+    second = lax.broadcasted_iota(jnp.int32, full.shape, 1) % SUB
+    blend[...] = jnp.where(first == second, full, 0.0).astype(bf16)
+
+
+def transform(gram, drive, members):
+    count = gram.shape[0]
+    return pl.pallas_call(
+        functools.partial(transform_body, members=members),
+        in_specs=[pl.BlockSpec(memory_space=pltpu.VMEM)] * 2,
+        out_specs=pl.BlockSpec(memory_space=pltpu.VMEM),
+        out_shape=jax.ShapeDtypeStruct((members * SUB, count * SUB), bf16),
+        cost_estimate=SMALL,
+        name="transform",
+    )(gram, drive)
+
+
+def after(value, *others):
+    return lax.optimization_barrier((value,) + others)[0]
+
+
+def halo(last, first):
     size = lax.axis_size("band")
     forward = [(i, i + 1) for i in range(size - 1)]
     backward = [(target, source) for source, target in forward]
-    part = x[start : start + count]
-    low = lax.ppermute(part[:, x.shape[1] - 2 :], "band", forward)
-    high = lax.ppermute(part[:, :2], "band", backward)
-    return low, high
+    return lax.ppermute(last, "band", forward), lax.ppermute(first, "band", backward)
 
 
 def swap(block, bit):
@@ -401,7 +459,6 @@
 ):
     x = starting_condition
     members, height, width, length = x.shape
-    weights = pair_matrix(filter_kernel_tensor)
     bias = jnp.broadcast_to(
         jnp.concatenate([filter_offset_vector] * 2)[:, None], (2 * width, LANES)
     )
@@ -411,36 +468,38 @@
     rows, lanes = slot_places(measured_cell_position, height, width, length)
     chosen = (lanes[:, None] == jnp.arange(LANES, dtype=jnp.int32)[None, :]).astype(f32)
 
-    inner_parts = [inner(x, weights, bias, 0, 1), inner(x, weights, bias, 1, members - 1)]
     half = members // 2
-    halos = [halo(x, 0, half), halo(x, half, members - half)]
-    tops, bottoms = [], []
-    for number, (low, high) in enumerate(halos):
-        top, bottom = outer(ends, x, low, high, weights, bias, number * half)
-        tops.append(top)
-        bottoms.append(bottom)
-
-    def place(parts, member):
-        for part in parts:
-            if member < part.shape[0]:
-                return part, member
-            member -= part.shape[0]
-
-    predicted = jnp.concatenate(
-        [
-            gather(
-                rows,
-                chosen,
-                [
-                    [place(inner_parts, m), place(tops, m), place(bottoms, m)]
-                    for m in range(first, first + half)
-                ],
-            )
-            for first in range(0, members, half)
-        ],
-        axis=0,
-    )[:, 0]
-    predicted = lax.all_gather(predicted, "member", axis=0, tiled=True).astype(f32)
+    inner0, weights = inner(x, filter_kernel_tensor, bias, 0, half)
+    inner0_across = swap(inner0, 2)
+    edges0 = edges(after(x, inner0), 0, half)
+    edges1 = edges(after(x, edges0[0]), half, members - half)
+    halo0 = halo(*edges0)
+    inner1 = inner(after(x, edges1[0]), weights, bias, half, members - half)
+    inner1_across = swap(inner1, 2)
+    halo1 = halo(*lax.optimization_barrier((*edges1, *halo0))[:2])
+
+    inner0_core = swap(after(inner0, edges0[0]), 1)
+    (outer0,) = outer(
+        ends, after(x, inner0_across, inner0_core), *halo0, weights, bias, 0, False
+    )
+    outer0_across = swap(outer0, 2)
+    seen0 = gather(rows, chosen, [[(inner0, m), (outer0, m)] for m in range(half)])
+    (outer1,) = outer(ends, after(x, seen0), *halo1, weights, bias, half, False)
+    seen1 = gather(
+        rows,
+        after(chosen, inner1_across),
+        [[(inner1, m), (outer1, m)] for m in range(members - half)],
+    )
+    inner1_core, outer0_core, inner0_far, inner1_far = [
+        swap(after(part, seen1), 1) for part in (inner1, outer0, inner0_across, inner1_across)
+    ]
+    seen1 = after(seen1, inner1_core, outer0_core, inner0_far, inner1_far, outer0_across)
+    seen = jnp.concatenate([seen0, seen1], axis=0)
+    seen_across = swap(seen, 2)
+    outer1_across = swap(after(outer1, seen), 2)
+    both = jnp.concatenate([seen, seen_across], axis=0)
+    both_core = swap(both, 1)
+    predicted = jnp.concatenate([both, both_core], axis=0)[:, 0].astype(f32)
     ensemble_vectors = predicted.shape[0]
     slots = jnp.arange(measured_cell_position.shape[0], dtype=jnp.int32)
     live = (slots < measured_slot_number[0]).astype(f32)
@@ -450,26 +509,19 @@
     gram_part = jnp.dot(weighted, anomaly.T, precision=lax.Precision.HIGHEST)
     drive_part = jnp.dot(weighted, measured_reading - mean, precision=lax.Precision.HIGHEST)
     gram, drive = lax.psum((gram_part, drive_part), "band")
-    mixing = transform(gram, drive, ensemble_vectors)
-
-    me = lax.axis_index("member")
-    owned = lax.dynamic_slice_in_dim(mixing, me * members, members, 1)
-    order = jnp.concatenate(
-        [jnp.arange(members, dtype=jnp.int32) + (me ^ bit) * members for bit in (0, 1, 2, 3)]
-    )
-    share = jnp.take(owned, order, axis=0)
-    blend = (
-        share.T[:, None, :, None] * jnp.eye(SUB, dtype=bf16)[None, :, None, :]
-    ).reshape(members * SUB, ensemble_vectors * SUB)
-
-    def everyone(parts):
-        across = [swap(part, 2) for part in parts]
-        return parts + [swap(p, 1) for p in parts] + across + [swap(p, 1) for p in across]
-
-    inner_all, top_all, bottom_all = everyone(inner_parts), everyone(tops), everyone(bottoms)
-    result = mix(blend, inner_all, x.shape, 2, None)
-    result = mix(blend, top_all, x.shape, 0, result)
-    return mix(blend, bottom_all, x.shape, height - 2, result)
+    outer0_far, outer1_core = [
+        swap(after(part, both_core), 1) for part in (outer0_across, outer1)
+    ]
+    blend = transform(gram, after(drive, outer0_far, outer1_core)[None, :], members)
+
+    pieces = (inner0, inner1, inner0_across, inner1_across)
+    pieces += (inner0_core, inner1_core, inner0_far, inner1_far)
+    result = mix(blend, [(piece, 0) for piece in pieces], x.shape, 2, height - 4, None)
+    outer1_far = swap(after(outer1_across, result), 1)
+    pieces = (outer0, outer1, outer0_across, outer1_across)
+    pieces += (outer0_core, outer1_core, outer0_far, outer1_far)
+    result = mix(blend, [(piece, 0) for piece in pieces], x.shape, 0, 2, result)
+    return mix(blend, [(piece, 2) for piece in pieces], x.shape, height - 2, 2, result)
 
 
 def solution(mesh):

time: 204 us -> 179 us (0.88)
  waiting for transfers between devices: 79 us -> 49.8 us
  Pallas kernels: 51.9 us -> 74.1 us
  matrix products: 8.84 us -> 0.55 us
  blocking collectives: 27.8 us -> 21.7 us
  local copies, waits for them, and re-layouts: 9.16 us -> 4.99 us
  other arithmetic: 2.03 us -> 5.89 us
  starting transfers between devices: 22.6 us -> 20.3 us
    ppermute x18 -> x14, waiting for transfers between devices: 50.6 us -> 16.2 us  [swap(): return lax.ppermute(block, 'member', [(i, i ^ bit) for i in range(size)])]
    pallas_call x4 -> x7, Pallas kernels: 21 us -> 39.4 us  [the longest x2 14.6 us: inner(): pl.pallas_call(functools.partial(opening_body if opening else inner_body,...]
    dot_general x50 -> x0, matrix products: 8.29 us -> none  [the longest x16 2.86 us: transform(): factor = 0.5 * (3.0 * eye - jnp.dot(root, iterate, precision=highest))]
    all_gather x1 -> x0, blocking collectives: 5.43 us -> none  [local(): lax.all_gather(predicted, 'member', axis=0, tiled=True).astype(f32)]
    ppermute x4, waiting for transfers between devices: 28.4 us -> 33.6 us  [the longest x2 30 us: halo(): lax.ppermute(last, 'band', forward)]
    slice x1 -> x0, local copies, waits for them, and re-layouts: 3.69 us -> none  [halo(): high = lax.ppermute(part[:, :2], 'band', backward)]
    pallas_call x2, Pallas kernels: 16.4 us -> 18.8 us  [outer(): pl.pallas_call(functools.partial(outer_body, width=width, length=length),...]
    ppermute x18 -> x14, starting transfers between devices: 8.85 us -> 6.73 us  [swap(): return lax.ppermute(block, 'member', [(i, i ^ bit) for i in range(size)])]
  transfers between devices with their start and end apart: 22 -> 18, of which waited for: 6 -> 8; matrix products, arithmetic and copies ran while one was open for 6% -> 3% of each run, Pallas kernels for 24% -> 33%
where the time goes in v1:
time: 179 us; the launch traced here: 178 us
  Pallas kernels  74.1 us (41%)
  waiting for transfers between devices  49.8 us (28%)
  blocking collectives  21.7 us (12%)
  starting transfers between devices  20.3 us (11%)
  other arithmetic  5.89 us (3%)
  local copies, waits for them, and re-layouts  4.99 us (3%)
    ppermute x2, waiting for transfers between devices, halo(): lax.ppermute(last, 'band', forward)  30 us
    psum x1, blocking collectives, local(): gram, drive = lax.psum((gram_part, drive_part), 'band')  21.7 us
    pallas_call x2, Pallas kernels, outer(): pl.pallas_call(functools.partial(outer_body, width=width, length=length),...  18.8 us
    ppermute x14, waiting for transfers between devices, swap(): return lax.ppermute(block, 'member', [(i, i ^ bit) for i in range(size)])  16.2 us
    pallas_call x3, Pallas kernels, mix(): pl.pallas_call(functools.partial(mix_body, width=width, length=length, so...  15.8 us
    pallas_call x2, Pallas kernels, inner(): pl.pallas_call(functools.partial(opening_body if opening else inner_body,...  14.6 us
    pallas_call x2, Pallas kernels, gather(): pl.pallas_call(functools.partial(gather_body, members=members, parts=len(...  12.6 us
    ppermute x2, starting transfers between devices, halo(): lax.ppermute(last, 'band', forward)  10.8 us
  transfers between devices with their start and end apart: 18, of which 8 were waited for; matrix products, arithmetic and copies ran while one was open for 3% of the time, Pallas kernels for 33%

profile of v1, /device:TPU:0, one launch (start us, length us, event | category | flops | bytes accessed | tf_op | source)
XLA Modules:
  0.0 178.1 jit_solution(16247367996837649397)
XLA Ops:
  0.0 0.8 pad_maximum_fusion.2
  0.8 0.7 broadcast_in_dim.9.bias
  1.5 7.4 %inner_rows.2 = (bf16[2,4,45,16,128]{4,3,2,1,0:T(8,128)(2,1)}, bf16[128,768]{1,0:T(8,128)(2,1)}) custom-call(bf16[4,8,64,1440]{3,2,1,0:T(8,128)(2,1)} %x.6, bf16[3,3,64,64]{3,2,1,0:T(8,128)(2,1)} %kernel.1, f32[128,128]{1,0:T(8,128)} %broadcast_in_dim.9.bias), custom_call_target="tpu_custom_call" | custom-call | flops 200000000 | bytes 500000 | tf_op jit(solution)/shard_map/inner_rows/pallas_call | solution.py:147
  8.9 3.0 %collective-permute-start = (bf16[2,4,45,16,128]{4,3,2,1,0:T(8,128)(2,1)}, bf16[2,4,45,16,128]{4,3,2,1,0:T(8,128)(2,1)S(1)}, u32[]{:S(2)}, u32[]{:S(2)}) collective-permute-start(bf16[2,4,45,16,128]{4,3,2,1,0:T(8,128)(2,1)} %get-tuple-element.33.refs_0_.refs_2_), channel_id=1, source_target_pairs={{0,16},{8,24},{16,0},{24,8},{1,17},{9,25},{17,1},{25,9},{2,18},{10... | collective-permute-start | bytes 4423688 | tf_op jit(solution)/shard_map/ppermute | solution.py:448
  11.9 2.8 %edge_rows.2 = (bf16[2,2,64,1440]{3,2,1,0:T(8,128)(2,1)}, bf16[2,2,64,1440]{3,2,1,0:T(8,128)(2,1)}) custom-call(bf16[4,8,64,1440]{3,2,1,0:T(8,128)(2,1)} %x.6), custom_call_target="tpu_custom_call" | custom-call | flops 200000000 | bytes 500000 | tf_op jit(solution)/shard_map/edge_rows/pallas_call | solution.py:178
  14.7 1.3 collective-permute-start.3
  16.0 5.5 %collective-permute-start.2 = (bf16[2,2,64,1440]{3,2,1,0:T(8,128)(2,1)}, bf16[2,2,64,1440]{3,2,1,0:T(8,128)(2,1)}, u32[]{:S(2)}, u32[]{:S(2)}) collective-permute-start(bf16[2,2,64,1440]{3,2,1,0:T(8,128)(2,1)} %get-tuple-element.32), channel_id=1, source_target_pairs={{0,1},{1,2},{2,3},{3,4},{4,5},{5,6},{6,7},{8,9},{9,10},{10,11},{11... | collective-permute-start | bytes 2211848 | tf_op jit(solution)/shard_map/ppermute | solution.py:443
  21.5 0.0 collective-permute-start.1
  21.5 2.8 %edge_rows.3 = (bf16[2,2,64,1440]{3,2,1,0:T(8,128)(2,1)}, bf16[2,2,64,1440]{3,2,1,0:T(8,128)(2,1)}) custom-call(bf16[4,8,64,1440]{3,2,1,0:T(8,128)(2,1)} %x.6), custom_call_target="tpu_custom_call" | custom-call | flops 200000000 | bytes 500000 | tf_op jit(solution)/shard_map/edge_rows/pallas_call | solution.py:178
  24.4 7.2 %inner_rows.3.refs_0_.refs_2_.refs_1_ = bf16[2,4,45,16,128]{4,3,2,1,0:T(8,128)(2,1)} custom-call(bf16[4,8,64,1440]{3,2,1,0:T(8,128)(2,1)} %x.6, bf16[128,768]{1,0:T(8,128)(2,1)} %get-tuple-element.36.weights, f32[128,128]{1,0:T(8,128)} %broadcast_in_dim.9.bias), custom_call_target="tpu_custom_call" | custom-call | flops 200000000 | bytes 500000 | tf_op jit(solution)/shard_map/inner_rows/pallas_call | solution.py:147
  31.5 0.1 collective-permute-start.4
  31.7 0.6 add_convert_fusion.ends
  32.3 3.6 %collective-permute-done.3.high = bf16[2,2,64,1440]{3,2,1,0:T(8,128)(2,1)} collective-permute-done((bf16[2,2,64,1440]{3,2,1,0:T(8,128)(2,1)}, bf16[2,2,64,1440]{3,2,1,0:T(8,128)(2,1)}, u32[]{:S(2)}, u32[]{:S(2)}) %collective-permute-start.3) | collective-permute-done | bytes 737312 | tf_op jit(solution)/shard_map/ppermute | solution.py:443
  35.9 16.8 %collective-permute-done.2.low = bf16[2,2,64,1440]{3,2,1,0:T(8,128)(2,1)} collective-permute-done((bf16[2,2,64,1440]{3,2,1,0:T(8,128)(2,1)}, bf16[2,2,64,1440]{3,2,1,0:T(8,128)(2,1)}, u32[]{:S(2)}, u32[]{:S(2)}) %collective-permute-start.2) | collective-permute-done | bytes 737312 | tf_op jit(solution)/shard_map/ppermute | solution.py:443
  52.7 5.3 %collective-permute-start.5 = (bf16[2,2,64,1440]{3,2,1,0:T(8,128)(2,1)}, bf16[2,2,64,1440]{3,2,1,0:T(8,128)(2,1)}, u32[]{:S(2)}, u32[]{:S(2)}) collective-permute-start(bf16[2,2,64,1440]{3,2,1,0:T(8,128)(2,1)} %get-tuple-element.43), channel_id=1, source_target_pairs={{0,1},{1,2},{2,3},{3,4},{4,5},{5,6},{6,7},{8,9},{9,10},{10,11},{11... | collective-permute-start | bytes 2211848 | tf_op jit(solution)/shard_map/ppermute | solution.py:443
  58.0 1.5 collective-permute-start.6
  59.5 0.6 fusion.26
  60.1 1.3 fusion.chosen
  61.4 0.0 collective-permute-done.refs_2_
  61.4 0.0 collective-permute-done.1.refs_4_
  61.4 9.7 %outer_rows.2.refs_1_.refs_3_.refs_0_ = bf16[2,4,45,16,128]{4,3,2,1,0:T(8,128)(2,1)} custom-call(s32[2]{0:T(128)} %add_convert_fusion.ends, bf16[4,8,64,1440]{3,2,1,0:T(8,128)(2,1)} %x.6, bf16[2,2,64,1440]{3,2,1,0:T(8,128)(2,1)} %collective-permute-done.2.low, bf16[2,2,64,1440]{3,2,1,0:T(8,128)(2,1)} %collective-permute-done.3.high, ...), custom_call_target="tpu_custom_call" | custom-call | flops 200000000 | bytes 500000 | tf_op jit(solution)/shard_map/outer_rows/pallas_call | solution.py:219
  71.1 0.6 collective-permute-start.11
  71.7 6.3 %gather_cells.2 = bf16[2,1,2048]{2,1,0:T(2,128)(2,1)} custom-call(s32[2048]{0:T(1024)} %get-tuple-element.62.rows, f32[2048,128]{1,0:T(8,128)} %fusion.chosen, bf16[2,4,45,16,128]{4,3,2,1,0:T(8,128)(2,1)} %get-tuple-element.33.refs_0_.refs_2_, bf16[2,4,45,16,128]{4,3,2,1,0:T(8,128)(2,1)} %outer_rows.2.refs_1_.refs_3_.refs_0_, ...), custom_call_target="tpu_custom_call" | custom-call | flops 200000000 | bytes 500000 | tf_op jit(solution)/shard_map/gather_cells/pallas_call | solution.py:286
  78.0 0.0 collective-permute-done.4.refs_3_
  78.0 13.2 %collective-permute-done.5.low = bf16[2,2,64,1440]{3,2,1,0:T(8,128)(2,1)} collective-permute-done((bf16[2,2,64,1440]{3,2,1,0:T(8,128)(2,1)}, bf16[2,2,64,1440]{3,2,1,0:T(8,128)(2,1)}, u32[]{:S(2)}, u32[]{:S(2)}) %collective-permute-start.5) | collective-permute-done | bytes 737312 | tf_op jit(solution)/shard_map/ppermute | solution.py:443
  91.2 0.0 collective-permute-done.6.high
  91.2 9.2 %outer_rows.3.refs_1_.refs_3_ = bf16[2,4,45,16,128]{4,3,2,1,0:T(8,128)(2,1)} custom-call(s32[2]{0:T(128)} %add_convert_fusion.ends, bf16[4,8,64,1440]{3,2,1,0:T(8,128)(2,1)} %x.6, bf16[2,2,64,1440]{3,2,1,0:T(8,128)(2,1)} %collective-permute-done.5.low, bf16[2,2,64,1440]{3,2,1,0:T(8,128)(2,1)} %collective-permute-done.6.high, ...), custom_call_target="tpu_custom_call" | custom-call | flops 200000000 | bytes 500000 | tf_op jit(solution)/shard_map/outer_rows/pallas_call | solution.py:219
  100.4 0.0 copy-start.11
  100.4 0.0 copy-start.12
  100.4 6.4 %gather_cells.3 = bf16[2,1,2048]{2,1,0:T(2,128)(2,1)} custom-call(s32[2048]{0:T(1024)} %get-tuple-element.62.rows, f32[2048,128]{1,0:T(8,128)} %fusion.chosen, bf16[2,4,45,16,128]{4,3,2,1,0:T(8,128)(2,1)} %inner_rows.3.refs_0_.refs_2_.refs_1_, bf16[2,4,45,16,128]{4,3,2,1,0:T(8,128)(2,1)} %outer_rows.3.refs_1_.refs_3_, ...), custom_call_target="tpu_custom_call" | custom-call | flops 200000000 | bytes 500000 | tf_op jit(solution)/shard_map/gather_cells/pallas_call | solution.py:286
  106.8 0.0 collective-permute-start.7
  106.8 0.5 collective-permute-start.8
  107.3 0.1 collective-permute-start.9
  107.4 0.4 collective-permute-start.10
  107.8 0.0 collective-permute-done.11.refs_2_
  107.8 3.9 %collective-permute-done.7.refs_5_ = bf16[2,4,45,16,128]{4,3,2,1,0:T(8,128)(2,1)S(1)} collective-permute-done((bf16[2,4,45,16,128]{4,3,2,1,0:T(8,128)(2,1)}, bf16[2,4,45,16,128]{4,3,2,1,0:T(8,128)(2,1)S(1)}, u32[]{:S(2)}, u32[]{:S(2)}) %collective-permute-start.7) | collective-permute-done | bytes 1474592 | tf_op jit(solution)/shard_map/ppermute | solution.py:448
  111.7 4.3 %collective-permute-done.8.refs_4_ = bf16[2,4,45,16,128]{4,3,2,1,0:T(8,128)(2,1)S(1)} collective-permute-done((bf16[2,4,45,16,128]{4,3,2,1,0:T(8,128)(2,1)S(1)}, bf16[2,4,45,16,128]{4,3,2,1,0:T(8,128)(2,1)S(1)}, u32[]{:S(2)}, u32[]{:S(2)}) %collective-permute-start.8) | collective-permute-done | bytes 1474592 | tf_op jit(solution)/shard_map/ppermute | solution.py:448
  116.0 1.2 copy-done.3
  117.2 0.0 collective-permute-done.9.refs_6_
  117.2 1.1 copy-done.8
  118.4 0.0 collective-permute-done.10.refs_7_
  118.4 0.8 pad_maximum_fusion.1
  119.2 0.7 collective-permute-start.12
  119.9 3.3 %collective-permute-done.12 = bf16[4,1,2048]{2,1,0:T(2,128)(2,1)S(1)} collective-permute-done((bf16[4,1,2048]{2,1,0:T(2,128)(2,1)S(1)}, bf16[4,1,2048]{2,1,0:T(2,128)(2,1)S(1)}, u32[]{:S(2)}, u32[]{:S(2)}) %collective-permute-start.12) | collective-permute-done | bytes 16416 | tf_op jit(solution)/shard_map/ppermute | solution.py:448
  123.2 0.8 pad_maximum_fusion
  124.0 0.1 collective-permute-start.13
  124.1 1.2 collective-permute-done.13
  125.3 0.2 collective-permute-start.14
  125.5 0.4 collective-permute-start.15
  125.8 0.6 collective-permute-start.16
  127.1 0.7 copy.25
  127.9 0.9 fusion.38
  128.8 0.2 convolution_bitcast_fusion
  129.1 0.3 fusion.4
  129.4 21.7 %all-reduce = (f32[16,16]{1,0:T(8,128)}, f32[16]{0:T(128)}) all-reduce(f32[16,16]{1,0:T(8,128)S(1)} %fusion.4, f32[16]{0:T(128)S(1)} %convolution_bitcast_fusion), channel_id=1, replica_groups=mesh['member'=4,'band'=8] {'band'}, use_global_device_ids=true, to_apply=%region_1.2 | all-reduce | flops 272 | bytes 2176 | tf_op jit(solution)/shard_map/psum | solution.py:511
  151.1 0.0 collective-permute-done.14.refs_6_
  151.1 0.0 collective-permute-done.15.refs_5_
  151.1 6.5 %transform.1.weights = bf16[64,256]{1,0:T(8,128)(2,1)} custom-call(f32[16,16]{1,0:T(8,128)} %get-tuple-element.55.gram, f32[1,16]{1,0:T(1,128)} %bitcast.37), custom_call_target="tpu_custom_call" | custom-call | flops 200000000 | bytes 500000 | tf_op jit(solution)/shard_map/transform/pallas_call | solution.py:425
  157.7 7.3 %mix_rows.3.refs_8_ = bf16[4,8,64,1440]{3,2,1,0:T(8,128)(2,1)} custom-call(bf16[64,256]{1,0:T(8,128)(2,1)} %transform.1.weights, bf16[2,4,45,16,128]{4,3,2,1,0:T(8,128)(2,1)} %get-tuple-element.33.refs_0_.refs_2_, bf16[2,4,45,16,128]{4,3,2,1,0:T(8,128)(2,1)} %inner_rows.3.refs_0_.refs_2_.refs_1_, bf16[2,4,45,16,128]{4,3,2,1,0:T(8,128)(2,1)} %copy-done.6, ...), custom_call_target="tpu_custom_call" | custom-call | flops 200000000 | bytes 500000 | tf_op jit(solution)/shard_map/mix_rows/pallas_call | solution.py:372
  165.0 0.1 collective-permute-start.17
  165.1 3.5 %collective-permute-done.17.refs_7_ = bf16[2,4,45,16,128]{4,3,2,1,0:T(8,128)(2,1)S(1)} collective-permute-done((bf16[2,4,45,16,128]{4,3,2,1,0:T(8,128)(2,1)}, bf16[2,4,45,16,128]{4,3,2,1,0:T(8,128)(2,1)S(1)}, u32[]{:S(2)}, u32[]{:S(2)}) %collective-permute-start.17) | collective-permute-done | bytes 1474592 | tf_op jit(solution)/shard_map/ppermute | solution.py:448
  168.6 1.1 copy-done.5
  169.7 4.2 %mix_rows.4.refs_8_ = bf16[4,8,64,1440]{3,2,1,0:T(8,128)(2,1)} custom-call(bf16[64,256]{1,0:T(8,128)(2,1)} %transform.1.weights, bf16[2,4,45,16,128]{4,3,2,1,0:T(8,128)(2,1)} %outer_rows.2.refs_1_.refs_3_.refs_0_, bf16[2,4,45,16,128]{4,3,2,1,0:T(8,128)(2,1)} %outer_rows.3.refs_1_.refs_3_, ...), custom_call_target="tpu_custom_call", output_to_operand_aliasing={{}: (9, {})} | custom-call | flops 200000000 | bytes 500000 | tf_op jit(solution)/shard_map/mix_rows/pallas_call | solution.py:372
  173.9 4.2 %mix_rows.5 = bf16[4,8,64,1440]{3,2,1,0:T(8,128)(2,1)} custom-call(bf16[64,256]{1,0:T(8,128)(2,1)} %transform.1.weights, bf16[2,4,45,16,128]{4,3,2,1,0:T(8,128)(2,1)} %outer_rows.2.refs_1_.refs_3_.refs_0_, bf16[2,4,45,16,128]{4,3,2,1,0:T(8,128)(2,1)} %outer_rows.3.refs_1_.refs_3_, ...), custom_call_target="tpu_custom_call", output_to_operand_aliasing={{}: (9, {})} | custom-call | flops 200000000 | bytes 500000 | tf_op jit(solution)/shard_map/mix_rows/pallas_call | solution.py:372
  (27 shorter events, 0.1 us)
Async XLA Ops:
  8.9 12.6 %copy-start.2 = (bf16[2,4,45,16,128]{4,3,2,1,0:T(8,128)(2,1)S(1)}, bf16[2,4,45,16,128]{4,3,2,1,0:T(8,128)(2,1)}, u32[]{:S(2)}) copy-start(bf16[2,4,45,16,128]{4,3,2,1,0:T(8,128)(2,1)} %get-tuple-element.33.refs_0_.refs_2_) | copy-start | bytes 4423684
  8.9 52.5 %collective-permute-start = (bf16[2,4,45,16,128]{4,3,2,1,0:T(8,128)(2,1)}, bf16[2,4,45,16,128]{4,3,2,1,0:T(8,128)(2,1)S(1)}, u32[]{:S(2)}, u32[]{:S(2)}) collective-permute-start(bf16[2,4,45,16,128]{4,3,2,1,0:T(8,128)(2,1)} %get-tuple-element.33.refs_0_.refs_2_), channel_id=1, source_target_pairs={{0,16},{8,24},{16,0},{24,8},{1,17},{9,25},{17,1},{25,9},{2,18},{10... | collective-permute-start | bytes 4423688 | tf_op jit(solution)/shard_map/ppermute | solution.py:448
  14.7 21.2 %collective-permute-start.3 = (bf16[2,2,64,1440]{3,2,1,0:T(8,128)(2,1)}, bf16[2,2,64,1440]{3,2,1,0:T(8,128)(2,1)}, u32[]{:S(2)}, u32[]{:S(2)}) collective-permute-start(bf16[2,2,64,1440]{3,2,1,0:T(8,128)(2,1)} %get-tuple-element.35), channel_id=1, source_target_pairs={{1,0},{2,1},{3,2},{4,3},{5,4},{6,5},{7,6},{9,8},{10,9},{11,10},{12... | collective-permute-start | bytes 2211848 | tf_op jit(solution)/shard_map/ppermute | solution.py:443
  16.0 36.7 %collective-permute-start.2 = (bf16[2,2,64,1440]{3,2,1,0:T(8,128)(2,1)}, bf16[2,2,64,1440]{3,2,1,0:T(8,128)(2,1)}, u32[]{:S(2)}, u32[]{:S(2)}) collective-permute-start(bf16[2,2,64,1440]{3,2,1,0:T(8,128)(2,1)} %get-tuple-element.32), channel_id=1, source_target_pairs={{0,1},{1,2},{2,3},{3,4},{4,5},{5,6},{6,7},{8,9},{9,10},{10,11},{11... | collective-permute-start | bytes 2211848 | tf_op jit(solution)/shard_map/ppermute | solution.py:443
  21.5 39.9 %collective-permute-start.1 = (bf16[2,4,45,16,128]{4,3,2,1,0:T(8,128)(2,1)S(1)}, bf16[2,4,45,16,128]{4,3,2,1,0:T(8,128)(2,1)}, u32[]{:S(2)}, u32[]{:S(2)}) collective-permute-start(bf16[2,4,45,16,128]{4,3,2,1,0:T(8,128)(2,1)S(1)} %copy-done.2), channel_id=1, source_target_pairs={{0,8},{8,0},{16,24},{24,16},{1,9},{9,1},{17,25},{25,17},{2,10},{10... | collective-permute-start | bytes 4423688 | tf_op jit(solution)/shard_map/ppermute | solution.py:448
  24.4 35.1 %copy-start.10 = (s32[2048]{0:T(1024)S(1)}, s32[2048]{0:T(1024)}, u32[]{:S(2)}) copy-start(s32[2048]{0:T(1024)} %param.10) | copy-start | bytes 24580
  31.5 46.5 %collective-permute-start.4 = (bf16[2,4,45,16,128]{4,3,2,1,0:T(8,128)(2,1)}, bf16[2,4,45,16,128]{4,3,2,1,0:T(8,128)(2,1)}, u32[]{:S(2)}, u32[]{:S(2)}) collective-permute-start(bf16[2,4,45,16,128]{4,3,2,1,0:T(8,128)(2,1)} %inner_rows.3.refs_0_.refs_2_.refs_1_), channel_id=1, source_target_pairs={{0,16},{8,24},{16,0},{24,8},{1,17},{9,25},{17,1},{25,9},{2,18},{10... | collective-permute-start | bytes 4423688 | tf_op jit(solution)/shard_map/ppermute | solution.py:448
  52.7 38.5 %collective-permute-start.5 = (bf16[2,2,64,1440]{3,2,1,0:T(8,128)(2,1)}, bf16[2,2,64,1440]{3,2,1,0:T(8,128)(2,1)}, u32[]{:S(2)}, u32[]{:S(2)}) collective-permute-start(bf16[2,2,64,1440]{3,2,1,0:T(8,128)(2,1)} %get-tuple-element.43), channel_id=1, source_target_pairs={{0,1},{1,2},{2,3},{3,4},{4,5},{5,6},{6,7},{8,9},{9,10},{10,11},{11... | collective-permute-start | bytes 2211848 | tf_op jit(solution)/shard_map/ppermute | solution.py:443
  58.0 33.2 %collective-permute-start.6 = (bf16[2,2,64,1440]{3,2,1,0:T(8,128)(2,1)}, bf16[2,2,64,1440]{3,2,1,0:T(8,128)(2,1)}, u32[]{:S(2)}, u32[]{:S(2)}) collective-permute-start(bf16[2,2,64,1440]{3,2,1,0:T(8,128)(2,1)} %get-tuple-element.44), channel_id=1, source_target_pairs={{1,0},{2,1},{3,2},{4,3},{5,4},{6,5},{7,6},{9,8},{10,9},{11,10},{12... | collective-permute-start | bytes 2211848 | tf_op jit(solution)/shard_map/ppermute | solution.py:443
  61.4 9.7 %copy-start.6 = (bf16[2,4,45,16,128]{4,3,2,1,0:T(8,128)(2,1)}, bf16[2,4,45,16,128]{4,3,2,1,0:T(8,128)(2,1)S(1)}, u32[]{:S(2)}) copy-start(bf16[2,4,45,16,128]{4,3,2,1,0:T(8,128)(2,1)S(1)} %collective-permute-done.refs_2_) | copy-start | bytes 4423684
  71.1 36.7 %collective-permute-start.11 = (bf16[2,4,45,16,128]{4,3,2,1,0:T(8,128)(2,1)}, bf16[2,4,45,16,128]{4,3,2,1,0:T(8,128)(2,1)}, u32[]{:S(2)}, u32[]{:S(2)}) collective-permute-start(bf16[2,4,45,16,128]{4,3,2,1,0:T(8,128)(2,1)} %outer_rows.2.refs_1_.refs_3_.refs_0_), channel_id=1, source_target_pairs={{0,16},{8,24},{16,0},{24,8},{1,17},{9,25},{17,1},{25,9},{2,18},{10... | collective-permute-start | bytes 4423688 | tf_op jit(solution)/shard_map/ppermute | solution.py:448
  100.4 6.4 %copy-start = (bf16[2,4,45,16,128]{4,3,2,1,0:T(8,128)(2,1)S(1)}, bf16[2,4,45,16,128]{4,3,2,1,0:T(8,128)(2,1)}, u32[]{:S(2)}) copy-start(bf16[2,4,45,16,128]{4,3,2,1,0:T(8,128)(2,1)} %outer_rows.2.refs_1_.refs_3_.refs_0_) | copy-start | bytes 4423684
  100.4 18.0 %copy-start.9 = (bf16[2,1,2048]{2,1,0:T(2,128)(2,1)S(1)}, bf16[2,1,2048]{2,1,0:T(2,128)(2,1)}, u32[]{:S(2)}) copy-start(bf16[2,1,2048]{2,1,0:T(2,128)(2,1)} %gather_cells.2) | copy-start | bytes 24580
  100.4 25.1 %copy-start.1 = (bf16[2,4,45,16,128]{4,3,2,1,0:T(8,128)(2,1)S(1)}, bf16[2,4,45,16,128]{4,3,2,1,0:T(8,128)(2,1)}, u32[]{:S(2)}) copy-start(bf16[2,4,45,16,128]{4,3,2,1,0:T(8,128)(2,1)} %outer_rows.3.refs_1_.refs_3_) | copy-start | bytes 4423684
  100.4 26.7 %copy-start.11 = (f32[2048]{0:T(1024)S(1)}, f32[2048]{0:T(1024)}, u32[]{:S(2)}) copy-start(f32[2048]{0:T(1024)} %param.13) | copy-start | bytes 24580
  100.4 28.4 %copy-start.12 = (f32[2048]{0:T(1024)S(1)}, f32[2048]{0:T(1024)}, u32[]{:S(2)}) copy-start(f32[2048]{0:T(1024)} %param.12) | copy-start | bytes 24580
  106.8 4.9 %collective-permute-start.7 = (bf16[2,4,45,16,128]{4,3,2,1,0:T(8,128)(2,1)}, bf16[2,4,45,16,128]{4,3,2,1,0:T(8,128)(2,1)S(1)}, u32[]{:S(2)}, u32[]{:S(2)}) collective-permute-start(bf16[2,4,45,16,128]{4,3,2,1,0:T(8,128)(2,1)} %inner_rows.3.refs_0_.refs_2_.refs_1_), channel_id=1, source_target_pairs={{0,8},{8,0},{16,24},{24,16},{1,9},{9,1},{17,25},{25,17},{2,10},{10... | collective-permute-start | bytes 4423688 | tf_op jit(solution)/shard_map/ppermute | solution.py:448
  106.8 9.2 %collective-permute-start.8 = (bf16[2,4,45,16,128]{4,3,2,1,0:T(8,128)(2,1)S(1)}, bf16[2,4,45,16,128]{4,3,2,1,0:T(8,128)(2,1)S(1)}, u32[]{:S(2)}, u32[]{:S(2)}) collective-permute-start(bf16[2,4,45,16,128]{4,3,2,1,0:T(8,128)(2,1)S(1)} %copy-done), channel_id=1, source_target_pairs={{0,8},{8,0},{16,24},{24,16},{1,9},{9,1},{17,25},{25,17},{2,10},{10... | collective-permute-start | bytes 4423688 | tf_op jit(solution)/shard_map/ppermute | solution.py:448
  107.3 9.9 %collective-permute-start.9 = (bf16[2,4,45,16,128]{4,3,2,1,0:T(8,128)(2,1)}, bf16[2,4,45,16,128]{4,3,2,1,0:T(8,128)(2,1)S(1)}, u32[]{:S(2)}, u32[]{:S(2)}) collective-permute-start(bf16[2,4,45,16,128]{4,3,2,1,0:T(8,128)(2,1)} %copy-done.6), channel_id=1, source_target_pairs={{0,8},{8,0},{16,24},{24,16},{1,9},{9,1},{17,25},{25,17},{2,10},{10... | collective-permute-start | bytes 4423688 | tf_op jit(solution)/shard_map/ppermute | solution.py:448
  107.4 11.0 %collective-permute-start.10 = (bf16[2,4,45,16,128]{4,3,2,1,0:T(8,128)(2,1)}, bf16[2,4,45,16,128]{4,3,2,1,0:T(8,128)(2,1)}, u32[]{:S(2)}, u32[]{:S(2)}) collective-permute-start(bf16[2,4,45,16,128]{4,3,2,1,0:T(8,128)(2,1)} %collective-permute-done.4.refs_3_), channel_id=1, source_target_pairs={{0,8},{8,0},{16,24},{24,16},{1,9},{9,1},{17,25},{25,17},{2,10},{10... | collective-permute-start | bytes 4423688 | tf_op jit(solution)/shard_map/ppermute | solution.py:448
  111.7 5.5 %copy-start.7 = (bf16[2,4,45,16,128]{4,3,2,1,0:T(8,128)(2,1)}, bf16[2,4,45,16,128]{4,3,2,1,0:T(8,128)(2,1)S(1)}, u32[]{:S(2)}) copy-start(bf16[2,4,45,16,128]{4,3,2,1,0:T(8,128)(2,1)S(1)} %collective-permute-done.7.refs_5_) | copy-start | bytes 4423684
  116.0 1.2 copy-start.3
  117.2 1.2 copy-start.8
  119.2 4.0 %collective-permute-start.12 = (bf16[4,1,2048]{2,1,0:T(2,128)(2,1)S(1)}, bf16[4,1,2048]{2,1,0:T(2,128)(2,1)S(1)}, u32[]{:S(2)}, u32[]{:S(2)}) collective-permute-start(bf16[4,1,2048]{2,1,0:T(2,128)(2,1)S(1)} %pad_maximum_fusion.1), channel_id=1, source_target_pairs={{0,16},{8,24},{16,0},{24,8},{1,17},{9,25},{17,1},{25,9},{2,18},{10... | collective-permute-start | bytes 49160 | tf_op jit(solution)/shard_map/ppermute | solution.py:448
  124.0 1.3 collective-permute-start.13
  125.3 25.8 %collective-permute-start.14 = (bf16[2,4,45,16,128]{4,3,2,1,0:T(8,128)(2,1)}, bf16[2,4,45,16,128]{4,3,2,1,0:T(8,128)(2,1)S(1)}, u32[]{:S(2)}, u32[]{:S(2)}) collective-permute-start(bf16[2,4,45,16,128]{4,3,2,1,0:T(8,128)(2,1)} %collective-permute-done.11.refs_2_), channel_id=1, source_target_pairs={{0,8},{8,0},{16,24},{24,16},{1,9},{9,1},{17,25},{25,17},{2,10},{10... | collective-permute-start | bytes 4423688 | tf_op jit(solution)/shard_map/ppermute | solution.py:448
  125.5 25.6 %collective-permute-start.15 = (bf16[2,4,45,16,128]{4,3,2,1,0:T(8,128)(2,1)S(1)}, bf16[2,4,45,16,128]{4,3,2,1,0:T(8,128)(2,1)}, u32[]{:S(2)}, u32[]{:S(2)}) collective-permute-start(bf16[2,4,45,16,128]{4,3,2,1,0:T(8,128)(2,1)S(1)} %copy-done.1), channel_id=1, source_target_pairs={{0,8},{8,0},{16,24},{24,16},{1,9},{9,1},{17,25},{25,17},{2,10},{10... | collective-permute-start | bytes 4423688 | tf_op jit(solution)/shard_map/ppermute | solution.py:448
  125.8 39.2 %collective-permute-start.16 = (bf16[2,4,45,16,128]{4,3,2,1,0:T(8,128)(2,1)S(1)}, bf16[2,4,45,16,128]{4,3,2,1,0:T(8,128)(2,1)}, u32[]{:S(2)}, u32[]{:S(2)}) collective-permute-start(bf16[2,4,45,16,128]{4,3,2,1,0:T(8,128)(2,1)S(1)} %copy-done.1), channel_id=1, source_target_pairs={{0,16},{8,24},{16,0},{24,8},{1,17},{9,25},{17,1},{25,9},{2,18},{10... | collective-permute-start | bytes 4423688 | tf_op jit(solution)/shard_map/ppermute | solution.py:448
  151.1 13.9 %copy-start.4 = (bf16[2,4,45,16,128]{4,3,2,1,0:T(8,128)(2,1)}, bf16[2,4,45,16,128]{4,3,2,1,0:T(8,128)(2,1)S(1)}, u32[]{:S(2)}) copy-start(bf16[2,4,45,16,128]{4,3,2,1,0:T(8,128)(2,1)S(1)} %collective-permute-done.14.refs_6_) | copy-start | bytes 4423684
  165.0 3.5 %collective-permute-start.17 = (bf16[2,4,45,16,128]{4,3,2,1,0:T(8,128)(2,1)}, bf16[2,4,45,16,128]{4,3,2,1,0:T(8,128)(2,1)S(1)}, u32[]{:S(2)}, u32[]{:S(2)}) collective-permute-start(bf16[2,4,45,16,128]{4,3,2,1,0:T(8,128)(2,1)} %collective-permute-done.16.refs_3_), channel_id=1, source_target_pairs={{0,8},{8,0},{16,24},{24,16},{1,9},{9,1},{17,25},{25,17},{2,10},{10... | collective-permute-start | bytes 4423688 | tf_op jit(solution)/shard_map/ppermute | solution.py:448
  168.6 1.1 copy-start.5

commit v2 on v1

--- a/solution.py
+++ b/solution.py
@@ -13,6 +13,7 @@
 bf16 = jnp.bfloat16
 f32 = jnp.float32
 MB = 1024 * 1024
+VMEM = 63 * MB
 SMALL = pl.CostEstimate(flops=200_000_000, bytes_accessed=500_000, transcendentals=0)
 
 
@@ -128,8 +129,13 @@
     inner_rows(x, weights, bias, out, first, second, width, length)
 
 
-def opening_body(x, kernel, bias, out, weights, first, second, *, width, length):
+def opening_body(x, kernel, offset, out, weights, bias, first, second, *, width, length):
     pair_matrix(kernel, weights, width)
+    shape = (width, width)
+    row = lax.broadcasted_iota(jnp.int32, shape, 0)
+    column = lax.broadcasted_iota(jnp.int32, shape, 1)
+    line = jnp.sum(jnp.where(row == column, offset[...], 0.0), axis=1, keepdims=True)
+    bias[...] = jnp.broadcast_to(jnp.concatenate([line] * 2, axis=0), bias.shape)
     inner_rows(x, weights, bias, out, first, second, width, length)
 
 
@@ -144,6 +150,8 @@
     if opening:
         out_specs.append(pl.BlockSpec((2 * width, 4 * unit), lambda m: (0, 0)))
         out_shape.append(jax.ShapeDtypeStruct((2 * width, 4 * unit), bf16))
+        out_specs.append(pl.BlockSpec((2 * width, LANES), lambda m: (0, 0)))
+        out_shape.append(jax.ShapeDtypeStruct((2 * width, LANES), f32))
     result = pl.pallas_call(
         functools.partial(
             opening_body if opening else inner_body, width=width, length=length
@@ -160,30 +168,33 @@
             pltpu.VMEM((height * unit, padded), bf16),
             pltpu.VMEM(((height - 2) * unit, padded), bf16),
         ],
-        compiler_params=pltpu.CompilerParams(vmem_limit_bytes=60 * MB),
+        compiler_params=pltpu.CompilerParams(vmem_limit_bytes=VMEM),
         cost_estimate=SMALL,
         name="inner_rows",
     )(x, weights, bias)
     return result if opening else result[0]
 
 
-def edges_body(x, last, first, *, height):
-    last[...] = x[:, height - 2 :]
-    first[...] = x[:, :2]
+def edges_body(last, first, last_out, first_out):
+    last_out[...] = last[...]
+    first_out[...] = first[...]
 
 
 def edges(x, start, count):
     _, height, width, length = x.shape
-    block = pl.BlockSpec((1, 2, width, length), lambda m: (m, 0, 0, 0))
+    block = (1, 2, width, length)
     return pl.pallas_call(
-        functools.partial(edges_body, height=height),
+        edges_body,
         grid=(count,),
-        in_specs=[pl.BlockSpec((1, height, width, length), lambda m: (m + start, 0, 0, 0))],
-        out_specs=[block] * 2,
-        out_shape=[jax.ShapeDtypeStruct((count, 2, width, length), bf16)] * 2,
+        in_specs=[
+            pl.BlockSpec(block, lambda m: (m + start, height // 2 - 1, 0, 0)),
+            pl.BlockSpec(block, lambda m: (m + start, 0, 0, 0)),
+        ],
+        out_specs=[pl.BlockSpec(block, lambda m: (m, 0, 0, 0))] * 2,
+        out_shape=[jax.ShapeDtypeStruct((count,) + block[1:], bf16)] * 2,
         cost_estimate=SMALL,
         name="edge_rows",
-    )(x)
+    )(x, x)
 
 
 def outer_body(ends, x, low, high, weights, bias, *refs, width, length):
@@ -233,23 +244,33 @@
             pltpu.VMEM((6 * unit, padded), bf16),
             pltpu.VMEM((4 * unit, padded), bf16),
         ],
-        compiler_params=pltpu.CompilerParams(vmem_limit_bytes=60 * MB),
+        compiler_params=pltpu.CompilerParams(vmem_limit_bytes=VMEM),
         cost_estimate=SMALL,
         name="outer_rows",
     )(ends, x, low, high, weights, bias)
 
 
-def gather_body(rows, chosen, *refs, members, parts):
-    blocks, (out, cells, picked) = refs[:-3], refs[-3:]
-    for member in range(members):
-        at = 0
-        for block in blocks[parts * member : parts * member + parts]:
-            for row in range(block.shape[1]):
-                size = block.shape[2] * SUB
-                cells[member, at : at + size] = (
-                    block[0, row].reshape(size, LANES).astype(f32)
-                )
-                at += size
+def gather_body(rows, chosen, *refs, pieces):
+    count = len(pieces)
+    arrays, (out, block, cells, picked, sems) = refs[:-5], refs[-5:]
+    members = out.shape[0]
+    copies = [
+        pltpu.make_async_copy(
+            arrays[number].at[index],
+            block.at[member, pl.ds(at, arrays[number].shape[1])],
+            sems.at[place],
+        )
+        for place, (number, index, member, at) in enumerate(pieces)
+    ]
+    for copy in copies:
+        copy.start()
+    size = block.shape[2] * SUB
+    for copy, (number, index, member, at) in zip(copies, pieces):
+        copy.wait()
+        for row in range(at, at + arrays[number].shape[1]):
+            cells[pl.ds(row * size * members + member, size, stride=members)] = (
+                block[member, row].reshape(size, LANES).astype(f32)
+            )
 
     slots = chosen.shape[0]
     group = 16
@@ -258,46 +279,40 @@
     def _(step):
         for inside in range(group):
             slot = step * group + inside
-            row = rows[slot]
-            for member in range(members):
-                picked[member, pl.ds(slot, 1)] = cells[member, pl.ds(row, 1)]
+            row = pl.multiple_of(rows[slot] * members, members)
+            picked[pl.ds(slot * members, members)] = cells[pl.ds(row, members)]
 
     ones = jnp.ones((8, LANES), bf16)
     for member in range(members):
-        single = jnp.where(chosen[...] > 0, picked[member], 0.0).astype(bf16)
+        mine = picked[pl.ds(member, slots, stride=members)]
+        single = jnp.where(chosen[...] > 0, mine, 0.0).astype(bf16)
         line = lax.dot_general(
             ones, single, (((1,), (1,)), ((), ())), preferred_element_type=f32
         )
         out[member] = line[0:1].astype(bf16)
 
 
-def gather(rows, chosen, pieces):
+def gather(rows, chosen, arrays, pieces):
     slots = chosen.shape[0]
-    specs, arrays, total = [], [], 0
-    for parts in pieces:
-        total = 0
-        for array, index in parts:
-            specs.append(
-                pl.BlockSpec((1,) + array.shape[1:], lambda i, index=index: (index, 0, 0, 0, 0))
-            )
-            arrays.append(array)
-            total += array.shape[1] * array.shape[2] * SUB
-    members = len(pieces)
+    members = 1 + max(member for _, _, member, _ in pieces)
+    height = max(at + arrays[number].shape[1] for number, _, _, at in pieces)
+    tiles = arrays[0].shape[2]
     return pl.pallas_call(
-        functools.partial(gather_body, members=members, parts=len(pieces[0])),
-        grid=(1,),
+        functools.partial(gather_body, pieces=pieces),
         in_specs=[
             pl.BlockSpec(memory_space=pltpu.SMEM),
-            pl.BlockSpec(chosen.shape, lambda i: (0, 0)),
+            pl.BlockSpec(memory_space=pltpu.VMEM),
         ]
-        + specs,
-        out_specs=pl.BlockSpec((members, 1, slots), lambda i: (0, 0, 0)),
+        + [pl.BlockSpec(memory_space=pl.ANY)] * len(arrays),
+        out_specs=pl.BlockSpec(memory_space=pltpu.VMEM),
         out_shape=jax.ShapeDtypeStruct((members, 1, slots), bf16),
         scratch_shapes=[
-            pltpu.VMEM((members, total, LANES), f32),
-            pltpu.VMEM((members, slots, LANES), f32),
-        ],
-        compiler_params=pltpu.CompilerParams(vmem_limit_bytes=60 * MB),
+            pltpu.VMEM((members, height, tiles, SUB, LANES), bf16),
+            pltpu.VMEM((height * tiles * SUB * members, LANES), f32),
+            pltpu.VMEM((slots * members, LANES), f32),
+            pltpu.SemaphoreType.DMA((len(pieces),)),
+        ],
+        compiler_params=pltpu.CompilerParams(vmem_limit_bytes=VMEM),
         cost_estimate=SMALL,
         name="gather_cells",
     )(rows, chosen, *arrays)
@@ -376,31 +391,40 @@
         out_specs=pl.BlockSpec((members, 1, width, length), lambda r: (0, r + place, 0, 0)),
         out_shape=jax.ShapeDtypeStruct(shape, bf16),
         input_output_aliases=alias,
-        compiler_params=pltpu.CompilerParams(vmem_limit_bytes=60 * MB),
+        compiler_params=pltpu.CompilerParams(vmem_limit_bytes=VMEM),
         cost_estimate=SMALL,
         name="mix_rows",
     )(weights, *arrays)
 
 
-def transform_body(gram, drive, blend, *, members):
-    highest = lax.Precision.HIGHEST
-    count = gram.shape[0]
+def product(left, right):
+    count = left.shape[1]
+    terms = [left[:, k : k + 1] * right[k : k + 1, :] for k in range(count)]
+    while len(terms) > 1:
+        terms = [a + b for a, b in zip(terms[::2], terms[1::2])]
+    return terms[0]
+
+
+def transform_body(terms, blend, *, members):
+    total = terms[0]
+    for band in range(1, terms.shape[0]):
+        total = total + terms[band]
+    count = total.shape[1]
+    gram, drive = total[:count], total[count : count + 1]
     row = lax.broadcasted_iota(jnp.int32, (count, count), 0)
     column = lax.broadcasted_iota(jnp.int32, (count, count), 1)
     eye = (row == column).astype(f32)
-    system = eye + gram[...] / (count - 1.0)
+    system = eye + gram / (count - 1.0)
     scale = jnp.sum(jnp.sum(system * eye, axis=1, keepdims=True), axis=0, keepdims=True)
     iterate = system / scale
     root = eye
     for number in range(NS_STEPS):
-        factor = 0.5 * (
-            3.0 * eye - jnp.dot(root, iterate, precision=highest, preferred_element_type=f32)
-        )
-        iterate = jnp.dot(iterate, factor, precision=highest, preferred_element_type=f32)
-        root = jnp.dot(factor, root, precision=highest, preferred_element_type=f32)
+        factor = 0.5 * (3.0 * eye - product(root, iterate))
+        iterate = product(iterate, factor)
+        root = product(factor, root)
     spread = root / jnp.sqrt(scale)
-    inverse = jnp.dot(root, root, precision=highest, preferred_element_type=f32)
-    mean_weights = jnp.sum(inverse * drive[...], axis=1, keepdims=True) / (scale * (count - 1.0))
+    inverse = product(root, root)
+    mean_weights = jnp.sum(inverse * drive, axis=1, keepdims=True) / (scale * (count - 1.0))
     combined = mean_weights + spread
     mixing = (
         1.0 / count + combined - jnp.sum(combined, axis=0, keepdims=True) * (1.0 / count)
@@ -420,16 +444,16 @@
     blend[...] = jnp.where(first == second, full, 0.0).astype(bf16)
 
 
-def transform(gram, drive, members):
-    count = gram.shape[0]
+def transform(terms, members):
+    count = terms.shape[2]
     return pl.pallas_call(
         functools.partial(transform_body, members=members),
-        in_specs=[pl.BlockSpec(memory_space=pltpu.VMEM)] * 2,
+        in_specs=[pl.BlockSpec(memory_space=pltpu.VMEM)],
         out_specs=pl.BlockSpec(memory_space=pltpu.VMEM),
         out_shape=jax.ShapeDtypeStruct((members * SUB, count * SUB), bf16),
         cost_estimate=SMALL,
         name="transform",
-    )(gram, drive)
+    )(terms)
 
 
 def after(value, *others):
@@ -459,9 +483,6 @@
 ):
     x = starting_condition
     members, height, width, length = x.shape
-    bias = jnp.broadcast_to(
-        jnp.concatenate([filter_offset_vector] * 2)[:, None], (2 * width, LANES)
-    )
     band = lax.axis_index("band")
     bands = lax.axis_size("band")
     ends = jnp.stack([band > 0, band < bands - 1]).astype(jnp.int32)
@@ -469,7 +490,9 @@
     chosen = (lanes[:, None] == jnp.arange(LANES, dtype=jnp.int32)[None, :]).astype(f32)
 
     half = members // 2
-    inner0, weights = inner(x, filter_kernel_tensor, bias, 0, half)
+    inner0, weights, bias = inner(
+        x, filter_kernel_tensor, filter_offset_vector[None, :], 0, half
+    )
     inner0_across = swap(inner0, 2)
     edges0 = edges(after(x, inner0), 0, half)
     edges1 = edges(after(x, edges0[0]), half, members - half)
@@ -479,27 +502,22 @@
     halo1 = halo(*lax.optimization_barrier((*edges1, *halo0))[:2])
 
     inner0_core = swap(after(inner0, edges0[0]), 1)
-    (outer0,) = outer(
-        ends, after(x, inner0_across, inner0_core), *halo0, weights, bias, 0, False
+    top0, bottom0 = outer(
+        ends, after(x, inner0_across, inner0_core), *halo0, weights, bias, 0, True
     )
-    outer0_across = swap(outer0, 2)
-    seen0 = gather(rows, chosen, [[(inner0, m), (outer0, m)] for m in range(half)])
+    top0_across, bottom0_across = swap(top0, 2), swap(bottom0, 2)
+
+    def pieces(*firsts):
+        return [(n, m, m, first) for n, first in enumerate(firsts) for m in range(half)]
+
+    edge = height - 4
+    seen0 = gather(rows, chosen, (inner0, top0, bottom0), pieces(0, edge, edge + 2))
     (outer1,) = outer(ends, after(x, seen0), *halo1, weights, bias, half, False)
-    seen1 = gather(
-        rows,
-        after(chosen, inner1_across),
-        [[(inner1, m), (outer1, m)] for m in range(members - half)],
-    )
-    inner1_core, outer0_core, inner0_far, inner1_far = [
-        swap(after(part, seen1), 1) for part in (inner1, outer0, inner0_across, inner1_across)
-    ]
-    seen1 = after(seen1, inner1_core, outer0_core, inner0_far, inner1_far, outer0_across)
-    seen = jnp.concatenate([seen0, seen1], axis=0)
-    seen_across = swap(seen, 2)
-    outer1_across = swap(after(outer1, seen), 2)
-    both = jnp.concatenate([seen, seen_across], axis=0)
-    both_core = swap(both, 1)
-    predicted = jnp.concatenate([both, both_core], axis=0)[:, 0].astype(f32)
+    seen1 = gather(rows, after(chosen, inner1_across), (inner1, outer1), pieces(0, edge))
+    seen = jnp.concatenate([seen0, after(seen1, top0_across, bottom0_across)], axis=0)
+    seen_parts = [seen] + [swap(seen, bits) for bits in (2, 1, 3)]
+    predicted = jnp.concatenate(seen_parts, axis=0)[:, 0].astype(f32)
+    outer1_across = swap(after(outer1, *seen_parts[1:]), 2)
     ensemble_vectors = predicted.shape[0]
     slots = jnp.arange(measured_cell_position.shape[0], dtype=jnp.int32)
     live = (slots < measured_slot_number[0]).astype(f32)
@@ -508,20 +526,36 @@
     weighted = anomaly * (measured_precision_factor * live)[None, :]
     gram_part = jnp.dot(weighted, anomaly.T, precision=lax.Precision.HIGHEST)
     drive_part = jnp.dot(weighted, measured_reading - mean, precision=lax.Precision.HIGHEST)
-    gram, drive = lax.psum((gram_part, drive_part), "band")
-    outer0_far, outer1_core = [
-        swap(after(part, both_core), 1) for part in (outer0_across, outer1)
+    terms = jnp.concatenate(
+        [gram_part, drive_part[None, :], jnp.zeros((7, ensemble_vectors), f32)], axis=0
+    )
+    terms = lax.all_to_all(jnp.broadcast_to(terms, (bands,) + terms.shape), "band", 0, 0)
+    inner1_core, inner0_far, inner1_far, outer1_core = [
+        swap(after(part, *seen_parts[1:]), 1)
+        for part in (inner1, inner0_across, inner1_across, outer1)
     ]
-    blend = transform(gram, after(drive, outer0_far, outer1_core)[None, :], members)
+    terms = after(terms, inner1_core, inner0_far, inner1_far, outer1_core)
+    top0_core, bottom0_core, top0_far = [
+        swap(after(part, terms), 1) for part in (top0, bottom0, top0_across)
+    ]
+    blend = transform(terms, members)
+    blend = after(blend, top0_core, bottom0_core, top0_far)
+    bottom0_far = swap(after(bottom0_across, blend), 1)
 
     pieces = (inner0, inner1, inner0_across, inner1_across)
     pieces += (inner0_core, inner1_core, inner0_far, inner1_far)
     result = mix(blend, [(piece, 0) for piece in pieces], x.shape, 2, height - 4, None)
     outer1_far = swap(after(outer1_across, result), 1)
-    pieces = (outer0, outer1, outer0_across, outer1_across)
-    pieces += (outer0_core, outer1_core, outer0_far, outer1_far)
-    result = mix(blend, [(piece, 0) for piece in pieces], x.shape, 0, 2, result)
-    return mix(blend, [(piece, 2) for piece in pieces], x.shape, height - 2, 2, result)
+    others = (outer1, outer1_across, outer1_core, outer1_far)
+    for place, first, parts in (
+        (0, 0, (top0, top0_across, top0_core, top0_far)),
+        (height - 2, 2, (bottom0, bottom0_across, bottom0_core, bottom0_far)),
+    ):
+        pieces = []
+        for part, other in zip(parts, others):
+            pieces += [(part, 0), (other, first)]
+        result = mix(blend, pieces, x.shape, place, 2, result)
+    return result
 
 
 def solution(mesh):

time: 179 us -> 166 us (0.927)
  blocking collectives: 21.7 us -> 12.2 us
  waiting for transfers between devices: 49.8 us -> 46.9 us
    psum x1 -> x0, blocking collectives: 21.7 us -> none  [local(): gram, drive = lax.psum((gram_part, drive_part), 'band')]
    all_to_all x0 -> x1, blocking collectives: none -> 12.2 us  [local(): lax.all_to_all(jnp.broadcast_to(terms, (bands,) + terms.shape), 'band', 0...]
    ppermute x2, waiting for transfers between devices: 3.62 us -> 0.01 us  [halo(): lax.ppermute(first, 'band', backward)]
    ppermute x14 -> x18, starting transfers between devices: 6.73 us -> 10 us  [swap(): return lax.ppermute(block, 'member', [(i, i ^ bit) for i in range(size)])]
    ppermute x2, starting transfers between devices: 10.8 us -> 8.62 us  [halo(): lax.ppermute(last, 'band', forward)]
    ppermute x14 -> x18, waiting for transfers between devices: 16.2 us -> 15.5 us  [swap(): return lax.ppermute(block, 'member', [(i, i ^ bit) for i in range(size)])]
  transfers between devices with their start and end apart: 18 -> 22, of which waited for: 8 -> 7; matrix products, arithmetic and copies ran while one was open for 3% -> 5% of each run, Pallas kernels for 33% -> 36%
where the time goes in v2:
time: 166 us
  Pallas kernels  74.3 us (45%)
  waiting for transfers between devices  46.9 us (28%)
  starting transfers between devices  21.4 us (13%)
  blocking collectives  12.2 us (7%)
  local copies, waits for them, and re-layouts  4.89 us (3%)
  other arithmetic  4.47 us (3%)
    ppermute x2, waiting for transfers between devices, halo(): lax.ppermute(last, 'band', forward)  31.5 us
    pallas_call x2, Pallas kernels, outer(): pl.pallas_call(functools.partial(outer_body, width=width, length=length),...  18.3 us
    pallas_call x3, Pallas kernels, mix(): pl.pallas_call(functools.partial(mix_body, width=width, length=length, so...  15.8 us
    pallas_call x2, Pallas kernels, inner(): pl.pallas_call(functools.partial(opening_body if opening else inner_body,...  15.5 us
    ppermute x18, waiting for transfers between devices, swap(): return lax.ppermute(block, 'member', [(i, i ^ bit) for i in range(size)])  15.5 us
    pallas_call x2, Pallas kernels, gather(): pl.pallas_call(functools.partial(gather_body, pieces=pieces), in_specs=[p...  13.9 us
    all_to_all x1, blocking collectives, local(): lax.all_to_all(jnp.broadcast_to(terms, (bands,) + terms.shape), 'band', 0...  12.2 us
    ppermute x18, starting transfers between devices, swap(): return lax.ppermute(block, 'member', [(i, i ^ bit) for i in range(size)])  10 us
  transfers between devices with their start and end apart: 22, of which 7 were waited for; matrix products, arithmetic and copies ran while one was open for 5% of the time, Pallas kernels for 36%

profile of v2, /device:TPU:0, one launch (start us, length us, event | category | flops | bytes accessed | tf_op | source)
XLA Modules:
  0.0 165.7 jit_solution(17946922068961167185)
XLA Ops:
  0.0 8.3 %inner_rows.2 = (bf16[2,4,45,16,128]{4,3,2,1,0:T(8,128)(2,1)}, bf16[128,768]{1,0:T(8,128)(2,1)}, f32[128,128]{1,0:T(8,128)}) custom-call(bf16[4,8,64,1440]{3,2,1,0:T(8,128)(2,1)} %x.4, bf16[3,3,64,64]{3,2,1,0:T(8,128)(2,1)} %kernel.1, f32[1,64]{1,0:T(1,128)} %bitcast.44), custom_call_target="tpu_custom_call" | custom-call | flops 200000000 | bytes 500000 | tf_op jit(solution)/shard_map/inner_rows/pallas_call | solution.py:155
  8.3 2.3 %edge_rows.2 = (bf16[2,2,64,1440]{3,2,1,0:T(8,128)(2,1)}, bf16[2,2,64,1440]{3,2,1,0:T(8,128)(2,1)}) custom-call(bf16[4,8,64,1440]{3,2,1,0:T(8,128)(2,1)} %x.4, bf16[4,8,64,1440]{3,2,1,0:T(8,128)(2,1)} %x.4), custom_call_target="tpu_custom_call" | custom-call | flops 200000000 | bytes 500000 | tf_op jit(solution)/shard_map/edge_rows/pallas_call | solution.py:186
  10.7 0.5 collective-permute-start.1
  11.1 2.5 %collective-permute-start = (bf16[2,4,45,16,128]{4,3,2,1,0:T(8,128)(2,1)}, bf16[2,4,45,16,128]{4,3,2,1,0:T(8,128)(2,1)}, u32[]{:S(2)}, u32[]{:S(2)}) collective-permute-start(bf16[2,4,45,16,128]{4,3,2,1,0:T(8,128)(2,1)} %get-tuple-element.38.refs_0_), channel_id=1, source_target_pairs={{0,16},{8,24},{16,0},{24,8},{1,17},{9,25},{17,1},{25,9},{2,18},{10... | collective-permute-start | bytes 4423688 | tf_op jit(solution)/shard_map/ppermute | solution.py:472
  13.6 3.4 %collective-permute-start.2 = (bf16[2,2,64,1440]{3,2,1,0:T(8,128)(2,1)}, bf16[2,2,64,1440]{3,2,1,0:T(8,128)(2,1)S(1)}, u32[]{:S(2)}, u32[]{:S(2)}) collective-permute-start(bf16[2,2,64,1440]{3,2,1,0:T(8,128)(2,1)} %get-tuple-element.37), channel_id=1, source_target_pairs={{0,1},{1,2},{2,3},{3,4},{4,5},{5,6},{6,7},{8,9},{9,10},{10,11},{11... | collective-permute-start | bytes 2211848 | tf_op jit(solution)/shard_map/ppermute | solution.py:467
  17.1 1.3 collective-permute-start.3
  18.4 2.4 %edge_rows.3 = (bf16[2,2,64,1440]{3,2,1,0:T(8,128)(2,1)}, bf16[2,2,64,1440]{3,2,1,0:T(8,128)(2,1)}) custom-call(bf16[4,8,64,1440]{3,2,1,0:T(8,128)(2,1)} %x.4, bf16[4,8,64,1440]{3,2,1,0:T(8,128)(2,1)} %x.4), custom_call_target="tpu_custom_call" | custom-call | flops 200000000 | bytes 500000 | tf_op jit(solution)/shard_map/edge_rows/pallas_call | solution.py:186
  20.8 7.2 %inner_rows.3.refs_0_.refs_1_ = bf16[2,4,45,16,128]{4,3,2,1,0:T(8,128)(2,1)} custom-call(bf16[4,8,64,1440]{3,2,1,0:T(8,128)(2,1)} %x.4, bf16[128,768]{1,0:T(8,128)(2,1)} %get-tuple-element.41.weights, f32[128,128]{1,0:T(8,128)} %get-tuple-element.42.bias), custom_call_target="tpu_custom_call" | custom-call | flops 200000000 | bytes 500000 | tf_op jit(solution)/shard_map/inner_rows/pallas_call | solution.py:155
  28.0 0.5 collective-permute-start.4
  29.2 0.1 pad.2.clone
  29.2 0.6 add_convert_fusion.ends
  29.8 0.6 fusion.20
  30.5 20.9 %collective-permute-done.2.low = bf16[2,2,64,1440]{3,2,1,0:T(8,128)(2,1)S(1)} collective-permute-done((bf16[2,2,64,1440]{3,2,1,0:T(8,128)(2,1)}, bf16[2,2,64,1440]{3,2,1,0:T(8,128)(2,1)S(1)}, u32[]{:S(2)}, u32[]{:S(2)}) %collective-permute-start.2) | collective-permute-done | bytes 737312 | tf_op jit(solution)/shard_map/ppermute | solution.py:467
  51.4 5.2 %collective-permute-start.5 = (bf16[2,2,64,1440]{3,2,1,0:T(8,128)(2,1)}, bf16[2,2,64,1440]{3,2,1,0:T(8,128)(2,1)}, u32[]{:S(2)}, u32[]{:S(2)}) collective-permute-start(bf16[2,2,64,1440]{3,2,1,0:T(8,128)(2,1)} %get-tuple-element.51), channel_id=1, source_target_pairs={{0,1},{1,2},{2,3},{3,4},{4,5},{5,6},{6,7},{8,9},{9,10},{10,11},{11... | collective-permute-start | bytes 2211848 | tf_op jit(solution)/shard_map/ppermute | solution.py:467
  56.6 1.5 collective-permute-start.6
  58.1 0.0 collective-permute-done.1.refs_4_
  58.1 9.1 %outer_rows.2 = (bf16[2,2,45,16,128]{4,3,2,1,0:T(8,128)(2,1)}, bf16[2,2,45,16,128]{4,3,2,1,0:T(8,128)(2,1)}) custom-call(s32[2]{0:T(128)} %add_convert_fusion.ends, bf16[4,8,64,1440]{3,2,1,0:T(8,128)(2,1)} %x.4, bf16[2,2,64,1440]{3,2,1,0:T(8,128)(2,1)} %copy-done.3, bf16[2,2,64,1440]{3,2,1,0:T(8,128)(2,1)} %collective-permute-done.3.high, ...), custom_call_target="tpu_custom_call" | custom-call | flops 200000000 | bytes 500000 | tf_op jit(solution)/shard_map/outer_rows/pallas_call | solution.py:230
  67.2 0.5 collective-permute-start.7
  67.7 1.5 collective-permute-start.8
  69.2 1.3 fusion.chosen
  70.5 6.9 %gather_cells.2 = bf16[2,1,2048]{2,1,0:T(2,128)(2,1)} custom-call(s32[2048]{0:T(1024)} %get-tuple-element.68.rows, f32[2048,128]{1,0:T(8,128)} %fusion.chosen, bf16[2,4,45,16,128]{4,3,2,1,0:T(8,128)(2,1)} %get-tuple-element.38.refs_0_, bf16[2,2,45,16,128]{4,3,2,1,0:T(8,128)(2,1)} %get-tuple-element.59.refs_1_.refs_0_, ...), custom_call_target="tpu_custom_call" | custom-call | flops 200000000 | bytes 500000 | tf_op jit(solution)/shard_map/gather_cells/pallas_call | solution.py:300
  77.5 0.7 copy.39
  78.2 0.5 collective-permute-done.4.refs_3_
  78.7 10.6 %collective-permute-done.5.low = bf16[2,2,64,1440]{3,2,1,0:T(8,128)(2,1)} collective-permute-done((bf16[2,2,64,1440]{3,2,1,0:T(8,128)(2,1)}, bf16[2,2,64,1440]{3,2,1,0:T(8,128)(2,1)}, u32[]{:S(2)}, u32[]{:S(2)}) %collective-permute-start.5) | collective-permute-done | bytes 737312 | tf_op jit(solution)/shard_map/ppermute | solution.py:467
  89.3 0.0 collective-permute-done.6.high
  89.3 9.2 %outer_rows.3.refs_1_ = bf16[2,4,45,16,128]{4,3,2,1,0:T(8,128)(2,1)} custom-call(s32[2]{0:T(128)} %add_convert_fusion.ends, bf16[4,8,64,1440]{3,2,1,0:T(8,128)(2,1)} %x.4, bf16[2,2,64,1440]{3,2,1,0:T(8,128)(2,1)} %collective-permute-done.5.low, bf16[2,2,64,1440]{3,2,1,0:T(8,128)(2,1)} %collective-permute-done.6.high, ...), custom_call_target="tpu_custom_call" | custom-call | flops 200000000 | bytes 500000 | tf_op jit(solution)/shard_map/outer_rows/pallas_call | solution.py:230
  98.5 7.0 %gather_cells.3 = bf16[2,1,2048]{2,1,0:T(2,128)(2,1)} custom-call(s32[2048]{0:T(1024)} %get-tuple-element.68.rows, f32[2048,128]{1,0:T(8,128)} %fusion.chosen, bf16[2,4,45,16,128]{4,3,2,1,0:T(8,128)(2,1)} %inner_rows.3.refs_0_.refs_1_, bf16[2,4,45,16,128]{4,3,2,1,0:T(8,128)(2,1)} %outer_rows.3.refs_1_), custom_call_target="tpu_custom_call" | custom-call | flops 200000000 | bytes 500000 | tf_op jit(solution)/shard_map/gather_cells/pallas_call | solution.py:300
  105.6 0.0 collective-permute-done.7.refs_2_
  105.6 4.5 %collective-permute-done.8.refs_2_ = bf16[2,2,45,16,128]{4,3,2,1,0:T(8,128)(2,1)} collective-permute-done((bf16[2,2,45,16,128]{4,3,2,1,0:T(8,128)(2,1)}, bf16[2,2,45,16,128]{4,3,2,1,0:T(8,128)(2,1)}, u32[]{:S(2)}, u32[]{:S(2)}) %collective-permute-start.8) | collective-permute-done | bytes 737312 | tf_op jit(solution)/shard_map/ppermute | solution.py:472
  110.1 0.8 pad_maximum_fusion
  110.9 0.1 collective-permute-start.10
  111.0 1.9 %collective-permute-start.11 = (bf16[4,1,2048]{2,1,0:T(2,128)(2,1)S(1)}, bf16[4,1,2048]{2,1,0:T(2,128)(2,1)S(1)}, u32[]{:S(2)}, u32[]{:S(2)}) collective-permute-start(bf16[4,1,2048]{2,1,0:T(2,128)(2,1)S(1)} %pad_maximum_fusion), channel_id=1, source_target_pairs={{0,24},{8,16},{16,8},{24,0},{1,25},{9,17},{17,9},{25,1},{2,26},{10... | collective-permute-start | bytes 49160 | tf_op jit(solution)/shard_map/ppermute | solution.py:472
  112.8 0.3 collective-permute-start.9
  113.1 0.7 constant_dynamic-update-slice_fusion.3
  113.8 0.7 copy.38
  114.6 0.0 collective-permute-done.10
  114.6 2.1 %collective-permute-done.9 = bf16[4,1,2048]{2,1,0:T(2,128)(2,1)S(1)} collective-permute-done((bf16[4,1,2048]{2,1,0:T(2,128)(2,1)S(1)}, bf16[4,1,2048]{2,1,0:T(2,128)(2,1)S(1)}, u32[]{:S(2)}, u32[]{:S(2)}) %collective-permute-start.9) | collective-permute-done | bytes 16416 | tf_op jit(solution)/shard_map/ppermute | solution.py:472
  116.7 0.4 collective-permute-start.19
  117.2 0.2 collective-permute-start.14
  117.4 0.3 collective-permute-start.13
  117.7 0.2 collective-permute-start.12
  118.0 0.1 concatenate.49
  118.2 0.1 convert_reduce_fusion
  118.3 0.2 fusion.5
  118.6 0.2 convert_element_type.41
  118.8 0.3 fusion.2
  119.1 0.1 maximum_maximum_fusion
  119.2 0.1 reshape.283
  119.3 12.2 %all_to_all.5 = f32[8,1,384]{2,1,0:T(1,128)S(1)} all-to-all(f32[8,1,384]{2,1,0:T(1,128)S(1)} %reshape.283), channel_id=1, replica_groups=mesh['member'=4,'band'=8] {'band'}, dimensions={0} | all-to-all | bytes 24576 | tf_op jit(solution)/shard_map/all_to_all | solution.py:532
  131.6 0.5 broadcast.104
  132.1 0.7 reduce.1
  132.8 0.1 reshape.284
  132.9 0.1 collective-permute-start.18
  133.0 0.5 collective-permute-start.17
  133.5 0.1 collective-permute-start.16
  133.6 0.7 copy.19.terms
  134.3 6.0 %transform.1.weights = bf16[64,256]{1,0:T(8,128)(2,1)} custom-call(f32[8,24,16]{2,1,0:T(8,128)} %copy.19.terms), custom_call_target="tpu_custom_call" | custom-call | flops 200000000 | bytes 500000 | tf_op jit(solution)/shard_map/transform/pallas_call | solution.py:449
  140.3 7.3 %mix_rows.3.refs_8_ = bf16[4,8,64,1440]{3,2,1,0:T(8,128)(2,1)} custom-call(bf16[64,256]{1,0:T(8,128)(2,1)} %transform.1.weights, bf16[2,4,45,16,128]{4,3,2,1,0:T(8,128)(2,1)} %get-tuple-element.38.refs_0_, bf16[2,4,45,16,128]{4,3,2,1,0:T(8,128)(2,1)} %inner_rows.3.refs_0_.refs_1_, bf16[2,4,45,16,128]{4,3,2,1,0:T(8,128)(2,1)} %collective-permute-done.refs_2_, ...), custom_call_target="tpu_custom_call" | custom-call | flops 200000000 | bytes 500000 | tf_op jit(solution)/shard_map/mix_rows/pallas_call | solution.py:387
  147.6 4.1 %collective-permute-done.19.refs_3_ = bf16[2,4,45,16,128]{4,3,2,1,0:T(8,128)(2,1)} collective-permute-done((bf16[2,4,45,16,128]{4,3,2,1,0:T(8,128)(2,1)}, bf16[2,4,45,16,128]{4,3,2,1,0:T(8,128)(2,1)}, u32[]{:S(2)}, u32[]{:S(2)}) %collective-permute-start.19) | collective-permute-done | bytes 1474592 | tf_op jit(solution)/shard_map/ppermute | solution.py:472
  151.8 0.5 collective-permute-start.20
  152.3 4.2 %collective-permute-done.21.refs_7_ = bf16[2,4,45,16,128]{4,3,2,1,0:T(8,128)(2,1)} collective-permute-done((bf16[2,4,45,16,128]{4,3,2,1,0:T(8,128)(2,1)}, bf16[2,4,45,16,128]{4,3,2,1,0:T(8,128)(2,1)}, u32[]{:S(2)}, u32[]{:S(2)}) %collective-permute-start.21) | collective-permute-done | bytes 1474592 | tf_op jit(solution)/shard_map/ppermute | solution.py:472
  156.4 4.2 %mix_rows.4.refs_8_ = bf16[4,8,64,1440]{3,2,1,0:T(8,128)(2,1)} custom-call(bf16[64,256]{1,0:T(8,128)(2,1)} %transform.1.weights, bf16[2,2,45,16,128]{4,3,2,1,0:T(8,128)(2,1)} %get-tuple-element.59.refs_1_.refs_0_, bf16[2,4,45,16,128]{4,3,2,1,0:T(8,128)(2,1)} %outer_rows.3.refs_1_, ...), custom_call_target="tpu_custom_call", output_to_operand_aliasing={{}: (9, {})} | custom-call | flops 200000000 | bytes 500000 | tf_op jit(solution)/shard_map/mix_rows/pallas_call | solution.py:387
  160.7 0.9 copy-done.4
  161.5 4.2 %mix_rows.5 = bf16[4,8,64,1440]{3,2,1,0:T(8,128)(2,1)} custom-call(bf16[64,256]{1,0:T(8,128)(2,1)} %transform.1.weights, bf16[2,2,45,16,128]{4,3,2,1,0:T(8,128)(2,1)} %get-tuple-element.60.refs_2_.refs_0_, bf16[2,4,45,16,128]{4,3,2,1,0:T(8,128)(2,1)} %outer_rows.3.refs_1_, ...), custom_call_target="tpu_custom_call", output_to_operand_aliasing={{}: (9, {})} | custom-call | flops 200000000 | bytes 500000 | tf_op jit(solution)/shard_map/mix_rows/pallas_call | solution.py:387
  (41 shorter events, 0.3 us)
Async XLA Ops:
  10.7 47.4 %collective-permute-start.1 = (bf16[2,4,45,16,128]{4,3,2,1,0:T(8,128)(2,1)}, bf16[2,4,45,16,128]{4,3,2,1,0:T(8,128)(2,1)}, u32[]{:S(2)}, u32[]{:S(2)}) collective-permute-start(bf16[2,4,45,16,128]{4,3,2,1,0:T(8,128)(2,1)} %get-tuple-element.38.refs_0_), channel_id=1, source_target_pairs={{0,8},{8,0},{16,24},{24,16},{1,9},{9,1},{17,25},{25,17},{2,10},{10... | collective-permute-start | bytes 4423688 | tf_op jit(solution)/shard_map/ppermute | solution.py:472
  11.1 46.9 %collective-permute-start = (bf16[2,4,45,16,128]{4,3,2,1,0:T(8,128)(2,1)}, bf16[2,4,45,16,128]{4,3,2,1,0:T(8,128)(2,1)}, u32[]{:S(2)}, u32[]{:S(2)}) collective-permute-start(bf16[2,4,45,16,128]{4,3,2,1,0:T(8,128)(2,1)} %get-tuple-element.38.refs_0_), channel_id=1, source_target_pairs={{0,16},{8,24},{16,0},{24,8},{1,17},{9,25},{17,1},{25,9},{2,18},{10... | collective-permute-start | bytes 4423688 | tf_op jit(solution)/shard_map/ppermute | solution.py:472
  13.6 37.7 %collective-permute-start.2 = (bf16[2,2,64,1440]{3,2,1,0:T(8,128)(2,1)}, bf16[2,2,64,1440]{3,2,1,0:T(8,128)(2,1)S(1)}, u32[]{:S(2)}, u32[]{:S(2)}) collective-permute-start(bf16[2,2,64,1440]{3,2,1,0:T(8,128)(2,1)} %get-tuple-element.37), channel_id=1, source_target_pairs={{0,1},{1,2},{2,3},{3,4},{4,5},{5,6},{6,7},{8,9},{9,10},{10,11},{11... | collective-permute-start | bytes 2211848 | tf_op jit(solution)/shard_map/ppermute | solution.py:467
  17.1 34.3 %collective-permute-start.3 = (bf16[2,2,64,1440]{3,2,1,0:T(8,128)(2,1)}, bf16[2,2,64,1440]{3,2,1,0:T(8,128)(2,1)}, u32[]{:S(2)}, u32[]{:S(2)}) collective-permute-start(bf16[2,2,64,1440]{3,2,1,0:T(8,128)(2,1)} %get-tuple-element.40), channel_id=1, source_target_pairs={{1,0},{2,1},{3,2},{4,3},{5,4},{6,5},{7,6},{9,8},{10,9},{11,10},{12... | collective-permute-start | bytes 2211848 | tf_op jit(solution)/shard_map/ppermute | solution.py:467
  20.8 9.1 %copy-start.6 = (s32[2048]{0:T(1024)S(1)}, s32[2048]{0:T(1024)}, u32[]{:S(2)}) copy-start(s32[2048]{0:T(1024)} %param.10) | copy-start | bytes 24580
  20.8 37.2 %copy-start.7 = (f32[2048]{0:T(1024)S(1)}, f32[2048]{0:T(1024)}, u32[]{:S(2)}) copy-start(f32[2048]{0:T(1024)} %param.13) | copy-start | bytes 24580
  28.0 50.7 %collective-permute-start.4 = (bf16[2,4,45,16,128]{4,3,2,1,0:T(8,128)(2,1)}, bf16[2,4,45,16,128]{4,3,2,1,0:T(8,128)(2,1)}, u32[]{:S(2)}, u32[]{:S(2)}) collective-permute-start(bf16[2,4,45,16,128]{4,3,2,1,0:T(8,128)(2,1)} %inner_rows.3.refs_0_.refs_1_), channel_id=1, source_target_pairs={{0,16},{8,24},{16,0},{24,8},{1,17},{9,25},{17,1},{25,9},{2,18},{10... | collective-permute-start | bytes 4423688 | tf_op jit(solution)/shard_map/ppermute | solution.py:472
  51.4 6.7 %copy-start.3 = (bf16[2,2,64,1440]{3,2,1,0:T(8,128)(2,1)}, bf16[2,2,64,1440]{3,2,1,0:T(8,128)(2,1)S(1)}, u32[]{:S(2)}) copy-start(bf16[2,2,64,1440]{3,2,1,0:T(8,128)(2,1)S(1)} %collective-permute-done.2.low) | copy-start | bytes 2211844
  51.4 37.9 %collective-permute-start.5 = (bf16[2,2,64,1440]{3,2,1,0:T(8,128)(2,1)}, bf16[2,2,64,1440]{3,2,1,0:T(8,128)(2,1)}, u32[]{:S(2)}, u32[]{:S(2)}) collective-permute-start(bf16[2,2,64,1440]{3,2,1,0:T(8,128)(2,1)} %get-tuple-element.51), channel_id=1, source_target_pairs={{0,1},{1,2},{2,3},{3,4},{4,5},{5,6},{6,7},{8,9},{9,10},{10,11},{11... | collective-permute-start | bytes 2211848 | tf_op jit(solution)/shard_map/ppermute | solution.py:467
  56.6 32.7 %collective-permute-start.6 = (bf16[2,2,64,1440]{3,2,1,0:T(8,128)(2,1)}, bf16[2,2,64,1440]{3,2,1,0:T(8,128)(2,1)}, u32[]{:S(2)}, u32[]{:S(2)}) collective-permute-start(bf16[2,2,64,1440]{3,2,1,0:T(8,128)(2,1)} %get-tuple-element.52), channel_id=1, source_target_pairs={{1,0},{2,1},{3,2},{4,3},{5,4},{6,5},{7,6},{9,8},{10,9},{11,10},{12... | collective-permute-start | bytes 2211848 | tf_op jit(solution)/shard_map/ppermute | solution.py:467
  67.2 38.4 %collective-permute-start.7 = (bf16[2,2,45,16,128]{4,3,2,1,0:T(8,128)(2,1)}, bf16[2,2,45,16,128]{4,3,2,1,0:T(8,128)(2,1)}, u32[]{:S(2)}, u32[]{:S(2)}) collective-permute-start(bf16[2,2,45,16,128]{4,3,2,1,0:T(8,128)(2,1)} %get-tuple-element.59.refs_1_.refs_0_), channel_id=1, source_target_pairs={{0,16},{8,24},{16,0},{24,8},{1,17},{9,25},{17,1},{25,9},{2,18},{10... | collective-permute-start | bytes 2211848 | tf_op jit(solution)/shard_map/ppermute | solution.py:472
  67.7 42.4 %collective-permute-start.8 = (bf16[2,2,45,16,128]{4,3,2,1,0:T(8,128)(2,1)}, bf16[2,2,45,16,128]{4,3,2,1,0:T(8,128)(2,1)}, u32[]{:S(2)}, u32[]{:S(2)}) collective-permute-start(bf16[2,2,45,16,128]{4,3,2,1,0:T(8,128)(2,1)} %get-tuple-element.60.refs_2_.refs_0_), channel_id=1, source_target_pairs={{0,16},{8,24},{16,0},{24,8},{1,17},{9,25},{17,1},{25,9},{2,18},{10... | collective-permute-start | bytes 2211848 | tf_op jit(solution)/shard_map/ppermute | solution.py:472
  98.5 7.0 %copy-start.5 = (bf16[2,1,2048]{2,1,0:T(2,128)(2,1)S(1)}, bf16[2,1,2048]{2,1,0:T(2,128)(2,1)}, u32[]{:S(2)}) copy-start(bf16[2,1,2048]{2,1,0:T(2,128)(2,1)} %gather_cells.2) | copy-start | bytes 24580
  98.5 19.8 %copy-start.8 = (f32[2048]{0:T(1024)S(1)}, f32[2048]{0:T(1024)}, u32[]{:S(2)}) copy-start(f32[2048]{0:T(1024)} %param.12) | copy-start | bytes 24580
  105.5 27.4 %copy-start = (bf16[2,2,45,16,128]{4,3,2,1,0:T(8,128)(2,1)S(1)}, bf16[2,2,45,16,128]{4,3,2,1,0:T(8,128)(2,1)}, u32[]{:S(2)}) copy-start(bf16[2,2,45,16,128]{4,3,2,1,0:T(8,128)(2,1)} %get-tuple-element.60.refs_2_.refs_0_) | copy-start | bytes 2211844
  105.5 27.9 %copy-start.1 = (bf16[2,2,45,16,128]{4,3,2,1,0:T(8,128)(2,1)S(1)}, bf16[2,2,45,16,128]{4,3,2,1,0:T(8,128)(2,1)}, u32[]{:S(2)}) copy-start(bf16[2,2,45,16,128]{4,3,2,1,0:T(8,128)(2,1)} %get-tuple-element.59.refs_1_.refs_0_) | copy-start | bytes 2211844
  110.9 3.7 %collective-permute-start.10 = (bf16[4,1,2048]{2,1,0:T(2,128)(2,1)S(1)}, bf16[4,1,2048]{2,1,0:T(2,128)(2,1)S(1)}, u32[]{:S(2)}, u32[]{:S(2)}) collective-permute-start(bf16[4,1,2048]{2,1,0:T(2,128)(2,1)S(1)} %pad_maximum_fusion), channel_id=1, source_target_pairs={{0,8},{8,0},{16,24},{24,16},{1,9},{9,1},{17,25},{25,17},{2,10},{10... | collective-permute-start | bytes 49160 | tf_op jit(solution)/shard_map/ppermute | solution.py:472
  111.0 3.6 %collective-permute-start.11 = (bf16[4,1,2048]{2,1,0:T(2,128)(2,1)S(1)}, bf16[4,1,2048]{2,1,0:T(2,128)(2,1)S(1)}, u32[]{:S(2)}, u32[]{:S(2)}) collective-permute-start(bf16[4,1,2048]{2,1,0:T(2,128)(2,1)S(1)} %pad_maximum_fusion), channel_id=1, source_target_pairs={{0,24},{8,16},{16,8},{24,0},{1,25},{9,17},{17,9},{25,1},{2,26},{10... | collective-permute-start | bytes 49160 | tf_op jit(solution)/shard_map/ppermute | solution.py:472
  112.8 3.9 %collective-permute-start.9 = (bf16[4,1,2048]{2,1,0:T(2,128)(2,1)S(1)}, bf16[4,1,2048]{2,1,0:T(2,128)(2,1)S(1)}, u32[]{:S(2)}, u32[]{:S(2)}) collective-permute-start(bf16[4,1,2048]{2,1,0:T(2,128)(2,1)S(1)} %pad_maximum_fusion), channel_id=1, source_target_pairs={{0,16},{8,24},{16,0},{24,8},{1,17},{9,25},{17,1},{25,9},{2,18},{10... | collective-permute-start | bytes 49160 | tf_op jit(solution)/shard_map/ppermute | solution.py:472
  116.7 16.1 %collective-permute-start.15 = (bf16[2,4,45,16,128]{4,3,2,1,0:T(8,128)(2,1)}, bf16[2,4,45,16,128]{4,3,2,1,0:T(8,128)(2,1)}, u32[]{:S(2)}, u32[]{:S(2)}) collective-permute-start(bf16[2,4,45,16,128]{4,3,2,1,0:T(8,128)(2,1)} %outer_rows.3.refs_1_), channel_id=1, source_target_pairs={{0,8},{8,0},{16,24},{24,16},{1,9},{9,1},{17,25},{25,17},{2,10},{10... | collective-permute-start | bytes 4423688 | tf_op jit(solution)/shard_map/ppermute | solution.py:472
  116.7 35.0 %collective-permute-start.19 = (bf16[2,4,45,16,128]{4,3,2,1,0:T(8,128)(2,1)}, bf16[2,4,45,16,128]{4,3,2,1,0:T(8,128)(2,1)}, u32[]{:S(2)}, u32[]{:S(2)}) collective-permute-start(bf16[2,4,45,16,128]{4,3,2,1,0:T(8,128)(2,1)} %outer_rows.3.refs_1_), channel_id=1, source_target_pairs={{0,16},{8,24},{16,0},{24,8},{1,17},{9,25},{17,1},{25,9},{2,18},{10... | collective-permute-start | bytes 4423688 | tf_op jit(solution)/shard_map/ppermute | solution.py:472
  117.2 15.7 %collective-permute-start.14 = (bf16[2,4,45,16,128]{4,3,2,1,0:T(8,128)(2,1)}, bf16[2,4,45,16,128]{4,3,2,1,0:T(8,128)(2,1)S(1)}, u32[]{:S(2)}, u32[]{:S(2)}) collective-permute-start(bf16[2,4,45,16,128]{4,3,2,1,0:T(8,128)(2,1)} %collective-permute-done.4.refs_3_), channel_id=1, source_target_pairs={{0,8},{8,0},{16,24},{24,16},{1,9},{9,1},{17,25},{25,17},{2,10},{10... | collective-permute-start | bytes 4423688 | tf_op jit(solution)/shard_map/ppermute | solution.py:472
  117.4 15.5 %collective-permute-start.13 = (bf16[2,4,45,16,128]{4,3,2,1,0:T(8,128)(2,1)}, bf16[2,4,45,16,128]{4,3,2,1,0:T(8,128)(2,1)}, u32[]{:S(2)}, u32[]{:S(2)}) collective-permute-start(bf16[2,4,45,16,128]{4,3,2,1,0:T(8,128)(2,1)} %collective-permute-done.refs_2_), channel_id=1, source_target_pairs={{0,8},{8,0},{16,24},{24,16},{1,9},{9,1},{17,25},{25,17},{2,10},{10... | collective-permute-start | bytes 4423688 | tf_op jit(solution)/shard_map/ppermute | solution.py:472
  117.7 15.2 %collective-permute-start.12 = (bf16[2,4,45,16,128]{4,3,2,1,0:T(8,128)(2,1)}, bf16[2,4,45,16,128]{4,3,2,1,0:T(8,128)(2,1)}, u32[]{:S(2)}, u32[]{:S(2)}) collective-permute-start(bf16[2,4,45,16,128]{4,3,2,1,0:T(8,128)(2,1)} %inner_rows.3.refs_0_.refs_1_), channel_id=1, source_target_pairs={{0,8},{8,0},{16,24},{24,16},{1,9},{9,1},{17,25},{25,17},{2,10},{10... | collective-permute-start | bytes 4423688 | tf_op jit(solution)/shard_map/ppermute | solution.py:472
  132.9 7.4 %copy-start.2 = (bf16[2,4,45,16,128]{4,3,2,1,0:T(8,128)(2,1)}, bf16[2,4,45,16,128]{4,3,2,1,0:T(8,128)(2,1)S(1)}, u32[]{:S(2)}) copy-start(bf16[2,4,45,16,128]{4,3,2,1,0:T(8,128)(2,1)S(1)} %collective-permute-done.14.refs_7_) | copy-start | bytes 4423684
  132.9 7.4 %collective-permute-start.18 = (bf16[2,2,45,16,128]{4,3,2,1,0:T(8,128)(2,1)}, bf16[2,2,45,16,128]{4,3,2,1,0:T(8,128)(2,1)}, u32[]{:S(2)}, u32[]{:S(2)}) collective-permute-start(bf16[2,2,45,16,128]{4,3,2,1,0:T(8,128)(2,1)} %collective-permute-done.7.refs_2_), channel_id=1, source_target_pairs={{0,8},{8,0},{16,24},{24,16},{1,9},{9,1},{17,25},{25,17},{2,10},{10... | collective-permute-start | bytes 2211848 | tf_op jit(solution)/shard_map/ppermute | solution.py:472
  133.0 7.3 %collective-permute-start.17 = (bf16[2,2,45,16,128]{4,3,2,1,0:T(8,128)(2,1)S(1)}, bf16[2,2,45,16,128]{4,3,2,1,0:T(8,128)(2,1)}, u32[]{:S(2)}, u32[]{:S(2)}) collective-permute-start(bf16[2,2,45,16,128]{4,3,2,1,0:T(8,128)(2,1)S(1)} %copy-done), channel_id=1, source_target_pairs={{0,8},{8,0},{16,24},{24,16},{1,9},{9,1},{17,25},{25,17},{2,10},{10... | collective-permute-start | bytes 2211848 | tf_op jit(solution)/shard_map/ppermute | solution.py:472
  133.5 6.8 %collective-permute-start.16 = (bf16[2,2,45,16,128]{4,3,2,1,0:T(8,128)(2,1)S(1)}, bf16[2,2,45,16,128]{4,3,2,1,0:T(8,128)(2,1)}, u32[]{:S(2)}, u32[]{:S(2)}) collective-permute-start(bf16[2,2,45,16,128]{4,3,2,1,0:T(8,128)(2,1)S(1)} %copy-done.1), channel_id=1, source_target_pairs={{0,8},{8,0},{16,24},{24,16},{1,9},{9,1},{17,25},{25,17},{2,10},{10... | collective-permute-start | bytes 2211848 | tf_op jit(solution)/shard_map/ppermute | solution.py:472
  151.8 4.7 %collective-permute-start.21 = (bf16[2,4,45,16,128]{4,3,2,1,0:T(8,128)(2,1)}, bf16[2,4,45,16,128]{4,3,2,1,0:T(8,128)(2,1)}, u32[]{:S(2)}, u32[]{:S(2)}) collective-permute-start(bf16[2,4,45,16,128]{4,3,2,1,0:T(8,128)(2,1)} %collective-permute-done.19.refs_3_), channel_id=1, source_target_pairs={{0,8},{8,0},{16,24},{24,16},{1,9},{9,1},{17,25},{25,17},{2,10},{10... | collective-permute-start | bytes 4423688 | tf_op jit(solution)/shard_map/ppermute | solution.py:472
  151.8 8.9 %collective-permute-start.20 = (bf16[2,2,45,16,128]{4,3,2,1,0:T(8,128)(2,1)}, bf16[2,2,45,16,128]{4,3,2,1,0:T(8,128)(2,1)S(1)}, u32[]{:S(2)}, u32[]{:S(2)}) collective-permute-start(bf16[2,2,45,16,128]{4,3,2,1,0:T(8,128)(2,1)} %collective-permute-done.8.refs_2_), channel_id=1, source_target_pairs={{0,8},{8,0},{16,24},{24,16},{1,9},{9,1},{17,25},{25,17},{2,10},{10... | collective-permute-start | bytes 2211848 | tf_op jit(solution)/shard_map/ppermute | solution.py:472
  160.6 0.9 copy-start.4

commit v3 on v2

--- a/solution.py
+++ b/solution.py
@@ -114,29 +114,27 @@
                 emit(top + half, value[half * width : (half + 1) * width], lanes.start)
 
 
-def inner_rows(x, weights, bias, out, first, second, width, length):
+def inner_body(x, weights, bias, out, last, first, stack, second, *, width, length):
     rows = x.shape[1]
+    last[0] = x[0, rows - 2 :]
+    first[0] = x[0, :2]
     for row in range(rows):
-        load_row(first, row * 3 * width, width, length, x[0, row])
+        load_row(stack, row * 3 * width, width, length, x[0, row])
 
     def emit(row, value, at):
         write_tiles(out, row, value, at, width, length)
 
-    two_steps(first, second, rows, weights, bias, emit, None, width, length)
-
-
-def inner_body(x, weights, bias, out, first, second, *, width, length):
-    inner_rows(x, weights, bias, out, first, second, width, length)
-
-
-def opening_body(x, kernel, offset, out, weights, bias, first, second, *, width, length):
+    two_steps(stack, second, rows, weights, bias, emit, None, width, length)
+
+
+def opening_body(x, kernel, offset, out, last, first, weights, bias, *scratch, width, length):
     pair_matrix(kernel, weights, width)
     shape = (width, width)
     row = lax.broadcasted_iota(jnp.int32, shape, 0)
     column = lax.broadcasted_iota(jnp.int32, shape, 1)
     line = jnp.sum(jnp.where(row == column, offset[...], 0.0), axis=1, keepdims=True)
     bias[...] = jnp.broadcast_to(jnp.concatenate([line] * 2, axis=0), bias.shape)
-    inner_rows(x, weights, bias, out, first, second, width, length)
+    inner_body(x, weights, bias, out, last, first, *scratch, width=width, length=length)
 
 
 def inner(x, weights, bias, start, count):
@@ -147,12 +145,14 @@
     opening = weights.ndim == 4
     out_specs = [pl.BlockSpec((1, height - 4, tiles, SUB, LANES), lambda m: (m, 0, 0, 0, 0))]
     out_shape = [jax.ShapeDtypeStruct((count, height - 4, tiles, SUB, LANES), bf16)]
+    out_specs += [pl.BlockSpec((1, 2, width, length), lambda m: (m, 0, 0, 0))] * 2
+    out_shape += [jax.ShapeDtypeStruct((count, 2, width, length), bf16)] * 2
     if opening:
         out_specs.append(pl.BlockSpec((2 * width, 4 * unit), lambda m: (0, 0)))
         out_shape.append(jax.ShapeDtypeStruct((2 * width, 4 * unit), bf16))
         out_specs.append(pl.BlockSpec((2 * width, LANES), lambda m: (0, 0)))
         out_shape.append(jax.ShapeDtypeStruct((2 * width, LANES), f32))
-    result = pl.pallas_call(
+    return pl.pallas_call(
         functools.partial(
             opening_body if opening else inner_body, width=width, length=length
         ),
@@ -172,32 +172,9 @@
         cost_estimate=SMALL,
         name="inner_rows",
     )(x, weights, bias)
-    return result if opening else result[0]
-
-
-def edges_body(last, first, last_out, first_out):
-    last_out[...] = last[...]
-    first_out[...] = first[...]
-
-
-def edges(x, start, count):
-    _, height, width, length = x.shape
-    block = (1, 2, width, length)
-    return pl.pallas_call(
-        edges_body,
-        grid=(count,),
-        in_specs=[
-            pl.BlockSpec(block, lambda m: (m + start, height // 2 - 1, 0, 0)),
-            pl.BlockSpec(block, lambda m: (m + start, 0, 0, 0)),
-        ],
-        out_specs=[pl.BlockSpec(block, lambda m: (m, 0, 0, 0))] * 2,
-        out_shape=[jax.ShapeDtypeStruct((count,) + block[1:], bf16)] * 2,
-        cost_estimate=SMALL,
-        name="edge_rows",
-    )(x, x)
-
-
-def outer_body(ends, x, low, high, weights, bias, *refs, width, length):
+
+
+def outer_body(ends, x, low, high, weights, bias, *refs, cut, width, length):
     outs, (first, second) = refs[:-2], refs[-2:]
     unit = 3 * width
     height = x.shape[1]
@@ -210,7 +187,8 @@
             load_row(first, row * unit, width, length, source)
 
         def emit(row, value, at, side=side):
-            write_tiles(outs[-1 if side else 0], 2 * side * (2 - len(outs)) + row, value, at, width, length)
+            place = 2 * side + row
+            write_tiles(outs[place // cut], place % cut, value, at, width, length)
 
         def mask(row, value, side=side):
             if row == (0 if side == 0 else 3):
@@ -220,15 +198,15 @@
         two_steps(first, second, 6, weights, bias, emit, mask, width, length)
 
 
-def outer(ends, x, low, high, weights, bias, start, split):
+def outer(ends, x, low, high, weights, bias, start, cut):
     _, height, width, length = x.shape
     count = low.shape[0]
-    arrays, each = (2, 2) if split else (1, 4)
+    sizes = (cut,) * (4 // cut)
     padded = round_up(length, LANES)
     tiles = width * length // (SUB * LANES)
     unit = 3 * width
     return pl.pallas_call(
-        functools.partial(outer_body, width=width, length=length),
+        functools.partial(outer_body, cut=cut, width=width, length=length),
         grid=(count,),
         in_specs=[
             pl.BlockSpec(memory_space=pltpu.SMEM),
@@ -238,8 +216,12 @@
             pl.BlockSpec(weights.shape, lambda m: (0, 0)),
             pl.BlockSpec(bias.shape, lambda m: (0, 0)),
         ],
-        out_specs=[pl.BlockSpec((1, each, tiles, SUB, LANES), lambda m: (m, 0, 0, 0, 0))] * arrays,
-        out_shape=[jax.ShapeDtypeStruct((count, each, tiles, SUB, LANES), bf16)] * arrays,
+        out_specs=[
+            pl.BlockSpec((1, size, tiles, SUB, LANES), lambda m: (m, 0, 0, 0, 0)) for size in sizes
+        ],
+        out_shape=[
+            jax.ShapeDtypeStruct((count, size, tiles, SUB, LANES), bf16) for size in sizes
+        ],
         scratch_shapes=[
             pltpu.VMEM((6 * unit, padded), bf16),
             pltpu.VMEM((4 * unit, padded), bf16),
@@ -250,10 +232,11 @@
     )(ends, x, low, high, weights, bias)
 
 
-def gather_body(rows, chosen, *refs, pieces):
-    count = len(pieces)
+def gather_body(rows, chosen, *refs, pieces, kept):
     arrays, (out, block, cells, picked, sems) = refs[:-5], refs[-5:]
-    members = out.shape[0]
+    members = block.shape[0]
+    if kept:
+        out[:kept] = arrays[-1][...]
     copies = [
         pltpu.make_async_copy(
             arrays[number].at[index],
@@ -289,23 +272,25 @@
         line = lax.dot_general(
             ones, single, (((1,), (1,)), ((), ())), preferred_element_type=f32
         )
-        out[member] = line[0:1].astype(bf16)
-
-
-def gather(rows, chosen, arrays, pieces):
+        out[kept + member] = line[0:1].astype(bf16)
+
+
+def gather(rows, chosen, arrays, pieces, earlier=()):
     slots = chosen.shape[0]
     members = 1 + max(member for _, _, member, _ in pieces)
     height = max(at + arrays[number].shape[1] for number, _, _, at in pieces)
     tiles = arrays[0].shape[2]
+    kept = sum(part.shape[0] for part in earlier)
     return pl.pallas_call(
-        functools.partial(gather_body, pieces=pieces),
+        functools.partial(gather_body, pieces=pieces, kept=kept),
         in_specs=[
             pl.BlockSpec(memory_space=pltpu.SMEM),
             pl.BlockSpec(memory_space=pltpu.VMEM),
         ]
-        + [pl.BlockSpec(memory_space=pl.ANY)] * len(arrays),
+        + [pl.BlockSpec(memory_space=pl.ANY)] * len(arrays)
+        + [pl.BlockSpec(memory_space=pltpu.VMEM)] * len(earlier),
         out_specs=pl.BlockSpec(memory_space=pltpu.VMEM),
-        out_shape=jax.ShapeDtypeStruct((members, 1, slots), bf16),
+        out_shape=jax.ShapeDtypeStruct((kept + members, 1, slots), bf16),
         scratch_shapes=[
             pltpu.VMEM((members, height, tiles, SUB, LANES), bf16),
             pltpu.VMEM((height * tiles * SUB * members, LANES), f32),
@@ -315,7 +300,7 @@
         compiler_params=pltpu.CompilerParams(vmem_limit_bytes=VMEM),
         cost_estimate=SMALL,
         name="gather_cells",
-    )(rows, chosen, *arrays)
+    )(rows, chosen, *arrays, *earlier)
 
 
 def slot_places(position, height, width, length):
@@ -332,69 +317,132 @@
     return ((order * tiles + tile) * SUB + sub).astype(jnp.int32), lane.astype(jnp.int32)
 
 
-def mix_body(weights, *refs, width, length, sources):
-    blocks, out = refs[:sources], refs[-1]
+def mix_body(weights, *refs, sources, kept):
+    arrays = refs[: len(refs) - 5 - kept]
+    out, tiles, fields, sems, out_sems = refs[-5:]
+    count, _, total = tiles.shape[:3]
+    members, width, length = fields.shape[1:]
     full = length // LANES
     tail = length - full * LANES
     chunks = width // SUB
-    members = out.shape[0]
-
-    def stacked(tile):
-        parts = []
-        for block in blocks:
-            for member in range(block.shape[0]):
-                parts.append(block[member, 0, tile])
-        return jnp.concatenate(parts, axis=0)
-
-    for chunk in range(chunks):
-        for lane in range(0, full, 2):
-            several = [stacked(chunk * full + at) for at in range(lane, min(lane + 2, full))]
-            value = jnp.concatenate(several, axis=1)
-            result = jnp.dot(weights[...], value, preferred_element_type=f32).astype(bf16)
+
+    copies = []
+    for row, (_, parts) in enumerate(sources):
+        copies.append([])
+        at = 0
+        for number, (index, first) in enumerate(parts):
+            size = arrays[index].shape[0]
+            copies[row].append(
+                pltpu.make_async_copy(
+                    arrays[index].at[:, first],
+                    tiles.at[row, pl.ds(at, size)],
+                    sems.at[row, number],
+                )
+            )
+            copies[row][-1].start()
+            at += size
+
+    results = []
+    for row in range(count):
+        for copy in copies[row]:
+            copy.wait()
+
+        def stacked(tile, row=row):
+            return tiles[row, :, tile].reshape(tiles.shape[1] * SUB, LANES)
+
+        for chunk in range(chunks):
+            for lane in range(0, full, 2):
+                several = [stacked(chunk * full + at) for at in range(lane, min(lane + 2, full))]
+                value = jnp.concatenate(several, axis=1)
+                result = jnp.dot(weights[...], value, preferred_element_type=f32).astype(bf16)
+                for member in range(members):
+                    fields[
+                        row,
+                        member,
+                        chunk * SUB : (chunk + 1) * SUB,
+                        lane * LANES : lane * LANES + value.shape[1],
+                    ] = result[member * SUB : (member + 1) * SUB]
+        result = jnp.dot(
+            weights[...], stacked(total - 1), preferred_element_type=f32
+        ).astype(bf16)
+        for chunk in range(chunks):
+            moved = pltpu.roll(result, LANES - chunk * tail, 1) if chunk else result
             for member in range(members):
-                out[
-                    member,
-                    0,
-                    chunk * SUB : (chunk + 1) * SUB,
-                    lane * LANES : lane * LANES + value.shape[1],
-                ] = result[member * SUB : (member + 1) * SUB]
-    result = jnp.dot(
-        weights[...], stacked(full * chunks), preferred_element_type=f32
-    ).astype(bf16)
-    for member in range(members):
-        for chunk in range(chunks):
-            part = result[member * SUB : (member + 1) * SUB]
-            if chunk:
-                part = pltpu.roll(part, LANES - chunk * tail, 1)
-            out[member, 0, chunk * SUB : (chunk + 1) * SUB, full * LANES : length] = part[:, :tail]
-
-
-def mix(weights, pieces, shape, place, count, before):
+                fields[
+                    row, member, chunk * SUB : (chunk + 1) * SUB, full * LANES : length
+                ] = moved[member * SUB : (member + 1) * SUB, :tail]
+        results.append(
+            pltpu.make_async_copy(fields.at[row], out.at[:, sources[row][0]], out_sems.at[row])
+        )
+        results[-1].start()
+    for copy in results:
+        copy.wait()
+
+
+def mix(weights, arrays, sources, shape, before):
     members, height, width, length = shape
-    tiles = pieces[0][0].shape[2]
-    specs = [
-        pl.BlockSpec(
-            (array.shape[0], 1, tiles, SUB, LANES), lambda r, first=first: (0, r + first, 0, 0, 0)
-        )
-        for array, first in pieces
-    ]
-    arrays = [array for array, _ in pieces]
+    tiles = arrays[0].shape[2]
+    everyone = sum(arrays[index].shape[0] for index, _ in sources[0][1])
+    count, parts = len(sources), len(sources[0][1])
+    arrays = list(arrays)
+    kept = before is not None
     alias = {}
-    if before is not None:
-        specs.append(pl.BlockSpec(memory_space=pl.ANY))
+    if kept:
         arrays.append(before)
         alias = {len(arrays): 0}
     return pl.pallas_call(
-        functools.partial(mix_body, width=width, length=length, sources=len(pieces)),
-        grid=(count,),
-        in_specs=[pl.BlockSpec(weights.shape, lambda r: (0, 0))] + specs,
-        out_specs=pl.BlockSpec((members, 1, width, length), lambda r: (0, r + place, 0, 0)),
+        functools.partial(mix_body, sources=sources, kept=int(kept)),
+        in_specs=[pl.BlockSpec(memory_space=pltpu.VMEM)]
+        + [pl.BlockSpec(memory_space=pl.ANY)] * len(arrays),
+        out_specs=pl.BlockSpec(memory_space=pl.ANY),
         out_shape=jax.ShapeDtypeStruct(shape, bf16),
+        scratch_shapes=[
+            pltpu.VMEM((count, everyone, tiles, SUB, LANES), bf16),
+            pltpu.VMEM((count, members, width, length), bf16),
+            pltpu.SemaphoreType.DMA((count, parts)),
+            pltpu.SemaphoreType.DMA((count,)),
+        ],
         input_output_aliases=alias,
-        compiler_params=pltpu.CompilerParams(vmem_limit_bytes=VMEM),
+        compiler_params=pltpu.CompilerParams(vmem_limit_bytes=20 * MB),
         cost_estimate=SMALL,
         name="mix_rows",
     )(weights, *arrays)
+
+
+def terms_body(live, factor, reading, *refs):
+    parts, out = refs[:-1], refs[-1]
+    predicted = jnp.concatenate(
+        [part[member].astype(f32) for part in parts for member in range(part.shape[0])], axis=0
+    )
+    count, slots = predicted.shape
+    mean = jnp.sum(predicted, axis=0, keepdims=True) * (1.0 / count)
+    anomaly = predicted - mean
+    slot = lax.broadcasted_iota(jnp.int32, (1, slots), 1)
+    weighted = anomaly * jnp.where(slot < live[0], factor[...], 0.0)
+    rest = jnp.zeros((LANES - count - 1, slots), f32)
+    gram = lax.dot_general(
+        weighted,
+        jnp.concatenate([anomaly, reading[...] - mean, rest], axis=0),
+        (((1,), (1,)), ((), ())),
+        precision=lax.Precision.HIGHEST,
+        preferred_element_type=f32,
+    )
+    line = jnp.concatenate([gram[member : member + 1] for member in range(count)], axis=1)
+    for band in range(out.shape[0]):
+        out[band] = line
+
+
+def band_terms(live, factor, reading, parts, bands):
+    count = sum(part.shape[0] for part in parts)
+    return pl.pallas_call(
+        terms_body,
+        in_specs=[pl.BlockSpec(memory_space=pltpu.SMEM)]
+        + [pl.BlockSpec(memory_space=pltpu.VMEM)] * (2 + len(parts)),
+        out_specs=pl.BlockSpec(memory_space=pltpu.VMEM),
+        out_shape=jax.ShapeDtypeStruct((bands, 1, count * LANES), f32),
+        cost_estimate=SMALL,
+        name="band_terms",
+    )(live, factor[None, :], reading[None, :], *parts)
 
 
 def product(left, right):
@@ -406,11 +454,14 @@
 
 
 def transform_body(terms, blend, *, members):
-    total = terms[0]
+    line = terms[0]
     for band in range(1, terms.shape[0]):
-        total = total + terms[band]
-    count = total.shape[1]
-    gram, drive = total[:count], total[count : count + 1]
+        line = line + terms[band]
+    count = line.shape[1] // LANES
+    total = jnp.concatenate(
+        [line[:, member * LANES : (member + 1) * LANES] for member in range(count)], axis=0
+    )
+    gram, drive = total[:, :count], total[:, count : count + 1]
     row = lax.broadcasted_iota(jnp.int32, (count, count), 0)
     column = lax.broadcasted_iota(jnp.int32, (count, count), 1)
     eye = (row == column).astype(f32)
@@ -424,7 +475,8 @@
         root = product(factor, root)
     spread = root / jnp.sqrt(scale)
     inverse = product(root, root)
-    mean_weights = jnp.sum(inverse * drive, axis=1, keepdims=True) / (scale * (count - 1.0))
+    line = jnp.sum(inverse * drive, axis=0, keepdims=True)
+    mean_weights = jnp.sum(eye * line, axis=1, keepdims=True) / (scale * (count - 1.0))
     combined = mean_weights + spread
     mixing = (
         1.0 / count + combined - jnp.sum(combined, axis=0, keepdims=True) * (1.0 / count)
@@ -445,7 +497,7 @@
 
 
 def transform(terms, members):
-    count = terms.shape[2]
+    count = terms.shape[2] // LANES
     return pl.pallas_call(
         functools.partial(transform_body, members=members),
         in_specs=[pl.BlockSpec(memory_space=pltpu.VMEM)],
@@ -490,20 +542,18 @@
     chosen = (lanes[:, None] == jnp.arange(LANES, dtype=jnp.int32)[None, :]).astype(f32)
 
     half = members // 2
-    inner0, weights, bias = inner(
+    inner0, last0, first0, weights, bias = inner(
         x, filter_kernel_tensor, filter_offset_vector[None, :], 0, half
     )
     inner0_across = swap(inner0, 2)
-    edges0 = edges(after(x, inner0), 0, half)
-    edges1 = edges(after(x, edges0[0]), half, members - half)
-    halo0 = halo(*edges0)
-    inner1 = inner(after(x, edges1[0]), weights, bias, half, members - half)
+    halo0 = halo(last0, first0)
+    inner1, last1, first1 = inner(after(x, inner0), weights, bias, half, members - half)
     inner1_across = swap(inner1, 2)
-    halo1 = halo(*lax.optimization_barrier((*edges1, *halo0))[:2])
-
-    inner0_core = swap(after(inner0, edges0[0]), 1)
+    halo1 = halo(*lax.optimization_barrier((last1, first1, *halo0))[:2])
+
+    inner0_core = swap(inner0, 1)
     top0, bottom0 = outer(
-        ends, after(x, inner0_across, inner0_core), *halo0, weights, bias, 0, True
+        ends, after(x, inner0_across, inner0_core), *halo0, weights, bias, 0, 2
     )
     top0_across, bottom0_across = swap(top0, 2), swap(bottom0, 2)
 
@@ -512,24 +562,21 @@
 
     edge = height - 4
     seen0 = gather(rows, chosen, (inner0, top0, bottom0), pieces(0, edge, edge + 2))
-    (outer1,) = outer(ends, after(x, seen0), *halo1, weights, bias, half, False)
-    seen1 = gather(rows, after(chosen, inner1_across), (inner1, outer1), pieces(0, edge))
-    seen = jnp.concatenate([seen0, after(seen1, top0_across, bottom0_across)], axis=0)
+    (outer1,) = outer(ends, after(x, seen0), *halo1, weights, bias, half, 4)
+    seen = gather(
+        rows,
+        after(chosen, inner1_across),
+        (inner1, outer1),
+        pieces(0, edge),
+        (seen0,),
+    )
     seen_parts = [seen] + [swap(seen, bits) for bits in (2, 1, 3)]
-    predicted = jnp.concatenate(seen_parts, axis=0)[:, 0].astype(f32)
+    seen_parts = lax.optimization_barrier((*seen_parts, top0_across, bottom0_across))[:4]
     outer1_across = swap(after(outer1, *seen_parts[1:]), 2)
-    ensemble_vectors = predicted.shape[0]
-    slots = jnp.arange(measured_cell_position.shape[0], dtype=jnp.int32)
-    live = (slots < measured_slot_number[0]).astype(f32)
-    mean = jnp.mean(predicted, axis=0)
-    anomaly = predicted - mean[None, :]
-    weighted = anomaly * (measured_precision_factor * live)[None, :]
-    gram_part = jnp.dot(weighted, anomaly.T, precision=lax.Precision.HIGHEST)
-    drive_part = jnp.dot(weighted, measured_reading - mean, precision=lax.Precision.HIGHEST)
-    terms = jnp.concatenate(
-        [gram_part, drive_part[None, :], jnp.zeros((7, ensemble_vectors), f32)], axis=0
-    )
-    terms = lax.all_to_all(jnp.broadcast_to(terms, (bands,) + terms.shape), "band", 0, 0)
+    terms = band_terms(
+        measured_slot_number, measured_precision_factor, measured_reading, seen_parts, bands
+    )
+    terms = lax.all_to_all(terms, "band", 0, 0, tiled=True)
     inner1_core, inner0_far, inner1_far, outer1_core = [
         swap(after(part, *seen_parts[1:]), 1)
         for part in (inner1, inner0_across, inner1_across, outer1)
@@ -542,20 +589,26 @@
     blend = after(blend, top0_core, bottom0_core, top0_far)
     bottom0_far = swap(after(bottom0_across, blend), 1)
 
-    pieces = (inner0, inner1, inner0_across, inner1_across)
-    pieces += (inner0_core, inner1_core, inner0_far, inner1_far)
-    result = mix(blend, [(piece, 0) for piece in pieces], x.shape, 2, height - 4, None)
+    arrays = (inner0, inner1, inner0_across, inner1_across)
+    arrays += (inner0_core, inner1_core, inner0_far, inner1_far)
+    sources = tuple(
+        (row + 2, tuple((index, row) for index in range(8))) for row in range(height - 4)
+    )
+    result = mix(blend, arrays, sources, x.shape, None)
     outer1_far = swap(after(outer1_across, result), 1)
-    others = (outer1, outer1_across, outer1_core, outer1_far)
-    for place, first, parts in (
-        (0, 0, (top0, top0_across, top0_core, top0_far)),
-        (height - 2, 2, (bottom0, bottom0_across, bottom0_core, bottom0_far)),
-    ):
-        pieces = []
-        for part, other in zip(parts, others):
-            pieces += [(part, 0), (other, first)]
-        result = mix(blend, pieces, x.shape, place, 2, result)
-    return result
+    arrays = (top0, top0_across, top0_core, top0_far)
+    arrays += (bottom0, bottom0_across, bottom0_core, bottom0_far)
+    arrays += (outer1, outer1_across, outer1_core, outer1_far)
+    sources = tuple(
+        (
+            row if row < 2 else height - 4 + row,
+            tuple(
+                pair for n in range(4) for pair in ((4 * (row // 2) + n, row % 2), (8 + n, row))
+            ),
+        )
+        for row in range(4)
+    )
+    return mix(blend, arrays, sources, x.shape, result)
 
 
 def solution(mesh):

time: 166 us -> 157 us (0.946); the launches traced: 166 us -> 155 us
  Pallas kernels: 74.3 us -> 67.6 us
  waiting for transfers between devices: 46.9 us -> 42.6 us
  blocking collectives: 12.2 us -> 14.8 us
  other arithmetic: 4.47 us -> 2.61 us
  local copies, waits for them, and re-layouts: 4.89 us -> 3.03 us
    ppermute x18, waiting for transfers between devices: 15.5 us -> 6.49 us  [swap(): return lax.ppermute(block, 'member', [(i, i ^ bit) for i in range(size)])]
    pallas_call x9 -> x7, Pallas kernels: 52.8 us -> 45.6 us  [the longest x2 18.3 us: outer(): pl.pallas_call(functools.partial(outer_body, cut=cut, width=width, length...]
    ppermute x2, waiting for transfers between devices: 31.5 us -> 36.1 us  [halo(): lax.ppermute(last, 'band', forward)]
    all_to_all x1, blocking collectives: 12.2 us -> 14.8 us  [local(): terms = lax.all_to_all(terms, 'band', 0, 0, tiled=True)]
    unnamed x30 -> x26, local copies, waits for them, and re-layouts: 3.45 us -> 3.03 us
  transfers between devices with their start and end apart: 22 -> 22, of which waited for: 7 -> 5; matrix products, arithmetic and copies ran while one was open for 5% -> 2% of each run, Pallas kernels for 36% -> 35%
where the time goes in v3:
time: 157 us; the launch traced here: 155 us
  Pallas kernels  67.6 us (43%)
  waiting for transfers between devices  42.6 us (27%)
  starting transfers between devices  22.8 us (15%)
  blocking collectives  14.8 us (9%)
  local copies, waits for them, and re-layouts  3.03 us (2%)
  other arithmetic  2.61 us (2%)
    ppermute x2, waiting for transfers between devices, halo(): lax.ppermute(last, 'band', forward)  36.1 us
    pallas_call x2, Pallas kernels, outer(): pl.pallas_call(functools.partial(outer_body, cut=cut, width=width, length...  18.3 us
    pallas_call x2, Pallas kernels, inner(): pl.pallas_call(functools.partial(opening_body if opening else inner_body,...  16 us
    all_to_all x1, blocking collectives, local(): terms = lax.all_to_all(terms, 'band', 0, 0, tiled=True)  14.8 us
    pallas_call x2, Pallas kernels, gather(): pl.pallas_call(functools.partial(gather_body, pieces=pieces, kept=kept),...  14 us
    pallas_call x2, Pallas kernels, mix(): pl.pallas_call(functools.partial(mix_body, sources=sources, kept=int(kept...  11.5 us
    ppermute x18, starting transfers between devices, swap(): return lax.ppermute(block, 'member', [(i, i ^ bit) for i in range(size)])  11.3 us
    ppermute x2, starting transfers between devices, halo(): lax.ppermute(last, 'band', forward)  8.72 us
  transfers between devices with their start and end apart: 22, of which 5 were waited for; matrix products, arithmetic and copies ran while one was open for 2% of the time, Pallas kernels for 35%

profile of v3, /device:TPU:0, one launch (start us, length us, event | category | flops | bytes accessed | tf_op | source)
XLA Modules:
  0.0 154.5 jit_solution(10114023286885264231)
XLA Ops:
  0.0 8.6 %inner_rows.2 = (bf16[2,4,45,16,128]{4,3,2,1,0:T(8,128)(2,1)}, bf16[2,2,64,1440]{3,2,1,0:T(8,128)(2,1)}, bf16[2,2,64,1440]{3,2,1,0:T(8,128)(2,1)}, bf16[128,768]{1,0:T(8,128)(2,1)}, f32[128,128]{1,0:T(8,128)}) custom-call(bf16[4,8,64,1440]{3,2,1,0:T(8,128)(2,1)} %x.4, bf16[3,3,64,64]{3,2,1,0:T(8,128)(2,1)} %kernel.1, f32[1,64]{1,0:T(1,128)} %bitcast.5), custom_call_target="tpu_custom_call" | custom-call | flops 200000000 | bytes 500000 | tf_op jit(solution)/shard_map/inner_rows/pallas_call | solution.py:155
  8.6 3.0 %collective-permute-start.1 = (bf16[2,4,45,16,128]{4,3,2,1,0:T(8,128)(2,1)}, bf16[2,4,45,16,128]{4,3,2,1,0:T(8,128)(2,1)}, u32[]{:S(2)}, u32[]{:S(2)}) collective-permute-start(bf16[2,4,45,16,128]{4,3,2,1,0:T(8,128)(2,1)} %get-tuple-element.36.refs_0_), channel_id=1, source_target_pairs={{0,16},{8,24},{16,0},{24,8},{1,17},{9,25},{17,1},{25,9},{2,18},{10... | collective-permute-start | bytes 4423688 | tf_op jit(solution)/shard_map/ppermute | solution.py:524
  11.6 0.0 collective-permute-start.2
  11.6 3.4 %collective-permute-start.3 = (bf16[2,2,64,1440]{3,2,1,0:T(8,128)(2,1)}, bf16[2,2,64,1440]{3,2,1,0:T(8,128)(2,1)S(1)}, u32[]{:S(2)}, u32[]{:S(2)}) collective-permute-start(bf16[2,2,64,1440]{3,2,1,0:T(8,128)(2,1)} %get-tuple-element.43), channel_id=1, source_target_pairs={{0,1},{1,2},{2,3},{3,4},{4,5},{5,6},{6,7},{8,9},{9,10},{10,11},{11... | collective-permute-start | bytes 2211848 | tf_op jit(solution)/shard_map/ppermute | solution.py:519
  15.0 1.3 collective-permute-start.4
  16.3 7.5 %inner_rows.3 = (bf16[2,4,45,16,128]{4,3,2,1,0:T(8,128)(2,1)}, bf16[2,2,64,1440]{3,2,1,0:T(8,128)(2,1)}, bf16[2,2,64,1440]{3,2,1,0:T(8,128)(2,1)}) custom-call(bf16[4,8,64,1440]{3,2,1,0:T(8,128)(2,1)} %x.4, bf16[128,768]{1,0:T(8,128)(2,1)} %get-tuple-element.38.weights, f32[128,128]{1,0:T(8,128)} %get-tuple-element.39.bias), custom_call_target="tpu_custom_call" | custom-call | flops 200000000 | bytes 500000 | tf_op jit(solution)/shard_map/inner_rows/pallas_call | solution.py:155
  23.8 0.5 collective-permute-start
  24.3 0.6 add_convert_fusion.ends
  24.8 24.8 %collective-permute-done.3.low = bf16[2,2,64,1440]{3,2,1,0:T(8,128)(2,1)S(1)} collective-permute-done((bf16[2,2,64,1440]{3,2,1,0:T(8,128)(2,1)}, bf16[2,2,64,1440]{3,2,1,0:T(8,128)(2,1)S(1)}, u32[]{:S(2)}, u32[]{:S(2)}) %collective-permute-start.3) | collective-permute-done | bytes 737312 | tf_op jit(solution)/shard_map/ppermute | solution.py:519
  49.6 0.0 collective-permute-done.4.high
  49.6 5.3 %collective-permute-start.5 = (bf16[2,2,64,1440]{3,2,1,0:T(8,128)(2,1)}, bf16[2,2,64,1440]{3,2,1,0:T(8,128)(2,1)}, u32[]{:S(2)}, u32[]{:S(2)}) collective-permute-start(bf16[2,2,64,1440]{3,2,1,0:T(8,128)(2,1)} %get-tuple-element.50), channel_id=1, source_target_pairs={{0,1},{1,2},{2,3},{3,4},{4,5},{5,6},{6,7},{8,9},{9,10},{10,11},{11... | collective-permute-start | bytes 2211848 | tf_op jit(solution)/shard_map/ppermute | solution.py:519
  54.9 1.5 collective-permute-start.6
  56.4 0.0 collective-permute-done.1.refs_2_
  56.4 0.0 collective-permute-done.2.refs_4_
  56.4 9.2 %outer_rows.2 = (bf16[2,2,45,16,128]{4,3,2,1,0:T(8,128)(2,1)}, bf16[2,2,45,16,128]{4,3,2,1,0:T(8,128)(2,1)}) custom-call(s32[2]{0:T(128)} %add_convert_fusion.ends, bf16[4,8,64,1440]{3,2,1,0:T(8,128)(2,1)} %x.4, bf16[2,2,64,1440]{3,2,1,0:T(8,128)(2,1)} %copy-done.8, bf16[2,2,64,1440]{3,2,1,0:T(8,128)(2,1)} %collective-permute-done.4.high, ...), custom_call_target="tpu_custom_call" | custom-call | flops 200000000 | bytes 500000 | tf_op jit(solution)/shard_map/outer_rows/pallas_call | solution.py:208
  65.5 0.5 collective-permute-start.10
  66.0 1.5 collective-permute-start.11
  67.6 0.0 copy-done.9
  67.6 0.6 fusion.6
  68.2 1.4 fusion.chosen
  69.6 6.9 %gather_cells.2.refs_2_ = bf16[2,1,2048]{2,1,0:T(2,128)(2,1)} custom-call(s32[2048]{0:T(1024)} %get-tuple-element.68.rows, f32[2048,128]{1,0:T(8,128)} %fusion.chosen, bf16[2,4,45,16,128]{4,3,2,1,0:T(8,128)(2,1)} %get-tuple-element.36.refs_0_, bf16[2,2,45,16,128]{4,3,2,1,0:T(8,128)(2,1)} %get-tuple-element.61.refs_1_.refs_0_, ...), custom_call_target="tpu_custom_call" | custom-call | flops 200000000 | bytes 500000 | tf_op jit(solution)/shard_map/gather_cells/pallas_call | solution.py:284
  76.6 0.0 collective-permute-done.refs_3_
  76.6 11.4 %collective-permute-done.5.low = bf16[2,2,64,1440]{3,2,1,0:T(8,128)(2,1)} collective-permute-done((bf16[2,2,64,1440]{3,2,1,0:T(8,128)(2,1)}, bf16[2,2,64,1440]{3,2,1,0:T(8,128)(2,1)}, u32[]{:S(2)}, u32[]{:S(2)}) %collective-permute-start.5) | collective-permute-done | bytes 737312 | tf_op jit(solution)/shard_map/ppermute | solution.py:519
  88.0 0.0 collective-permute-done.6.high
  88.0 9.1 %outer_rows.3.refs_1_.refs_8_ = bf16[2,4,45,16,128]{4,3,2,1,0:T(8,128)(2,1)} custom-call(s32[2]{0:T(128)} %add_convert_fusion.ends, bf16[4,8,64,1440]{3,2,1,0:T(8,128)(2,1)} %x.4, bf16[2,2,64,1440]{3,2,1,0:T(8,128)(2,1)} %collective-permute-done.5.low, bf16[2,2,64,1440]{3,2,1,0:T(8,128)(2,1)} %collective-permute-done.6.high, ...), custom_call_target="tpu_custom_call" | custom-call | flops 200000000 | bytes 500000 | tf_op jit(solution)/shard_map/outer_rows/pallas_call | solution.py:208
  97.1 7.1 %gather_cells.3.refs_0_ = bf16[4,1,2048]{2,1,0:T(2,128)(2,1)} custom-call(s32[2048]{0:T(1024)} %get-tuple-element.68.rows, f32[2048,128]{1,0:T(8,128)} %fusion.chosen, bf16[2,4,45,16,128]{4,3,2,1,0:T(8,128)(2,1)} %get-tuple-element.56.refs_0_.refs_1_, bf16[2,4,45,16,128]{4,3,2,1,0:T(8,128)(2,1)} %outer_rows.3.refs_1_.refs_8_, ...), custom_call_target="tpu_custom_call" | custom-call | flops 200000000 | bytes 500000 | tf_op jit(solution)/shard_map/gather_cells/pallas_call | solution.py:284
  104.2 0.0 copy-start.1
  104.2 0.6 collective-permute-start.7
  104.8 0.0 collective-permute-start.8
  104.8 1.6 %collective-permute-start.9 = (bf16[4,1,2048]{2,1,0:T(2,128)(2,1)}, bf16[4,1,2048]{2,1,0:T(2,128)(2,1)S(1)}, u32[]{:S(2)}, u32[]{:S(2)}) collective-permute-start(bf16[4,1,2048]{2,1,0:T(2,128)(2,1)} %gather_cells.3.refs_0_), channel_id=1, source_target_pairs={{0,24},{8,16},{16,8},{24,0},{1,25},{9,17},{17,9},{25,1},{2,26},{10... | collective-permute-start | bytes 49160 | tf_op jit(solution)/shard_map/ppermute | solution.py:524
  106.4 2.3 %collective-permute-done.7.refs_1_ = bf16[4,1,2048]{2,1,0:T(2,128)(2,1)S(1)} collective-permute-done((bf16[4,1,2048]{2,1,0:T(2,128)(2,1)}, bf16[4,1,2048]{2,1,0:T(2,128)(2,1)S(1)}, u32[]{:S(2)}, u32[]{:S(2)}) %collective-permute-start.7) | collective-permute-done | bytes 16416 | tf_op jit(solution)/shard_map/ppermute | solution.py:524
  108.7 0.0 collective-permute-done.8.refs_2_
  108.7 0.0 collective-permute-done.9.refs_3_
  108.7 0.0 collective-permute-done.10.refs_1_
  108.7 0.0 collective-permute-done.11.refs_5_
  108.7 0.2 collective-permute-start.15
  108.9 0.4 collective-permute-start.14
  109.3 0.1 collective-permute-start.13
  109.4 0.4 collective-permute-start.12
  109.8 1.4 collective-permute-start.20
  111.8 0.0 copy-done.10
  111.8 1.9 %band_terms.1 = f32[8,1,2048]{2,1,0:T(1,128)} custom-call(s32[1]{0:T(128)S(6)} %copy.10.live, f32[1,2048]{1,0:T(1,128)} %bitcast.6, f32[1,2048]{1,0:T(1,128)} %bitcast.7, bf16[4,1,2048]{2,1,0:T(2,128)(2,1)} %gather_cells.3.refs_0_, bf16[4,1,2048]{2,1,0:T(2,128)(2,1)} %copy-done.10, bf16[4,1,2048]{2,1,0:T(2,128)(2,1)} %copy-done.11, ...), custom_call_target="tpu_custom_call" | custom-call | flops 200000000 | bytes 500000 | tf_op jit(solution)/shard_map/band_terms/pallas_call | solution.py:437
  113.7 14.8 %all_to_all.5.terms = f32[8,1,2048]{2,1,0:T(1,128)} all-to-all(f32[8,1,2048]{2,1,0:T(1,128)} %band_terms.1), channel_id=1, replica_groups=mesh['member'=4,'band'=8] {'band'}, dimensions={0} | all-to-all | bytes 131072 | tf_op jit(solution)/shard_map/all_to_all | solution.py:579
  128.5 0.0 collective-permute-done.15.refs_10_
  128.5 0.0 collective-permute-done.14.refs_7_
  128.5 0.0 collective-permute-done.13.refs_6_
  128.5 0.0 collective-permute-done.12.refs_5_
  128.5 0.1 collective-permute-start.18
  128.6 0.5 collective-permute-start.17
  129.1 0.1 collective-permute-start.16
  129.2 5.9 %transform.1.weights = bf16[64,256]{1,0:T(8,128)(2,1)} custom-call(f32[8,1,2048]{2,1,0:T(1,128)} %all_to_all.5.terms), custom_call_target="tpu_custom_call" | custom-call | flops 200000000 | bytes 500000 | tf_op jit(solution)/shard_map/transform/pallas_call | solution.py:501
  135.1 0.0 collective-permute-done.18.refs_3_
  135.1 0.9 copy-done.5
  136.0 0.0 collective-permute-done.17.refs_6_
  136.0 0.0 collective-permute-done.16.refs_2_
  136.0 1.4 copy-done.2
  137.4 0.8 copy-done.7
  138.1 6.2 %mix_rows.2.refs_12_ = bf16[4,8,64,1440]{3,2,1,0:T(8,128)(2,1)} custom-call(bf16[64,256]{1,0:T(8,128)(2,1)S(1)} %copy-done.7, bf16[2,4,45,16,128]{4,3,2,1,0:T(8,128)(2,1)S(1)} %copy-done.1, bf16[2,4,45,16,128]{4,3,2,1,0:T(8,128)(2,1)S(1)} %copy-done.2, bf16[2,4,45,16,128]{4,3,2,1,0:T(8,128)(2,1)} %collective-permute-done.1.refs_2_, ...), custom_call_target="tpu_custom_call" | custom-call | flops 200000000 | bytes 500000 | tf_op jit(solution)/shard_map/mix_rows/pallas_call | solution.py:393
  144.3 0.1 collective-permute-done.20.refs_9_
  144.4 0.4 collective-permute-start.21
  144.8 0.1 collective-permute-start.19
  144.9 4.1 %collective-permute-done.19.refs_7_ = bf16[2,2,45,16,128]{4,3,2,1,0:T(8,128)(2,1)S(1)} collective-permute-done((bf16[2,2,45,16,128]{4,3,2,1,0:T(8,128)(2,1)}, bf16[2,2,45,16,128]{4,3,2,1,0:T(8,128)(2,1)S(1)}, u32[]{:S(2)}, u32[]{:S(2)}) %collective-permute-start.19) | collective-permute-done | bytes 737312 | tf_op jit(solution)/shard_map/ppermute | solution.py:524
  149.0 0.0 collective-permute-done.21.refs_11_
  149.0 5.3 %mix_rows.3 = bf16[4,8,64,1440]{3,2,1,0:T(8,128)(2,1)} custom-call(bf16[64,256]{1,0:T(8,128)(2,1)S(1)} %copy-done.7, bf16[2,2,45,16,128]{4,3,2,1,0:T(8,128)(2,1)S(1)} %copy-done.3, bf16[2,2,45,16,128]{4,3,2,1,0:T(8,128)(2,1)} %collective-permute-done.10.refs_1_, ...), custom_call_target="tpu_custom_call", output_to_operand_aliasing={{}: (13, {})} | custom-call | flops 200000000 | bytes 500000 | tf_op jit(solution)/shard_map/mix_rows/pallas_call | solution.py:393
  (20 shorter events, 0.0 us)
Async XLA Ops:
  8.6 47.8 %collective-permute-start.1 = (bf16[2,4,45,16,128]{4,3,2,1,0:T(8,128)(2,1)}, bf16[2,4,45,16,128]{4,3,2,1,0:T(8,128)(2,1)}, u32[]{:S(2)}, u32[]{:S(2)}) collective-permute-start(bf16[2,4,45,16,128]{4,3,2,1,0:T(8,128)(2,1)} %get-tuple-element.36.refs_0_), channel_id=1, source_target_pairs={{0,16},{8,24},{16,0},{24,8},{1,17},{9,25},{17,1},{25,9},{2,18},{10... | collective-permute-start | bytes 4423688 | tf_op jit(solution)/shard_map/ppermute | solution.py:524
  11.6 44.8 %collective-permute-start.2 = (bf16[2,4,45,16,128]{4,3,2,1,0:T(8,128)(2,1)}, bf16[2,4,45,16,128]{4,3,2,1,0:T(8,128)(2,1)}, u32[]{:S(2)}, u32[]{:S(2)}) collective-permute-start(bf16[2,4,45,16,128]{4,3,2,1,0:T(8,128)(2,1)} %get-tuple-element.36.refs_0_), channel_id=1, source_target_pairs={{0,8},{8,0},{16,24},{24,16},{1,9},{9,1},{17,25},{25,17},{2,10},{10... | collective-permute-start | bytes 4423688 | tf_op jit(solution)/shard_map/ppermute | solution.py:524
  11.6 38.0 %collective-permute-start.3 = (bf16[2,2,64,1440]{3,2,1,0:T(8,128)(2,1)}, bf16[2,2,64,1440]{3,2,1,0:T(8,128)(2,1)S(1)}, u32[]{:S(2)}, u32[]{:S(2)}) collective-permute-start(bf16[2,2,64,1440]{3,2,1,0:T(8,128)(2,1)} %get-tuple-element.43), channel_id=1, source_target_pairs={{0,1},{1,2},{2,3},{3,4},{4,5},{5,6},{6,7},{8,9},{9,10},{10,11},{11... | collective-permute-start | bytes 2211848 | tf_op jit(solution)/shard_map/ppermute | solution.py:519
  15.0 34.6 %collective-permute-start.4 = (bf16[2,2,64,1440]{3,2,1,0:T(8,128)(2,1)}, bf16[2,2,64,1440]{3,2,1,0:T(8,128)(2,1)}, u32[]{:S(2)}, u32[]{:S(2)}) collective-permute-start(bf16[2,2,64,1440]{3,2,1,0:T(8,128)(2,1)} %get-tuple-element.44), channel_id=1, source_target_pairs={{1,0},{2,1},{3,2},{4,3},{5,4},{6,5},{7,6},{9,8},{10,9},{11,10},{12... | collective-permute-start | bytes 2211848 | tf_op jit(solution)/shard_map/ppermute | solution.py:519
  23.8 52.8 %collective-permute-start = (bf16[2,4,45,16,128]{4,3,2,1,0:T(8,128)(2,1)}, bf16[2,4,45,16,128]{4,3,2,1,0:T(8,128)(2,1)}, u32[]{:S(2)}, u32[]{:S(2)}) collective-permute-start(bf16[2,4,45,16,128]{4,3,2,1,0:T(8,128)(2,1)} %get-tuple-element.56.refs_0_.refs_1_), channel_id=1, source_target_pairs={{0,16},{8,24},{16,0},{24,8},{1,17},{9,25},{17,1},{25,9},{2,18},{10... | collective-permute-start | bytes 4423688 | tf_op jit(solution)/shard_map/ppermute | solution.py:524
  49.6 6.8 %copy-start.8 = (bf16[2,2,64,1440]{3,2,1,0:T(8,128)(2,1)}, bf16[2,2,64,1440]{3,2,1,0:T(8,128)(2,1)S(1)}, u32[]{:S(2)}) copy-start(bf16[2,2,64,1440]{3,2,1,0:T(8,128)(2,1)S(1)} %collective-permute-done.3.low) | copy-start | bytes 2211844
  49.6 18.0 %copy-start.9 = (s32[2048]{0:T(1024)S(1)}, s32[2048]{0:T(1024)}, u32[]{:S(2)}) copy-start(s32[2048]{0:T(1024)} %param.10) | copy-start | bytes 24580
  49.6 38.4 %collective-permute-start.5 = (bf16[2,2,64,1440]{3,2,1,0:T(8,128)(2,1)}, bf16[2,2,64,1440]{3,2,1,0:T(8,128)(2,1)}, u32[]{:S(2)}, u32[]{:S(2)}) collective-permute-start(bf16[2,2,64,1440]{3,2,1,0:T(8,128)(2,1)} %get-tuple-element.50), channel_id=1, source_target_pairs={{0,1},{1,2},{2,3},{3,4},{4,5},{5,6},{6,7},{8,9},{9,10},{10,11},{11... | collective-permute-start | bytes 2211848 | tf_op jit(solution)/shard_map/ppermute | solution.py:519
  54.9 33.1 %collective-permute-start.6 = (bf16[2,2,64,1440]{3,2,1,0:T(8,128)(2,1)}, bf16[2,2,64,1440]{3,2,1,0:T(8,128)(2,1)}, u32[]{:S(2)}, u32[]{:S(2)}) collective-permute-start(bf16[2,2,64,1440]{3,2,1,0:T(8,128)(2,1)} %get-tuple-element.51), channel_id=1, source_target_pairs={{1,0},{2,1},{3,2},{4,3},{5,4},{6,5},{7,6},{9,8},{10,9},{11,10},{12... | collective-permute-start | bytes 2211848 | tf_op jit(solution)/shard_map/ppermute | solution.py:519
  65.5 43.1 %collective-permute-start.10 = (bf16[2,2,45,16,128]{4,3,2,1,0:T(8,128)(2,1)}, bf16[2,2,45,16,128]{4,3,2,1,0:T(8,128)(2,1)}, u32[]{:S(2)}, u32[]{:S(2)}) collective-permute-start(bf16[2,2,45,16,128]{4,3,2,1,0:T(8,128)(2,1)} %get-tuple-element.61.refs_1_.refs_0_), channel_id=1, source_target_pairs={{0,16},{8,24},{16,0},{24,8},{1,17},{9,25},{17,1},{25,9},{2,18},{10... | collective-permute-start | bytes 2211848 | tf_op jit(solution)/shard_map/ppermute | solution.py:524
  66.0 42.7 %collective-permute-start.11 = (bf16[2,2,45,16,128]{4,3,2,1,0:T(8,128)(2,1)}, bf16[2,2,45,16,128]{4,3,2,1,0:T(8,128)(2,1)}, u32[]{:S(2)}, u32[]{:S(2)}) collective-permute-start(bf16[2,2,45,16,128]{4,3,2,1,0:T(8,128)(2,1)} %get-tuple-element.62.refs_2_.refs_4_), channel_id=1, source_target_pairs={{0,16},{8,24},{16,0},{24,8},{1,17},{9,25},{17,1},{25,9},{2,18},{10... | collective-permute-start | bytes 2211848 | tf_op jit(solution)/shard_map/ppermute | solution.py:524
  97.1 32.0 %copy-start.3 = (bf16[2,2,45,16,128]{4,3,2,1,0:T(8,128)(2,1)S(1)}, bf16[2,2,45,16,128]{4,3,2,1,0:T(8,128)(2,1)}, u32[]{:S(2)}) copy-start(bf16[2,2,45,16,128]{4,3,2,1,0:T(8,128)(2,1)} %get-tuple-element.61.refs_1_.refs_0_) | copy-start | bytes 2211844
  104.2 31.8 %copy-start.1 = (bf16[2,4,45,16,128]{4,3,2,1,0:T(8,128)(2,1)S(1)}, bf16[2,4,45,16,128]{4,3,2,1,0:T(8,128)(2,1)}, u32[]{:S(2)}) copy-start(bf16[2,4,45,16,128]{4,3,2,1,0:T(8,128)(2,1)} %get-tuple-element.36.refs_0_) | copy-start | bytes 4423684
  104.2 4.5 %collective-permute-start.7 = (bf16[4,1,2048]{2,1,0:T(2,128)(2,1)}, bf16[4,1,2048]{2,1,0:T(2,128)(2,1)S(1)}, u32[]{:S(2)}, u32[]{:S(2)}) collective-permute-start(bf16[4,1,2048]{2,1,0:T(2,128)(2,1)} %gather_cells.3.refs_0_), channel_id=1, source_target_pairs={{0,16},{8,24},{16,0},{24,8},{1,17},{9,25},{17,1},{25,9},{2,18},{10... | collective-permute-start | bytes 49160 | tf_op jit(solution)/shard_map/ppermute | solution.py:524
  104.8 3.9 %collective-permute-start.8 = (bf16[4,1,2048]{2,1,0:T(2,128)(2,1)}, bf16[4,1,2048]{2,1,0:T(2,128)(2,1)S(1)}, u32[]{:S(2)}, u32[]{:S(2)}) collective-permute-start(bf16[4,1,2048]{2,1,0:T(2,128)(2,1)} %gather_cells.3.refs_0_), channel_id=1, source_target_pairs={{0,8},{8,0},{16,24},{24,16},{1,9},{9,1},{17,25},{25,17},{2,10},{10... | collective-permute-start | bytes 49160 | tf_op jit(solution)/shard_map/ppermute | solution.py:524
  104.8 3.9 %collective-permute-start.9 = (bf16[4,1,2048]{2,1,0:T(2,128)(2,1)}, bf16[4,1,2048]{2,1,0:T(2,128)(2,1)S(1)}, u32[]{:S(2)}, u32[]{:S(2)}) collective-permute-start(bf16[4,1,2048]{2,1,0:T(2,128)(2,1)} %gather_cells.3.refs_0_), channel_id=1, source_target_pairs={{0,24},{8,16},{16,8},{24,0},{1,25},{9,17},{17,9},{25,1},{2,26},{10... | collective-permute-start | bytes 49160 | tf_op jit(solution)/shard_map/ppermute | solution.py:524
  108.7 3.2 %copy-start.10 = (bf16[4,1,2048]{2,1,0:T(2,128)(2,1)}, bf16[4,1,2048]{2,1,0:T(2,128)(2,1)S(1)}, u32[]{:S(2)}) copy-start(bf16[4,1,2048]{2,1,0:T(2,128)(2,1)S(1)} %collective-permute-done.7.refs_1_) | copy-start | bytes 49156
  108.7 3.2 %copy-start.11 = (bf16[4,1,2048]{2,1,0:T(2,128)(2,1)}, bf16[4,1,2048]{2,1,0:T(2,128)(2,1)S(1)}, u32[]{:S(2)}) copy-start(bf16[4,1,2048]{2,1,0:T(2,128)(2,1)S(1)} %collective-permute-done.8.refs_2_) | copy-start | bytes 49156
  108.7 3.2 %copy-start.12 = (bf16[4,1,2048]{2,1,0:T(2,128)(2,1)}, bf16[4,1,2048]{2,1,0:T(2,128)(2,1)S(1)}, u32[]{:S(2)}) copy-start(bf16[4,1,2048]{2,1,0:T(2,128)(2,1)S(1)} %collective-permute-done.9.refs_3_) | copy-start | bytes 49156
  108.7 19.8 %collective-permute-start.15 = (bf16[2,4,45,16,128]{4,3,2,1,0:T(8,128)(2,1)}, bf16[2,4,45,16,128]{4,3,2,1,0:T(8,128)(2,1)}, u32[]{:S(2)}, u32[]{:S(2)}) collective-permute-start(bf16[2,4,45,16,128]{4,3,2,1,0:T(8,128)(2,1)} %outer_rows.3.refs_1_.refs_8_), channel_id=1, source_target_pairs={{0,8},{8,0},{16,24},{24,16},{1,9},{9,1},{17,25},{25,17},{2,10},{10... | collective-permute-start | bytes 4423688 | tf_op jit(solution)/shard_map/ppermute | solution.py:524
  108.9 19.6 %collective-permute-start.14 = (bf16[2,4,45,16,128]{4,3,2,1,0:T(8,128)(2,1)}, bf16[2,4,45,16,128]{4,3,2,1,0:T(8,128)(2,1)}, u32[]{:S(2)}, u32[]{:S(2)}) collective-permute-start(bf16[2,4,45,16,128]{4,3,2,1,0:T(8,128)(2,1)} %collective-permute-done.refs_3_), channel_id=1, source_target_pairs={{0,8},{8,0},{16,24},{24,16},{1,9},{9,1},{17,25},{25,17},{2,10},{10... | collective-permute-start | bytes 4423688 | tf_op jit(solution)/shard_map/ppermute | solution.py:524
  109.3 19.3 %collective-permute-start.13 = (bf16[2,4,45,16,128]{4,3,2,1,0:T(8,128)(2,1)}, bf16[2,4,45,16,128]{4,3,2,1,0:T(8,128)(2,1)}, u32[]{:S(2)}, u32[]{:S(2)}) collective-permute-start(bf16[2,4,45,16,128]{4,3,2,1,0:T(8,128)(2,1)} %collective-permute-done.1.refs_2_), channel_id=1, source_target_pairs={{0,8},{8,0},{16,24},{24,16},{1,9},{9,1},{17,25},{25,17},{2,10},{10... | collective-permute-start | bytes 4423688 | tf_op jit(solution)/shard_map/ppermute | solution.py:524
  109.4 19.1 %collective-permute-start.12 = (bf16[2,4,45,16,128]{4,3,2,1,0:T(8,128)(2,1)}, bf16[2,4,45,16,128]{4,3,2,1,0:T(8,128)(2,1)}, u32[]{:S(2)}, u32[]{:S(2)}) collective-permute-start(bf16[2,4,45,16,128]{4,3,2,1,0:T(8,128)(2,1)} %get-tuple-element.56.refs_0_.refs_1_), channel_id=1, source_target_pairs={{0,8},{8,0},{16,24},{24,16},{1,9},{9,1},{17,25},{25,17},{2,10},{10... | collective-permute-start | bytes 4423688 | tf_op jit(solution)/shard_map/ppermute | solution.py:524
  109.8 34.6 %collective-permute-start.20 = (bf16[2,4,45,16,128]{4,3,2,1,0:T(8,128)(2,1)}, bf16[2,4,45,16,128]{4,3,2,1,0:T(8,128)(2,1)}, u32[]{:S(2)}, u32[]{:S(2)}) collective-permute-start(bf16[2,4,45,16,128]{4,3,2,1,0:T(8,128)(2,1)} %outer_rows.3.refs_1_.refs_8_), channel_id=1, source_target_pairs={{0,16},{8,24},{16,0},{24,8},{1,17},{9,25},{17,1},{25,9},{2,18},{10... | collective-permute-start | bytes 4423688 | tf_op jit(solution)/shard_map/ppermute | solution.py:524
  128.5 6.6 %collective-permute-start.18 = (bf16[2,2,45,16,128]{4,3,2,1,0:T(8,128)(2,1)}, bf16[2,2,45,16,128]{4,3,2,1,0:T(8,128)(2,1)S(1)}, u32[]{:S(2)}, u32[]{:S(2)}) collective-permute-start(bf16[2,2,45,16,128]{4,3,2,1,0:T(8,128)(2,1)} %collective-permute-done.10.refs_1_), channel_id=1, source_target_pairs={{0,8},{8,0},{16,24},{24,16},{1,9},{9,1},{17,25},{25,17},{2,10},{10... | collective-permute-start | bytes 2211848 | tf_op jit(solution)/shard_map/ppermute | solution.py:524
  128.6 7.4 %collective-permute-start.17 = (bf16[2,2,45,16,128]{4,3,2,1,0:T(8,128)(2,1)}, bf16[2,2,45,16,128]{4,3,2,1,0:T(8,128)(2,1)}, u32[]{:S(2)}, u32[]{:S(2)}) collective-permute-start(bf16[2,2,45,16,128]{4,3,2,1,0:T(8,128)(2,1)} %get-tuple-element.62.refs_2_.refs_4_), channel_id=1, source_target_pairs={{0,8},{8,0},{16,24},{24,16},{1,9},{9,1},{17,25},{25,17},{2,10},{10... | collective-permute-start | bytes 2211848 | tf_op jit(solution)/shard_map/ppermute | solution.py:524
  129.1 6.9 %collective-permute-start.16 = (bf16[2,2,45,16,128]{4,3,2,1,0:T(8,128)(2,1)S(1)}, bf16[2,2,45,16,128]{4,3,2,1,0:T(8,128)(2,1)}, u32[]{:S(2)}, u32[]{:S(2)}) collective-permute-start(bf16[2,2,45,16,128]{4,3,2,1,0:T(8,128)(2,1)S(1)} %copy-done.3), channel_id=1, source_target_pairs={{0,8},{8,0},{16,24},{24,16},{1,9},{9,1},{17,25},{25,17},{2,10},{10... | collective-permute-start | bytes 2211848 | tf_op jit(solution)/shard_map/ppermute | solution.py:524
  135.1 13.9 %copy-start = (bf16[2,4,45,16,128]{4,3,2,1,0:T(8,128)(2,1)S(1)}, bf16[2,4,45,16,128]{4,3,2,1,0:T(8,128)(2,1)}, u32[]{:S(2)}) copy-start(bf16[2,4,45,16,128]{4,3,2,1,0:T(8,128)(2,1)} %outer_rows.3.refs_1_.refs_8_) | copy-start | bytes 4423684
  135.1 0.9 copy-start.5
  136.0 1.4 copy-start.2
  137.4 0.8 copy-start.7
  138.1 10.9 %copy-start.4 = (bf16[2,2,45,16,128]{4,3,2,1,0:T(8,128)(2,1)S(1)}, bf16[2,2,45,16,128]{4,3,2,1,0:T(8,128)(2,1)}, u32[]{:S(2)}) copy-start(bf16[2,2,45,16,128]{4,3,2,1,0:T(8,128)(2,1)} %get-tuple-element.62.refs_2_.refs_4_) | copy-start | bytes 2211844
  138.1 10.9 %copy-start.6 = (bf16[2,2,45,16,128]{4,3,2,1,0:T(8,128)(2,1)S(1)}, bf16[2,2,45,16,128]{4,3,2,1,0:T(8,128)(2,1)}, u32[]{:S(2)}) copy-start(bf16[2,2,45,16,128]{4,3,2,1,0:T(8,128)(2,1)} %copy-done.5) | copy-start | bytes 2211844
  144.4 4.6 %collective-permute-start.21 = (bf16[2,4,45,16,128]{4,3,2,1,0:T(8,128)(2,1)}, bf16[2,4,45,16,128]{4,3,2,1,0:T(8,128)(2,1)S(1)}, u32[]{:S(2)}, u32[]{:S(2)}) collective-permute-start(bf16[2,4,45,16,128]{4,3,2,1,0:T(8,128)(2,1)} %collective-permute-done.20.refs_9_), channel_id=1, source_target_pairs={{0,8},{8,0},{16,24},{24,16},{1,9},{9,1},{17,25},{25,17},{2,10},{10... | collective-permute-start | bytes 4423688 | tf_op jit(solution)/shard_map/ppermute | solution.py:524
  144.8 4.2 %collective-permute-start.19 = (bf16[2,2,45,16,128]{4,3,2,1,0:T(8,128)(2,1)}, bf16[2,2,45,16,128]{4,3,2,1,0:T(8,128)(2,1)S(1)}, u32[]{:S(2)}, u32[]{:S(2)}) collective-permute-start(bf16[2,2,45,16,128]{4,3,2,1,0:T(8,128)(2,1)} %collective-permute-done.11.refs_5_), channel_id=1, source_target_pairs={{0,8},{8,0},{16,24},{24,16},{1,9},{9,1},{17,25},{25,17},{2,10},{10... | collective-permute-start | bytes 2211848 | tf_op jit(solution)/shard_map/ppermute | solution.py:524

commit v4 on v3

--- a/solution.py
+++ b/solution.py
@@ -51,6 +51,21 @@
 
 def load_row(stack, base, width, length, row):
     stack[pl.ds(base + width, width), 0:length] = row
+    close_circle(stack, base, width, length)
+    shift_both(stack, base, width)
+
+
+def load_tiles(stack, base, width, length, tiles):
+    full = length // LANES
+    tail = length - full * LANES
+    chunks = width // SUB
+    packed = tiles(full * chunks)
+    for chunk in range(chunks):
+        rows = pl.ds(base + width + chunk * SUB, SUB)
+        for lane in range(full):
+            stack[rows, lane * LANES : (lane + 1) * LANES] = tiles(chunk * full + lane)
+        moved = pltpu.roll(packed, LANES - chunk * tail, 1) if chunk else packed
+        stack[rows, full * LANES : length] = moved[:, :tail]
     close_circle(stack, base, width, length)
     shift_both(stack, base, width)
 
@@ -116,10 +131,12 @@
 
 def inner_body(x, weights, bias, out, last, first, stack, second, *, width, length):
     rows = x.shape[1]
-    last[0] = x[0, rows - 2 :]
-    first[0] = x[0, :2]
     for row in range(rows):
-        load_row(stack, row * 3 * width, width, length, x[0, row])
+        base = row * 3 * width
+        load_row(stack, base, width, length, x[0, row])
+        if row < 2 or row >= rows - 2:
+            edge = first if row < 2 else last
+            write_tiles(edge, row % 2, stack[pl.ds(base + width, width), :], 0, width, length)
 
     def emit(row, value, at):
         write_tiles(out, row, value, at, width, length)
@@ -145,8 +162,8 @@
     opening = weights.ndim == 4
     out_specs = [pl.BlockSpec((1, height - 4, tiles, SUB, LANES), lambda m: (m, 0, 0, 0, 0))]
     out_shape = [jax.ShapeDtypeStruct((count, height - 4, tiles, SUB, LANES), bf16)]
-    out_specs += [pl.BlockSpec((1, 2, width, length), lambda m: (m, 0, 0, 0))] * 2
-    out_shape += [jax.ShapeDtypeStruct((count, 2, width, length), bf16)] * 2
+    out_specs += [pl.BlockSpec((1, 2, tiles, SUB, LANES), lambda m: (m, 0, 0, 0, 0))] * 2
+    out_shape += [jax.ShapeDtypeStruct((count, 2, tiles, SUB, LANES), bf16)] * 2
     if opening:
         out_specs.append(pl.BlockSpec((2 * width, 4 * unit), lambda m: (0, 0)))
         out_shape.append(jax.ShapeDtypeStruct((2 * width, 4 * unit), bf16))
@@ -180,11 +197,15 @@
     height = x.shape[1]
     for side in range(2):
         for row in range(6):
-            if side == 0:
-                source = low[0, row] if row < 2 else x[0, row - 2]
+            beyond = low if side == 0 else high
+            at = row if side == 0 else row - 4
+            if 0 <= at < 2:
+                load_tiles(
+                    first, row * unit, width, length, lambda tile, b=beyond, r=at: b[0, r, tile]
+                )
             else:
-                source = x[0, height - 4 + row] if row < 4 else high[0, row - 4]
-            load_row(first, row * unit, width, length, source)
+                inside = row - 2 if side == 0 else height - 4 + row
+                load_row(first, row * unit, width, length, x[0, inside])
 
         def emit(row, value, at, side=side):
             place = 2 * side + row
@@ -211,8 +232,8 @@
         in_specs=[
             pl.BlockSpec(memory_space=pltpu.SMEM),
             pl.BlockSpec((1, height, width, length), lambda m: (m + start, 0, 0, 0)),
-            pl.BlockSpec((1, 2, width, length), lambda m: (m, 0, 0, 0)),
-            pl.BlockSpec((1, 2, width, length), lambda m: (m, 0, 0, 0)),
+            pl.BlockSpec((1, 2, tiles, SUB, LANES), lambda m: (m, 0, 0, 0, 0)),
+            pl.BlockSpec((1, 2, tiles, SUB, LANES), lambda m: (m, 0, 0, 0, 0)),
             pl.BlockSpec(weights.shape, lambda m: (0, 0)),
             pl.BlockSpec(bias.shape, lambda m: (0, 0)),
         ],
@@ -403,7 +424,7 @@
             pltpu.SemaphoreType.DMA((count,)),
         ],
         input_output_aliases=alias,
-        compiler_params=pltpu.CompilerParams(vmem_limit_bytes=20 * MB),
+        compiler_params=pltpu.CompilerParams(vmem_limit_bytes=36 * MB),
         cost_estimate=SMALL,
         name="mix_rows",
     )(weights, *arrays)

time: 157 us -> 155 us (0.987)
  blocking collectives: 14.8 us -> 12.8 us
    ppermute x18, waiting for transfers between devices: 6.49 us -> 14 us  [swap(): return lax.ppermute(block, 'member', [(i, i ^ bit) for i in range(size)])]
    ppermute x2, waiting for transfers between devices: 36.1 us -> 29.9 us  [halo(): lax.ppermute(last, 'band', forward)]
    all_to_all x1, blocking collectives: 14.8 us -> 12.8 us  [local(): terms = lax.all_to_all(terms, 'band', 0, 0, tiled=True)]
  transfers between devices with their start and end apart: 22 -> 22, of which waited for: 5 -> 6; matrix products, arithmetic and copies ran while one was open for 2% -> 2% of each run, Pallas kernels for 35% -> 35%
where the time goes in v4:
time: 155 us; the launch traced here: 154 us
  Pallas kernels  67.4 us (43%)
  waiting for transfers between devices  43.8 us (28%)
  starting transfers between devices  23.2 us (15%)
  blocking collectives  12.8 us (8%)
  local copies, waits for them, and re-layouts  3.03 us (2%)
  other arithmetic  2.7 us (2%)
    ppermute x2, waiting for transfers between devices, halo(): lax.ppermute(last, 'band', forward)  29.9 us
    pallas_call x2, Pallas kernels, outer(): pl.pallas_call(functools.partial(outer_body, cut=cut, width=width, length...  18.4 us
    pallas_call x2, Pallas kernels, inner(): pl.pallas_call(functools.partial(opening_body if opening else inner_body,...  15.8 us
    ppermute x18, waiting for transfers between devices, swap(): return lax.ppermute(block, 'member', [(i, i ^ bit) for i in range(size)])  14 us
    pallas_call x2, Pallas kernels, gather(): pl.pallas_call(functools.partial(gather_body, pieces=pieces, kept=kept),...  14 us
    all_to_all x1, blocking collectives, local(): terms = lax.all_to_all(terms, 'band', 0, 0, tiled=True)  12.8 us
    ppermute x18, starting transfers between devices, swap(): return lax.ppermute(block, 'member', [(i, i ^ bit) for i in range(size)])  11.7 us
    pallas_call x2, Pallas kernels, mix(): pl.pallas_call(functools.partial(mix_body, sources=sources, kept=int(kept...  11.5 us
  transfers between devices with their start and end apart: 22, of which 6 were waited for; matrix products, arithmetic and copies ran while one was open for 2% of the time, Pallas kernels for 35%

profile of v4, /device:TPU:0, one launch (start us, length us, event | category | flops | bytes accessed | tf_op | source)
XLA Modules:
  0.0 154.1 jit_solution(4448325455992756463)
XLA Ops:
  0.0 8.5 %inner_rows.2 = (bf16[2,4,45,16,128]{4,3,2,1,0:T(8,128)(2,1)}, bf16[2,2,45,16,128]{4,3,2,1,0:T(8,128)(2,1)}, bf16[2,2,45,16,128]{4,3,2,1,0:T(8,128)(2,1)}, bf16[128,768]{1,0:T(8,128)(2,1)}, f32[128,128]{1,0:T(8,128)}) custom-call(bf16[4,8,64,1440]{3,2,1,0:T(8,128)(2,1)} %x.4, bf16[3,3,64,64]{3,2,1,0:T(8,128)(2,1)} %kernel.1, f32[1,64]{1,0:T(1,128)} %bitcast.5), custom_call_target="tpu_custom_call" | custom-call | flops 200000000 | bytes 500000 | tf_op jit(solution)/shard_map/inner_rows/pallas_call | solution.py:172
  8.5 3.0 %collective-permute-start.1 = (bf16[2,4,45,16,128]{4,3,2,1,0:T(8,128)(2,1)}, bf16[2,4,45,16,128]{4,3,2,1,0:T(8,128)(2,1)}, u32[]{:S(2)}, u32[]{:S(2)}) collective-permute-start(bf16[2,4,45,16,128]{4,3,2,1,0:T(8,128)(2,1)} %get-tuple-element.36.refs_0_), channel_id=1, source_target_pairs={{0,16},{8,24},{16,0},{24,8},{1,17},{9,25},{17,1},{25,9},{2,18},{10... | collective-permute-start | bytes 4423688 | tf_op jit(solution)/shard_map/ppermute | solution.py:545
  11.5 0.0 collective-permute-start.2
  11.5 3.4 %collective-permute-start.3 = (bf16[2,2,45,16,128]{4,3,2,1,0:T(8,128)(2,1)}, bf16[2,2,45,16,128]{4,3,2,1,0:T(8,128)(2,1)S(1)}, u32[]{:S(2)}, u32[]{:S(2)}) collective-permute-start(bf16[2,2,45,16,128]{4,3,2,1,0:T(8,128)(2,1)} %get-tuple-element.43), channel_id=1, source_target_pairs={{0,1},{1,2},{2,3},{3,4},{4,5},{5,6},{6,7},{8,9},{9,10},{10,11},{11... | collective-permute-start | bytes 2211848 | tf_op jit(solution)/shard_map/ppermute | solution.py:540
  14.9 1.3 collective-permute-start.4
  16.2 7.3 %inner_rows.3 = (bf16[2,4,45,16,128]{4,3,2,1,0:T(8,128)(2,1)}, bf16[2,2,45,16,128]{4,3,2,1,0:T(8,128)(2,1)}, bf16[2,2,45,16,128]{4,3,2,1,0:T(8,128)(2,1)}) custom-call(bf16[4,8,64,1440]{3,2,1,0:T(8,128)(2,1)} %x.4, bf16[128,768]{1,0:T(8,128)(2,1)} %get-tuple-element.38.weights, f32[128,128]{1,0:T(8,128)} %get-tuple-element.39.bias), custom_call_target="tpu_custom_call" | custom-call | flops 200000000 | bytes 500000 | tf_op jit(solution)/shard_map/inner_rows/pallas_call | solution.py:172
  23.6 0.5 collective-permute-start
  24.1 0.6 add_convert_fusion.ends
  24.7 22.7 %collective-permute-done.3.low = bf16[2,2,45,16,128]{4,3,2,1,0:T(8,128)(2,1)S(1)} collective-permute-done((bf16[2,2,45,16,128]{4,3,2,1,0:T(8,128)(2,1)}, bf16[2,2,45,16,128]{4,3,2,1,0:T(8,128)(2,1)S(1)}, u32[]{:S(2)}, u32[]{:S(2)}) %collective-permute-start.3) | collective-permute-done | bytes 737312 | tf_op jit(solution)/shard_map/ppermute | solution.py:540
  47.4 0.0 collective-permute-done.4.high
  47.4 5.3 %collective-permute-start.5 = (bf16[2,2,45,16,128]{4,3,2,1,0:T(8,128)(2,1)}, bf16[2,2,45,16,128]{4,3,2,1,0:T(8,128)(2,1)}, u32[]{:S(2)}, u32[]{:S(2)}) collective-permute-start(bf16[2,2,45,16,128]{4,3,2,1,0:T(8,128)(2,1)} %get-tuple-element.50), channel_id=1, source_target_pairs={{0,1},{1,2},{2,3},{3,4},{4,5},{5,6},{6,7},{8,9},{9,10},{10,11},{11... | collective-permute-start | bytes 2211848 | tf_op jit(solution)/shard_map/ppermute | solution.py:540
  52.8 1.5 collective-permute-start.6
  54.2 0.0 collective-permute-done.1.refs_2_
  54.2 0.0 collective-permute-done.2.refs_4_
  54.2 0.0 copy-done.8
  54.2 9.2 %outer_rows.2 = (bf16[2,2,45,16,128]{4,3,2,1,0:T(8,128)(2,1)}, bf16[2,2,45,16,128]{4,3,2,1,0:T(8,128)(2,1)}) custom-call(s32[2]{0:T(128)} %add_convert_fusion.ends, bf16[4,8,64,1440]{3,2,1,0:T(8,128)(2,1)} %x.4, bf16[2,2,45,16,128]{4,3,2,1,0:T(8,128)(2,1)} %copy-done.8, bf16[2,2,45,16,128]{4,3,2,1,0:T(8,128)(2,1)} %collective-permute-done.4.high, ...), custom_call_target="tpu_custom_call" | custom-call | flops 200000000 | bytes 500000 | tf_op jit(solution)/shard_map/outer_rows/pallas_call | solution.py:229
  63.4 0.5 collective-permute-start.10
  63.9 1.5 collective-permute-start.11
  65.5 0.6 fusion.6
  66.1 1.4 fusion.chosen
  67.5 6.9 %gather_cells.2.refs_2_ = bf16[2,1,2048]{2,1,0:T(2,128)(2,1)} custom-call(s32[2048]{0:T(1024)} %get-tuple-element.68.rows, f32[2048,128]{1,0:T(8,128)} %fusion.chosen, bf16[2,4,45,16,128]{4,3,2,1,0:T(8,128)(2,1)} %get-tuple-element.36.refs_0_, bf16[2,2,45,16,128]{4,3,2,1,0:T(8,128)(2,1)} %get-tuple-element.61.refs_1_.refs_0_, ...), custom_call_target="tpu_custom_call" | custom-call | flops 200000000 | bytes 500000 | tf_op jit(solution)/shard_map/gather_cells/pallas_call | solution.py:305
  74.4 2.1 %collective-permute-done.refs_3_ = bf16[2,4,45,16,128]{4,3,2,1,0:T(8,128)(2,1)} collective-permute-done((bf16[2,4,45,16,128]{4,3,2,1,0:T(8,128)(2,1)}, bf16[2,4,45,16,128]{4,3,2,1,0:T(8,128)(2,1)}, u32[]{:S(2)}, u32[]{:S(2)}) %collective-permute-start) | collective-permute-done | bytes 1474592 | tf_op jit(solution)/shard_map/ppermute | solution.py:545
  76.5 7.2 %collective-permute-done.5.low = bf16[2,2,45,16,128]{4,3,2,1,0:T(8,128)(2,1)} collective-permute-done((bf16[2,2,45,16,128]{4,3,2,1,0:T(8,128)(2,1)}, bf16[2,2,45,16,128]{4,3,2,1,0:T(8,128)(2,1)}, u32[]{:S(2)}, u32[]{:S(2)}) %collective-permute-start.5) | collective-permute-done | bytes 737312 | tf_op jit(solution)/shard_map/ppermute | solution.py:540
  83.7 0.0 collective-permute-done.6.high
  83.7 9.2 %outer_rows.3.refs_1_.refs_8_ = bf16[2,4,45,16,128]{4,3,2,1,0:T(8,128)(2,1)} custom-call(s32[2]{0:T(128)} %add_convert_fusion.ends, bf16[4,8,64,1440]{3,2,1,0:T(8,128)(2,1)} %x.4, bf16[2,2,45,16,128]{4,3,2,1,0:T(8,128)(2,1)} %collective-permute-done.5.low, bf16[2,2,45,16,128]{4,3,2,1,0:T(8,128)(2,1)} %collective-permute-done.6.high, ...), custom_call_target="tpu_custom_call" | custom-call | flops 200000000 | bytes 500000 | tf_op jit(solution)/shard_map/outer_rows/pallas_call | solution.py:229
  92.9 7.1 %gather_cells.3.refs_0_ = bf16[4,1,2048]{2,1,0:T(2,128)(2,1)} custom-call(s32[2048]{0:T(1024)} %get-tuple-element.68.rows, f32[2048,128]{1,0:T(8,128)} %fusion.chosen, bf16[2,4,45,16,128]{4,3,2,1,0:T(8,128)(2,1)} %get-tuple-element.56.refs_0_.refs_1_, bf16[2,4,45,16,128]{4,3,2,1,0:T(8,128)(2,1)} %outer_rows.3.refs_1_.refs_8_, ...), custom_call_target="tpu_custom_call" | custom-call | flops 200000000 | bytes 500000 | tf_op jit(solution)/shard_map/gather_cells/pallas_call | solution.py:305
  99.9 0.0 copy-start.1
  99.9 0.6 collective-permute-start.7
  100.5 0.0 collective-permute-start.8
  100.5 1.6 %collective-permute-start.9 = (bf16[4,1,2048]{2,1,0:T(2,128)(2,1)}, bf16[4,1,2048]{2,1,0:T(2,128)(2,1)S(1)}, u32[]{:S(2)}, u32[]{:S(2)}) collective-permute-start(bf16[4,1,2048]{2,1,0:T(2,128)(2,1)} %gather_cells.3.refs_0_), channel_id=1, source_target_pairs={{0,24},{8,16},{16,8},{24,0},{1,25},{9,17},{17,9},{25,1},{2,26},{10... | collective-permute-start | bytes 49160 | tf_op jit(solution)/shard_map/ppermute | solution.py:545
  102.1 6.1 %collective-permute-done.7.refs_1_ = bf16[4,1,2048]{2,1,0:T(2,128)(2,1)S(1)} collective-permute-done((bf16[4,1,2048]{2,1,0:T(2,128)(2,1)}, bf16[4,1,2048]{2,1,0:T(2,128)(2,1)S(1)}, u32[]{:S(2)}, u32[]{:S(2)}) %collective-permute-start.7) | collective-permute-done | bytes 16416 | tf_op jit(solution)/shard_map/ppermute | solution.py:545
  108.2 0.0 collective-permute-done.8.refs_2_
  108.3 0.0 collective-permute-done.9.refs_3_
  108.3 0.0 collective-permute-done.10.refs_1_
  108.3 0.0 collective-permute-done.11.refs_5_
  108.3 0.2 collective-permute-start.15
  108.5 0.4 collective-permute-start.14
  108.9 0.1 collective-permute-start.13
  109.0 0.4 collective-permute-start.12
  109.4 1.7 %collective-permute-start.20 = (bf16[2,4,45,16,128]{4,3,2,1,0:T(8,128)(2,1)}, bf16[2,4,45,16,128]{4,3,2,1,0:T(8,128)(2,1)}, u32[]{:S(2)}, u32[]{:S(2)}) collective-permute-start(bf16[2,4,45,16,128]{4,3,2,1,0:T(8,128)(2,1)} %outer_rows.3.refs_1_.refs_8_), channel_id=1, source_target_pairs={{0,16},{8,24},{16,0},{24,8},{1,17},{9,25},{17,1},{25,9},{2,18},{10... | collective-permute-start | bytes 4423688 | tf_op jit(solution)/shard_map/ppermute | solution.py:545
  111.8 1.9 %band_terms.1 = f32[8,1,2048]{2,1,0:T(1,128)} custom-call(s32[1]{0:T(128)S(6)} %copy.10.live, f32[1,2048]{1,0:T(1,128)} %bitcast.6, f32[1,2048]{1,0:T(1,128)} %bitcast.7, bf16[4,1,2048]{2,1,0:T(2,128)(2,1)} %gather_cells.3.refs_0_, bf16[4,1,2048]{2,1,0:T(2,128)(2,1)} %copy-done.10, bf16[4,1,2048]{2,1,0:T(2,128)(2,1)} %copy-done.11, ...), custom_call_target="tpu_custom_call" | custom-call | flops 200000000 | bytes 500000 | tf_op jit(solution)/shard_map/band_terms/pallas_call | solution.py:458
  113.7 12.8 %all_to_all.5.terms = f32[8,1,2048]{2,1,0:T(1,128)} all-to-all(f32[8,1,2048]{2,1,0:T(1,128)} %band_terms.1), channel_id=1, replica_groups=mesh['member'=4,'band'=8] {'band'}, dimensions={0} | all-to-all | bytes 131072 | tf_op jit(solution)/shard_map/all_to_all | solution.py:600
  126.5 0.0 collective-permute-done.15.refs_10_
  126.5 0.0 collective-permute-done.14.refs_7_
  126.5 0.0 collective-permute-done.13.refs_6_
  126.5 0.0 collective-permute-done.12.refs_5_
  126.5 0.1 collective-permute-start.18
  126.6 0.5 collective-permute-start.17
  127.1 0.1 collective-permute-start.16
  127.2 5.9 %transform.1.weights = bf16[64,256]{1,0:T(8,128)(2,1)} custom-call(f32[8,1,2048]{2,1,0:T(1,128)} %all_to_all.5.terms), custom_call_target="tpu_custom_call" | custom-call | flops 200000000 | bytes 500000 | tf_op jit(solution)/shard_map/transform/pallas_call | solution.py:522
  133.1 0.0 collective-permute-done.18.refs_3_
  133.1 0.9 copy-done.5
  133.9 0.0 collective-permute-done.17.refs_6_
  133.9 0.0 collective-permute-done.16.refs_2_
  134.0 1.4 copy-done.2
  135.3 0.8 copy-done.7
  136.1 6.2 %mix_rows.2.refs_12_ = bf16[4,8,64,1440]{3,2,1,0:T(8,128)(2,1)} custom-call(bf16[64,256]{1,0:T(8,128)(2,1)S(1)} %copy-done.7, bf16[2,4,45,16,128]{4,3,2,1,0:T(8,128)(2,1)S(1)} %copy-done.1, bf16[2,4,45,16,128]{4,3,2,1,0:T(8,128)(2,1)S(1)} %copy-done.2, bf16[2,4,45,16,128]{4,3,2,1,0:T(8,128)(2,1)} %collective-permute-done.1.refs_2_, ...), custom_call_target="tpu_custom_call" | custom-call | flops 200000000 | bytes 500000 | tf_op jit(solution)/shard_map/mix_rows/pallas_call | solution.py:414
  142.3 1.7 %collective-permute-done.20.refs_9_ = bf16[2,4,45,16,128]{4,3,2,1,0:T(8,128)(2,1)} collective-permute-done((bf16[2,4,45,16,128]{4,3,2,1,0:T(8,128)(2,1)}, bf16[2,4,45,16,128]{4,3,2,1,0:T(8,128)(2,1)}, u32[]{:S(2)}, u32[]{:S(2)}) %collective-permute-start.20) | collective-permute-done | bytes 1474592 | tf_op jit(solution)/shard_map/ppermute | solution.py:545
  144.0 0.0 collective-permute-start.21
  144.0 0.5 collective-permute-start.19
  144.5 4.0 %collective-permute-done.19.refs_7_ = bf16[2,2,45,16,128]{4,3,2,1,0:T(8,128)(2,1)S(1)} collective-permute-done((bf16[2,2,45,16,128]{4,3,2,1,0:T(8,128)(2,1)}, bf16[2,2,45,16,128]{4,3,2,1,0:T(8,128)(2,1)S(1)}, u32[]{:S(2)}, u32[]{:S(2)}) %collective-permute-start.19) | collective-permute-done | bytes 737312 | tf_op jit(solution)/shard_map/ppermute | solution.py:545
  148.6 0.0 collective-permute-done.21.refs_11_
  148.6 0.0 copy-done.6
  148.6 5.3 %mix_rows.3 = bf16[4,8,64,1440]{3,2,1,0:T(8,128)(2,1)} custom-call(bf16[64,256]{1,0:T(8,128)(2,1)S(1)} %copy-done.7, bf16[2,2,45,16,128]{4,3,2,1,0:T(8,128)(2,1)S(1)} %copy-done.3, bf16[2,2,45,16,128]{4,3,2,1,0:T(8,128)(2,1)} %collective-permute-done.10.refs_1_, ...), custom_call_target="tpu_custom_call", output_to_operand_aliasing={{}: (13, {})} | custom-call | flops 200000000 | bytes 500000 | tf_op jit(solution)/shard_map/mix_rows/pallas_call | solution.py:414
  (20 shorter events, 0.0 us)
Async XLA Ops:
  8.5 45.7 %collective-permute-start.1 = (bf16[2,4,45,16,128]{4,3,2,1,0:T(8,128)(2,1)}, bf16[2,4,45,16,128]{4,3,2,1,0:T(8,128)(2,1)}, u32[]{:S(2)}, u32[]{:S(2)}) collective-permute-start(bf16[2,4,45,16,128]{4,3,2,1,0:T(8,128)(2,1)} %get-tuple-element.36.refs_0_), channel_id=1, source_target_pairs={{0,16},{8,24},{16,0},{24,8},{1,17},{9,25},{17,1},{25,9},{2,18},{10... | collective-permute-start | bytes 4423688 | tf_op jit(solution)/shard_map/ppermute | solution.py:545
  11.5 42.7 %collective-permute-start.2 = (bf16[2,4,45,16,128]{4,3,2,1,0:T(8,128)(2,1)}, bf16[2,4,45,16,128]{4,3,2,1,0:T(8,128)(2,1)}, u32[]{:S(2)}, u32[]{:S(2)}) collective-permute-start(bf16[2,4,45,16,128]{4,3,2,1,0:T(8,128)(2,1)} %get-tuple-element.36.refs_0_), channel_id=1, source_target_pairs={{0,8},{8,0},{16,24},{24,16},{1,9},{9,1},{17,25},{25,17},{2,10},{10... | collective-permute-start | bytes 4423688 | tf_op jit(solution)/shard_map/ppermute | solution.py:545
  11.5 35.9 %collective-permute-start.3 = (bf16[2,2,45,16,128]{4,3,2,1,0:T(8,128)(2,1)}, bf16[2,2,45,16,128]{4,3,2,1,0:T(8,128)(2,1)S(1)}, u32[]{:S(2)}, u32[]{:S(2)}) collective-permute-start(bf16[2,2,45,16,128]{4,3,2,1,0:T(8,128)(2,1)} %get-tuple-element.43), channel_id=1, source_target_pairs={{0,1},{1,2},{2,3},{3,4},{4,5},{5,6},{6,7},{8,9},{9,10},{10,11},{11... | collective-permute-start | bytes 2211848 | tf_op jit(solution)/shard_map/ppermute | solution.py:540
  14.9 32.5 %collective-permute-start.4 = (bf16[2,2,45,16,128]{4,3,2,1,0:T(8,128)(2,1)}, bf16[2,2,45,16,128]{4,3,2,1,0:T(8,128)(2,1)}, u32[]{:S(2)}, u32[]{:S(2)}) collective-permute-start(bf16[2,2,45,16,128]{4,3,2,1,0:T(8,128)(2,1)} %get-tuple-element.44), channel_id=1, source_target_pairs={{1,0},{2,1},{3,2},{4,3},{5,4},{6,5},{7,6},{9,8},{10,9},{11,10},{12... | collective-permute-start | bytes 2211848 | tf_op jit(solution)/shard_map/ppermute | solution.py:540
  23.6 53.0 %collective-permute-start = (bf16[2,4,45,16,128]{4,3,2,1,0:T(8,128)(2,1)}, bf16[2,4,45,16,128]{4,3,2,1,0:T(8,128)(2,1)}, u32[]{:S(2)}, u32[]{:S(2)}) collective-permute-start(bf16[2,4,45,16,128]{4,3,2,1,0:T(8,128)(2,1)} %get-tuple-element.56.refs_0_.refs_1_), channel_id=1, source_target_pairs={{0,16},{8,24},{16,0},{24,8},{1,17},{9,25},{17,1},{25,9},{2,18},{10... | collective-permute-start | bytes 4423688 | tf_op jit(solution)/shard_map/ppermute | solution.py:545
  47.4 6.8 %copy-start.8 = (bf16[2,2,45,16,128]{4,3,2,1,0:T(8,128)(2,1)}, bf16[2,2,45,16,128]{4,3,2,1,0:T(8,128)(2,1)S(1)}, u32[]{:S(2)}) copy-start(bf16[2,2,45,16,128]{4,3,2,1,0:T(8,128)(2,1)S(1)} %collective-permute-done.3.low) | copy-start | bytes 2211844
  47.4 18.0 %copy-start.9 = (s32[2048]{0:T(1024)S(1)}, s32[2048]{0:T(1024)}, u32[]{:S(2)}) copy-start(s32[2048]{0:T(1024)} %param.10) | copy-start | bytes 24580
  47.4 36.3 %collective-permute-start.5 = (bf16[2,2,45,16,128]{4,3,2,1,0:T(8,128)(2,1)}, bf16[2,2,45,16,128]{4,3,2,1,0:T(8,128)(2,1)}, u32[]{:S(2)}, u32[]{:S(2)}) collective-permute-start(bf16[2,2,45,16,128]{4,3,2,1,0:T(8,128)(2,1)} %get-tuple-element.50), channel_id=1, source_target_pairs={{0,1},{1,2},{2,3},{3,4},{4,5},{5,6},{6,7},{8,9},{9,10},{10,11},{11... | collective-permute-start | bytes 2211848 | tf_op jit(solution)/shard_map/ppermute | solution.py:540
  52.8 30.9 %collective-permute-start.6 = (bf16[2,2,45,16,128]{4,3,2,1,0:T(8,128)(2,1)}, bf16[2,2,45,16,128]{4,3,2,1,0:T(8,128)(2,1)}, u32[]{:S(2)}, u32[]{:S(2)}) collective-permute-start(bf16[2,2,45,16,128]{4,3,2,1,0:T(8,128)(2,1)} %get-tuple-element.51), channel_id=1, source_target_pairs={{1,0},{2,1},{3,2},{4,3},{5,4},{6,5},{7,6},{9,8},{10,9},{11,10},{12... | collective-permute-start | bytes 2211848 | tf_op jit(solution)/shard_map/ppermute | solution.py:540
  63.4 44.8 %collective-permute-start.10 = (bf16[2,2,45,16,128]{4,3,2,1,0:T(8,128)(2,1)}, bf16[2,2,45,16,128]{4,3,2,1,0:T(8,128)(2,1)}, u32[]{:S(2)}, u32[]{:S(2)}) collective-permute-start(bf16[2,2,45,16,128]{4,3,2,1,0:T(8,128)(2,1)} %get-tuple-element.61.refs_1_.refs_0_), channel_id=1, source_target_pairs={{0,16},{8,24},{16,0},{24,8},{1,17},{9,25},{17,1},{25,9},{2,18},{10... | collective-permute-start | bytes 2211848 | tf_op jit(solution)/shard_map/ppermute | solution.py:545
  63.9 44.3 %collective-permute-start.11 = (bf16[2,2,45,16,128]{4,3,2,1,0:T(8,128)(2,1)}, bf16[2,2,45,16,128]{4,3,2,1,0:T(8,128)(2,1)}, u32[]{:S(2)}, u32[]{:S(2)}) collective-permute-start(bf16[2,2,45,16,128]{4,3,2,1,0:T(8,128)(2,1)} %get-tuple-element.62.refs_2_.refs_4_), channel_id=1, source_target_pairs={{0,16},{8,24},{16,0},{24,8},{1,17},{9,25},{17,1},{25,9},{2,18},{10... | collective-permute-start | bytes 2211848 | tf_op jit(solution)/shard_map/ppermute | solution.py:545
  92.9 34.2 %copy-start.3 = (bf16[2,2,45,16,128]{4,3,2,1,0:T(8,128)(2,1)S(1)}, bf16[2,2,45,16,128]{4,3,2,1,0:T(8,128)(2,1)}, u32[]{:S(2)}) copy-start(bf16[2,2,45,16,128]{4,3,2,1,0:T(8,128)(2,1)} %get-tuple-element.61.refs_1_.refs_0_) | copy-start | bytes 2211844
  99.9 34.0 %copy-start.1 = (bf16[2,4,45,16,128]{4,3,2,1,0:T(8,128)(2,1)S(1)}, bf16[2,4,45,16,128]{4,3,2,1,0:T(8,128)(2,1)}, u32[]{:S(2)}) copy-start(bf16[2,4,45,16,128]{4,3,2,1,0:T(8,128)(2,1)} %get-tuple-element.36.refs_0_) | copy-start | bytes 4423684
  99.9 8.3 %collective-permute-start.7 = (bf16[4,1,2048]{2,1,0:T(2,128)(2,1)}, bf16[4,1,2048]{2,1,0:T(2,128)(2,1)S(1)}, u32[]{:S(2)}, u32[]{:S(2)}) collective-permute-start(bf16[4,1,2048]{2,1,0:T(2,128)(2,1)} %gather_cells.3.refs_0_), channel_id=1, source_target_pairs={{0,16},{8,24},{16,0},{24,8},{1,17},{9,25},{17,1},{25,9},{2,18},{10... | collective-permute-start | bytes 49160 | tf_op jit(solution)/shard_map/ppermute | solution.py:545
  100.5 7.8 %collective-permute-start.8 = (bf16[4,1,2048]{2,1,0:T(2,128)(2,1)}, bf16[4,1,2048]{2,1,0:T(2,128)(2,1)S(1)}, u32[]{:S(2)}, u32[]{:S(2)}) collective-permute-start(bf16[4,1,2048]{2,1,0:T(2,128)(2,1)} %gather_cells.3.refs_0_), channel_id=1, source_target_pairs={{0,8},{8,0},{16,24},{24,16},{1,9},{9,1},{17,25},{25,17},{2,10},{10... | collective-permute-start | bytes 49160 | tf_op jit(solution)/shard_map/ppermute | solution.py:545
  100.5 7.8 %collective-permute-start.9 = (bf16[4,1,2048]{2,1,0:T(2,128)(2,1)}, bf16[4,1,2048]{2,1,0:T(2,128)(2,1)S(1)}, u32[]{:S(2)}, u32[]{:S(2)}) collective-permute-start(bf16[4,1,2048]{2,1,0:T(2,128)(2,1)} %gather_cells.3.refs_0_), channel_id=1, source_target_pairs={{0,24},{8,16},{16,8},{24,0},{1,25},{9,17},{17,9},{25,1},{2,26},{10... | collective-permute-start | bytes 49160 | tf_op jit(solution)/shard_map/ppermute | solution.py:545
  108.2 3.5 %copy-start.10 = (bf16[4,1,2048]{2,1,0:T(2,128)(2,1)}, bf16[4,1,2048]{2,1,0:T(2,128)(2,1)S(1)}, u32[]{:S(2)}) copy-start(bf16[4,1,2048]{2,1,0:T(2,128)(2,1)S(1)} %collective-permute-done.7.refs_1_) | copy-start | bytes 49156
  108.3 3.5 %copy-start.11 = (bf16[4,1,2048]{2,1,0:T(2,128)(2,1)}, bf16[4,1,2048]{2,1,0:T(2,128)(2,1)S(1)}, u32[]{:S(2)}) copy-start(bf16[4,1,2048]{2,1,0:T(2,128)(2,1)S(1)} %collective-permute-done.8.refs_2_) | copy-start | bytes 49156
  108.3 3.5 %copy-start.12 = (bf16[4,1,2048]{2,1,0:T(2,128)(2,1)}, bf16[4,1,2048]{2,1,0:T(2,128)(2,1)S(1)}, u32[]{:S(2)}) copy-start(bf16[4,1,2048]{2,1,0:T(2,128)(2,1)S(1)} %collective-permute-done.9.refs_3_) | copy-start | bytes 49156
  108.3 18.2 %collective-permute-start.15 = (bf16[2,4,45,16,128]{4,3,2,1,0:T(8,128)(2,1)}, bf16[2,4,45,16,128]{4,3,2,1,0:T(8,128)(2,1)}, u32[]{:S(2)}, u32[]{:S(2)}) collective-permute-start(bf16[2,4,45,16,128]{4,3,2,1,0:T(8,128)(2,1)} %outer_rows.3.refs_1_.refs_8_), channel_id=1, source_target_pairs={{0,8},{8,0},{16,24},{24,16},{1,9},{9,1},{17,25},{25,17},{2,10},{10... | collective-permute-start | bytes 4423688 | tf_op jit(solution)/shard_map/ppermute | solution.py:545
  108.5 18.0 %collective-permute-start.14 = (bf16[2,4,45,16,128]{4,3,2,1,0:T(8,128)(2,1)}, bf16[2,4,45,16,128]{4,3,2,1,0:T(8,128)(2,1)}, u32[]{:S(2)}, u32[]{:S(2)}) collective-permute-start(bf16[2,4,45,16,128]{4,3,2,1,0:T(8,128)(2,1)} %collective-permute-done.refs_3_), channel_id=1, source_target_pairs={{0,8},{8,0},{16,24},{24,16},{1,9},{9,1},{17,25},{25,17},{2,10},{10... | collective-permute-start | bytes 4423688 | tf_op jit(solution)/shard_map/ppermute | solution.py:545
  108.9 17.6 %collective-permute-start.13 = (bf16[2,4,45,16,128]{4,3,2,1,0:T(8,128)(2,1)}, bf16[2,4,45,16,128]{4,3,2,1,0:T(8,128)(2,1)}, u32[]{:S(2)}, u32[]{:S(2)}) collective-permute-start(bf16[2,4,45,16,128]{4,3,2,1,0:T(8,128)(2,1)} %collective-permute-done.1.refs_2_), channel_id=1, source_target_pairs={{0,8},{8,0},{16,24},{24,16},{1,9},{9,1},{17,25},{25,17},{2,10},{10... | collective-permute-start | bytes 4423688 | tf_op jit(solution)/shard_map/ppermute | solution.py:545
  109.0 17.5 %collective-permute-start.12 = (bf16[2,4,45,16,128]{4,3,2,1,0:T(8,128)(2,1)}, bf16[2,4,45,16,128]{4,3,2,1,0:T(8,128)(2,1)}, u32[]{:S(2)}, u32[]{:S(2)}) collective-permute-start(bf16[2,4,45,16,128]{4,3,2,1,0:T(8,128)(2,1)} %get-tuple-element.56.refs_0_.refs_1_), channel_id=1, source_target_pairs={{0,8},{8,0},{16,24},{24,16},{1,9},{9,1},{17,25},{25,17},{2,10},{10... | collective-permute-start | bytes 4423688 | tf_op jit(solution)/shard_map/ppermute | solution.py:545
  109.4 34.6 %collective-permute-start.20 = (bf16[2,4,45,16,128]{4,3,2,1,0:T(8,128)(2,1)}, bf16[2,4,45,16,128]{4,3,2,1,0:T(8,128)(2,1)}, u32[]{:S(2)}, u32[]{:S(2)}) collective-permute-start(bf16[2,4,45,16,128]{4,3,2,1,0:T(8,128)(2,1)} %outer_rows.3.refs_1_.refs_8_), channel_id=1, source_target_pairs={{0,16},{8,24},{16,0},{24,8},{1,17},{9,25},{17,1},{25,9},{2,18},{10... | collective-permute-start | bytes 4423688 | tf_op jit(solution)/shard_map/ppermute | solution.py:545
  126.5 6.6 %collective-permute-start.18 = (bf16[2,2,45,16,128]{4,3,2,1,0:T(8,128)(2,1)}, bf16[2,2,45,16,128]{4,3,2,1,0:T(8,128)(2,1)S(1)}, u32[]{:S(2)}, u32[]{:S(2)}) collective-permute-start(bf16[2,2,45,16,128]{4,3,2,1,0:T(8,128)(2,1)} %collective-permute-done.10.refs_1_), channel_id=1, source_target_pairs={{0,8},{8,0},{16,24},{24,16},{1,9},{9,1},{17,25},{25,17},{2,10},{10... | collective-permute-start | bytes 2211848 | tf_op jit(solution)/shard_map/ppermute | solution.py:545
  126.6 7.4 %collective-permute-start.17 = (bf16[2,2,45,16,128]{4,3,2,1,0:T(8,128)(2,1)}, bf16[2,2,45,16,128]{4,3,2,1,0:T(8,128)(2,1)}, u32[]{:S(2)}, u32[]{:S(2)}) collective-permute-start(bf16[2,2,45,16,128]{4,3,2,1,0:T(8,128)(2,1)} %get-tuple-element.62.refs_2_.refs_4_), channel_id=1, source_target_pairs={{0,8},{8,0},{16,24},{24,16},{1,9},{9,1},{17,25},{25,17},{2,10},{10... | collective-permute-start | bytes 2211848 | tf_op jit(solution)/shard_map/ppermute | solution.py:545
  127.1 6.9 %collective-permute-start.16 = (bf16[2,2,45,16,128]{4,3,2,1,0:T(8,128)(2,1)S(1)}, bf16[2,2,45,16,128]{4,3,2,1,0:T(8,128)(2,1)}, u32[]{:S(2)}, u32[]{:S(2)}) collective-permute-start(bf16[2,2,45,16,128]{4,3,2,1,0:T(8,128)(2,1)S(1)} %copy-done.3), channel_id=1, source_target_pairs={{0,8},{8,0},{16,24},{24,16},{1,9},{9,1},{17,25},{25,17},{2,10},{10... | collective-permute-start | bytes 2211848 | tf_op jit(solution)/shard_map/ppermute | solution.py:545
  133.1 15.5 %copy-start = (bf16[2,4,45,16,128]{4,3,2,1,0:T(8,128)(2,1)S(1)}, bf16[2,4,45,16,128]{4,3,2,1,0:T(8,128)(2,1)}, u32[]{:S(2)}) copy-start(bf16[2,4,45,16,128]{4,3,2,1,0:T(8,128)(2,1)} %outer_rows.3.refs_1_.refs_8_) | copy-start | bytes 4423684
  133.1 0.9 copy-start.5
  133.9 1.4 copy-start.2
  135.3 0.8 copy-start.7
  136.1 12.5 %copy-start.4 = (bf16[2,2,45,16,128]{4,3,2,1,0:T(8,128)(2,1)S(1)}, bf16[2,2,45,16,128]{4,3,2,1,0:T(8,128)(2,1)}, u32[]{:S(2)}) copy-start(bf16[2,2,45,16,128]{4,3,2,1,0:T(8,128)(2,1)} %get-tuple-element.62.refs_2_.refs_4_) | copy-start | bytes 2211844
  136.1 12.5 %copy-start.6 = (bf16[2,2,45,16,128]{4,3,2,1,0:T(8,128)(2,1)S(1)}, bf16[2,2,45,16,128]{4,3,2,1,0:T(8,128)(2,1)}, u32[]{:S(2)}) copy-start(bf16[2,2,45,16,128]{4,3,2,1,0:T(8,128)(2,1)} %copy-done.5) | copy-start | bytes 2211844
  144.0 4.5 %collective-permute-start.21 = (bf16[2,4,45,16,128]{4,3,2,1,0:T(8,128)(2,1)}, bf16[2,4,45,16,128]{4,3,2,1,0:T(8,128)(2,1)S(1)}, u32[]{:S(2)}, u32[]{:S(2)}) collective-permute-start(bf16[2,4,45,16,128]{4,3,2,1,0:T(8,128)(2,1)} %collective-permute-done.20.refs_9_), channel_id=1, source_target_pairs={{0,8},{8,0},{16,24},{24,16},{1,9},{9,1},{17,25},{25,17},{2,10},{10... | collective-permute-start | bytes 4423688 | tf_op jit(solution)/shard_map/ppermute | solution.py:545
  144.0 4.5 %collective-permute-start.19 = (bf16[2,2,45,16,128]{4,3,2,1,0:T(8,128)(2,1)}, bf16[2,2,45,16,128]{4,3,2,1,0:T(8,128)(2,1)S(1)}, u32[]{:S(2)}, u32[]{:S(2)}) collective-permute-start(bf16[2,2,45,16,128]{4,3,2,1,0:T(8,128)(2,1)} %collective-permute-done.11.refs_5_), channel_id=1, source_target_pairs={{0,8},{8,0},{16,24},{24,16},{1,9},{9,1},{17,25},{25,17},{2,10},{10... | collective-permute-start | bytes 2211848 | tf_op jit(solution)/shard_map/ppermute | solution.py:545

commit v5 on v4

--- a/solution.py
+++ b/solution.py
@@ -129,13 +129,13 @@
                 emit(top + half, value[half * width : (half + 1) * width], lanes.start)
 
 
-def inner_body(x, weights, bias, out, last, first, stack, second, *, width, length):
+def inner_tiles(x, weights, bias, out, edges, stack, second, width, length):
     rows = x.shape[1]
     for row in range(rows):
         base = row * 3 * width
         load_row(stack, base, width, length, x[0, row])
-        if row < 2 or row >= rows - 2:
-            edge = first if row < 2 else last
+        if edges and (row < 2 or row >= rows - 2):
+            edge = edges[1] if row < 2 else edges[0]
             write_tiles(edge, row % 2, stack[pl.ds(base + width, width), :], 0, width, length)
 
     def emit(row, value, at):
@@ -144,47 +144,119 @@
     two_steps(stack, second, rows, weights, bias, emit, None, width, length)
 
 
-def opening_body(x, kernel, offset, out, last, first, weights, bias, *scratch, width, length):
+def inner_body(x, weights, bias, out, *refs, width, length):
+    inner_tiles(x, weights, bias, out, refs[:-2], *refs[-2:], width, length)
+
+
+def opening_body(
+    x, more_last, more_first, kernel, offset, out, last, first, weights, bias, stack, second, *,
+    width, length,
+):
     pair_matrix(kernel, weights, width)
     shape = (width, width)
     row = lax.broadcasted_iota(jnp.int32, shape, 0)
     column = lax.broadcasted_iota(jnp.int32, shape, 1)
     line = jnp.sum(jnp.where(row == column, offset[...], 0.0), axis=1, keepdims=True)
     bias[...] = jnp.broadcast_to(jnp.concatenate([line] * 2, axis=0), bias.shape)
-    inner_body(x, weights, bias, out, last, first, *scratch, width=width, length=length)
-
-
-def inner(x, weights, bias, start, count):
+    for more, edge in ((more_last, last), (more_first, first)):
+        for row in range(2):
+            stack[0:width, 0:length] = more[0, row]
+            write_tiles(edge.at[1:2], row, stack[0:width, :], 0, width, length)
+    edges = (last.at[0:1], first.at[0:1])
+    inner_tiles(x, weights, bias, out, edges, stack, second, width, length)
+
+
+def second_body(x, weights, bias, inner0, out, both, *scratch, width, length):
+    both[0:1] = inner0[...]
+    inner_tiles(x, weights, bias, out, (), *scratch, width, length)
+    both[1:2] = out[...]
+
+
+def inner_layout(x, count, edged):
     _, height, width, length = x.shape
     padded = round_up(length, LANES)
     tiles = width * length // (SUB * LANES)
     unit = 3 * width
-    opening = weights.ndim == 4
-    out_specs = [pl.BlockSpec((1, height - 4, tiles, SUB, LANES), lambda m: (m, 0, 0, 0, 0))]
-    out_shape = [jax.ShapeDtypeStruct((count, height - 4, tiles, SUB, LANES), bf16)]
-    out_specs += [pl.BlockSpec((1, 2, tiles, SUB, LANES), lambda m: (m, 0, 0, 0, 0))] * 2
-    out_shape += [jax.ShapeDtypeStruct((count, 2, tiles, SUB, LANES), bf16)] * 2
-    if opening:
-        out_specs.append(pl.BlockSpec((2 * width, 4 * unit), lambda m: (0, 0)))
-        out_shape.append(jax.ShapeDtypeStruct((2 * width, 4 * unit), bf16))
-        out_specs.append(pl.BlockSpec((2 * width, LANES), lambda m: (0, 0)))
-        out_shape.append(jax.ShapeDtypeStruct((2 * width, LANES), f32))
+    shapes = [
+        jax.ShapeDtypeStruct((members, rows, tiles, SUB, LANES), bf16)
+        for members, rows in ((count, height - 4), (edged, 2), (edged, 2))
+    ]
+    scratch = [
+        pltpu.VMEM((height * unit, padded), bf16),
+        pltpu.VMEM(((height - 2) * unit, padded), bf16),
+    ]
+    return shapes, scratch
+
+
+def opening(x, kernel, offset):
+    _, height, width, length = x.shape
+    shapes, scratch = inner_layout(x, 1, 2)
+    edge = (1, 2, width, length)
     return pl.pallas_call(
-        functools.partial(
-            opening_body if opening else inner_body, width=width, length=length
-        ),
+        functools.partial(opening_body, width=width, length=length),
+        grid=(1,),
+        in_specs=[
+            pl.BlockSpec((1, height, width, length), lambda i: (0, 0, 0, 0)),
+            pl.BlockSpec(edge, lambda i: (1, height // 2 - 1, 0, 0)),
+            pl.BlockSpec(edge, lambda i: (1, 0, 0, 0)),
+            pl.BlockSpec(kernel.shape, lambda i: (0, 0, 0, 0)),
+            pl.BlockSpec(offset.shape, lambda i: (0, 0)),
+        ],
+        out_specs=[pl.BlockSpec(shape.shape, lambda i: (0, 0, 0, 0, 0)) for shape in shapes]
+        + [
+            pl.BlockSpec((2 * width, 12 * width), lambda i: (0, 0)),
+            pl.BlockSpec((2 * width, LANES), lambda i: (0, 0)),
+        ],
+        out_shape=shapes
+        + [
+            jax.ShapeDtypeStruct((2 * width, 12 * width), bf16),
+            jax.ShapeDtypeStruct((2 * width, LANES), f32),
+        ],
+        scratch_shapes=scratch,
+        compiler_params=pltpu.CompilerParams(vmem_limit_bytes=VMEM),
+        cost_estimate=SMALL,
+        name="opening_rows",
+    )(x, x, x, kernel, offset)
+
+
+def second(x, weights, bias, inner0):
+    _, height, width, length = x.shape
+    shapes, scratch = inner_layout(x, 1, 2)
+    shapes = [shapes[0], jax.ShapeDtypeStruct((2,) + shapes[0].shape[1:], bf16)]
+    return pl.pallas_call(
+        functools.partial(second_body, width=width, length=length),
+        grid=(1,),
+        in_specs=[
+            pl.BlockSpec((1, height, width, length), lambda i: (1, 0, 0, 0)),
+            pl.BlockSpec(weights.shape, lambda i: (0, 0)),
+            pl.BlockSpec(bias.shape, lambda i: (0, 0)),
+            pl.BlockSpec(inner0.shape, lambda i: (0, 0, 0, 0, 0)),
+        ],
+        out_specs=[pl.BlockSpec(shape.shape, lambda i: (0, 0, 0, 0, 0)) for shape in shapes],
+        out_shape=shapes,
+        scratch_shapes=scratch,
+        compiler_params=pltpu.CompilerParams(vmem_limit_bytes=VMEM),
+        cost_estimate=SMALL,
+        name="second_rows",
+    )(x, weights, bias, inner0)
+
+
+def inner(x, weights, bias, start, count):
+    _, height, width, length = x.shape
+    shapes, scratch = inner_layout(x, count, count)
+    return pl.pallas_call(
+        functools.partial(inner_body, width=width, length=length),
         grid=(count,),
         in_specs=[
             pl.BlockSpec((1, height, width, length), lambda m: (m + start, 0, 0, 0)),
-            pl.BlockSpec(weights.shape, lambda m: (0,) * weights.ndim),
+            pl.BlockSpec(weights.shape, lambda m: (0, 0)),
             pl.BlockSpec(bias.shape, lambda m: (0, 0)),
         ],
-        out_specs=out_specs,
-        out_shape=out_shape,
-        scratch_shapes=[
-            pltpu.VMEM((height * unit, padded), bf16),
-            pltpu.VMEM(((height - 2) * unit, padded), bf16),
-        ],
+        out_specs=[
+            pl.BlockSpec((1,) + shape.shape[1:], lambda m: (m, 0, 0, 0, 0)) for shape in shapes
+        ],
+        out_shape=shapes,
+        scratch_shapes=scratch,
         compiler_params=pltpu.CompilerParams(vmem_limit_bytes=VMEM),
         cost_estimate=SMALL,
         name="inner_rows",
@@ -560,35 +632,43 @@
     bands = lax.axis_size("band")
     ends = jnp.stack([band > 0, band < bands - 1]).astype(jnp.int32)
     rows, lanes = slot_places(measured_cell_position, height, width, length)
-    chosen = (lanes[:, None] == jnp.arange(LANES, dtype=jnp.int32)[None, :]).astype(f32)
 
     half = members // 2
-    inner0, last0, first0, weights, bias = inner(
-        x, filter_kernel_tensor, filter_offset_vector[None, :], 0, half
+    inner0, last0, first0, weights, bias = opening(
+        x, filter_kernel_tensor, filter_offset_vector[None, :]
     )
     inner0_across = swap(inner0, 2)
     halo0 = halo(last0, first0)
-    inner1, last1, first1 = inner(after(x, inner0), weights, bias, half, members - half)
+    inner1, inner01 = second(x, weights, bias, inner0)
     inner1_across = swap(inner1, 2)
-    halo1 = halo(*lax.optimization_barrier((last1, first1, *halo0))[:2])
-
-    inner0_core = swap(inner0, 1)
-    top0, bottom0 = outer(
-        ends, after(x, inner0_across, inner0_core), *halo0, weights, bias, 0, 2
-    )
+    inner2, last2, first2 = inner(after(x, inner1), weights, bias, half, members - half)
+    inner2_across = swap(inner2, 2)
+    halo1 = halo(*lax.optimization_barrier((last2, first2, *halo0))[:2])
+
+    lanes = after(lanes, inner0_across)
+    chosen = (lanes[:, None] == jnp.arange(LANES, dtype=jnp.int32)[None, :]).astype(f32)
+    top0, bottom0 = outer(ends, after(x, chosen, inner1_across), *halo0, weights, bias, 0, 2)
     top0_across, bottom0_across = swap(top0, 2), swap(bottom0, 2)
 
-    def pieces(*firsts):
-        return [(n, m, m, first) for n, first in enumerate(firsts) for m in range(half)]
+    def pieces(members_at, *firsts):
+        inside = 1 + max(n for n, _ in members_at)
+        return [(n, index, m, 0) for m, (n, index) in enumerate(members_at)] + [
+            (n + inside, m, m, first) for n, first in enumerate(firsts) for m in range(half)
+        ]
 
     edge = height - 4
-    seen0 = gather(rows, chosen, (inner0, top0, bottom0), pieces(0, edge, edge + 2))
+    seen0 = gather(
+        rows,
+        chosen,
+        (inner01, top0, bottom0),
+        pieces([(0, m) for m in range(half)], edge, edge + 2),
+    )
     (outer1,) = outer(ends, after(x, seen0), *halo1, weights, bias, half, 4)
     seen = gather(
         rows,
-        after(chosen, inner1_across),
-        (inner1, outer1),
-        pieces(0, edge),
+        after(chosen, inner2_across),
+        (inner2, outer1),
+        pieces([(0, m) for m in range(members - half)], edge),
         (seen0,),
     )
     seen_parts = [seen] + [swap(seen, bits) for bits in (2, 1, 3)]
@@ -598,22 +678,23 @@
         measured_slot_number, measured_precision_factor, measured_reading, seen_parts, bands
     )
     terms = lax.all_to_all(terms, "band", 0, 0, tiled=True)
-    inner1_core, inner0_far, inner1_far, outer1_core = [
-        swap(after(part, *seen_parts[1:]), 1)
-        for part in (inner1, inner0_across, inner1_across, outer1)
+    inner01_core, inner2_core, inner2_far, outer1_core = [
+        swap(after(part, *seen_parts[1:]), 1) for part in (inner01, inner2, inner2_across, outer1)
     ]
-    terms = after(terms, inner1_core, inner0_far, inner1_far, outer1_core)
-    top0_core, bottom0_core, top0_far = [
-        swap(after(part, terms), 1) for part in (top0, bottom0, top0_across)
+    terms = after(terms, inner01_core, inner2_core, inner2_far, outer1_core)
+    inner0_far, inner1_far, top0_core, bottom0_core = [
+        swap(after(part, terms), 1) for part in (inner0_across, inner1_across, top0, bottom0)
     ]
     blend = transform(terms, members)
-    blend = after(blend, top0_core, bottom0_core, top0_far)
-    bottom0_far = swap(after(bottom0_across, blend), 1)
-
-    arrays = (inner0, inner1, inner0_across, inner1_across)
-    arrays += (inner0_core, inner1_core, inner0_far, inner1_far)
+    blend = after(blend, inner0_far, inner1_far, top0_core, bottom0_core)
+    top0_far, bottom0_far = [
+        swap(after(part, blend), 1) for part in (top0_across, bottom0_across)
+    ]
+
+    arrays = (inner01, inner2, inner0_across, inner1_across, inner2_across)
+    arrays += (inner01_core, inner2_core, inner0_far, inner1_far, inner2_far)
     sources = tuple(
-        (row + 2, tuple((index, row) for index in range(8))) for row in range(height - 4)
+        (row + 2, tuple((index, row) for index in range(10))) for row in range(height - 4)
     )
     result = mix(blend, arrays, sources, x.shape, None)
     outer1_far = swap(after(outer1_across, result), 1)

time: 155 us -> 153 us (0.987)
  waiting for transfers between devices: 43.8 us -> 35.6 us
  Pallas kernels: 67.4 us -> 70.6 us
  starting transfers between devices: 23.2 us -> 25.9 us
    ppermute x2, waiting for transfers between devices: 29.9 us -> 18.1 us  [halo(): lax.ppermute(last, 'band', forward)]
    ppermute x18 -> x20, waiting for transfers between devices: 14 us -> 17.4 us  [swap(): return lax.ppermute(block, 'member', [(i, i ^ bit) for i in range(size)])]
    pallas_call x2 -> x3, Pallas kernels: 15.8 us -> 19 us  [the longest x1 7.28 us: inner(): pl.pallas_call(functools.partial(inner_body, width=width, length=length),...]
    ppermute x18 -> x20, starting transfers between devices: 11.7 us -> 13.7 us  [swap(): return lax.ppermute(block, 'member', [(i, i ^ bit) for i in range(size)])]
    unnamed x26 -> x28, local copies, waits for them, and re-layouts: 3.03 us -> 4.16 us
  transfers between devices with their start and end apart: 22 -> 24, of which waited for: 6 -> 8; matrix products, arithmetic and copies ran while one was open for 2% -> 2% of each run, Pallas kernels for 35% -> 39%
where the time goes in v5:
time: 153 us
  Pallas kernels  70.6 us (46%)
  waiting for transfers between devices  35.6 us (23%)
  starting transfers between devices  25.9 us (17%)
  blocking collectives  12.8 us (8%)
  local copies, waits for them, and re-layouts  4.16 us (3%)
  other arithmetic  2.63 us (2%)
    pallas_call x2, Pallas kernels, outer(): pl.pallas_call(functools.partial(outer_body, cut=cut, width=width, length...  18.3 us
    ppermute x2, waiting for transfers between devices, halo(): lax.ppermute(last, 'band', forward)  18.1 us
    ppermute x20, waiting for transfers between devices, swap(): return lax.ppermute(block, 'member', [(i, i ^ bit) for i in range(size)])  17.4 us
    pallas_call x2, Pallas kernels, gather(): pl.pallas_call(functools.partial(gather_body, pieces=pieces, kept=kept),...  14 us
    ppermute x20, starting transfers between devices, swap(): return lax.ppermute(block, 'member', [(i, i ^ bit) for i in range(size)])  13.7 us
    all_to_all x1, blocking collectives, local(): terms = lax.all_to_all(terms, 'band', 0, 0, tiled=True)  12.8 us
    pallas_call x2, Pallas kernels, mix(): pl.pallas_call(functools.partial(mix_body, sources=sources, kept=int(kept...  11.5 us
    ppermute x2, starting transfers between devices, halo(): lax.ppermute(last, 'band', forward)  9.49 us
  transfers between devices with their start and end apart: 24, of which 8 were waited for; matrix products, arithmetic and copies ran while one was open for 2% of the time, Pallas kernels for 39%

profile of v5, /device:TPU:0, one launch (start us, length us, event | category | flops | bytes accessed | tf_op | source)
XLA Modules:
  0.0 152.7 jit_solution(4998536150429096438)
XLA Ops:
  0.0 6.1 %opening_rows.1 = (bf16[1,4,45,16,128]{4,3,2,1,0:T(8,128)(2,1)}, bf16[2,2,45,16,128]{4,3,2,1,0:T(8,128)(2,1)}, bf16[2,2,45,16,128]{4,3,2,1,0:T(8,128)(2,1)}, bf16[128,768]{1,0:T(8,128)(2,1)}, f32[128,128]{1,0:T(8,128)}) custom-call(bf16[4,8,64,1440]{3,2,1,0:T(8,128)(2,1)} %x.6, bf16[4,8,64,1440]{3,2,1,0:T(8,128)(2,1)} %x.6, bf16[4,8,64,1440]{3,2,1,0:T(8,128)(2,1)} %x.6, ...), custom_call_target="tpu_custom_call" | custom-call | flops 200000000 | bytes 500000 | tf_op jit(solution)/shard_map/opening_rows/pallas_call | solution.py:195
  6.1 3.0 %collective-permute-start = (bf16[1,4,45,16,128]{4,3,2,1,0:T(8,128)(2,1)}, bf16[1,4,45,16,128]{4,3,2,1,0:T(8,128)(2,1)S(1)}, u32[]{:S(2)}, u32[]{:S(2)}) collective-permute-start(bf16[1,4,45,16,128]{4,3,2,1,0:T(8,128)(2,1)} %get-tuple-element.41.inner0), channel_id=1, source_target_pairs={{0,16},{8,24},{16,0},{24,8},{1,17},{9,25},{17,1},{25,9},{2,18},{10... | collective-permute-start | bytes 2211848 | tf_op jit(solution)/shard_map/ppermute | solution.py:617
  9.1 4.3 %collective-permute-start.3 = (bf16[2,2,45,16,128]{4,3,2,1,0:T(8,128)(2,1)}, bf16[2,2,45,16,128]{4,3,2,1,0:T(8,128)(2,1)}, u32[]{:S(2)}, u32[]{:S(2)}) collective-permute-start(bf16[2,2,45,16,128]{4,3,2,1,0:T(8,128)(2,1)} %get-tuple-element.51), channel_id=1, source_target_pairs={{0,1},{1,2},{2,3},{3,4},{4,5},{5,6},{6,7},{8,9},{9,10},{10,11},{11... | collective-permute-start | bytes 2211848 | tf_op jit(solution)/shard_map/ppermute | solution.py:612
  13.3 1.3 collective-permute-start.4
  14.6 5.6 %second_rows.1 = (bf16[1,4,45,16,128]{4,3,2,1,0:T(8,128)(2,1)}, bf16[2,4,45,16,128]{4,3,2,1,0:T(8,128)(2,1)}) custom-call(bf16[4,8,64,1440]{3,2,1,0:T(8,128)(2,1)} %x.6, bf16[128,768]{1,0:T(8,128)(2,1)} %get-tuple-element.43.weights, f32[128,128]{1,0:T(8,128)} %get-tuple-element.44.bias, bf16[1,4,45,16,128]{4,3,2,1,0:T(8,128)(2,1)} %get-tuple-element.41.inner0), custom_call_target="tpu_custom_call" | custom-call | flops 200000000 | bytes 500000 | tf_op jit(solution)/shard_map/second_rows/pallas_call | solution.py:226
  20.3 0.5 collective-permute-start.2
  20.8 7.3 %inner_rows.1 = (bf16[2,4,45,16,128]{4,3,2,1,0:T(8,128)(2,1)}, bf16[2,2,45,16,128]{4,3,2,1,0:T(8,128)(2,1)}, bf16[2,2,45,16,128]{4,3,2,1,0:T(8,128)(2,1)}) custom-call(bf16[4,8,64,1440]{3,2,1,0:T(8,128)(2,1)} %x.6, bf16[128,768]{1,0:T(8,128)(2,1)} %get-tuple-element.43.weights, f32[128,128]{1,0:T(8,128)} %get-tuple-element.44.bias), custom_call_target="tpu_custom_call" | custom-call | flops 200000000 | bytes 500000 | tf_op jit(solution)/shard_map/inner_rows/pallas_call | solution.py:247
  28.1 1.5 collective-permute-start.1
  29.6 0.6 add_convert_fusion.ends
  30.2 0.6 fusion.6
  30.9 0.0 collective-permute-done.refs_2_
  30.9 13.2 %collective-permute-done.3.low = bf16[2,2,45,16,128]{4,3,2,1,0:T(8,128)(2,1)} collective-permute-done((bf16[2,2,45,16,128]{4,3,2,1,0:T(8,128)(2,1)}, bf16[2,2,45,16,128]{4,3,2,1,0:T(8,128)(2,1)}, u32[]{:S(2)}, u32[]{:S(2)}) %collective-permute-start.3) | collective-permute-done | bytes 737312 | tf_op jit(solution)/shard_map/ppermute | solution.py:612
  44.0 0.0 collective-permute-done.4.high
  44.1 5.2 %collective-permute-start.5 = (bf16[2,2,45,16,128]{4,3,2,1,0:T(8,128)(2,1)}, bf16[2,2,45,16,128]{4,3,2,1,0:T(8,128)(2,1)}, u32[]{:S(2)}, u32[]{:S(2)}) collective-permute-start(bf16[2,2,45,16,128]{4,3,2,1,0:T(8,128)(2,1)} %get-tuple-element.58), channel_id=1, source_target_pairs={{0,1},{1,2},{2,3},{3,4},{4,5},{5,6},{6,7},{8,9},{9,10},{10,11},{11... | collective-permute-start | bytes 2211848 | tf_op jit(solution)/shard_map/ppermute | solution.py:612
  49.3 1.5 collective-permute-start.6
  50.8 1.3 fusion.chosen
  52.1 0.0 collective-permute-done.2.refs_3_
  52.1 9.1 %outer_rows.2 = (bf16[2,2,45,16,128]{4,3,2,1,0:T(8,128)(2,1)}, bf16[2,2,45,16,128]{4,3,2,1,0:T(8,128)(2,1)}) custom-call(s32[2]{0:T(128)} %add_convert_fusion.ends, bf16[4,8,64,1440]{3,2,1,0:T(8,128)(2,1)} %x.6, bf16[2,2,45,16,128]{4,3,2,1,0:T(8,128)(2,1)} %collective-permute-done.3.low, bf16[2,2,45,16,128]{4,3,2,1,0:T(8,128)(2,1)} %collective-permute-done.4.high, ...), custom_call_target="tpu_custom_call" | custom-call | flops 200000000 | bytes 500000 | tf_op jit(solution)/shard_map/outer_rows/pallas_call | solution.py:301
  61.2 0.6 collective-permute-start.10
  61.8 1.5 collective-permute-start.11
  63.3 6.9 %gather_cells.2.refs_2_ = bf16[2,1,2048]{2,1,0:T(2,128)(2,1)} custom-call(s32[2048]{0:T(1024)} %get-tuple-element.78.rows, f32[2048,128]{1,0:T(8,128)} %fusion.chosen, bf16[2,4,45,16,128]{4,3,2,1,0:T(8,128)(2,1)} %get-tuple-element.64.refs_0_, bf16[2,2,45,16,128]{4,3,2,1,0:T(8,128)(2,1)} %get-tuple-element.71.refs_1_.refs_0_, ...), custom_call_target="tpu_custom_call" | custom-call | flops 200000000 | bytes 500000 | tf_op jit(solution)/shard_map/gather_cells/pallas_call | solution.py:377
  70.2 3.9 %collective-permute-done.1.refs_4_ = bf16[2,4,45,16,128]{4,3,2,1,0:T(8,128)(2,1)} collective-permute-done((bf16[2,4,45,16,128]{4,3,2,1,0:T(8,128)(2,1)}, bf16[2,4,45,16,128]{4,3,2,1,0:T(8,128)(2,1)}, u32[]{:S(2)}, u32[]{:S(2)}) %collective-permute-start.1) | collective-permute-done | bytes 1474592 | tf_op jit(solution)/shard_map/ppermute | solution.py:617
  74.1 5.0 %collective-permute-done.5.low = bf16[2,2,45,16,128]{4,3,2,1,0:T(8,128)(2,1)} collective-permute-done((bf16[2,2,45,16,128]{4,3,2,1,0:T(8,128)(2,1)}, bf16[2,2,45,16,128]{4,3,2,1,0:T(8,128)(2,1)}, u32[]{:S(2)}, u32[]{:S(2)}) %collective-permute-start.5) | collective-permute-done | bytes 737312 | tf_op jit(solution)/shard_map/ppermute | solution.py:612
  79.1 0.0 collective-permute-done.6.high
  79.1 9.2 %outer_rows.3.refs_1_.refs_8_ = bf16[2,4,45,16,128]{4,3,2,1,0:T(8,128)(2,1)} custom-call(s32[2]{0:T(128)} %add_convert_fusion.ends, bf16[4,8,64,1440]{3,2,1,0:T(8,128)(2,1)} %x.6, bf16[2,2,45,16,128]{4,3,2,1,0:T(8,128)(2,1)} %collective-permute-done.5.low, bf16[2,2,45,16,128]{4,3,2,1,0:T(8,128)(2,1)} %collective-permute-done.6.high, ...), custom_call_target="tpu_custom_call" | custom-call | flops 200000000 | bytes 500000 | tf_op jit(solution)/shard_map/outer_rows/pallas_call | solution.py:301
  88.3 7.1 %gather_cells.3.refs_0_ = bf16[4,1,2048]{2,1,0:T(2,128)(2,1)} custom-call(s32[2048]{0:T(1024)} %get-tuple-element.78.rows, f32[2048,128]{1,0:T(8,128)} %fusion.chosen, bf16[2,4,45,16,128]{4,3,2,1,0:T(8,128)(2,1)} %get-tuple-element.65.refs_0_.refs_1_, bf16[2,4,45,16,128]{4,3,2,1,0:T(8,128)(2,1)} %outer_rows.3.refs_1_.refs_8_, ...), custom_call_target="tpu_custom_call" | custom-call | flops 200000000 | bytes 500000 | tf_op jit(solution)/shard_map/gather_cells/pallas_call | solution.py:377
  95.4 0.6 collective-permute-start.7
  95.9 0.0 collective-permute-start.8
  96.0 1.6 %collective-permute-start.9 = (bf16[4,1,2048]{2,1,0:T(2,128)(2,1)}, bf16[4,1,2048]{2,1,0:T(2,128)(2,1)S(1)}, u32[]{:S(2)}, u32[]{:S(2)}) collective-permute-start(bf16[4,1,2048]{2,1,0:T(2,128)(2,1)} %gather_cells.3.refs_0_), channel_id=1, source_target_pairs={{0,24},{8,16},{16,8},{24,0},{1,25},{9,17},{17,9},{25,1},{2,26},{10... | collective-permute-start | bytes 49160 | tf_op jit(solution)/shard_map/ppermute | solution.py:617
  97.6 0.0 collective-permute-done.10.refs_1_
  97.6 8.0 %collective-permute-done.11.refs_5_ = bf16[2,2,45,16,128]{4,3,2,1,0:T(8,128)(2,1)} collective-permute-done((bf16[2,2,45,16,128]{4,3,2,1,0:T(8,128)(2,1)}, bf16[2,2,45,16,128]{4,3,2,1,0:T(8,128)(2,1)}, u32[]{:S(2)}, u32[]{:S(2)}) %collective-permute-start.11) | collective-permute-done | bytes 737312 | tf_op jit(solution)/shard_map/ppermute | solution.py:617
  105.6 0.2 collective-permute-done.7.refs_1_
  105.9 0.1 collective-permute-start.15
  106.0 0.4 collective-permute-start.14
  106.4 0.1 collective-permute-start.13
  106.5 0.4 collective-permute-start.12
  107.0 1.7 %collective-permute-start.22 = (bf16[2,4,45,16,128]{4,3,2,1,0:T(8,128)(2,1)}, bf16[2,4,45,16,128]{4,3,2,1,0:T(8,128)(2,1)}, u32[]{:S(2)}, u32[]{:S(2)}) collective-permute-start(bf16[2,4,45,16,128]{4,3,2,1,0:T(8,128)(2,1)} %outer_rows.3.refs_1_.refs_8_), channel_id=1, source_target_pairs={{0,16},{8,24},{16,0},{24,8},{1,17},{9,25},{17,1},{25,9},{2,18},{10... | collective-permute-start | bytes 4423688 | tf_op jit(solution)/shard_map/ppermute | solution.py:617
  109.4 1.9 %band_terms.1 = f32[8,1,2048]{2,1,0:T(1,128)} custom-call(s32[1]{0:T(128)S(6)} %copy.10.live, f32[1,2048]{1,0:T(1,128)} %bitcast.6, f32[1,2048]{1,0:T(1,128)} %bitcast.7, bf16[4,1,2048]{2,1,0:T(2,128)(2,1)} %gather_cells.3.refs_0_, bf16[4,1,2048]{2,1,0:T(2,128)(2,1)} %copy-done.11, bf16[4,1,2048]{2,1,0:T(2,128)(2,1)} %copy-done.12, ...), custom_call_target="tpu_custom_call" | custom-call | flops 200000000 | bytes 500000 | tf_op jit(solution)/shard_map/band_terms/pallas_call | solution.py:530
  111.2 12.8 %all_to_all.5.terms = f32[8,1,2048]{2,1,0:T(1,128)} all-to-all(f32[8,1,2048]{2,1,0:T(1,128)} %band_terms.1), channel_id=1, replica_groups=mesh['member'=4,'band'=8] {'band'}, dimensions={0} | all-to-all | bytes 131072 | tf_op jit(solution)/shard_map/all_to_all | solution.py:680
  124.1 0.0 collective-permute-done.15.refs_10_
  124.1 0.0 collective-permute-done.14.refs_9_
  124.1 0.1 collective-permute-start.19
  124.2 0.5 collective-permute-start.18
  124.7 0.1 collective-permute-start.17
  124.7 0.4 collective-permute-start.16
  125.2 5.9 %transform.1.weights = bf16[64,256]{1,0:T(8,128)(2,1)} custom-call(f32[8,1,2048]{2,1,0:T(1,128)} %all_to_all.5.terms), custom_call_target="tpu_custom_call" | custom-call | flops 200000000 | bytes 500000 | tf_op jit(solution)/shard_map/transform/pallas_call | solution.py:594
  131.1 0.0 collective-permute-done.19.refs_6_
  131.1 0.9 copy-done.7
  132.0 0.0 collective-permute-done.18.refs_2_
  132.0 0.0 collective-permute-done.17.refs_8_
  132.0 0.0 collective-permute-done.16.refs_7_
  132.0 0.0 copy-start.2
  132.0 1.4 copy-done.2
  133.4 1.1 copy-done.6
  134.5 0.8 copy-done.9
  135.2 6.1 %mix_rows.2.refs_12_ = bf16[4,8,64,1440]{3,2,1,0:T(8,128)(2,1)} custom-call(bf16[64,256]{1,0:T(8,128)(2,1)S(1)} %copy-done.9, bf16[2,4,45,16,128]{4,3,2,1,0:T(8,128)(2,1)S(1)} %copy-done.1, bf16[2,4,45,16,128]{4,3,2,1,0:T(8,128)(2,1)S(1)} %copy-done.2, bf16[1,4,45,16,128]{4,3,2,1,0:T(8,128)(2,1)S(1)} %copy-done.6, ...), custom_call_target="tpu_custom_call" | custom-call | flops 200000000 | bytes 500000 | tf_op jit(solution)/shard_map/mix_rows/pallas_call | solution.py:486
  141.4 0.2 collective-permute-done.22.refs_9_
  141.5 0.0 collective-permute-start.23
  141.6 0.5 collective-permute-start.21
  142.1 0.0 collective-permute-start.20
  142.1 4.0 %collective-permute-done.21.refs_7_ = bf16[2,2,45,16,128]{4,3,2,1,0:T(8,128)(2,1)S(1)} collective-permute-done((bf16[2,2,45,16,128]{4,3,2,1,0:T(8,128)(2,1)}, bf16[2,2,45,16,128]{4,3,2,1,0:T(8,128)(2,1)S(1)}, u32[]{:S(2)}, u32[]{:S(2)}) %collective-permute-start.21) | collective-permute-done | bytes 737312 | tf_op jit(solution)/shard_map/ppermute | solution.py:617
  146.1 1.1 collective-permute-done.20.refs_3_
  147.1 0.0 collective-permute-done.23.refs_11_
  147.2 5.4 %mix_rows.3 = bf16[4,8,64,1440]{3,2,1,0:T(8,128)(2,1)} custom-call(bf16[64,256]{1,0:T(8,128)(2,1)S(1)} %copy-done.9, bf16[2,2,45,16,128]{4,3,2,1,0:T(8,128)(2,1)S(1)} %copy-done.3, bf16[2,2,45,16,128]{4,3,2,1,0:T(8,128)(2,1)} %collective-permute-done.10.refs_1_, ...), custom_call_target="tpu_custom_call", output_to_operand_aliasing={{}: (13, {})} | custom-call | flops 200000000 | bytes 500000 | tf_op jit(solution)/shard_map/mix_rows/pallas_call | solution.py:486
  (27 shorter events, 0.1 us)
Async XLA Ops:
  6.1 24.8 %collective-permute-start = (bf16[1,4,45,16,128]{4,3,2,1,0:T(8,128)(2,1)}, bf16[1,4,45,16,128]{4,3,2,1,0:T(8,128)(2,1)S(1)}, u32[]{:S(2)}, u32[]{:S(2)}) collective-permute-start(bf16[1,4,45,16,128]{4,3,2,1,0:T(8,128)(2,1)} %get-tuple-element.41.inner0), channel_id=1, source_target_pairs={{0,16},{8,24},{16,0},{24,8},{1,17},{9,25},{17,1},{25,9},{2,18},{10... | collective-permute-start | bytes 2211848 | tf_op jit(solution)/shard_map/ppermute | solution.py:617
  9.1 35.0 %collective-permute-start.3 = (bf16[2,2,45,16,128]{4,3,2,1,0:T(8,128)(2,1)}, bf16[2,2,45,16,128]{4,3,2,1,0:T(8,128)(2,1)}, u32[]{:S(2)}, u32[]{:S(2)}) collective-permute-start(bf16[2,2,45,16,128]{4,3,2,1,0:T(8,128)(2,1)} %get-tuple-element.51), channel_id=1, source_target_pairs={{0,1},{1,2},{2,3},{3,4},{4,5},{5,6},{6,7},{8,9},{9,10},{10,11},{11... | collective-permute-start | bytes 2211848 | tf_op jit(solution)/shard_map/ppermute | solution.py:612
  13.3 30.7 %collective-permute-start.4 = (bf16[2,2,45,16,128]{4,3,2,1,0:T(8,128)(2,1)}, bf16[2,2,45,16,128]{4,3,2,1,0:T(8,128)(2,1)}, u32[]{:S(2)}, u32[]{:S(2)}) collective-permute-start(bf16[2,2,45,16,128]{4,3,2,1,0:T(8,128)(2,1)} %get-tuple-element.52), channel_id=1, source_target_pairs={{1,0},{2,1},{3,2},{4,3},{5,4},{6,5},{7,6},{9,8},{10,9},{11,10},{12... | collective-permute-start | bytes 2211848 | tf_op jit(solution)/shard_map/ppermute | solution.py:612
  20.3 10.0 %copy-start.10 = (s32[2048]{0:T(1024)S(1)}, s32[2048]{0:T(1024)}, u32[]{:S(2)}) copy-start(s32[2048]{0:T(1024)} %param.10) | copy-start | bytes 24580
  20.3 31.8 %collective-permute-start.2 = (bf16[1,4,45,16,128]{4,3,2,1,0:T(8,128)(2,1)}, bf16[1,4,45,16,128]{4,3,2,1,0:T(8,128)(2,1)}, u32[]{:S(2)}, u32[]{:S(2)}) collective-permute-start(bf16[1,4,45,16,128]{4,3,2,1,0:T(8,128)(2,1)} %get-tuple-element.45), channel_id=1, source_target_pairs={{0,16},{8,24},{16,0},{24,8},{1,17},{9,25},{17,1},{25,9},{2,18},{10... | collective-permute-start | bytes 2211848 | tf_op jit(solution)/shard_map/ppermute | solution.py:617
  28.1 46.1 %collective-permute-start.1 = (bf16[2,4,45,16,128]{4,3,2,1,0:T(8,128)(2,1)}, bf16[2,4,45,16,128]{4,3,2,1,0:T(8,128)(2,1)}, u32[]{:S(2)}, u32[]{:S(2)}) collective-permute-start(bf16[2,4,45,16,128]{4,3,2,1,0:T(8,128)(2,1)} %get-tuple-element.65.refs_0_.refs_1_), channel_id=1, source_target_pairs={{0,16},{8,24},{16,0},{24,8},{1,17},{9,25},{17,1},{25,9},{2,18},{10... | collective-permute-start | bytes 4423688 | tf_op jit(solution)/shard_map/ppermute | solution.py:617
  30.9 30.4 %copy-start.5 = (bf16[1,4,45,16,128]{4,3,2,1,0:T(8,128)(2,1)}, bf16[1,4,45,16,128]{4,3,2,1,0:T(8,128)(2,1)S(1)}, u32[]{:S(2)}) copy-start(bf16[1,4,45,16,128]{4,3,2,1,0:T(8,128)(2,1)S(1)} %collective-permute-done.refs_2_) | copy-start | bytes 2211844
  44.1 35.0 %collective-permute-start.5 = (bf16[2,2,45,16,128]{4,3,2,1,0:T(8,128)(2,1)}, bf16[2,2,45,16,128]{4,3,2,1,0:T(8,128)(2,1)}, u32[]{:S(2)}, u32[]{:S(2)}) collective-permute-start(bf16[2,2,45,16,128]{4,3,2,1,0:T(8,128)(2,1)} %get-tuple-element.58), channel_id=1, source_target_pairs={{0,1},{1,2},{2,3},{3,4},{4,5},{5,6},{6,7},{8,9},{9,10},{10,11},{11... | collective-permute-start | bytes 2211848 | tf_op jit(solution)/shard_map/ppermute | solution.py:612
  49.3 29.8 %collective-permute-start.6 = (bf16[2,2,45,16,128]{4,3,2,1,0:T(8,128)(2,1)}, bf16[2,2,45,16,128]{4,3,2,1,0:T(8,128)(2,1)}, u32[]{:S(2)}, u32[]{:S(2)}) collective-permute-start(bf16[2,2,45,16,128]{4,3,2,1,0:T(8,128)(2,1)} %get-tuple-element.59), channel_id=1, source_target_pairs={{1,0},{2,1},{3,2},{4,3},{5,4},{6,5},{7,6},{9,8},{10,9},{11,10},{12... | collective-permute-start | bytes 2211848 | tf_op jit(solution)/shard_map/ppermute | solution.py:612
  61.2 36.3 %collective-permute-start.10 = (bf16[2,2,45,16,128]{4,3,2,1,0:T(8,128)(2,1)}, bf16[2,2,45,16,128]{4,3,2,1,0:T(8,128)(2,1)}, u32[]{:S(2)}, u32[]{:S(2)}) collective-permute-start(bf16[2,2,45,16,128]{4,3,2,1,0:T(8,128)(2,1)} %get-tuple-element.71.refs_1_.refs_0_), channel_id=1, source_target_pairs={{0,16},{8,24},{16,0},{24,8},{1,17},{9,25},{17,1},{25,9},{2,18},{10... | collective-permute-start | bytes 2211848 | tf_op jit(solution)/shard_map/ppermute | solution.py:617
  61.8 43.8 %collective-permute-start.11 = (bf16[2,2,45,16,128]{4,3,2,1,0:T(8,128)(2,1)}, bf16[2,2,45,16,128]{4,3,2,1,0:T(8,128)(2,1)}, u32[]{:S(2)}, u32[]{:S(2)}) collective-permute-start(bf16[2,2,45,16,128]{4,3,2,1,0:T(8,128)(2,1)} %get-tuple-element.72.refs_2_.refs_4_), channel_id=1, source_target_pairs={{0,16},{8,24},{16,0},{24,8},{1,17},{9,25},{17,1},{25,9},{2,18},{10... | collective-permute-start | bytes 2211848 | tf_op jit(solution)/shard_map/ppermute | solution.py:617
  88.3 35.9 %copy-start.3 = (bf16[2,2,45,16,128]{4,3,2,1,0:T(8,128)(2,1)S(1)}, bf16[2,2,45,16,128]{4,3,2,1,0:T(8,128)(2,1)}, u32[]{:S(2)}) copy-start(bf16[2,2,45,16,128]{4,3,2,1,0:T(8,128)(2,1)} %get-tuple-element.71.refs_1_.refs_0_) | copy-start | bytes 2211844
  95.4 36.6 %copy-start.1 = (bf16[2,4,45,16,128]{4,3,2,1,0:T(8,128)(2,1)S(1)}, bf16[2,4,45,16,128]{4,3,2,1,0:T(8,128)(2,1)}, u32[]{:S(2)}) copy-start(bf16[2,4,45,16,128]{4,3,2,1,0:T(8,128)(2,1)} %get-tuple-element.64.refs_0_) | copy-start | bytes 4423684
  95.4 10.5 %collective-permute-start.7 = (bf16[4,1,2048]{2,1,0:T(2,128)(2,1)}, bf16[4,1,2048]{2,1,0:T(2,128)(2,1)S(1)}, u32[]{:S(2)}, u32[]{:S(2)}) collective-permute-start(bf16[4,1,2048]{2,1,0:T(2,128)(2,1)} %gather_cells.3.refs_0_), channel_id=1, source_target_pairs={{0,16},{8,24},{16,0},{24,8},{1,17},{9,25},{17,1},{25,9},{2,18},{10... | collective-permute-start | bytes 49160 | tf_op jit(solution)/shard_map/ppermute | solution.py:617
  95.9 9.9 %collective-permute-start.8 = (bf16[4,1,2048]{2,1,0:T(2,128)(2,1)}, bf16[4,1,2048]{2,1,0:T(2,128)(2,1)S(1)}, u32[]{:S(2)}, u32[]{:S(2)}) collective-permute-start(bf16[4,1,2048]{2,1,0:T(2,128)(2,1)} %gather_cells.3.refs_0_), channel_id=1, source_target_pairs={{0,8},{8,0},{16,24},{24,16},{1,9},{9,1},{17,25},{25,17},{2,10},{10... | collective-permute-start | bytes 49160 | tf_op jit(solution)/shard_map/ppermute | solution.py:617
  96.0 9.9 %collective-permute-start.9 = (bf16[4,1,2048]{2,1,0:T(2,128)(2,1)}, bf16[4,1,2048]{2,1,0:T(2,128)(2,1)S(1)}, u32[]{:S(2)}, u32[]{:S(2)}) collective-permute-start(bf16[4,1,2048]{2,1,0:T(2,128)(2,1)} %gather_cells.3.refs_0_), channel_id=1, source_target_pairs={{0,24},{8,16},{16,8},{24,0},{1,25},{9,17},{17,9},{25,1},{2,26},{10... | collective-permute-start | bytes 49160 | tf_op jit(solution)/shard_map/ppermute | solution.py:617
  105.8 3.5 %copy-start.11 = (bf16[4,1,2048]{2,1,0:T(2,128)(2,1)}, bf16[4,1,2048]{2,1,0:T(2,128)(2,1)S(1)}, u32[]{:S(2)}) copy-start(bf16[4,1,2048]{2,1,0:T(2,128)(2,1)S(1)} %collective-permute-done.7.refs_1_) | copy-start | bytes 49156
  105.8 3.5 %copy-start.12 = (bf16[4,1,2048]{2,1,0:T(2,128)(2,1)}, bf16[4,1,2048]{2,1,0:T(2,128)(2,1)S(1)}, u32[]{:S(2)}) copy-start(bf16[4,1,2048]{2,1,0:T(2,128)(2,1)S(1)} %collective-permute-done.8.refs_2_) | copy-start | bytes 49156
  105.9 3.5 %copy-start.13 = (bf16[4,1,2048]{2,1,0:T(2,128)(2,1)}, bf16[4,1,2048]{2,1,0:T(2,128)(2,1)S(1)}, u32[]{:S(2)}) copy-start(bf16[4,1,2048]{2,1,0:T(2,128)(2,1)S(1)} %collective-permute-done.9.refs_3_) | copy-start | bytes 49156
  105.9 18.2 %collective-permute-start.15 = (bf16[2,4,45,16,128]{4,3,2,1,0:T(8,128)(2,1)}, bf16[2,4,45,16,128]{4,3,2,1,0:T(8,128)(2,1)}, u32[]{:S(2)}, u32[]{:S(2)}) collective-permute-start(bf16[2,4,45,16,128]{4,3,2,1,0:T(8,128)(2,1)} %outer_rows.3.refs_1_.refs_8_), channel_id=1, source_target_pairs={{0,8},{8,0},{16,24},{24,16},{1,9},{9,1},{17,25},{25,17},{2,10},{10... | collective-permute-start | bytes 4423688 | tf_op jit(solution)/shard_map/ppermute | solution.py:617
  106.0 18.0 %collective-permute-start.14 = (bf16[2,4,45,16,128]{4,3,2,1,0:T(8,128)(2,1)}, bf16[2,4,45,16,128]{4,3,2,1,0:T(8,128)(2,1)}, u32[]{:S(2)}, u32[]{:S(2)}) collective-permute-start(bf16[2,4,45,16,128]{4,3,2,1,0:T(8,128)(2,1)} %collective-permute-done.1.refs_4_), channel_id=1, source_target_pairs={{0,8},{8,0},{16,24},{24,16},{1,9},{9,1},{17,25},{25,17},{2,10},{10... | collective-permute-start | bytes 4423688 | tf_op jit(solution)/shard_map/ppermute | solution.py:617
  106.4 17.6 %collective-permute-start.13 = (bf16[2,4,45,16,128]{4,3,2,1,0:T(8,128)(2,1)}, bf16[2,4,45,16,128]{4,3,2,1,0:T(8,128)(2,1)}, u32[]{:S(2)}, u32[]{:S(2)}) collective-permute-start(bf16[2,4,45,16,128]{4,3,2,1,0:T(8,128)(2,1)} %get-tuple-element.65.refs_0_.refs_1_), channel_id=1, source_target_pairs={{0,8},{8,0},{16,24},{24,16},{1,9},{9,1},{17,25},{25,17},{2,10},{10... | collective-permute-start | bytes 4423688 | tf_op jit(solution)/shard_map/ppermute | solution.py:617
  106.5 17.5 %collective-permute-start.12 = (bf16[2,4,45,16,128]{4,3,2,1,0:T(8,128)(2,1)}, bf16[2,4,45,16,128]{4,3,2,1,0:T(8,128)(2,1)}, u32[]{:S(2)}, u32[]{:S(2)}) collective-permute-start(bf16[2,4,45,16,128]{4,3,2,1,0:T(8,128)(2,1)} %get-tuple-element.64.refs_0_), channel_id=1, source_target_pairs={{0,8},{8,0},{16,24},{24,16},{1,9},{9,1},{17,25},{25,17},{2,10},{10... | collective-permute-start | bytes 4423688 | tf_op jit(solution)/shard_map/ppermute | solution.py:617
  107.0 34.6 %collective-permute-start.22 = (bf16[2,4,45,16,128]{4,3,2,1,0:T(8,128)(2,1)}, bf16[2,4,45,16,128]{4,3,2,1,0:T(8,128)(2,1)}, u32[]{:S(2)}, u32[]{:S(2)}) collective-permute-start(bf16[2,4,45,16,128]{4,3,2,1,0:T(8,128)(2,1)} %outer_rows.3.refs_1_.refs_8_), channel_id=1, source_target_pairs={{0,16},{8,24},{16,0},{24,8},{1,17},{9,25},{17,1},{25,9},{2,18},{10... | collective-permute-start | bytes 4423688 | tf_op jit(solution)/shard_map/ppermute | solution.py:617
  124.1 7.0 %collective-permute-start.19 = (bf16[2,2,45,16,128]{4,3,2,1,0:T(8,128)(2,1)}, bf16[2,2,45,16,128]{4,3,2,1,0:T(8,128)(2,1)S(1)}, u32[]{:S(2)}, u32[]{:S(2)}) collective-permute-start(bf16[2,2,45,16,128]{4,3,2,1,0:T(8,128)(2,1)} %get-tuple-element.72.refs_2_.refs_4_), channel_id=1, source_target_pairs={{0,8},{8,0},{16,24},{24,16},{1,9},{9,1},{17,25},{25,17},{2,10},{10... | collective-permute-start | bytes 2211848 | tf_op jit(solution)/shard_map/ppermute | solution.py:617
  124.2 7.8 %collective-permute-start.18 = (bf16[2,2,45,16,128]{4,3,2,1,0:T(8,128)(2,1)S(1)}, bf16[2,2,45,16,128]{4,3,2,1,0:T(8,128)(2,1)}, u32[]{:S(2)}, u32[]{:S(2)}) collective-permute-start(bf16[2,2,45,16,128]{4,3,2,1,0:T(8,128)(2,1)S(1)} %copy-done.3), channel_id=1, source_target_pairs={{0,8},{8,0},{16,24},{24,16},{1,9},{9,1},{17,25},{25,17},{2,10},{10... | collective-permute-start | bytes 2211848 | tf_op jit(solution)/shard_map/ppermute | solution.py:617
  124.7 7.3 %collective-permute-start.17 = (bf16[1,4,45,16,128]{4,3,2,1,0:T(8,128)(2,1)}, bf16[1,4,45,16,128]{4,3,2,1,0:T(8,128)(2,1)}, u32[]{:S(2)}, u32[]{:S(2)}) collective-permute-start(bf16[1,4,45,16,128]{4,3,2,1,0:T(8,128)(2,1)} %collective-permute-done.2.refs_3_), channel_id=1, source_target_pairs={{0,8},{8,0},{16,24},{24,16},{1,9},{9,1},{17,25},{25,17},{2,10},{10... | collective-permute-start | bytes 2211848 | tf_op jit(solution)/shard_map/ppermute | solution.py:617
  124.7 7.2 %collective-permute-start.16 = (bf16[1,4,45,16,128]{4,3,2,1,0:T(8,128)(2,1)}, bf16[1,4,45,16,128]{4,3,2,1,0:T(8,128)(2,1)}, u32[]{:S(2)}, u32[]{:S(2)}) collective-permute-start(bf16[1,4,45,16,128]{4,3,2,1,0:T(8,128)(2,1)} %copy-done.5), channel_id=1, source_target_pairs={{0,8},{8,0},{16,24},{24,16},{1,9},{9,1},{17,25},{25,17},{2,10},{10... | collective-permute-start | bytes 2211848 | tf_op jit(solution)/shard_map/ppermute | solution.py:617
  131.1 16.1 %copy-start = (bf16[2,4,45,16,128]{4,3,2,1,0:T(8,128)(2,1)S(1)}, bf16[2,4,45,16,128]{4,3,2,1,0:T(8,128)(2,1)}, u32[]{:S(2)}) copy-start(bf16[2,4,45,16,128]{4,3,2,1,0:T(8,128)(2,1)} %outer_rows.3.refs_1_.refs_8_) | copy-start | bytes 4423684
  131.1 0.9 copy-start.7
  132.0 1.4 copy-start.2
  133.4 1.1 copy-start.6
  134.5 0.8 copy-start.9
  135.2 11.9 %copy-start.4 = (bf16[2,2,45,16,128]{4,3,2,1,0:T(8,128)(2,1)S(1)}, bf16[2,2,45,16,128]{4,3,2,1,0:T(8,128)(2,1)}, u32[]{:S(2)}) copy-start(bf16[2,2,45,16,128]{4,3,2,1,0:T(8,128)(2,1)} %get-tuple-element.72.refs_2_.refs_4_) | copy-start | bytes 2211844
  135.2 11.9 %copy-start.8 = (bf16[2,2,45,16,128]{4,3,2,1,0:T(8,128)(2,1)S(1)}, bf16[2,2,45,16,128]{4,3,2,1,0:T(8,128)(2,1)}, u32[]{:S(2)}) copy-start(bf16[2,2,45,16,128]{4,3,2,1,0:T(8,128)(2,1)} %copy-done.7) | copy-start | bytes 2211844
  141.5 5.6 %collective-permute-start.23 = (bf16[2,4,45,16,128]{4,3,2,1,0:T(8,128)(2,1)}, bf16[2,4,45,16,128]{4,3,2,1,0:T(8,128)(2,1)S(1)}, u32[]{:S(2)}, u32[]{:S(2)}) collective-permute-start(bf16[2,4,45,16,128]{4,3,2,1,0:T(8,128)(2,1)} %collective-permute-done.22.refs_9_), channel_id=1, source_target_pairs={{0,8},{8,0},{16,24},{24,16},{1,9},{9,1},{17,25},{25,17},{2,10},{10... | collective-permute-start | bytes 4423688 | tf_op jit(solution)/shard_map/ppermute | solution.py:617
  141.6 4.5 %collective-permute-start.21 = (bf16[2,2,45,16,128]{4,3,2,1,0:T(8,128)(2,1)}, bf16[2,2,45,16,128]{4,3,2,1,0:T(8,128)(2,1)S(1)}, u32[]{:S(2)}, u32[]{:S(2)}) collective-permute-start(bf16[2,2,45,16,128]{4,3,2,1,0:T(8,128)(2,1)} %collective-permute-done.11.refs_5_), channel_id=1, source_target_pairs={{0,8},{8,0},{16,24},{24,16},{1,9},{9,1},{17,25},{25,17},{2,10},{10... | collective-permute-start | bytes 2211848 | tf_op jit(solution)/shard_map/ppermute | solution.py:617
  142.1 5.1 %collective-permute-start.20 = (bf16[2,2,45,16,128]{4,3,2,1,0:T(8,128)(2,1)}, bf16[2,2,45,16,128]{4,3,2,1,0:T(8,128)(2,1)S(1)}, u32[]{:S(2)}, u32[]{:S(2)}) collective-permute-start(bf16[2,2,45,16,128]{4,3,2,1,0:T(8,128)(2,1)} %collective-permute-done.10.refs_1_), channel_id=1, source_target_pairs={{0,8},{8,0},{16,24},{24,16},{1,9},{9,1},{17,25},{25,17},{2,10},{10... | collective-permute-start | bytes 2211848 | tf_op jit(solution)/shard_map/ppermute | solution.py:617

commit v6 on v5

--- a/solution.py
+++ b/solution.py
@@ -386,8 +386,8 @@
         out_shape=jax.ShapeDtypeStruct((kept + members, 1, slots), bf16),
         scratch_shapes=[
             pltpu.VMEM((members, height, tiles, SUB, LANES), bf16),
-            pltpu.VMEM((height * tiles * SUB * members, LANES), f32),
-            pltpu.VMEM((slots * members, LANES), f32),
+            pltpu.VMEM((height * tiles * SUB * members + SUB, LANES), f32),
+            pltpu.VMEM((slots * members + SUB, LANES), f32),
             pltpu.SemaphoreType.DMA((len(pieces),)),
         ],
         compiler_params=pltpu.CompilerParams(vmem_limit_bytes=VMEM),

time: 153 us -> 153 us (level)
  no operation moved by 1% of the time
where the time goes in v6:
time: 153 us
  Pallas kernels  70.6 us (46%)
  waiting for transfers between devices  35.6 us (23%)
  starting transfers between devices  25.9 us (17%)
  blocking collectives  12.8 us (8%)
  local copies, waits for them, and re-layouts  4.16 us (3%)
  other arithmetic  2.63 us (2%)
    pallas_call x2, Pallas kernels, outer(): pl.pallas_call(functools.partial(outer_body, cut=cut, width=width, length...  18.3 us
    ppermute x2, waiting for transfers between devices, halo(): lax.ppermute(last, 'band', forward)  18.1 us
    ppermute x20, waiting for transfers between devices, swap(): return lax.ppermute(block, 'member', [(i, i ^ bit) for i in range(size)])  17.4 us
    pallas_call x2, Pallas kernels, gather(): pl.pallas_call(functools.partial(gather_body, pieces=pieces, kept=kept),...  14 us
    ppermute x20, starting transfers between devices, swap(): return lax.ppermute(block, 'member', [(i, i ^ bit) for i in range(size)])  13.7 us
    all_to_all x1, blocking collectives, local(): terms = lax.all_to_all(terms, 'band', 0, 0, tiled=True)  12.8 us
    pallas_call x2, Pallas kernels, mix(): pl.pallas_call(functools.partial(mix_body, sources=sources, kept=int(kept...  11.5 us
    ppermute x2, starting transfers between devices, halo(): lax.ppermute(last, 'band', forward)  9.49 us
  transfers between devices with their start and end apart: 24, of which 8 were waited for; matrix products, arithmetic and copies ran while one was open for 2% of the time, Pallas kernels for 39%

profile of v6, /device:TPU:0, one launch (start us, length us, event | category | flops | bytes accessed | tf_op | source)
XLA Modules:
  0.0 152.7 jit_solution(15075360246034418008)
XLA Ops:
  0.0 6.1 %opening_rows.1 = (bf16[1,4,45,16,128]{4,3,2,1,0:T(8,128)(2,1)}, bf16[2,2,45,16,128]{4,3,2,1,0:T(8,128)(2,1)}, bf16[2,2,45,16,128]{4,3,2,1,0:T(8,128)(2,1)}, bf16[128,768]{1,0:T(8,128)(2,1)}, f32[128,128]{1,0:T(8,128)}) custom-call(bf16[4,8,64,1440]{3,2,1,0:T(8,128)(2,1)} %x.6, bf16[4,8,64,1440]{3,2,1,0:T(8,128)(2,1)} %x.6, bf16[4,8,64,1440]{3,2,1,0:T(8,128)(2,1)} %x.6, ...), custom_call_target="tpu_custom_call" | custom-call | flops 200000000 | bytes 500000 | tf_op jit(solution)/shard_map/opening_rows/pallas_call | solution.py:195
  6.1 3.0 %collective-permute-start = (bf16[1,4,45,16,128]{4,3,2,1,0:T(8,128)(2,1)}, bf16[1,4,45,16,128]{4,3,2,1,0:T(8,128)(2,1)S(1)}, u32[]{:S(2)}, u32[]{:S(2)}) collective-permute-start(bf16[1,4,45,16,128]{4,3,2,1,0:T(8,128)(2,1)} %get-tuple-element.41.inner0), channel_id=1, source_target_pairs={{0,16},{8,24},{16,0},{24,8},{1,17},{9,25},{17,1},{25,9},{2,18},{10... | collective-permute-start | bytes 2211848 | tf_op jit(solution)/shard_map/ppermute | solution.py:617
  9.1 4.3 %collective-permute-start.3 = (bf16[2,2,45,16,128]{4,3,2,1,0:T(8,128)(2,1)}, bf16[2,2,45,16,128]{4,3,2,1,0:T(8,128)(2,1)}, u32[]{:S(2)}, u32[]{:S(2)}) collective-permute-start(bf16[2,2,45,16,128]{4,3,2,1,0:T(8,128)(2,1)} %get-tuple-element.51), channel_id=1, source_target_pairs={{0,1},{1,2},{2,3},{3,4},{4,5},{5,6},{6,7},{8,9},{9,10},{10,11},{11... | collective-permute-start | bytes 2211848 | tf_op jit(solution)/shard_map/ppermute | solution.py:612
  13.3 1.3 collective-permute-start.4
  14.6 5.6 %second_rows.1 = (bf16[1,4,45,16,128]{4,3,2,1,0:T(8,128)(2,1)}, bf16[2,4,45,16,128]{4,3,2,1,0:T(8,128)(2,1)}) custom-call(bf16[4,8,64,1440]{3,2,1,0:T(8,128)(2,1)} %x.6, bf16[128,768]{1,0:T(8,128)(2,1)} %get-tuple-element.43.weights, f32[128,128]{1,0:T(8,128)} %get-tuple-element.44.bias, bf16[1,4,45,16,128]{4,3,2,1,0:T(8,128)(2,1)} %get-tuple-element.41.inner0), custom_call_target="tpu_custom_call" | custom-call | flops 200000000 | bytes 500000 | tf_op jit(solution)/shard_map/second_rows/pallas_call | solution.py:226
  20.3 0.5 collective-permute-start.2
  20.8 7.3 %inner_rows.1 = (bf16[2,4,45,16,128]{4,3,2,1,0:T(8,128)(2,1)}, bf16[2,2,45,16,128]{4,3,2,1,0:T(8,128)(2,1)}, bf16[2,2,45,16,128]{4,3,2,1,0:T(8,128)(2,1)}) custom-call(bf16[4,8,64,1440]{3,2,1,0:T(8,128)(2,1)} %x.6, bf16[128,768]{1,0:T(8,128)(2,1)} %get-tuple-element.43.weights, f32[128,128]{1,0:T(8,128)} %get-tuple-element.44.bias), custom_call_target="tpu_custom_call" | custom-call | flops 200000000 | bytes 500000 | tf_op jit(solution)/shard_map/inner_rows/pallas_call | solution.py:247
  28.1 1.5 collective-permute-start.1
  29.6 0.6 add_convert_fusion.ends
  30.2 0.6 fusion.6
  30.9 0.0 collective-permute-done.refs_2_
  30.9 13.2 %collective-permute-done.3.low = bf16[2,2,45,16,128]{4,3,2,1,0:T(8,128)(2,1)} collective-permute-done((bf16[2,2,45,16,128]{4,3,2,1,0:T(8,128)(2,1)}, bf16[2,2,45,16,128]{4,3,2,1,0:T(8,128)(2,1)}, u32[]{:S(2)}, u32[]{:S(2)}) %collective-permute-start.3) | collective-permute-done | bytes 737312 | tf_op jit(solution)/shard_map/ppermute | solution.py:612
  44.0 0.0 collective-permute-done.4.high
  44.1 5.2 %collective-permute-start.5 = (bf16[2,2,45,16,128]{4,3,2,1,0:T(8,128)(2,1)}, bf16[2,2,45,16,128]{4,3,2,1,0:T(8,128)(2,1)}, u32[]{:S(2)}, u32[]{:S(2)}) collective-permute-start(bf16[2,2,45,16,128]{4,3,2,1,0:T(8,128)(2,1)} %get-tuple-element.58), channel_id=1, source_target_pairs={{0,1},{1,2},{2,3},{3,4},{4,5},{5,6},{6,7},{8,9},{9,10},{10,11},{11... | collective-permute-start | bytes 2211848 | tf_op jit(solution)/shard_map/ppermute | solution.py:612
  49.3 1.5 collective-permute-start.6
  50.8 1.3 fusion.chosen
  52.1 0.0 collective-permute-done.2.refs_3_
  52.1 9.1 %outer_rows.2 = (bf16[2,2,45,16,128]{4,3,2,1,0:T(8,128)(2,1)}, bf16[2,2,45,16,128]{4,3,2,1,0:T(8,128)(2,1)}) custom-call(s32[2]{0:T(128)} %add_convert_fusion.ends, bf16[4,8,64,1440]{3,2,1,0:T(8,128)(2,1)} %x.6, bf16[2,2,45,16,128]{4,3,2,1,0:T(8,128)(2,1)} %collective-permute-done.3.low, bf16[2,2,45,16,128]{4,3,2,1,0:T(8,128)(2,1)} %collective-permute-done.4.high, ...), custom_call_target="tpu_custom_call" | custom-call | flops 200000000 | bytes 500000 | tf_op jit(solution)/shard_map/outer_rows/pallas_call | solution.py:301
  61.2 0.6 collective-permute-start.10
  61.8 1.5 collective-permute-start.11
  63.3 6.9 %gather_cells.2.refs_2_ = bf16[2,1,2048]{2,1,0:T(2,128)(2,1)} custom-call(s32[2048]{0:T(1024)} %get-tuple-element.78.rows, f32[2048,128]{1,0:T(8,128)} %fusion.chosen, bf16[2,4,45,16,128]{4,3,2,1,0:T(8,128)(2,1)} %get-tuple-element.64.refs_0_, bf16[2,2,45,16,128]{4,3,2,1,0:T(8,128)(2,1)} %get-tuple-element.71.refs_1_.refs_0_, ...), custom_call_target="tpu_custom_call" | custom-call | flops 200000000 | bytes 500000 | tf_op jit(solution)/shard_map/gather_cells/pallas_call | solution.py:377
  70.2 3.9 %collective-permute-done.1.refs_4_ = bf16[2,4,45,16,128]{4,3,2,1,0:T(8,128)(2,1)} collective-permute-done((bf16[2,4,45,16,128]{4,3,2,1,0:T(8,128)(2,1)}, bf16[2,4,45,16,128]{4,3,2,1,0:T(8,128)(2,1)}, u32[]{:S(2)}, u32[]{:S(2)}) %collective-permute-start.1) | collective-permute-done | bytes 1474592 | tf_op jit(solution)/shard_map/ppermute | solution.py:617
  74.1 5.0 %collective-permute-done.5.low = bf16[2,2,45,16,128]{4,3,2,1,0:T(8,128)(2,1)} collective-permute-done((bf16[2,2,45,16,128]{4,3,2,1,0:T(8,128)(2,1)}, bf16[2,2,45,16,128]{4,3,2,1,0:T(8,128)(2,1)}, u32[]{:S(2)}, u32[]{:S(2)}) %collective-permute-start.5) | collective-permute-done | bytes 737312 | tf_op jit(solution)/shard_map/ppermute | solution.py:612
  79.1 0.0 collective-permute-done.6.high
  79.1 9.2 %outer_rows.3.refs_1_.refs_8_ = bf16[2,4,45,16,128]{4,3,2,1,0:T(8,128)(2,1)} custom-call(s32[2]{0:T(128)} %add_convert_fusion.ends, bf16[4,8,64,1440]{3,2,1,0:T(8,128)(2,1)} %x.6, bf16[2,2,45,16,128]{4,3,2,1,0:T(8,128)(2,1)} %collective-permute-done.5.low, bf16[2,2,45,16,128]{4,3,2,1,0:T(8,128)(2,1)} %collective-permute-done.6.high, ...), custom_call_target="tpu_custom_call" | custom-call | flops 200000000 | bytes 500000 | tf_op jit(solution)/shard_map/outer_rows/pallas_call | solution.py:301
  88.3 7.1 %gather_cells.3.refs_0_ = bf16[4,1,2048]{2,1,0:T(2,128)(2,1)} custom-call(s32[2048]{0:T(1024)} %get-tuple-element.78.rows, f32[2048,128]{1,0:T(8,128)} %fusion.chosen, bf16[2,4,45,16,128]{4,3,2,1,0:T(8,128)(2,1)} %get-tuple-element.65.refs_0_.refs_1_, bf16[2,4,45,16,128]{4,3,2,1,0:T(8,128)(2,1)} %outer_rows.3.refs_1_.refs_8_, ...), custom_call_target="tpu_custom_call" | custom-call | flops 200000000 | bytes 500000 | tf_op jit(solution)/shard_map/gather_cells/pallas_call | solution.py:377
  95.4 0.6 collective-permute-start.7
  95.9 0.0 collective-permute-start.8
  96.0 1.6 %collective-permute-start.9 = (bf16[4,1,2048]{2,1,0:T(2,128)(2,1)}, bf16[4,1,2048]{2,1,0:T(2,128)(2,1)S(1)}, u32[]{:S(2)}, u32[]{:S(2)}) collective-permute-start(bf16[4,1,2048]{2,1,0:T(2,128)(2,1)} %gather_cells.3.refs_0_), channel_id=1, source_target_pairs={{0,24},{8,16},{16,8},{24,0},{1,25},{9,17},{17,9},{25,1},{2,26},{10... | collective-permute-start | bytes 49160 | tf_op jit(solution)/shard_map/ppermute | solution.py:617
  97.6 0.0 collective-permute-done.10.refs_1_
  97.6 8.0 %collective-permute-done.11.refs_5_ = bf16[2,2,45,16,128]{4,3,2,1,0:T(8,128)(2,1)} collective-permute-done((bf16[2,2,45,16,128]{4,3,2,1,0:T(8,128)(2,1)}, bf16[2,2,45,16,128]{4,3,2,1,0:T(8,128)(2,1)}, u32[]{:S(2)}, u32[]{:S(2)}) %collective-permute-start.11) | collective-permute-done | bytes 737312 | tf_op jit(solution)/shard_map/ppermute | solution.py:617
  105.6 0.2 collective-permute-done.7.refs_1_
  105.9 0.1 collective-permute-start.15
  106.0 0.4 collective-permute-start.14
  106.4 0.1 collective-permute-start.13
  106.5 0.4 collective-permute-start.12
  107.0 1.7 %collective-permute-start.22 = (bf16[2,4,45,16,128]{4,3,2,1,0:T(8,128)(2,1)}, bf16[2,4,45,16,128]{4,3,2,1,0:T(8,128)(2,1)}, u32[]{:S(2)}, u32[]{:S(2)}) collective-permute-start(bf16[2,4,45,16,128]{4,3,2,1,0:T(8,128)(2,1)} %outer_rows.3.refs_1_.refs_8_), channel_id=1, source_target_pairs={{0,16},{8,24},{16,0},{24,8},{1,17},{9,25},{17,1},{25,9},{2,18},{10... | collective-permute-start | bytes 4423688 | tf_op jit(solution)/shard_map/ppermute | solution.py:617
  109.4 1.9 %band_terms.1 = f32[8,1,2048]{2,1,0:T(1,128)} custom-call(s32[1]{0:T(128)S(6)} %copy.10.live, f32[1,2048]{1,0:T(1,128)} %bitcast.6, f32[1,2048]{1,0:T(1,128)} %bitcast.7, bf16[4,1,2048]{2,1,0:T(2,128)(2,1)} %gather_cells.3.refs_0_, bf16[4,1,2048]{2,1,0:T(2,128)(2,1)} %copy-done.11, bf16[4,1,2048]{2,1,0:T(2,128)(2,1)} %copy-done.12, ...), custom_call_target="tpu_custom_call" | custom-call | flops 200000000 | bytes 500000 | tf_op jit(solution)/shard_map/band_terms/pallas_call | solution.py:530
  111.2 12.8 %all_to_all.5.terms = f32[8,1,2048]{2,1,0:T(1,128)} all-to-all(f32[8,1,2048]{2,1,0:T(1,128)} %band_terms.1), channel_id=1, replica_groups=mesh['member'=4,'band'=8] {'band'}, dimensions={0} | all-to-all | bytes 131072 | tf_op jit(solution)/shard_map/all_to_all | solution.py:680
  124.1 0.0 collective-permute-done.15.refs_10_
  124.1 0.0 collective-permute-done.14.refs_9_
  124.1 0.1 collective-permute-start.19
  124.2 0.5 collective-permute-start.18
  124.7 0.1 collective-permute-start.17
  124.7 0.4 collective-permute-start.16
  125.2 5.9 %transform.1.weights = bf16[64,256]{1,0:T(8,128)(2,1)} custom-call(f32[8,1,2048]{2,1,0:T(1,128)} %all_to_all.5.terms), custom_call_target="tpu_custom_call" | custom-call | flops 200000000 | bytes 500000 | tf_op jit(solution)/shard_map/transform/pallas_call | solution.py:594
  131.1 0.0 collective-permute-done.19.refs_6_
  131.1 0.9 copy-done.7
  132.0 0.0 collective-permute-done.18.refs_2_
  132.0 0.0 collective-permute-done.17.refs_8_
  132.0 0.0 collective-permute-done.16.refs_7_
  132.0 0.0 copy-start.2
  132.0 1.4 copy-done.2
  133.4 1.1 copy-done.6
  134.5 0.8 copy-done.9
  135.2 6.1 %mix_rows.2.refs_12_ = bf16[4,8,64,1440]{3,2,1,0:T(8,128)(2,1)} custom-call(bf16[64,256]{1,0:T(8,128)(2,1)S(1)} %copy-done.9, bf16[2,4,45,16,128]{4,3,2,1,0:T(8,128)(2,1)S(1)} %copy-done.1, bf16[2,4,45,16,128]{4,3,2,1,0:T(8,128)(2,1)S(1)} %copy-done.2, bf16[1,4,45,16,128]{4,3,2,1,0:T(8,128)(2,1)S(1)} %copy-done.6, ...), custom_call_target="tpu_custom_call" | custom-call | flops 200000000 | bytes 500000 | tf_op jit(solution)/shard_map/mix_rows/pallas_call | solution.py:486
  141.4 0.2 collective-permute-done.22.refs_9_
  141.5 0.0 collective-permute-start.23
  141.6 0.5 collective-permute-start.21
  142.1 0.0 collective-permute-start.20
  142.1 4.0 %collective-permute-done.21.refs_7_ = bf16[2,2,45,16,128]{4,3,2,1,0:T(8,128)(2,1)S(1)} collective-permute-done((bf16[2,2,45,16,128]{4,3,2,1,0:T(8,128)(2,1)}, bf16[2,2,45,16,128]{4,3,2,1,0:T(8,128)(2,1)S(1)}, u32[]{:S(2)}, u32[]{:S(2)}) %collective-permute-start.21) | collective-permute-done | bytes 737312 | tf_op jit(solution)/shard_map/ppermute | solution.py:617
  146.1 1.1 collective-permute-done.20.refs_3_
  147.1 0.0 collective-permute-done.23.refs_11_
  147.2 5.4 %mix_rows.3 = bf16[4,8,64,1440]{3,2,1,0:T(8,128)(2,1)} custom-call(bf16[64,256]{1,0:T(8,128)(2,1)S(1)} %copy-done.9, bf16[2,2,45,16,128]{4,3,2,1,0:T(8,128)(2,1)S(1)} %copy-done.3, bf16[2,2,45,16,128]{4,3,2,1,0:T(8,128)(2,1)} %collective-permute-done.10.refs_1_, ...), custom_call_target="tpu_custom_call", output_to_operand_aliasing={{}: (13, {})} | custom-call | flops 200000000 | bytes 500000 | tf_op jit(solution)/shard_map/mix_rows/pallas_call | solution.py:486
  (27 shorter events, 0.1 us)
Async XLA Ops:
  6.1 24.8 %collective-permute-start = (bf16[1,4,45,16,128]{4,3,2,1,0:T(8,128)(2,1)}, bf16[1,4,45,16,128]{4,3,2,1,0:T(8,128)(2,1)S(1)}, u32[]{:S(2)}, u32[]{:S(2)}) collective-permute-start(bf16[1,4,45,16,128]{4,3,2,1,0:T(8,128)(2,1)} %get-tuple-element.41.inner0), channel_id=1, source_target_pairs={{0,16},{8,24},{16,0},{24,8},{1,17},{9,25},{17,1},{25,9},{2,18},{10... | collective-permute-start | bytes 2211848 | tf_op jit(solution)/shard_map/ppermute | solution.py:617
  9.1 35.0 %collective-permute-start.3 = (bf16[2,2,45,16,128]{4,3,2,1,0:T(8,128)(2,1)}, bf16[2,2,45,16,128]{4,3,2,1,0:T(8,128)(2,1)}, u32[]{:S(2)}, u32[]{:S(2)}) collective-permute-start(bf16[2,2,45,16,128]{4,3,2,1,0:T(8,128)(2,1)} %get-tuple-element.51), channel_id=1, source_target_pairs={{0,1},{1,2},{2,3},{3,4},{4,5},{5,6},{6,7},{8,9},{9,10},{10,11},{11... | collective-permute-start | bytes 2211848 | tf_op jit(solution)/shard_map/ppermute | solution.py:612
  13.3 30.7 %collective-permute-start.4 = (bf16[2,2,45,16,128]{4,3,2,1,0:T(8,128)(2,1)}, bf16[2,2,45,16,128]{4,3,2,1,0:T(8,128)(2,1)}, u32[]{:S(2)}, u32[]{:S(2)}) collective-permute-start(bf16[2,2,45,16,128]{4,3,2,1,0:T(8,128)(2,1)} %get-tuple-element.52), channel_id=1, source_target_pairs={{1,0},{2,1},{3,2},{4,3},{5,4},{6,5},{7,6},{9,8},{10,9},{11,10},{12... | collective-permute-start | bytes 2211848 | tf_op jit(solution)/shard_map/ppermute | solution.py:612
  20.3 10.0 %copy-start.10 = (s32[2048]{0:T(1024)S(1)}, s32[2048]{0:T(1024)}, u32[]{:S(2)}) copy-start(s32[2048]{0:T(1024)} %param.10) | copy-start | bytes 24580
  20.3 31.8 %collective-permute-start.2 = (bf16[1,4,45,16,128]{4,3,2,1,0:T(8,128)(2,1)}, bf16[1,4,45,16,128]{4,3,2,1,0:T(8,128)(2,1)}, u32[]{:S(2)}, u32[]{:S(2)}) collective-permute-start(bf16[1,4,45,16,128]{4,3,2,1,0:T(8,128)(2,1)} %get-tuple-element.45), channel_id=1, source_target_pairs={{0,16},{8,24},{16,0},{24,8},{1,17},{9,25},{17,1},{25,9},{2,18},{10... | collective-permute-start | bytes 2211848 | tf_op jit(solution)/shard_map/ppermute | solution.py:617
  28.1 46.1 %collective-permute-start.1 = (bf16[2,4,45,16,128]{4,3,2,1,0:T(8,128)(2,1)}, bf16[2,4,45,16,128]{4,3,2,1,0:T(8,128)(2,1)}, u32[]{:S(2)}, u32[]{:S(2)}) collective-permute-start(bf16[2,4,45,16,128]{4,3,2,1,0:T(8,128)(2,1)} %get-tuple-element.65.refs_0_.refs_1_), channel_id=1, source_target_pairs={{0,16},{8,24},{16,0},{24,8},{1,17},{9,25},{17,1},{25,9},{2,18},{10... | collective-permute-start | bytes 4423688 | tf_op jit(solution)/shard_map/ppermute | solution.py:617
  30.9 30.4 %copy-start.5 = (bf16[1,4,45,16,128]{4,3,2,1,0:T(8,128)(2,1)}, bf16[1,4,45,16,128]{4,3,2,1,0:T(8,128)(2,1)S(1)}, u32[]{:S(2)}) copy-start(bf16[1,4,45,16,128]{4,3,2,1,0:T(8,128)(2,1)S(1)} %collective-permute-done.refs_2_) | copy-start | bytes 2211844
  44.1 35.0 %collective-permute-start.5 = (bf16[2,2,45,16,128]{4,3,2,1,0:T(8,128)(2,1)}, bf16[2,2,45,16,128]{4,3,2,1,0:T(8,128)(2,1)}, u32[]{:S(2)}, u32[]{:S(2)}) collective-permute-start(bf16[2,2,45,16,128]{4,3,2,1,0:T(8,128)(2,1)} %get-tuple-element.58), channel_id=1, source_target_pairs={{0,1},{1,2},{2,3},{3,4},{4,5},{5,6},{6,7},{8,9},{9,10},{10,11},{11... | collective-permute-start | bytes 2211848 | tf_op jit(solution)/shard_map/ppermute | solution.py:612
  49.3 29.8 %collective-permute-start.6 = (bf16[2,2,45,16,128]{4,3,2,1,0:T(8,128)(2,1)}, bf16[2,2,45,16,128]{4,3,2,1,0:T(8,128)(2,1)}, u32[]{:S(2)}, u32[]{:S(2)}) collective-permute-start(bf16[2,2,45,16,128]{4,3,2,1,0:T(8,128)(2,1)} %get-tuple-element.59), channel_id=1, source_target_pairs={{1,0},{2,1},{3,2},{4,3},{5,4},{6,5},{7,6},{9,8},{10,9},{11,10},{12... | collective-permute-start | bytes 2211848 | tf_op jit(solution)/shard_map/ppermute | solution.py:612
  61.2 36.3 %collective-permute-start.10 = (bf16[2,2,45,16,128]{4,3,2,1,0:T(8,128)(2,1)}, bf16[2,2,45,16,128]{4,3,2,1,0:T(8,128)(2,1)}, u32[]{:S(2)}, u32[]{:S(2)}) collective-permute-start(bf16[2,2,45,16,128]{4,3,2,1,0:T(8,128)(2,1)} %get-tuple-element.71.refs_1_.refs_0_), channel_id=1, source_target_pairs={{0,16},{8,24},{16,0},{24,8},{1,17},{9,25},{17,1},{25,9},{2,18},{10... | collective-permute-start | bytes 2211848 | tf_op jit(solution)/shard_map/ppermute | solution.py:617
  61.8 43.8 %collective-permute-start.11 = (bf16[2,2,45,16,128]{4,3,2,1,0:T(8,128)(2,1)}, bf16[2,2,45,16,128]{4,3,2,1,0:T(8,128)(2,1)}, u32[]{:S(2)}, u32[]{:S(2)}) collective-permute-start(bf16[2,2,45,16,128]{4,3,2,1,0:T(8,128)(2,1)} %get-tuple-element.72.refs_2_.refs_4_), channel_id=1, source_target_pairs={{0,16},{8,24},{16,0},{24,8},{1,17},{9,25},{17,1},{25,9},{2,18},{10... | collective-permute-start | bytes 2211848 | tf_op jit(solution)/shard_map/ppermute | solution.py:617
  88.3 35.9 %copy-start.3 = (bf16[2,2,45,16,128]{4,3,2,1,0:T(8,128)(2,1)S(1)}, bf16[2,2,45,16,128]{4,3,2,1,0:T(8,128)(2,1)}, u32[]{:S(2)}) copy-start(bf16[2,2,45,16,128]{4,3,2,1,0:T(8,128)(2,1)} %get-tuple-element.71.refs_1_.refs_0_) | copy-start | bytes 2211844
  95.4 36.6 %copy-start.1 = (bf16[2,4,45,16,128]{4,3,2,1,0:T(8,128)(2,1)S(1)}, bf16[2,4,45,16,128]{4,3,2,1,0:T(8,128)(2,1)}, u32[]{:S(2)}) copy-start(bf16[2,4,45,16,128]{4,3,2,1,0:T(8,128)(2,1)} %get-tuple-element.64.refs_0_) | copy-start | bytes 4423684
  95.4 10.5 %collective-permute-start.7 = (bf16[4,1,2048]{2,1,0:T(2,128)(2,1)}, bf16[4,1,2048]{2,1,0:T(2,128)(2,1)S(1)}, u32[]{:S(2)}, u32[]{:S(2)}) collective-permute-start(bf16[4,1,2048]{2,1,0:T(2,128)(2,1)} %gather_cells.3.refs_0_), channel_id=1, source_target_pairs={{0,16},{8,24},{16,0},{24,8},{1,17},{9,25},{17,1},{25,9},{2,18},{10... | collective-permute-start | bytes 49160 | tf_op jit(solution)/shard_map/ppermute | solution.py:617
  95.9 9.9 %collective-permute-start.8 = (bf16[4,1,2048]{2,1,0:T(2,128)(2,1)}, bf16[4,1,2048]{2,1,0:T(2,128)(2,1)S(1)}, u32[]{:S(2)}, u32[]{:S(2)}) collective-permute-start(bf16[4,1,2048]{2,1,0:T(2,128)(2,1)} %gather_cells.3.refs_0_), channel_id=1, source_target_pairs={{0,8},{8,0},{16,24},{24,16},{1,9},{9,1},{17,25},{25,17},{2,10},{10... | collective-permute-start | bytes 49160 | tf_op jit(solution)/shard_map/ppermute | solution.py:617
  96.0 9.9 %collective-permute-start.9 = (bf16[4,1,2048]{2,1,0:T(2,128)(2,1)}, bf16[4,1,2048]{2,1,0:T(2,128)(2,1)S(1)}, u32[]{:S(2)}, u32[]{:S(2)}) collective-permute-start(bf16[4,1,2048]{2,1,0:T(2,128)(2,1)} %gather_cells.3.refs_0_), channel_id=1, source_target_pairs={{0,24},{8,16},{16,8},{24,0},{1,25},{9,17},{17,9},{25,1},{2,26},{10... | collective-permute-start | bytes 49160 | tf_op jit(solution)/shard_map/ppermute | solution.py:617
  105.8 3.5 %copy-start.11 = (bf16[4,1,2048]{2,1,0:T(2,128)(2,1)}, bf16[4,1,2048]{2,1,0:T(2,128)(2,1)S(1)}, u32[]{:S(2)}) copy-start(bf16[4,1,2048]{2,1,0:T(2,128)(2,1)S(1)} %collective-permute-done.7.refs_1_) | copy-start | bytes 49156
  105.8 3.5 %copy-start.12 = (bf16[4,1,2048]{2,1,0:T(2,128)(2,1)}, bf16[4,1,2048]{2,1,0:T(2,128)(2,1)S(1)}, u32[]{:S(2)}) copy-start(bf16[4,1,2048]{2,1,0:T(2,128)(2,1)S(1)} %collective-permute-done.8.refs_2_) | copy-start | bytes 49156
  105.9 3.5 %copy-start.13 = (bf16[4,1,2048]{2,1,0:T(2,128)(2,1)}, bf16[4,1,2048]{2,1,0:T(2,128)(2,1)S(1)}, u32[]{:S(2)}) copy-start(bf16[4,1,2048]{2,1,0:T(2,128)(2,1)S(1)} %collective-permute-done.9.refs_3_) | copy-start | bytes 49156
  105.9 18.2 %collective-permute-start.15 = (bf16[2,4,45,16,128]{4,3,2,1,0:T(8,128)(2,1)}, bf16[2,4,45,16,128]{4,3,2,1,0:T(8,128)(2,1)}, u32[]{:S(2)}, u32[]{:S(2)}) collective-permute-start(bf16[2,4,45,16,128]{4,3,2,1,0:T(8,128)(2,1)} %outer_rows.3.refs_1_.refs_8_), channel_id=1, source_target_pairs={{0,8},{8,0},{16,24},{24,16},{1,9},{9,1},{17,25},{25,17},{2,10},{10... | collective-permute-start | bytes 4423688 | tf_op jit(solution)/shard_map/ppermute | solution.py:617
  106.0 18.0 %collective-permute-start.14 = (bf16[2,4,45,16,128]{4,3,2,1,0:T(8,128)(2,1)}, bf16[2,4,45,16,128]{4,3,2,1,0:T(8,128)(2,1)}, u32[]{:S(2)}, u32[]{:S(2)}) collective-permute-start(bf16[2,4,45,16,128]{4,3,2,1,0:T(8,128)(2,1)} %collective-permute-done.1.refs_4_), channel_id=1, source_target_pairs={{0,8},{8,0},{16,24},{24,16},{1,9},{9,1},{17,25},{25,17},{2,10},{10... | collective-permute-start | bytes 4423688 | tf_op jit(solution)/shard_map/ppermute | solution.py:617
  106.4 17.6 %collective-permute-start.13 = (bf16[2,4,45,16,128]{4,3,2,1,0:T(8,128)(2,1)}, bf16[2,4,45,16,128]{4,3,2,1,0:T(8,128)(2,1)}, u32[]{:S(2)}, u32[]{:S(2)}) collective-permute-start(bf16[2,4,45,16,128]{4,3,2,1,0:T(8,128)(2,1)} %get-tuple-element.65.refs_0_.refs_1_), channel_id=1, source_target_pairs={{0,8},{8,0},{16,24},{24,16},{1,9},{9,1},{17,25},{25,17},{2,10},{10... | collective-permute-start | bytes 4423688 | tf_op jit(solution)/shard_map/ppermute | solution.py:617
  106.5 17.5 %collective-permute-start.12 = (bf16[2,4,45,16,128]{4,3,2,1,0:T(8,128)(2,1)}, bf16[2,4,45,16,128]{4,3,2,1,0:T(8,128)(2,1)}, u32[]{:S(2)}, u32[]{:S(2)}) collective-permute-start(bf16[2,4,45,16,128]{4,3,2,1,0:T(8,128)(2,1)} %get-tuple-element.64.refs_0_), channel_id=1, source_target_pairs={{0,8},{8,0},{16,24},{24,16},{1,9},{9,1},{17,25},{25,17},{2,10},{10... | collective-permute-start | bytes 4423688 | tf_op jit(solution)/shard_map/ppermute | solution.py:617
  107.0 34.6 %collective-permute-start.22 = (bf16[2,4,45,16,128]{4,3,2,1,0:T(8,128)(2,1)}, bf16[2,4,45,16,128]{4,3,2,1,0:T(8,128)(2,1)}, u32[]{:S(2)}, u32[]{:S(2)}) collective-permute-start(bf16[2,4,45,16,128]{4,3,2,1,0:T(8,128)(2,1)} %outer_rows.3.refs_1_.refs_8_), channel_id=1, source_target_pairs={{0,16},{8,24},{16,0},{24,8},{1,17},{9,25},{17,1},{25,9},{2,18},{10... | collective-permute-start | bytes 4423688 | tf_op jit(solution)/shard_map/ppermute | solution.py:617
  124.1 7.0 %collective-permute-start.19 = (bf16[2,2,45,16,128]{4,3,2,1,0:T(8,128)(2,1)}, bf16[2,2,45,16,128]{4,3,2,1,0:T(8,128)(2,1)S(1)}, u32[]{:S(2)}, u32[]{:S(2)}) collective-permute-start(bf16[2,2,45,16,128]{4,3,2,1,0:T(8,128)(2,1)} %get-tuple-element.72.refs_2_.refs_4_), channel_id=1, source_target_pairs={{0,8},{8,0},{16,24},{24,16},{1,9},{9,1},{17,25},{25,17},{2,10},{10... | collective-permute-start | bytes 2211848 | tf_op jit(solution)/shard_map/ppermute | solution.py:617
  124.2 7.8 %collective-permute-start.18 = (bf16[2,2,45,16,128]{4,3,2,1,0:T(8,128)(2,1)S(1)}, bf16[2,2,45,16,128]{4,3,2,1,0:T(8,128)(2,1)}, u32[]{:S(2)}, u32[]{:S(2)}) collective-permute-start(bf16[2,2,45,16,128]{4,3,2,1,0:T(8,128)(2,1)S(1)} %copy-done.3), channel_id=1, source_target_pairs={{0,8},{8,0},{16,24},{24,16},{1,9},{9,1},{17,25},{25,17},{2,10},{10... | collective-permute-start | bytes 2211848 | tf_op jit(solution)/shard_map/ppermute | solution.py:617
  124.7 7.3 %collective-permute-start.17 = (bf16[1,4,45,16,128]{4,3,2,1,0:T(8,128)(2,1)}, bf16[1,4,45,16,128]{4,3,2,1,0:T(8,128)(2,1)}, u32[]{:S(2)}, u32[]{:S(2)}) collective-permute-start(bf16[1,4,45,16,128]{4,3,2,1,0:T(8,128)(2,1)} %collective-permute-done.2.refs_3_), channel_id=1, source_target_pairs={{0,8},{8,0},{16,24},{24,16},{1,9},{9,1},{17,25},{25,17},{2,10},{10... | collective-permute-start | bytes 2211848 | tf_op jit(solution)/shard_map/ppermute | solution.py:617
  124.7 7.2 %collective-permute-start.16 = (bf16[1,4,45,16,128]{4,3,2,1,0:T(8,128)(2,1)}, bf16[1,4,45,16,128]{4,3,2,1,0:T(8,128)(2,1)}, u32[]{:S(2)}, u32[]{:S(2)}) collective-permute-start(bf16[1,4,45,16,128]{4,3,2,1,0:T(8,128)(2,1)} %copy-done.5), channel_id=1, source_target_pairs={{0,8},{8,0},{16,24},{24,16},{1,9},{9,1},{17,25},{25,17},{2,10},{10... | collective-permute-start | bytes 2211848 | tf_op jit(solution)/shard_map/ppermute | solution.py:617
  131.1 16.1 %copy-start = (bf16[2,4,45,16,128]{4,3,2,1,0:T(8,128)(2,1)S(1)}, bf16[2,4,45,16,128]{4,3,2,1,0:T(8,128)(2,1)}, u32[]{:S(2)}) copy-start(bf16[2,4,45,16,128]{4,3,2,1,0:T(8,128)(2,1)} %outer_rows.3.refs_1_.refs_8_) | copy-start | bytes 4423684
  131.1 0.9 copy-start.7
  132.0 1.4 copy-start.2
  133.4 1.1 copy-start.6
  134.5 0.8 copy-start.9
  135.2 11.9 %copy-start.4 = (bf16[2,2,45,16,128]{4,3,2,1,0:T(8,128)(2,1)S(1)}, bf16[2,2,45,16,128]{4,3,2,1,0:T(8,128)(2,1)}, u32[]{:S(2)}) copy-start(bf16[2,2,45,16,128]{4,3,2,1,0:T(8,128)(2,1)} %get-tuple-element.72.refs_2_.refs_4_) | copy-start | bytes 2211844
  135.2 11.9 %copy-start.8 = (bf16[2,2,45,16,128]{4,3,2,1,0:T(8,128)(2,1)S(1)}, bf16[2,2,45,16,128]{4,3,2,1,0:T(8,128)(2,1)}, u32[]{:S(2)}) copy-start(bf16[2,2,45,16,128]{4,3,2,1,0:T(8,128)(2,1)} %copy-done.7) | copy-start | bytes 2211844
  141.5 5.6 %collective-permute-start.23 = (bf16[2,4,45,16,128]{4,3,2,1,0:T(8,128)(2,1)}, bf16[2,4,45,16,128]{4,3,2,1,0:T(8,128)(2,1)S(1)}, u32[]{:S(2)}, u32[]{:S(2)}) collective-permute-start(bf16[2,4,45,16,128]{4,3,2,1,0:T(8,128)(2,1)} %collective-permute-done.22.refs_9_), channel_id=1, source_target_pairs={{0,8},{8,0},{16,24},{24,16},{1,9},{9,1},{17,25},{25,17},{2,10},{10... | collective-permute-start | bytes 4423688 | tf_op jit(solution)/shard_map/ppermute | solution.py:617
  141.6 4.5 %collective-permute-start.21 = (bf16[2,2,45,16,128]{4,3,2,1,0:T(8,128)(2,1)}, bf16[2,2,45,16,128]{4,3,2,1,0:T(8,128)(2,1)S(1)}, u32[]{:S(2)}, u32[]{:S(2)}) collective-permute-start(bf16[2,2,45,16,128]{4,3,2,1,0:T(8,128)(2,1)} %collective-permute-done.11.refs_5_), channel_id=1, source_target_pairs={{0,8},{8,0},{16,24},{24,16},{1,9},{9,1},{17,25},{25,17},{2,10},{10... | collective-permute-start | bytes 2211848 | tf_op jit(solution)/shard_map/ppermute | solution.py:617
  142.1 5.1 %collective-permute-start.20 = (bf16[2,2,45,16,128]{4,3,2,1,0:T(8,128)(2,1)}, bf16[2,2,45,16,128]{4,3,2,1,0:T(8,128)(2,1)S(1)}, u32[]{:S(2)}, u32[]{:S(2)}) collective-permute-start(bf16[2,2,45,16,128]{4,3,2,1,0:T(8,128)(2,1)} %collective-permute-done.10.refs_1_), channel_id=1, source_target_pairs={{0,8},{8,0},{16,24},{24,16},{1,9},{9,1},{17,25},{25,17},{2,10},{10... | collective-permute-start | bytes 2211848 | tf_op jit(solution)/shard_map/ppermute | solution.py:617

commit v7 on v6

--- a/solution.py
+++ b/solution.py
@@ -144,8 +144,15 @@
     two_steps(stack, second, rows, weights, bias, emit, None, width, length)
 
 
-def inner_body(x, weights, bias, out, *refs, width, length):
-    inner_tiles(x, weights, bias, out, refs[:-2], *refs[-2:], width, length)
+def inner_body(x, weights, bias, earlier, out, last, first, every, *scratch, width, length):
+    inner_tiles(x, weights, bias, out, (last, first), *scratch, width, length)
+    count = earlier.shape[0]
+
+    @pl.when(pl.program_id(0) == 0)
+    def _():
+        every[:count] = earlier[...]
+
+    every[pl.ds(count + pl.program_id(0), 1)] = out[...]
 
 
 def opening_body(
@@ -241,9 +248,10 @@
     )(x, weights, bias, inner0)
 
 
-def inner(x, weights, bias, start, count):
+def inner(x, weights, bias, earlier, start, count):
     _, height, width, length = x.shape
     shapes, scratch = inner_layout(x, count, count)
+    whole = (earlier.shape[0] + count,) + earlier.shape[1:]
     return pl.pallas_call(
         functools.partial(inner_body, width=width, length=length),
         grid=(count,),
@@ -251,16 +259,18 @@
             pl.BlockSpec((1, height, width, length), lambda m: (m + start, 0, 0, 0)),
             pl.BlockSpec(weights.shape, lambda m: (0, 0)),
             pl.BlockSpec(bias.shape, lambda m: (0, 0)),
+            pl.BlockSpec(earlier.shape, lambda m: (0, 0, 0, 0, 0)),
         ],
         out_specs=[
             pl.BlockSpec((1,) + shape.shape[1:], lambda m: (m, 0, 0, 0, 0)) for shape in shapes
-        ],
-        out_shape=shapes,
+        ]
+        + [pl.BlockSpec(whole, lambda m: (0, 0, 0, 0, 0))],
+        out_shape=shapes + [jax.ShapeDtypeStruct(whole, bf16)],
         scratch_shapes=scratch,
         compiler_params=pltpu.CompilerParams(vmem_limit_bytes=VMEM),
         cost_estimate=SMALL,
         name="inner_rows",
-    )(x, weights, bias)
+    )(x, weights, bias, earlier)
 
 
 def outer_body(ends, x, low, high, weights, bias, *refs, cut, width, length):
@@ -641,7 +651,9 @@
     halo0 = halo(last0, first0)
     inner1, inner01 = second(x, weights, bias, inner0)
     inner1_across = swap(inner1, 2)
-    inner2, last2, first2 = inner(after(x, inner1), weights, bias, half, members - half)
+    inner2, last2, first2, inners = inner(
+        after(x, inner1), weights, bias, inner01, half, members - half
+    )
     inner2_across = swap(inner2, 2)
     halo1 = halo(*lax.optimization_barrier((last2, first2, *halo0))[:2])
 
@@ -678,23 +690,22 @@
         measured_slot_number, measured_precision_factor, measured_reading, seen_parts, bands
     )
     terms = lax.all_to_all(terms, "band", 0, 0, tiled=True)
-    inner01_core, inner2_core, inner2_far, outer1_core = [
-        swap(after(part, *seen_parts[1:]), 1) for part in (inner01, inner2, inner2_across, outer1)
+    inners_core, inner0_far, inner2_far, outer1_core = [
+        swap(after(part, *seen_parts[1:]), 1)
+        for part in (inners, inner0_across, inner2_across, outer1)
     ]
-    terms = after(terms, inner01_core, inner2_core, inner2_far, outer1_core)
-    inner0_far, inner1_far, top0_core, bottom0_core = [
-        swap(after(part, terms), 1) for part in (inner0_across, inner1_across, top0, bottom0)
+    terms = after(terms, inners_core, inner0_far, inner2_far, outer1_core)
+    inner1_far, top0_core, bottom0_core, top0_far = [
+        swap(after(part, terms), 1) for part in (inner1_across, top0, bottom0, top0_across)
     ]
     blend = transform(terms, members)
-    blend = after(blend, inner0_far, inner1_far, top0_core, bottom0_core)
-    top0_far, bottom0_far = [
-        swap(after(part, blend), 1) for part in (top0_across, bottom0_across)
-    ]
-
-    arrays = (inner01, inner2, inner0_across, inner1_across, inner2_across)
-    arrays += (inner01_core, inner2_core, inner0_far, inner1_far, inner2_far)
+    blend = after(blend, inner1_far, top0_core, bottom0_core, top0_far)
+    bottom0_far = swap(after(bottom0_across, blend), 1)
+
+    arrays = (inners, inner0_across, inner1_across, inner2_across)
+    arrays += (inners_core, inner0_far, inner1_far, inner2_far)
     sources = tuple(
-        (row + 2, tuple((index, row) for index in range(10))) for row in range(height - 4)
+        (row + 2, tuple((index, row) for index in range(8))) for row in range(height - 4)
     )
     result = mix(blend, arrays, sources, x.shape, None)
     outer1_far = swap(after(outer1_across, result), 1)

time: 153 us -> 152 us (level)
  waiting for transfers between devices: 35.6 us -> 33.5 us
    ppermute x2, waiting for transfers between devices: 18.1 us -> 16.3 us  [halo(): lax.ppermute(last, 'band', forward)]
    pallas_call x1, Pallas kernels: 7.28 us -> 9.08 us  [inner(): pl.pallas_call(functools.partial(inner_body, width=width, length=length),...]
    ppermute x20 -> x19, waiting for transfers between devices: 17.4 us -> 17.2 us  [swap(): return lax.ppermute(block, 'member', [(i, i ^ bit) for i in range(size)])]
    ppermute x20 -> x19, starting transfers between devices: 13.7 us -> 13.8 us  [swap(): return lax.ppermute(block, 'member', [(i, i ^ bit) for i in range(size)])]
  transfers between devices with their start and end apart: 24 -> 23, of which waited for: 8 -> 7; matrix products, arithmetic and copies ran while one was open for 2% -> 2% of each run, Pallas kernels for 39% -> 40%
where the time goes in v7:
time: 152 us
  Pallas kernels  71.8 us (47%)
  waiting for transfers between devices  33.5 us (22%)
  starting transfers between devices  26.1 us (17%)
  blocking collectives  12.8 us (8%)
  local copies, waits for them, and re-layouts  3.85 us (3%)
  other arithmetic  2.61 us (2%)
    pallas_call x2, Pallas kernels, outer(): pl.pallas_call(functools.partial(outer_body, cut=cut, width=width, length...  18.3 us
    ppermute x19, waiting for transfers between devices, swap(): return lax.ppermute(block, 'member', [(i, i ^ bit) for i in range(size)])  17.2 us
    ppermute x2, waiting for transfers between devices, halo(): lax.ppermute(last, 'band', forward)  16.3 us
    pallas_call x2, Pallas kernels, gather(): pl.pallas_call(functools.partial(gather_body, pieces=pieces, kept=kept),...  13.9 us
    ppermute x19, starting transfers between devices, swap(): return lax.ppermute(block, 'member', [(i, i ^ bit) for i in range(size)])  13.8 us
    all_to_all x1, blocking collectives, local(): terms = lax.all_to_all(terms, 'band', 0, 0, tiled=True)  12.8 us
    pallas_call x2, Pallas kernels, mix(): pl.pallas_call(functools.partial(mix_body, sources=sources, kept=int(kept...  11 us
    ppermute x2, starting transfers between devices, halo(): lax.ppermute(last, 'band', forward)  9.58 us
  transfers between devices with their start and end apart: 23, of which 7 were waited for; matrix products, arithmetic and copies ran while one was open for 2% of the time, Pallas kernels for 40%

profile of v7, /device:TPU:0, one launch (start us, length us, event | category | flops | bytes accessed | tf_op | source)
XLA Modules:
  0.0 151.7 jit_solution(2722770535117214068)
XLA Ops:
  0.0 6.2 %opening_rows.1 = (bf16[1,4,45,16,128]{4,3,2,1,0:T(8,128)(2,1)}, bf16[2,2,45,16,128]{4,3,2,1,0:T(8,128)(2,1)}, bf16[2,2,45,16,128]{4,3,2,1,0:T(8,128)(2,1)}, bf16[128,768]{1,0:T(8,128)(2,1)}, f32[128,128]{1,0:T(8,128)}) custom-call(bf16[4,8,64,1440]{3,2,1,0:T(8,128)(2,1)} %x.6, bf16[4,8,64,1440]{3,2,1,0:T(8,128)(2,1)} %x.6, bf16[4,8,64,1440]{3,2,1,0:T(8,128)(2,1)} %x.6, ...), custom_call_target="tpu_custom_call" | custom-call | flops 200000000 | bytes 500000 | tf_op jit(solution)/shard_map/opening_rows/pallas_call | solution.py:202
  6.2 3.0 %collective-permute-start = (bf16[1,4,45,16,128]{4,3,2,1,0:T(8,128)(2,1)}, bf16[1,4,45,16,128]{4,3,2,1,0:T(8,128)(2,1)S(1)}, u32[]{:S(2)}, u32[]{:S(2)}) collective-permute-start(bf16[1,4,45,16,128]{4,3,2,1,0:T(8,128)(2,1)} %get-tuple-element.41.inner0), channel_id=1, source_target_pairs={{0,16},{8,24},{16,0},{24,8},{1,17},{9,25},{17,1},{25,9},{2,18},{10... | collective-permute-start | bytes 2211848 | tf_op jit(solution)/shard_map/ppermute | solution.py:627
  9.1 4.3 %collective-permute-start.3 = (bf16[2,2,45,16,128]{4,3,2,1,0:T(8,128)(2,1)}, bf16[2,2,45,16,128]{4,3,2,1,0:T(8,128)(2,1)}, u32[]{:S(2)}, u32[]{:S(2)}) collective-permute-start(bf16[2,2,45,16,128]{4,3,2,1,0:T(8,128)(2,1)} %get-tuple-element.51), channel_id=1, source_target_pairs={{0,1},{1,2},{2,3},{3,4},{4,5},{5,6},{6,7},{8,9},{9,10},{10,11},{11... | collective-permute-start | bytes 2211848 | tf_op jit(solution)/shard_map/ppermute | solution.py:622
  13.4 1.3 collective-permute-start.4
  14.7 5.6 %second_rows.1 = (bf16[1,4,45,16,128]{4,3,2,1,0:T(8,128)(2,1)}, bf16[2,4,45,16,128]{4,3,2,1,0:T(8,128)(2,1)}) custom-call(bf16[4,8,64,1440]{3,2,1,0:T(8,128)(2,1)} %x.6, bf16[128,768]{1,0:T(8,128)(2,1)} %get-tuple-element.43.weights, f32[128,128]{1,0:T(8,128)} %get-tuple-element.44.bias, bf16[1,4,45,16,128]{4,3,2,1,0:T(8,128)(2,1)} %get-tuple-element.41.inner0), custom_call_target="tpu_custom_call" | custom-call | flops 200000000 | bytes 500000 | tf_op jit(solution)/shard_map/second_rows/pallas_call | solution.py:233
  20.3 0.5 collective-permute-start.2
  20.8 9.1 %inner_rows.1 = (bf16[2,4,45,16,128]{4,3,2,1,0:T(8,128)(2,1)}, bf16[2,2,45,16,128]{4,3,2,1,0:T(8,128)(2,1)}, bf16[2,2,45,16,128]{4,3,2,1,0:T(8,128)(2,1)}, bf16[4,4,45,16,128]{4,3,2,1,0:T(8,128)(2,1)}) custom-call(bf16[4,8,64,1440]{3,2,1,0:T(8,128)(2,1)} %x.6, bf16[128,768]{1,0:T(8,128)(2,1)} %get-tuple-element.43.weights, ...), custom_call_target="tpu_custom_call" | custom-call | flops 200000000 | bytes 500000 | tf_op jit(solution)/shard_map/inner_rows/pallas_call | solution.py:255
  29.9 1.6 %collective-permute-start.1 = (bf16[2,4,45,16,128]{4,3,2,1,0:T(8,128)(2,1)}, bf16[2,4,45,16,128]{4,3,2,1,0:T(8,128)(2,1)}, u32[]{:S(2)}, u32[]{:S(2)}) collective-permute-start(bf16[2,4,45,16,128]{4,3,2,1,0:T(8,128)(2,1)} %get-tuple-element.48.refs_0_), channel_id=1, source_target_pairs={{0,16},{8,24},{16,0},{24,8},{1,17},{9,25},{17,1},{25,9},{2,18},{10... | collective-permute-start | bytes 4423688 | tf_op jit(solution)/shard_map/ppermute | solution.py:627
  31.5 0.7 add_convert_fusion.ends
  32.1 0.6 fusion.6
  32.8 0.0 collective-permute-done.refs_1_
  32.8 11.3 %collective-permute-done.3.low = bf16[2,2,45,16,128]{4,3,2,1,0:T(8,128)(2,1)} collective-permute-done((bf16[2,2,45,16,128]{4,3,2,1,0:T(8,128)(2,1)}, bf16[2,2,45,16,128]{4,3,2,1,0:T(8,128)(2,1)}, u32[]{:S(2)}, u32[]{:S(2)}) %collective-permute-start.3) | collective-permute-done | bytes 737312 | tf_op jit(solution)/shard_map/ppermute | solution.py:622
  44.1 0.0 collective-permute-done.4.high
  44.1 5.3 %collective-permute-start.5 = (bf16[2,2,45,16,128]{4,3,2,1,0:T(8,128)(2,1)}, bf16[2,2,45,16,128]{4,3,2,1,0:T(8,128)(2,1)}, u32[]{:S(2)}, u32[]{:S(2)}) collective-permute-start(bf16[2,2,45,16,128]{4,3,2,1,0:T(8,128)(2,1)} %get-tuple-element.58), channel_id=1, source_target_pairs={{0,1},{1,2},{2,3},{3,4},{4,5},{5,6},{6,7},{8,9},{9,10},{10,11},{11... | collective-permute-start | bytes 2211848 | tf_op jit(solution)/shard_map/ppermute | solution.py:622
  49.4 1.5 collective-permute-start.6
  50.9 1.3 fusion.chosen
  52.2 0.0 collective-permute-done.2.refs_2_
  52.2 9.1 %outer_rows.2 = (bf16[2,2,45,16,128]{4,3,2,1,0:T(8,128)(2,1)}, bf16[2,2,45,16,128]{4,3,2,1,0:T(8,128)(2,1)}) custom-call(s32[2]{0:T(128)} %add_convert_fusion.ends, bf16[4,8,64,1440]{3,2,1,0:T(8,128)(2,1)} %x.6, bf16[2,2,45,16,128]{4,3,2,1,0:T(8,128)(2,1)} %collective-permute-done.3.low, bf16[2,2,45,16,128]{4,3,2,1,0:T(8,128)(2,1)} %collective-permute-done.4.high, ...), custom_call_target="tpu_custom_call" | custom-call | flops 200000000 | bytes 500000 | tf_op jit(solution)/shard_map/outer_rows/pallas_call | solution.py:311
  61.3 0.6 collective-permute-start.10
  61.9 1.5 %collective-permute-start.11 = (bf16[2,2,45,16,128]{4,3,2,1,0:T(8,128)(2,1)}, bf16[2,2,45,16,128]{4,3,2,1,0:T(8,128)(2,1)}, u32[]{:S(2)}, u32[]{:S(2)}) collective-permute-start(bf16[2,2,45,16,128]{4,3,2,1,0:T(8,128)(2,1)} %get-tuple-element.72.refs_2_.refs_4_), channel_id=1, source_target_pairs={{0,16},{8,24},{16,0},{24,8},{1,17},{9,25},{17,1},{25,9},{2,18},{10... | collective-permute-start | bytes 2211848 | tf_op jit(solution)/shard_map/ppermute | solution.py:627
  63.4 6.9 %gather_cells.2.refs_2_ = bf16[2,1,2048]{2,1,0:T(2,128)(2,1)} custom-call(s32[2048]{0:T(1024)} %get-tuple-element.78.rows, f32[2048,128]{1,0:T(8,128)} %fusion.chosen, bf16[2,4,45,16,128]{4,3,2,1,0:T(8,128)(2,1)} %get-tuple-element.47.earlier.refs_0_, bf16[2,2,45,16,128]{4,3,2,1,0:T(8,128)(2,1)} %get-tuple-element.71.refs_1_.refs_0_, ...), custom_call_target="tpu_custom_call" | custom-call | flops 200000000 | bytes 500000 | tf_op jit(solution)/shard_map/gather_cells/pallas_call | solution.py:387
  70.3 3.8 %collective-permute-done.1.refs_3_ = bf16[2,4,45,16,128]{4,3,2,1,0:T(8,128)(2,1)} collective-permute-done((bf16[2,4,45,16,128]{4,3,2,1,0:T(8,128)(2,1)}, bf16[2,4,45,16,128]{4,3,2,1,0:T(8,128)(2,1)}, u32[]{:S(2)}, u32[]{:S(2)}) %collective-permute-start.1) | collective-permute-done | bytes 1474592 | tf_op jit(solution)/shard_map/ppermute | solution.py:627
  74.2 5.0 %collective-permute-done.5.low = bf16[2,2,45,16,128]{4,3,2,1,0:T(8,128)(2,1)} collective-permute-done((bf16[2,2,45,16,128]{4,3,2,1,0:T(8,128)(2,1)}, bf16[2,2,45,16,128]{4,3,2,1,0:T(8,128)(2,1)}, u32[]{:S(2)}, u32[]{:S(2)}) %collective-permute-start.5) | collective-permute-done | bytes 737312 | tf_op jit(solution)/shard_map/ppermute | solution.py:622
  79.1 0.0 collective-permute-done.6.high
  79.1 9.2 %outer_rows.3.refs_1_.refs_8_ = bf16[2,4,45,16,128]{4,3,2,1,0:T(8,128)(2,1)} custom-call(s32[2]{0:T(128)} %add_convert_fusion.ends, bf16[4,8,64,1440]{3,2,1,0:T(8,128)(2,1)} %x.6, bf16[2,2,45,16,128]{4,3,2,1,0:T(8,128)(2,1)} %collective-permute-done.5.low, bf16[2,2,45,16,128]{4,3,2,1,0:T(8,128)(2,1)} %collective-permute-done.6.high, ...), custom_call_target="tpu_custom_call" | custom-call | flops 200000000 | bytes 500000 | tf_op jit(solution)/shard_map/outer_rows/pallas_call | solution.py:311
  88.3 7.0 %gather_cells.3.refs_0_ = bf16[4,1,2048]{2,1,0:T(2,128)(2,1)} custom-call(s32[2048]{0:T(1024)} %get-tuple-element.78.rows, f32[2048,128]{1,0:T(8,128)} %fusion.chosen, bf16[2,4,45,16,128]{4,3,2,1,0:T(8,128)(2,1)} %get-tuple-element.48.refs_0_, bf16[2,4,45,16,128]{4,3,2,1,0:T(8,128)(2,1)} %outer_rows.3.refs_1_.refs_8_, bf16[2,1,2048]{2,1,0:T(2,128)(2,1)} %gather_cells.2.refs_2_), custom_call_target="tpu_custom_call" | custom-call | flops 200000000 | bytes 500000 | tf_op jit(solution)/shard_map/gather_cells/pallas_call | solution.py:387
  95.3 0.6 collective-permute-start.7
  95.9 0.0 collective-permute-start.8
  95.9 1.6 %collective-permute-start.9 = (bf16[4,1,2048]{2,1,0:T(2,128)(2,1)}, bf16[4,1,2048]{2,1,0:T(2,128)(2,1)S(1)}, u32[]{:S(2)}, u32[]{:S(2)}) collective-permute-start(bf16[4,1,2048]{2,1,0:T(2,128)(2,1)} %gather_cells.3.refs_0_), channel_id=1, source_target_pairs={{0,24},{8,16},{16,8},{24,0},{1,25},{9,17},{17,9},{25,1},{2,26},{10... | collective-permute-start | bytes 49160 | tf_op jit(solution)/shard_map/ppermute | solution.py:627
  97.5 0.0 collective-permute-done.10.refs_1_
  97.5 8.1 %collective-permute-done.11.refs_5_ = bf16[2,2,45,16,128]{4,3,2,1,0:T(8,128)(2,1)} collective-permute-done((bf16[2,2,45,16,128]{4,3,2,1,0:T(8,128)(2,1)}, bf16[2,2,45,16,128]{4,3,2,1,0:T(8,128)(2,1)}, u32[]{:S(2)}, u32[]{:S(2)}) %collective-permute-start.11) | collective-permute-done | bytes 737312 | tf_op jit(solution)/shard_map/ppermute | solution.py:627
  105.6 0.2 collective-permute-done.7.refs_1_
  105.9 0.0 collective-permute-done.8.refs_2_
  105.9 0.0 collective-permute-done.9.refs_3_
  105.9 0.1 collective-permute-start.12
  106.1 0.4 collective-permute-start.15
  106.5 0.1 collective-permute-start.14
  106.6 0.4 collective-permute-start.13
  107.0 1.7 %collective-permute-start.21 = (bf16[2,4,45,16,128]{4,3,2,1,0:T(8,128)(2,1)}, bf16[2,4,45,16,128]{4,3,2,1,0:T(8,128)(2,1)}, u32[]{:S(2)}, u32[]{:S(2)}) collective-permute-start(bf16[2,4,45,16,128]{4,3,2,1,0:T(8,128)(2,1)} %outer_rows.3.refs_1_.refs_8_), channel_id=1, source_target_pairs={{0,16},{8,24},{16,0},{24,8},{1,17},{9,25},{17,1},{25,9},{2,18},{10... | collective-permute-start | bytes 4423688 | tf_op jit(solution)/shard_map/ppermute | solution.py:627
  109.4 1.9 %band_terms.1 = f32[8,1,2048]{2,1,0:T(1,128)} custom-call(s32[1]{0:T(128)S(6)} %copy.10.live, f32[1,2048]{1,0:T(1,128)} %bitcast.6, f32[1,2048]{1,0:T(1,128)} %bitcast.7, bf16[4,1,2048]{2,1,0:T(2,128)(2,1)} %gather_cells.3.refs_0_, bf16[4,1,2048]{2,1,0:T(2,128)(2,1)} %copy-done.11, bf16[4,1,2048]{2,1,0:T(2,128)(2,1)} %copy-done.12, ...), custom_call_target="tpu_custom_call" | custom-call | flops 200000000 | bytes 500000 | tf_op jit(solution)/shard_map/band_terms/pallas_call | solution.py:540
  111.3 12.8 %all_to_all.5.terms = f32[8,1,2048]{2,1,0:T(1,128)} all-to-all(f32[8,1,2048]{2,1,0:T(1,128)} %band_terms.1), channel_id=1, replica_groups=mesh['member'=4,'band'=8] {'band'}, dimensions={0} | all-to-all | bytes 131072 | tf_op jit(solution)/shard_map/all_to_all | solution.py:692
  124.1 0.0 collective-permute-done.13.refs_5_
  124.1 0.0 collective-permute-done.15.refs_10_
  124.1 0.0 collective-permute-done.14.refs_7_
  124.1 0.0 collective-permute-done.12.refs_4_
  124.1 0.1 collective-permute-start.19
  124.2 0.5 collective-permute-start.18
  124.7 0.1 collective-permute-start.17
  124.8 0.4 collective-permute-start.16
  125.2 5.9 %transform.1.weights = bf16[64,256]{1,0:T(8,128)(2,1)} custom-call(f32[8,1,2048]{2,1,0:T(1,128)} %all_to_all.5.terms), custom_call_target="tpu_custom_call" | custom-call | flops 200000000 | bytes 500000 | tf_op jit(solution)/shard_map/transform/pallas_call | solution.py:604
  131.1 0.0 collective-permute-done.19.refs_3_
  131.1 0.0 collective-permute-done.18.refs_6_
  131.2 0.0 collective-permute-done.16.refs_6_
  131.2 0.0 copy-start.1
  131.2 1.9 %copy-done.1 = bf16[4,4,45,16,128]{4,3,2,1,0:T(8,128)(2,1)S(1)} copy-done((bf16[4,4,45,16,128]{4,3,2,1,0:T(8,128)(2,1)S(1)}, bf16[4,4,45,16,128]{4,3,2,1,0:T(8,128)(2,1)}, u32[]{:S(2)}) %copy-start.1) | copy-done | bytes 2949144
  133.1 1.1 copy-done.5
  134.2 0.8 copy-done.8
  135.0 5.6 %mix_rows.2.refs_12_ = bf16[4,8,64,1440]{3,2,1,0:T(8,128)(2,1)} custom-call(bf16[64,256]{1,0:T(8,128)(2,1)S(1)} %copy-done.8, bf16[4,4,45,16,128]{4,3,2,1,0:T(8,128)(2,1)S(1)} %copy-done.1, bf16[1,4,45,16,128]{4,3,2,1,0:T(8,128)(2,1)S(1)} %copy-done.5, bf16[1,4,45,16,128]{4,3,2,1,0:T(8,128)(2,1)} %collective-permute-done.2.refs_2_, ...), custom_call_target="tpu_custom_call" | custom-call | flops 200000000 | bytes 500000 | tf_op jit(solution)/shard_map/mix_rows/pallas_call | solution.py:496
  140.6 1.0 collective-permute-done.21.refs_9_
  141.6 0.0 collective-permute-start.22
  141.6 0.5 collective-permute-start.20
  142.1 4.0 %collective-permute-done.20.refs_7_ = bf16[2,2,45,16,128]{4,3,2,1,0:T(8,128)(2,1)S(1)} collective-permute-done((bf16[2,2,45,16,128]{4,3,2,1,0:T(8,128)(2,1)}, bf16[2,2,45,16,128]{4,3,2,1,0:T(8,128)(2,1)S(1)}, u32[]{:S(2)}, u32[]{:S(2)}) %collective-permute-start.20) | collective-permute-done | bytes 737312 | tf_op jit(solution)/shard_map/ppermute | solution.py:627
  146.1 0.0 collective-permute-done.22.refs_11_
  146.2 5.4 %mix_rows.3 = bf16[4,8,64,1440]{3,2,1,0:T(8,128)(2,1)} custom-call(bf16[64,256]{1,0:T(8,128)(2,1)S(1)} %copy-done.9, bf16[2,2,45,16,128]{4,3,2,1,0:T(8,128)(2,1)S(1)} %copy-done.2, bf16[2,2,45,16,128]{4,3,2,1,0:T(8,128)(2,1)S(1)} %copy-done.7, bf16[2,2,45,16,128]{4,3,2,1,0:T(8,128)(2,1)} %collective-permute-done.17.refs_2_, ...), custom_call_target="tpu_custom_call", output_to_operand_aliasing={{}: (13, {})} | custom-call | flops 200000000 | bytes 500000 | tf_op jit(solution)/shard_map/mix_rows/pallas_call | solution.py:496
  (25 shorter events, 0.0 us)
Async XLA Ops:
  6.2 26.6 %collective-permute-start = (bf16[1,4,45,16,128]{4,3,2,1,0:T(8,128)(2,1)}, bf16[1,4,45,16,128]{4,3,2,1,0:T(8,128)(2,1)S(1)}, u32[]{:S(2)}, u32[]{:S(2)}) collective-permute-start(bf16[1,4,45,16,128]{4,3,2,1,0:T(8,128)(2,1)} %get-tuple-element.41.inner0), channel_id=1, source_target_pairs={{0,16},{8,24},{16,0},{24,8},{1,17},{9,25},{17,1},{25,9},{2,18},{10... | collective-permute-start | bytes 2211848 | tf_op jit(solution)/shard_map/ppermute | solution.py:627
  9.1 35.0 %collective-permute-start.3 = (bf16[2,2,45,16,128]{4,3,2,1,0:T(8,128)(2,1)}, bf16[2,2,45,16,128]{4,3,2,1,0:T(8,128)(2,1)}, u32[]{:S(2)}, u32[]{:S(2)}) collective-permute-start(bf16[2,2,45,16,128]{4,3,2,1,0:T(8,128)(2,1)} %get-tuple-element.51), channel_id=1, source_target_pairs={{0,1},{1,2},{2,3},{3,4},{4,5},{5,6},{6,7},{8,9},{9,10},{10,11},{11... | collective-permute-start | bytes 2211848 | tf_op jit(solution)/shard_map/ppermute | solution.py:622
  13.4 30.7 %collective-permute-start.4 = (bf16[2,2,45,16,128]{4,3,2,1,0:T(8,128)(2,1)}, bf16[2,2,45,16,128]{4,3,2,1,0:T(8,128)(2,1)}, u32[]{:S(2)}, u32[]{:S(2)}) collective-permute-start(bf16[2,2,45,16,128]{4,3,2,1,0:T(8,128)(2,1)} %get-tuple-element.52), channel_id=1, source_target_pairs={{1,0},{2,1},{3,2},{4,3},{5,4},{6,5},{7,6},{9,8},{10,9},{11,10},{12... | collective-permute-start | bytes 2211848 | tf_op jit(solution)/shard_map/ppermute | solution.py:622
  20.3 31.9 %collective-permute-start.2 = (bf16[1,4,45,16,128]{4,3,2,1,0:T(8,128)(2,1)}, bf16[1,4,45,16,128]{4,3,2,1,0:T(8,128)(2,1)}, u32[]{:S(2)}, u32[]{:S(2)}) collective-permute-start(bf16[1,4,45,16,128]{4,3,2,1,0:T(8,128)(2,1)} %get-tuple-element.45), channel_id=1, source_target_pairs={{0,16},{8,24},{16,0},{24,8},{1,17},{9,25},{17,1},{25,9},{2,18},{10... | collective-permute-start | bytes 2211848 | tf_op jit(solution)/shard_map/ppermute | solution.py:627
  20.8 11.3 %copy-start.10 = (s32[2048]{0:T(1024)S(1)}, s32[2048]{0:T(1024)}, u32[]{:S(2)}) copy-start(s32[2048]{0:T(1024)} %param.10) | copy-start | bytes 24580
  29.9 44.3 %collective-permute-start.1 = (bf16[2,4,45,16,128]{4,3,2,1,0:T(8,128)(2,1)}, bf16[2,4,45,16,128]{4,3,2,1,0:T(8,128)(2,1)}, u32[]{:S(2)}, u32[]{:S(2)}) collective-permute-start(bf16[2,4,45,16,128]{4,3,2,1,0:T(8,128)(2,1)} %get-tuple-element.48.refs_0_), channel_id=1, source_target_pairs={{0,16},{8,24},{16,0},{24,8},{1,17},{9,25},{17,1},{25,9},{2,18},{10... | collective-permute-start | bytes 4423688 | tf_op jit(solution)/shard_map/ppermute | solution.py:627
  32.8 28.5 %copy-start.4 = (bf16[1,4,45,16,128]{4,3,2,1,0:T(8,128)(2,1)}, bf16[1,4,45,16,128]{4,3,2,1,0:T(8,128)(2,1)S(1)}, u32[]{:S(2)}) copy-start(bf16[1,4,45,16,128]{4,3,2,1,0:T(8,128)(2,1)S(1)} %collective-permute-done.refs_1_) | copy-start | bytes 2211844
  44.1 35.0 %collective-permute-start.5 = (bf16[2,2,45,16,128]{4,3,2,1,0:T(8,128)(2,1)}, bf16[2,2,45,16,128]{4,3,2,1,0:T(8,128)(2,1)}, u32[]{:S(2)}, u32[]{:S(2)}) collective-permute-start(bf16[2,2,45,16,128]{4,3,2,1,0:T(8,128)(2,1)} %get-tuple-element.58), channel_id=1, source_target_pairs={{0,1},{1,2},{2,3},{3,4},{4,5},{5,6},{6,7},{8,9},{9,10},{10,11},{11... | collective-permute-start | bytes 2211848 | tf_op jit(solution)/shard_map/ppermute | solution.py:622
  49.4 29.8 %collective-permute-start.6 = (bf16[2,2,45,16,128]{4,3,2,1,0:T(8,128)(2,1)}, bf16[2,2,45,16,128]{4,3,2,1,0:T(8,128)(2,1)}, u32[]{:S(2)}, u32[]{:S(2)}) collective-permute-start(bf16[2,2,45,16,128]{4,3,2,1,0:T(8,128)(2,1)} %get-tuple-element.59), channel_id=1, source_target_pairs={{1,0},{2,1},{3,2},{4,3},{5,4},{6,5},{7,6},{9,8},{10,9},{11,10},{12... | collective-permute-start | bytes 2211848 | tf_op jit(solution)/shard_map/ppermute | solution.py:622
  61.3 36.2 %collective-permute-start.10 = (bf16[2,2,45,16,128]{4,3,2,1,0:T(8,128)(2,1)}, bf16[2,2,45,16,128]{4,3,2,1,0:T(8,128)(2,1)S(1)}, u32[]{:S(2)}, u32[]{:S(2)}) collective-permute-start(bf16[2,2,45,16,128]{4,3,2,1,0:T(8,128)(2,1)} %get-tuple-element.71.refs_1_.refs_0_), channel_id=1, source_target_pairs={{0,16},{8,24},{16,0},{24,8},{1,17},{9,25},{17,1},{25,9},{2,18},{10... | collective-permute-start | bytes 2211848 | tf_op jit(solution)/shard_map/ppermute | solution.py:627
  61.9 43.8 %collective-permute-start.11 = (bf16[2,2,45,16,128]{4,3,2,1,0:T(8,128)(2,1)}, bf16[2,2,45,16,128]{4,3,2,1,0:T(8,128)(2,1)}, u32[]{:S(2)}, u32[]{:S(2)}) collective-permute-start(bf16[2,2,45,16,128]{4,3,2,1,0:T(8,128)(2,1)} %get-tuple-element.72.refs_2_.refs_4_), channel_id=1, source_target_pairs={{0,16},{8,24},{16,0},{24,8},{1,17},{9,25},{17,1},{25,9},{2,18},{10... | collective-permute-start | bytes 2211848 | tf_op jit(solution)/shard_map/ppermute | solution.py:627
  95.3 10.6 %collective-permute-start.7 = (bf16[4,1,2048]{2,1,0:T(2,128)(2,1)}, bf16[4,1,2048]{2,1,0:T(2,128)(2,1)S(1)}, u32[]{:S(2)}, u32[]{:S(2)}) collective-permute-start(bf16[4,1,2048]{2,1,0:T(2,128)(2,1)} %gather_cells.3.refs_0_), channel_id=1, source_target_pairs={{0,16},{8,24},{16,0},{24,8},{1,17},{9,25},{17,1},{25,9},{2,18},{10... | collective-permute-start | bytes 49160 | tf_op jit(solution)/shard_map/ppermute | solution.py:627
  95.9 10.0 %collective-permute-start.8 = (bf16[4,1,2048]{2,1,0:T(2,128)(2,1)}, bf16[4,1,2048]{2,1,0:T(2,128)(2,1)S(1)}, u32[]{:S(2)}, u32[]{:S(2)}) collective-permute-start(bf16[4,1,2048]{2,1,0:T(2,128)(2,1)} %gather_cells.3.refs_0_), channel_id=1, source_target_pairs={{0,8},{8,0},{16,24},{24,16},{1,9},{9,1},{17,25},{25,17},{2,10},{10... | collective-permute-start | bytes 49160 | tf_op jit(solution)/shard_map/ppermute | solution.py:627
  95.9 10.0 %collective-permute-start.9 = (bf16[4,1,2048]{2,1,0:T(2,128)(2,1)}, bf16[4,1,2048]{2,1,0:T(2,128)(2,1)S(1)}, u32[]{:S(2)}, u32[]{:S(2)}) collective-permute-start(bf16[4,1,2048]{2,1,0:T(2,128)(2,1)} %gather_cells.3.refs_0_), channel_id=1, source_target_pairs={{0,24},{8,16},{16,8},{24,0},{1,25},{9,17},{17,9},{25,1},{2,26},{10... | collective-permute-start | bytes 49160 | tf_op jit(solution)/shard_map/ppermute | solution.py:627
  97.5 8.4 %copy-start.6 = (bf16[2,2,45,16,128]{4,3,2,1,0:T(8,128)(2,1)}, bf16[2,2,45,16,128]{4,3,2,1,0:T(8,128)(2,1)S(1)}, u32[]{:S(2)}) copy-start(bf16[2,2,45,16,128]{4,3,2,1,0:T(8,128)(2,1)S(1)} %collective-permute-done.10.refs_1_) | copy-start | bytes 2211844
  105.9 3.5 %copy-start.11 = (bf16[4,1,2048]{2,1,0:T(2,128)(2,1)}, bf16[4,1,2048]{2,1,0:T(2,128)(2,1)S(1)}, u32[]{:S(2)}) copy-start(bf16[4,1,2048]{2,1,0:T(2,128)(2,1)S(1)} %collective-permute-done.7.refs_1_) | copy-start | bytes 49156
  105.9 3.5 %copy-start.12 = (bf16[4,1,2048]{2,1,0:T(2,128)(2,1)}, bf16[4,1,2048]{2,1,0:T(2,128)(2,1)S(1)}, u32[]{:S(2)}) copy-start(bf16[4,1,2048]{2,1,0:T(2,128)(2,1)S(1)} %collective-permute-done.8.refs_2_) | copy-start | bytes 49156
  105.9 3.5 %copy-start.13 = (bf16[4,1,2048]{2,1,0:T(2,128)(2,1)}, bf16[4,1,2048]{2,1,0:T(2,128)(2,1)S(1)}, u32[]{:S(2)}) copy-start(bf16[4,1,2048]{2,1,0:T(2,128)(2,1)S(1)} %collective-permute-done.9.refs_3_) | copy-start | bytes 49156
  105.9 18.2 %collective-permute-start.12 = (bf16[4,4,45,16,128]{4,3,2,1,0:T(8,128)(2,1)}, bf16[4,4,45,16,128]{4,3,2,1,0:T(8,128)(2,1)S(1)}, u32[]{:S(2)}, u32[]{:S(2)}) collective-permute-start(bf16[4,4,45,16,128]{4,3,2,1,0:T(8,128)(2,1)} %get-tuple-element.65.refs_0_), channel_id=1, source_target_pairs={{0,8},{8,0},{16,24},{24,16},{1,9},{9,1},{17,25},{25,17},{2,10},{10... | collective-permute-start | bytes 8847368 | tf_op jit(solution)/shard_map/ppermute | solution.py:627
  106.1 18.1 %collective-permute-start.15 = (bf16[2,4,45,16,128]{4,3,2,1,0:T(8,128)(2,1)}, bf16[2,4,45,16,128]{4,3,2,1,0:T(8,128)(2,1)}, u32[]{:S(2)}, u32[]{:S(2)}) collective-permute-start(bf16[2,4,45,16,128]{4,3,2,1,0:T(8,128)(2,1)} %outer_rows.3.refs_1_.refs_8_), channel_id=1, source_target_pairs={{0,8},{8,0},{16,24},{24,16},{1,9},{9,1},{17,25},{25,17},{2,10},{10... | collective-permute-start | bytes 4423688 | tf_op jit(solution)/shard_map/ppermute | solution.py:627
  106.5 17.6 %collective-permute-start.14 = (bf16[2,4,45,16,128]{4,3,2,1,0:T(8,128)(2,1)}, bf16[2,4,45,16,128]{4,3,2,1,0:T(8,128)(2,1)}, u32[]{:S(2)}, u32[]{:S(2)}) collective-permute-start(bf16[2,4,45,16,128]{4,3,2,1,0:T(8,128)(2,1)} %collective-permute-done.1.refs_3_), channel_id=1, source_target_pairs={{0,8},{8,0},{16,24},{24,16},{1,9},{9,1},{17,25},{25,17},{2,10},{10... | collective-permute-start | bytes 4423688 | tf_op jit(solution)/shard_map/ppermute | solution.py:627
  106.6 17.5 %collective-permute-start.13 = (bf16[1,4,45,16,128]{4,3,2,1,0:T(8,128)(2,1)}, bf16[1,4,45,16,128]{4,3,2,1,0:T(8,128)(2,1)}, u32[]{:S(2)}, u32[]{:S(2)}) collective-permute-start(bf16[1,4,45,16,128]{4,3,2,1,0:T(8,128)(2,1)} %copy-done.4), channel_id=1, source_target_pairs={{0,8},{8,0},{16,24},{24,16},{1,9},{9,1},{17,25},{25,17},{2,10},{10... | collective-permute-start | bytes 2211848 | tf_op jit(solution)/shard_map/ppermute | solution.py:627
  107.0 34.6 %collective-permute-start.21 = (bf16[2,4,45,16,128]{4,3,2,1,0:T(8,128)(2,1)}, bf16[2,4,45,16,128]{4,3,2,1,0:T(8,128)(2,1)}, u32[]{:S(2)}, u32[]{:S(2)}) collective-permute-start(bf16[2,4,45,16,128]{4,3,2,1,0:T(8,128)(2,1)} %outer_rows.3.refs_1_.refs_8_), channel_id=1, source_target_pairs={{0,16},{8,24},{16,0},{24,8},{1,17},{9,25},{17,1},{25,9},{2,18},{10... | collective-permute-start | bytes 4423688 | tf_op jit(solution)/shard_map/ppermute | solution.py:627
  124.1 7.0 %collective-permute-start.19 = (bf16[2,2,45,16,128]{4,3,2,1,0:T(8,128)(2,1)}, bf16[2,2,45,16,128]{4,3,2,1,0:T(8,128)(2,1)}, u32[]{:S(2)}, u32[]{:S(2)}) collective-permute-start(bf16[2,2,45,16,128]{4,3,2,1,0:T(8,128)(2,1)} %copy-done.6), channel_id=1, source_target_pairs={{0,8},{8,0},{16,24},{24,16},{1,9},{9,1},{17,25},{25,17},{2,10},{10... | collective-permute-start | bytes 2211848 | tf_op jit(solution)/shard_map/ppermute | solution.py:627
  124.2 6.9 %collective-permute-start.18 = (bf16[2,2,45,16,128]{4,3,2,1,0:T(8,128)(2,1)}, bf16[2,2,45,16,128]{4,3,2,1,0:T(8,128)(2,1)}, u32[]{:S(2)}, u32[]{:S(2)}) collective-permute-start(bf16[2,2,45,16,128]{4,3,2,1,0:T(8,128)(2,1)} %get-tuple-element.72.refs_2_.refs_4_), channel_id=1, source_target_pairs={{0,8},{8,0},{16,24},{24,16},{1,9},{9,1},{17,25},{25,17},{2,10},{10... | collective-permute-start | bytes 2211848 | tf_op jit(solution)/shard_map/ppermute | solution.py:627
  124.7 6.4 %collective-permute-start.17 = (bf16[2,2,45,16,128]{4,3,2,1,0:T(8,128)(2,1)}, bf16[2,2,45,16,128]{4,3,2,1,0:T(8,128)(2,1)}, u32[]{:S(2)}, u32[]{:S(2)}) collective-permute-start(bf16[2,2,45,16,128]{4,3,2,1,0:T(8,128)(2,1)} %get-tuple-element.71.refs_1_.refs_0_), channel_id=1, source_target_pairs={{0,8},{8,0},{16,24},{24,16},{1,9},{9,1},{17,25},{25,17},{2,10},{10... | collective-permute-start | bytes 2211848 | tf_op jit(solution)/shard_map/ppermute | solution.py:627
  124.8 6.4 %collective-permute-start.16 = (bf16[1,4,45,16,128]{4,3,2,1,0:T(8,128)(2,1)}, bf16[1,4,45,16,128]{4,3,2,1,0:T(8,128)(2,1)}, u32[]{:S(2)}, u32[]{:S(2)}) collective-permute-start(bf16[1,4,45,16,128]{4,3,2,1,0:T(8,128)(2,1)} %collective-permute-done.2.refs_2_), channel_id=1, source_target_pairs={{0,8},{8,0},{16,24},{24,16},{1,9},{9,1},{17,25},{25,17},{2,10},{10... | collective-permute-start | bytes 2211848 | tf_op jit(solution)/shard_map/ppermute | solution.py:627
  131.1 15.0 %copy-start = (bf16[2,4,45,16,128]{4,3,2,1,0:T(8,128)(2,1)S(1)}, bf16[2,4,45,16,128]{4,3,2,1,0:T(8,128)(2,1)}, u32[]{:S(2)}) copy-start(bf16[2,4,45,16,128]{4,3,2,1,0:T(8,128)(2,1)} %outer_rows.3.refs_1_.refs_8_) | copy-start | bytes 4423684
  131.2 1.9 %copy-start.1 = (bf16[4,4,45,16,128]{4,3,2,1,0:T(8,128)(2,1)S(1)}, bf16[4,4,45,16,128]{4,3,2,1,0:T(8,128)(2,1)}, u32[]{:S(2)}) copy-start(bf16[4,4,45,16,128]{4,3,2,1,0:T(8,128)(2,1)} %get-tuple-element.65.refs_0_) | copy-start | bytes 8847364
  133.1 1.1 copy-start.5
  134.2 0.8 copy-start.8
  135.0 11.2 %copy-start.2 = (bf16[2,2,45,16,128]{4,3,2,1,0:T(8,128)(2,1)S(1)}, bf16[2,2,45,16,128]{4,3,2,1,0:T(8,128)(2,1)}, u32[]{:S(2)}) copy-start(bf16[2,2,45,16,128]{4,3,2,1,0:T(8,128)(2,1)} %get-tuple-element.71.refs_1_.refs_0_) | copy-start | bytes 2211844
  135.0 11.2 %copy-start.3 = (bf16[2,2,45,16,128]{4,3,2,1,0:T(8,128)(2,1)S(1)}, bf16[2,2,45,16,128]{4,3,2,1,0:T(8,128)(2,1)}, u32[]{:S(2)}) copy-start(bf16[2,2,45,16,128]{4,3,2,1,0:T(8,128)(2,1)} %get-tuple-element.72.refs_2_.refs_4_) | copy-start | bytes 2211844
  135.0 11.2 %copy-start.7 = (bf16[2,2,45,16,128]{4,3,2,1,0:T(8,128)(2,1)S(1)}, bf16[2,2,45,16,128]{4,3,2,1,0:T(8,128)(2,1)}, u32[]{:S(2)}) copy-start(bf16[2,2,45,16,128]{4,3,2,1,0:T(8,128)(2,1)} %copy-done.6) | copy-start | bytes 2211844
  135.0 11.2 %copy-start.9 = (bf16[64,256]{1,0:T(8,128)(2,1)S(1)}, bf16[64,256]{1,0:T(8,128)(2,1)}, u32[]{:S(2)}) copy-start(bf16[64,256]{1,0:T(8,128)(2,1)} %transform.1.weights) | copy-start | bytes 98308
  141.6 4.5 %collective-permute-start.22 = (bf16[2,4,45,16,128]{4,3,2,1,0:T(8,128)(2,1)}, bf16[2,4,45,16,128]{4,3,2,1,0:T(8,128)(2,1)S(1)}, u32[]{:S(2)}, u32[]{:S(2)}) collective-permute-start(bf16[2,4,45,16,128]{4,3,2,1,0:T(8,128)(2,1)} %collective-permute-done.21.refs_9_), channel_id=1, source_target_pairs={{0,8},{8,0},{16,24},{24,16},{1,9},{9,1},{17,25},{25,17},{2,10},{10... | collective-permute-start | bytes 4423688 | tf_op jit(solution)/shard_map/ppermute | solution.py:627
  141.6 4.5 %collective-permute-start.20 = (bf16[2,2,45,16,128]{4,3,2,1,0:T(8,128)(2,1)}, bf16[2,2,45,16,128]{4,3,2,1,0:T(8,128)(2,1)S(1)}, u32[]{:S(2)}, u32[]{:S(2)}) collective-permute-start(bf16[2,2,45,16,128]{4,3,2,1,0:T(8,128)(2,1)} %collective-permute-done.11.refs_5_), channel_id=1, source_target_pairs={{0,8},{8,0},{16,24},{24,16},{1,9},{9,1},{17,25},{25,17},{2,10},{10... | collective-permute-start | bytes 2211848 | tf_op jit(solution)/shard_map/ppermute | solution.py:627
